TPU v7x, 32 devices: a whole 2x2x4 slice. The times are simulated.
32 devices in a mesh: dp: 16 (over z, x, core), seq: 2 (over y).
Axes of the slice: x: 2, y: 2, z: 4, core: 2. Of those that a mesh axis runs over, the one named last changes fastest.
Arguments:
- tokens: bfloat16 [16, 512, 768], P('dp', 'seq'), may hold values from -6 to 6
- segment_ids: int32 [16, 512], P('dp', 'seq'), may hold values from 0 to 3, as said below
- padding: int32 [16, 512], P('dp', 'seq'), may hold values from 0 to 1, as said below
- query_weight: bfloat16 [3, 768, 768], P(None, 'dp'), may hold values from -0.21875 to 0.21875
- key_weight: bfloat16 [3, 768, 768], P(None, 'dp'), may hold values from -0.21875 to 0.21875
- value_weight: bfloat16 [3, 768, 768], P(None, 'dp'), may hold values from -0.21875 to 0.21875
- output_weight: bfloat16 [3, 768, 768], P(None, 'dp'), may hold values from -0.625 to 0.625
- query_bias: bfloat16 [3, 768], P(None, 'dp'), may hold values from -3 to 3
- value_bias: bfloat16 [3, 768], P(None, 'dp'), may hold values from -3 to 3
- output_bias: bfloat16 [3, 768], P(None, 'dp'), may hold values from -3 to 3
- attn_gain: bfloat16 [3, 768], P(None, 'dp'), may hold values from 0.5 to 1.5
- attn_shift: bfloat16 [3, 768], P(None, 'dp'), may hold values from -3 to 3
- inner_weight: bfloat16 [3, 768, 3072], P(None, 'dp'), may hold values from -0.21875 to 0.21875
- inner_bias: bfloat16 [3, 3072], P(None, 'dp'), may hold values from -3 to 3
- outer_weight: bfloat16 [3, 3072, 768], P(None, 'dp'), may hold values from -0.109375 to 0.109375
- outer_bias: bfloat16 [3, 768], P(None, 'dp'), may hold values from -3 to 3
- ffn_gain: bfloat16 [3, 768], P(None, 'dp'), may hold values from 0.5 to 1.5
- ffn_shift: bfloat16 [3, 768], P(None, 'dp'), may hold values from -3 to 3
- upstream: bfloat16 [16, 512, 768], P('dp', 'seq'), may hold values from -6 to 6
Outputs:
- hidden_out: bfloat16 [16, 512, 768], P('dp', 'seq')
- pooled: float32 [16, 4, 768], P('dp')
- tokens_grad: float32 [16, 512, 768], P('dp', 'seq')
- query_weight_grad: float32 [3, 768, 768], P(None, 'dp')
- key_weight_grad: float32 [3, 768, 768], P(None, 'dp')
- value_weight_grad: float32 [3, 768, 768], P(None, 'dp')
- output_weight_grad: float32 [3, 768, 768], P(None, 'dp')
- query_bias_grad: float32 [3, 768], P(None, 'dp')
- value_bias_grad: float32 [3, 768], P(None, 'dp')
- output_bias_grad: float32 [3, 768], P(None, 'dp')
- attn_gain_grad: float32 [3, 768], P(None, 'dp')
- attn_shift_grad: float32 [3, 768], P(None, 'dp')
- inner_weight_grad: float32 [3, 768, 3072], P(None, 'dp')
- inner_bias_grad: float32 [3, 3072], P(None, 'dp')
- outer_weight_grad: float32 [3, 3072, 768], P(None, 'dp')
- outer_bias_grad: float32 [3, 768], P(None, 'dp')
- ffn_gain_grad: float32 [3, 768], P(None, 'dp')
- ffn_shift_grad: float32 [3, 768], P(None, 'dp')
Inputs may be any that keep to these rules, and one draw needn't show every extreme that they name: `segment_ids`: within each row the ids start at 0, never fall and rise by one at each new text; every id names at least one real position. `padding`: in each row the zeros form a tail that lies after position 256 and inside the last text.
All inputs are finite; a program needn't handle non-finite values.
Results may differ from a plain program's by a relative error of at most 0.025.
Values may be sent and summed in bfloat16 or wider, within the bound.
No kernel may reach another device: no remote copies, remote signals or barrier semaphores. Data moves between devices by JAX's collectives and lax.ppermute only.
A program may use at most 320 MiB of HBM per device.

v0:
```python
import jax
import jax.numpy as jnp
from jax import lax
from jax.sharding import PartitionSpec as P

HD = 64
SEGS = 4


epsilon = 1e-06
masked_score = -1e30


def matmul(left, right):
    return jnp.einsum("rsd,de->rse", left, right, preferred_element_type=jnp.float32)


def matmul_back(grad, right):
    return jnp.einsum("rse,de->rsd", grad, right, preferred_element_type=jnp.float32)


def outer_sum(left, grad):
    return jnp.einsum("rsd,rse->de", left, grad, preferred_element_type=jnp.float32)


def column_sum(grad):
    return jnp.sum(grad, axis=(0, 1), dtype=jnp.float32)


def gelu_exact(values):
    return jax.nn.gelu(values, approximate=False)


def normalize(values):
    center = values - jnp.mean(values, axis=-1, keepdims=True)
    inverse = lax.rsqrt(jnp.mean(center * center, axis=-1, keepdims=True) + epsilon)
    return (center * inverse, inverse)


def norm_back(normed, inverse, gain, grad):
    scaled = grad * gain
    back = inverse * (
        scaled
        - jnp.mean(scaled, axis=-1, keepdims=True)
        - normed * jnp.mean(scaled * normed, axis=-1, keepdims=True)
    )
    return (back, jnp.sum(grad * normed, axis=(0, 1)), jnp.sum(grad, axis=(0, 1)))


def split_heads(values):
    rows, length, width = values.shape
    return values.reshape(rows, length, width // HD, HD).transpose(2, 0, 1, 3)


def join_heads(values):
    count, rows, length, size = values.shape
    return values.transpose(1, 2, 0, 3).reshape(rows, length, count * size)


def head_scores(query_head, key_head, allowed):
    scores = jnp.einsum(
        "rqd,rkd->rqk", query_head, key_head, preferred_element_type=jnp.float32
    ) * HD ** (-0.5)
    return jnp.where(allowed, scores, masked_score)


def attend(query_low, key_low, value_low, allowed):

    def one_head(items):
        query_head, key_head, value_head = items
        scores = head_scores(query_head, key_head, allowed)
        largest = jnp.max(scores, axis=-1, keepdims=True)
        expos = jnp.exp(scores - largest)
        totals = jnp.sum(expos, axis=-1, keepdims=True)
        probs_low = (expos / totals).astype(jnp.bfloat16)
        mixed = jnp.einsum(
            "rqk,rkd->rqd", probs_low, value_head, preferred_element_type=jnp.float32
        )
        return (mixed, largest[..., 0] + jnp.log(totals[..., 0]))

    mixed, log_totals = lax.map(
        one_head, (split_heads(query_low), split_heads(key_low), split_heads(value_low))
    )
    return (join_heads(mixed), log_totals)


def attend_back(query_low, key_low, value_low, allowed, log_totals, grad_low):

    def one_head(items):
        query_head, key_head, value_head, log_head, grad_head = items
        scores = head_scores(query_head, key_head, allowed)
        probs = jnp.exp(scores - log_head[..., None])
        probs_low = probs.astype(jnp.bfloat16)
        grad_probs = jnp.einsum(
            "rqd,rkd->rqk", grad_head, value_head, preferred_element_type=jnp.float32
        )
        grad_scores = probs * (grad_probs - jnp.sum(probs * grad_probs, axis=-1, keepdims=True))
        scores_low = grad_scores.astype(jnp.bfloat16)
        grad_query = jnp.einsum(
            "rqk,rkd->rqd", scores_low, key_head, preferred_element_type=jnp.float32
        ) * HD ** (-0.5)
        grad_key = jnp.einsum(
            "rqk,rqd->rkd", scores_low, query_head, preferred_element_type=jnp.float32
        ) * HD ** (-0.5)
        grad_value = jnp.einsum(
            "rqk,rqd->rkd", probs_low, grad_head, preferred_element_type=jnp.float32
        )
        return (grad_query, grad_key, grad_value)

    grad_query, grad_key, grad_value = lax.map(
        one_head,
        (
            split_heads(query_low),
            split_heads(key_low),
            split_heads(value_low),
            log_totals,
            split_heads(grad_low),
        ),
    )
    return (join_heads(grad_query), join_heads(grad_key), join_heads(grad_value))


def project(current, weights):
    tokens_low = current.astype(jnp.bfloat16)
    query_low = (matmul(tokens_low, weights[0]) + weights[4].astype(jnp.float32)).astype(
        jnp.bfloat16
    )
    key_low = matmul(tokens_low, weights[1]).astype(jnp.bfloat16)
    value_low = (matmul(tokens_low, weights[2]) + weights[5].astype(jnp.float32)).astype(
        jnp.bfloat16
    )
    return (tokens_low, query_low, key_low, value_low)


def layer_rest(current, query_low, key_value, allowed, weights):
    mixed, log_totals = attend(query_low, key_value[0], key_value[1], allowed)
    mixed_low = mixed.astype(jnp.bfloat16)
    branch = matmul(mixed_low, weights[3]) + weights[6].astype(jnp.float32)
    normed_one, inverse_one = normalize(current + branch)
    hidden = normed_one * weights[7].astype(jnp.float32) + weights[8].astype(jnp.float32)
    hidden_low = hidden.astype(jnp.bfloat16)
    inner = matmul(hidden_low, weights[9]) + weights[10].astype(jnp.float32)
    active_low = gelu_exact(inner).astype(jnp.bfloat16)
    outer = matmul(active_low, weights[11]) + weights[12].astype(jnp.float32)
    normed_two, inverse_two = normalize(hidden + outer)
    result = normed_two * weights[13].astype(jnp.float32) + weights[14].astype(jnp.float32)
    saved = (
        mixed_low,
        log_totals,
        normed_one,
        inverse_one,
        hidden_low,
        inner,
        active_low,
        normed_two,
        inverse_two,
    )
    return (result, saved)


def body(
    tokens,
    segment_ids,
    padding,
    query_weight,
    key_weight,
    value_weight,
    output_weight,
    query_bias,
    value_bias,
    output_bias,
    attn_gain,
    attn_shift,
    inner_weight,
    inner_bias,
    outer_weight,
    outer_bias,
    ffn_gain,
    ffn_shift,
    upstream,
):
    layers = query_weight.shape[0]
    labels_own = jnp.where(padding == 1, segment_ids, -1)
    labels_row = lax.all_gather(labels_own, "seq", axis=1, tiled=True)
    allowed = segment_ids[:, :, None] == labels_row[:, None, :]
    current = tokens.astype(jnp.float32)
    inputs_list = []
    weights_list = []
    pairs_list = []
    for layer_index in range(layers):
        weights = (
            lax.all_gather(query_weight[layer_index], "dp", axis=0, tiled=True),
            lax.all_gather(key_weight[layer_index], "dp", axis=0, tiled=True),
            lax.all_gather(value_weight[layer_index], "dp", axis=0, tiled=True),
            lax.all_gather(output_weight[layer_index], "dp", axis=0, tiled=True),
            lax.all_gather(query_bias[layer_index], "dp", axis=0, tiled=True),
            lax.all_gather(value_bias[layer_index], "dp", axis=0, tiled=True),
            lax.all_gather(output_bias[layer_index], "dp", axis=0, tiled=True),
            lax.all_gather(attn_gain[layer_index], "dp", axis=0, tiled=True),
            lax.all_gather(attn_shift[layer_index], "dp", axis=0, tiled=True),
            lax.all_gather(inner_weight[layer_index], "dp", axis=0, tiled=True),
            lax.all_gather(inner_bias[layer_index], "dp", axis=0, tiled=True),
            lax.all_gather(outer_weight[layer_index], "dp", axis=0, tiled=True),
            lax.all_gather(outer_bias[layer_index], "dp", axis=0, tiled=True),
            lax.all_gather(ffn_gain[layer_index], "dp", axis=0, tiled=True),
            lax.all_gather(ffn_shift[layer_index], "dp", axis=0, tiled=True),
        )
        inputs_list.append(current)
        weights_list.append(weights)
        tokens_low, query_low, key_low, value_low = project(current, weights)
        key_value = (
            lax.all_gather(key_low, "seq", axis=1, tiled=True),
            lax.all_gather(value_low, "seq", axis=1, tiled=True),
        )
        pairs_list.append(key_value)
        current, saved = layer_rest(current, query_low, key_value, allowed, weights)
    hidden_out = current.astype(jnp.bfloat16)
    labels_range = jnp.arange(SEGS, dtype=jnp.int32)
    onehot = ((segment_ids[..., None] == labels_range) & (padding[..., None] == 1)).astype(
        jnp.float32
    )
    sums = jnp.einsum("rls,rld->rsd", onehot, current, precision=lax.Precision.HIGHEST)
    sums = lax.psum(sums, "seq")
    counts = jnp.sum((labels_row[..., None] == labels_range).astype(jnp.float32), axis=1)
    pooled = sums / counts[..., None]
    grad_out = upstream.astype(jnp.float32)
    collected = [None] * layers
    for layer_index in reversed(range(layers)):
        weights = (
            lax.all_gather(query_weight[layer_index], "dp", axis=0, tiled=True),
            lax.all_gather(key_weight[layer_index], "dp", axis=0, tiled=True),
            lax.all_gather(value_weight[layer_index], "dp", axis=0, tiled=True),
            lax.all_gather(output_weight[layer_index], "dp", axis=0, tiled=True),
            lax.all_gather(query_bias[layer_index], "dp", axis=0, tiled=True),
            lax.all_gather(value_bias[layer_index], "dp", axis=0, tiled=True),
            lax.all_gather(output_bias[layer_index], "dp", axis=0, tiled=True),
            lax.all_gather(attn_gain[layer_index], "dp", axis=0, tiled=True),
            lax.all_gather(attn_shift[layer_index], "dp", axis=0, tiled=True),
            lax.all_gather(inner_weight[layer_index], "dp", axis=0, tiled=True),
            lax.all_gather(inner_bias[layer_index], "dp", axis=0, tiled=True),
            lax.all_gather(outer_weight[layer_index], "dp", axis=0, tiled=True),
            lax.all_gather(outer_bias[layer_index], "dp", axis=0, tiled=True),
            lax.all_gather(ffn_gain[layer_index], "dp", axis=0, tiled=True),
            lax.all_gather(ffn_shift[layer_index], "dp", axis=0, tiled=True),
        )
        layer_input = inputs_list[layer_index]
        tokens_low, query_low, key_low, value_low = project(layer_input, weights)
        key_value = (
            lax.all_gather(key_low, "seq", axis=1, tiled=True),
            lax.all_gather(value_low, "seq", axis=1, tiled=True),
        )
        result, saved = layer_rest(layer_input, query_low, key_value, allowed, weights)
        (
            mixed_low,
            log_totals,
            normed_one,
            inverse_one,
            hidden_low,
            inner,
            active_low,
            normed_two,
            inverse_two,
        ) = saved
        grad_two, ffn_gain_part, ffn_shift_part = norm_back(
            normed_two, inverse_two, weights[13].astype(jnp.float32), grad_out
        )
        outer_low = grad_two.astype(jnp.bfloat16)
        outer_weight_part = outer_sum(active_low, outer_low)
        outer_bias_part = column_sum(outer_low)
        grad_active = matmul_back(outer_low, weights[11])
        unused_value, gelu_back = jax.vjp(gelu_exact, inner)
        inner_low = gelu_back(grad_active)[0].astype(jnp.bfloat16)
        inner_weight_part = outer_sum(hidden_low, inner_low)
        inner_bias_part = column_sum(inner_low)
        grad_hidden = grad_two + matmul_back(inner_low, weights[9])
        grad_one, attn_gain_part, attn_shift_part = norm_back(
            normed_one, inverse_one, weights[7].astype(jnp.float32), grad_hidden
        )
        branch_low = grad_one.astype(jnp.bfloat16)
        output_weight_part = outer_sum(mixed_low, branch_low)
        output_bias_part = column_sum(branch_low)
        grad_mixed = matmul_back(branch_low, weights[3]).astype(jnp.bfloat16)
        grad_query, grad_key_row, grad_value_row = attend_back(
            query_low, key_value[0], key_value[1], allowed, log_totals, grad_mixed
        )
        grad_key, grad_value = (
            lax.psum_scatter(
                grad_key_row.astype(jnp.bfloat16), "seq", scatter_dimension=1, tiled=True
            ).astype(jnp.float32),
            lax.psum_scatter(
                grad_value_row.astype(jnp.bfloat16), "seq", scatter_dimension=1, tiled=True
            ).astype(jnp.float32),
        )
        query_grad_low = grad_query.astype(jnp.bfloat16)
        key_grad_low = grad_key.astype(jnp.bfloat16)
        value_grad_low = grad_value.astype(jnp.bfloat16)
        query_weight_part = outer_sum(tokens_low, query_grad_low)
        query_bias_part = column_sum(query_grad_low)
        key_weight_part = outer_sum(tokens_low, key_grad_low)
        value_weight_part = outer_sum(tokens_low, value_grad_low)
        value_bias_part = column_sum(value_grad_low)
        grad_out = (
            grad_one
            + matmul_back(query_grad_low, weights[0])
            + matmul_back(key_grad_low, weights[1])
            + matmul_back(value_grad_low, weights[2])
        )
        shares = (
            lax.psum_scatter(query_weight_part, ("dp", "seq"), scatter_dimension=0, tiled=True),
            lax.psum_scatter(key_weight_part, ("dp", "seq"), scatter_dimension=0, tiled=True),
            lax.psum_scatter(value_weight_part, ("dp", "seq"), scatter_dimension=0, tiled=True),
            lax.psum_scatter(output_weight_part, ("dp", "seq"), scatter_dimension=0, tiled=True),
            lax.psum_scatter(query_bias_part, ("dp", "seq"), scatter_dimension=0, tiled=True),
            lax.psum_scatter(value_bias_part, ("dp", "seq"), scatter_dimension=0, tiled=True),
            lax.psum_scatter(output_bias_part, ("dp", "seq"), scatter_dimension=0, tiled=True),
            lax.psum_scatter(attn_gain_part, ("dp", "seq"), scatter_dimension=0, tiled=True),
            lax.psum_scatter(attn_shift_part, ("dp", "seq"), scatter_dimension=0, tiled=True),
            lax.psum_scatter(inner_weight_part, ("dp", "seq"), scatter_dimension=0, tiled=True),
            lax.psum_scatter(inner_bias_part, ("dp", "seq"), scatter_dimension=0, tiled=True),
            lax.psum_scatter(outer_weight_part, ("dp", "seq"), scatter_dimension=0, tiled=True),
            lax.psum_scatter(outer_bias_part, ("dp", "seq"), scatter_dimension=0, tiled=True),
            lax.psum_scatter(ffn_gain_part, ("dp", "seq"), scatter_dimension=0, tiled=True),
            lax.psum_scatter(ffn_shift_part, ("dp", "seq"), scatter_dimension=0, tiled=True),
        )
        collected[layer_index] = (
            lax.all_gather(shares[0].astype(jnp.bfloat16), "seq", axis=0, tiled=True).astype(
                jnp.float32
            ),
            lax.all_gather(shares[1].astype(jnp.bfloat16), "seq", axis=0, tiled=True).astype(
                jnp.float32
            ),
            lax.all_gather(shares[2].astype(jnp.bfloat16), "seq", axis=0, tiled=True).astype(
                jnp.float32
            ),
            lax.all_gather(shares[3].astype(jnp.bfloat16), "seq", axis=0, tiled=True).astype(
                jnp.float32
            ),
            lax.all_gather(shares[4].astype(jnp.bfloat16), "seq", axis=0, tiled=True).astype(
                jnp.float32
            ),
            lax.all_gather(shares[5].astype(jnp.bfloat16), "seq", axis=0, tiled=True).astype(
                jnp.float32
            ),
            lax.all_gather(shares[6].astype(jnp.bfloat16), "seq", axis=0, tiled=True).astype(
                jnp.float32
            ),
            lax.all_gather(shares[7].astype(jnp.bfloat16), "seq", axis=0, tiled=True).astype(
                jnp.float32
            ),
            lax.all_gather(shares[8].astype(jnp.bfloat16), "seq", axis=0, tiled=True).astype(
                jnp.float32
            ),
            lax.all_gather(shares[9].astype(jnp.bfloat16), "seq", axis=0, tiled=True).astype(
                jnp.float32
            ),
            lax.all_gather(shares[10].astype(jnp.bfloat16), "seq", axis=0, tiled=True).astype(
                jnp.float32
            ),
            lax.all_gather(shares[11].astype(jnp.bfloat16), "seq", axis=0, tiled=True).astype(
                jnp.float32
            ),
            lax.all_gather(shares[12].astype(jnp.bfloat16), "seq", axis=0, tiled=True).astype(
                jnp.float32
            ),
            lax.all_gather(shares[13].astype(jnp.bfloat16), "seq", axis=0, tiled=True).astype(
                jnp.float32
            ),
            lax.all_gather(shares[14].astype(jnp.bfloat16), "seq", axis=0, tiled=True).astype(
                jnp.float32
            ),
        )
    stacked = [
        jnp.stack([collected[index][member] for index in range(layers)]) for member in range(15)
    ]
    return (
        hidden_out,
        pooled,
        grad_out,
        stacked[0],
        stacked[1],
        stacked[2],
        stacked[3],
        stacked[4],
        stacked[5],
        stacked[6],
        stacked[7],
        stacked[8],
        stacked[9],
        stacked[10],
        stacked[11],
        stacked[12],
        stacked[13],
        stacked[14],
    )


def solution(mesh):
    return jax.shard_map(
        body,
        mesh=mesh,
        in_specs=(
            P("dp", "seq", None),
            P("dp", "seq"),
            P("dp", "seq"),
            P(None, "dp", None),
            P(None, "dp", None),
            P(None, "dp", None),
            P(None, "dp", None),
            P(None, "dp"),
            P(None, "dp"),
            P(None, "dp"),
            P(None, "dp"),
            P(None, "dp"),
            P(None, "dp", None),
            P(None, "dp"),
            P(None, "dp", None),
            P(None, "dp"),
            P(None, "dp"),
            P(None, "dp"),
            P("dp", "seq", None),
        ),
        out_specs=(
            P("dp", "seq", None),
            P("dp", None, None),
            P("dp", "seq", None),
            P(None, "dp", None),
            P(None, "dp", None),
            P(None, "dp", None),
            P(None, "dp", None),
            P(None, "dp"),
            P(None, "dp"),
            P(None, "dp"),
            P(None, "dp"),
            P(None, "dp"),
            P(None, "dp", None),
            P(None, "dp"),
            P(None, "dp", None),
            P(None, "dp"),
            P(None, "dp"),
            P(None, "dp"),
        ),
        check_vma=False,
    )
```

profile of v0, /device:TPU:0, one launch (start us, length us, event | category | flops | bytes accessed | tf_op | source)
XLA Modules:
  0.0 3438.9 jit_solution(12353466489797969938)
XLA Ops:
  33.1 64.3 %all-reduce.82 = (bf16[3072]{0:T(1024)(128)(2,1)S(1)}, bf16[3072]{0:T(1024)(128)(2,1)S(1)}, bf16[3072]{0:T(1024)(128)(2,1)S(1)}, bf16[768]{0:T(1024)(128)(2,1)S(...) all-reduce(bf16[3072]{0:T(1024)(128)(2,1)S(1)} %dynamic-update-slic, ...), channel_id=48, replica_groups=mesh['dp'=16,'seq'=2] {'dp'}, use_global_device_ids=true, to_apply=%add.23 | all-reduce | flops 27648 | bytes 110592
  117.7 8.5 all-gather.6
  134.8 12.2 all-gather.3
  150.7 27.9 while.117
  182.8 44.7 %all-gather.78.cloned.1.call-done = bf16[1,768,3072]{2,1,0:T(8,128)(2,1)} async-done(((bf16[1,48,3072]{2,1,0:T(8,128)(2,1)}), bf16[1,768,3072]{2,1,0:T(8,128)(2,1)}) %all-gather.78.cloned.1.call-update) | async-done | bytes 4718608 | tf_op jit(solution)/shard_map/all_gather | solution.py:201
  227.5 54.5 %all-gather.80.cloned.1.call-done = bf16[1,3072,768]{2,1,0:T(8,128)(2,1)} async-done(((bf16[1,192,768]{2,1,0:T(8,128)(2,1)}), bf16[1,3072,768]{2,1,0:T(8,128)(2,1)}) %all-gather.80.cloned.1.call-update) | async-done | bytes 4718608 | tf_op jit(solution)/shard_map/all_gather | solution.py:203
  282.0 14.1 fusion.793
  298.9 22.3 all-gather.86.cloned.1.call-done
  323.0 12.0 all-gather.23
  336.1 24.7 all-gather.84.cloned.1.call-done
  362.6 12.0 all-gather.20
  377.5 22.9 all-gather.82.cloned.1.call-done
  405.3 29.3 while.118
  443.1 51.9 %all-gather.90.cloned.1.call-done = bf16[1,768,3072]{2,1,0:T(8,128)(2,1)} async-done(((bf16[1,48,3072]{2,1,0:T(8,128)(2,1)}), bf16[1,768,3072]{2,1,0:T(8,128)(2,1)}) %all-gather.90.cloned.1.call-update) | async-done | bytes 4718608 | tf_op jit(solution)/shard_map/all_gather | solution.py:201
  495.1 54.0 %all-gather.92.cloned.1.call-done = bf16[1,3072,768]{2,1,0:T(8,128)(2,1)} async-done(((bf16[1,192,768]{2,1,0:T(8,128)(2,1)}), bf16[1,3072,768]{2,1,0:T(8,128)(2,1)}) %all-gather.92.cloned.1.call-update) | async-done | bytes 4718608 | tf_op jit(solution)/shard_map/all_gather | solution.py:203
  549.0 14.2 fusion.799
  566.0 22.3 all-gather.96.cloned.1.call-done
  590.0 37.7 %all-gather.98.cloned.1.call-done = bf16[1,768,768]{2,1,0:T(8,128)(2,1)} async-done(((bf16[1,48,768]{2,1,0:T(8,128)(2,1)}), bf16[1,768,768]{2,1,0:T(8,128)(2,1)}) %all-gather.98.cloned.1.call-update) | async-done | bytes 1179664 | tf_op jit(solution)/shard_map/all_gather | solution.py:194
  629.4 12.0 all-gather.40
  643.2 11.4 all-gather.37
  656.1 11.0 all-gather.94.cloned.1.call-done
  669.5 21.3 while.119
  690.8 15.9 all-gather.100.cloned.1.call-done
  709.7 51.9 %all-gather.102.cloned.1.call-done = bf16[1,768,3072]{2,1,0:T(8,128)(2,1)} async-done(((bf16[1,48,3072]{2,1,0:T(8,128)(2,1)}), bf16[1,768,3072]{2,1,0:T(8,128)(2,1)}) %all-gather.102.cloned.1.call-update) | async-done | bytes 4718608 | tf_op jit(solution)/shard_map/all_gather | solution.py:201
  761.6 54.0 %all-gather.104.cloned.1.call-done = bf16[1,3072,768]{2,1,0:T(8,128)(2,1)} async-done(((bf16[1,192,768]{2,1,0:T(8,128)(2,1)}), bf16[1,3072,768]{2,1,0:T(8,128)(2,1)}) %all-gather.104.cloned.1.call-update) | async-done | bytes 4718608 | tf_op jit(solution)/shard_map/all_gather | solution.py:203
  815.6 13.4 fusion.807
  830.8 38.5 %while.122 = (s32[]{:T(128)}, bf16[12,1,256,64]{2,3,1,0:T(8,128)(2,1)S(1)}, f32[12,1,256]{2,1,0:T(1,128)}, bf16[12,1,256,64]{3,2,1,0:T(8,128)(2,1)}, bf16[12,1,5...) while((s32[]{:T(128)}, ...), condition=%wide.region_45.46_spmd.clone, body=%wide.region_42.45_spmd.clone.sunk | while | flops 34733824 | bytes 1982045 | solution.py:81
  872.4 9.8 multiply_convert_fusion.3
  893.7 67.9 %while.123 = (s32[]{:T(128)}, bf16[12,1,256,64]{2,3,1,0:T(8,128)(2,1)S(1)}, bf16[12,1,512,64]{2,3,1,0:T(8,128)(2,1)S(1)}, bf16[12,1,512,64]{2,3,1,0:T(8,128)(2,1...) while((s32[]{:T(128)}, ...), condition=%wide.region_56.57_spmd.clone, body=%wide.region_54.56_spmd.clone.sunk | while | flops 85245696 | bytes 4863097 | solution.py:110
  962.8 33.0 while.121
  998.3 11.8 multiply_convert_fusion.4
  1022.7 6.4 convert_reduce_fusion.1
  1034.9 82.9 %while.124 = (s32[]{:T(128)}, bf16[12,1,256,64]{2,3,1,0:T(8,128)(2,1)S(1)}, bf16[12,1,512,64]{2,3,1,0:T(8,128)(2,1)}, bf16[12,1,512,64]{2,3,1,0:T(8,128)(2,1)}, ...) while((s32[]{:T(128)}, ...), condition=%wide.region_65.66_spmd.clone, body=%wide.region_63.65_spmd.clone.sunk | while | flops 85245696 | bytes 4863097 | solution.py:110
  1118.6 32.9 while.120
  1154.4 11.5 multiply_convert_fusion.5
  1180.5 6.4 convert_reduce_fusion.2
  1196.0 99.4 %while.125 = (s32[]{:T(128)}, bf16[12,1,256,64]{2,3,1,0:T(8,128)(2,1)}, bf16[12,1,512,64]{2,3,1,0:T(8,128)(2,1)}, bf16[12,1,512,64]{2,3,1,0:T(8,128)(2,1)}, bf16...) while((s32[]{:T(128)}, ...), condition=%wide.region_74.75_spmd.clone, body=%wide.region_72.74_spmd.clone.sunk | while | flops 85245696 | bytes 4863097 | solution.py:110
  1337.4 6.5 fusion.623
  1345.0 6.7 fusion.773
  1352.9 6.6 fusion.611
  1360.6 6.7 fusion.770
  1368.4 6.5 fusion.599
  1375.6 6.5 fusion.767
  1390.2 7.6 psum.7
  1400.8 34.8 %reduce-scatter.59.cloned.1.call-done = f32[24,768]{1,0:T(8,128)} async-done(((f32[768,768]{1,0:T(8,128)}), f32[24,768]{1,0:T(8,128)}) %reduce-scatter.59.cloned.1.call-update) | async-done | bytes 73744 | tf_op jit(solution)/shard_map/reduce_scatter | solution.py:312
  1436.5 103.2 %reduce-scatter.77.cloned.1.call-done = f32[24,768]{1,0:T(8,128)} async-done(((f32[768,768]{1,0:T(8,128)}), f32[24,768]{1,0:T(8,128)}) %reduce-scatter.77.cloned.1.call-update) | async-done | bytes 73744 | tf_op jit(solution)/shard_map/reduce_scatter | solution.py:309
  1550.4 43.7 %all-reduce.81 = (bf16[768]{0:T(1024)(128)(2,1)S(1)}, bf16[768]{0:T(1024)(128)(2,1)S(1)}, bf16[768]{0:T(1024)(128)(2,1)S(1)}, bf16[768]{0:T(1024)(128)(2,1)S(1)}...) all-reduce(f32[768]{0:T(1024)S(1)} %reduce_sum.705, ...), channel_id=73, replica_groups=mesh['dp'=16,'seq'=2] {'dp','seq'}, use_global_device_ids=true, to_apply=%region_94.95.clone | all-reduce | flops 27648 | bytes 165888
  1602.0 8.5 all-reduce.83
  1610.6 32.3 reduce-scatter.57.cloned.1.call-done
  1643.8 103.3 %reduce-scatter.89.cloned.1.call-done = f32[24,768]{1,0:T(8,128)} async-done(((f32[768,768]{1,0:T(8,128)}), f32[24,768]{1,0:T(8,128)}) %reduce-scatter.89.cloned.1.call-update) | async-done | bytes 73744 | tf_op jit(solution)/shard_map/reduce_scatter | solution.py:311
  1748.0 102.4 %reduce-scatter.83.cloned.1.call-done = f32[24,768]{1,0:T(8,128)} async-done(((f32[768,768]{1,0:T(8,128)}), f32[24,768]{1,0:T(8,128)}) %reduce-scatter.83.cloned.1.call-update) | async-done | bytes 73744 | tf_op jit(solution)/shard_map/reduce_scatter | solution.py:310
  1851.4 103.2 %reduce-scatter.75.cloned.1.call-done = f32[24,768]{1,0:T(8,128)} async-done(((f32[768,768]{1,0:T(8,128)}), f32[24,768]{1,0:T(8,128)}) %reduce-scatter.75.cloned.1.call-update) | async-done | bytes 73744 | tf_op jit(solution)/shard_map/reduce_scatter | solution.py:309
  1984.8 73.1 %reduce-scatter.55.cloned.1.call-done = f32[24,768]{1,0:T(8,128)} async-done(((f32[768,768]{1,0:T(8,128)}), f32[24,768]{1,0:T(8,128)}) %reduce-scatter.55.cloned.1.call-update) | async-done | bytes 73744 | tf_op jit(solution)/shard_map/reduce_scatter | solution.py:312
  2058.8 103.3 %reduce-scatter.87.cloned.1.call-done = f32[24,768]{1,0:T(8,128)} async-done(((f32[768,768]{1,0:T(8,128)}), f32[24,768]{1,0:T(8,128)}) %reduce-scatter.87.cloned.1.call-update) | async-done | bytes 73744 | tf_op jit(solution)/shard_map/reduce_scatter | solution.py:311
  2163.0 102.3 %reduce-scatter.81.cloned.1.call-done = f32[24,768]{1,0:T(8,128)} async-done(((f32[768,768]{1,0:T(8,128)}), f32[24,768]{1,0:T(8,128)}) %reduce-scatter.81.cloned.1.call-update) | async-done | bytes 73744 | tf_op jit(solution)/shard_map/reduce_scatter | solution.py:310
  2266.2 103.3 %reduce-scatter.73.cloned.1.call-done = f32[24,768]{1,0:T(8,128)} async-done(((f32[768,768]{1,0:T(8,128)}), f32[24,768]{1,0:T(8,128)}) %reduce-scatter.73.cloned.1.call-update) | async-done | bytes 73744 | tf_op jit(solution)/shard_map/reduce_scatter | solution.py:309
  2390.6 82.3 %reduce-scatter.85.cloned.1.call-done = f32[24,768]{1,0:T(8,128)} async-done(((f32[768,768]{1,0:T(8,128)}), f32[24,768]{1,0:T(8,128)}) %reduce-scatter.85.cloned.1.call-update) | async-done | bytes 73744 | tf_op jit(solution)/shard_map/reduce_scatter | solution.py:311
  2473.8 103.2 %reduce-scatter.79.cloned.1.call-done = f32[24,768]{1,0:T(8,128)} async-done(((f32[768,768]{1,0:T(8,128)}), f32[24,768]{1,0:T(8,128)}) %reduce-scatter.79.cloned.1.call-update) | async-done | bytes 73744 | tf_op jit(solution)/shard_map/reduce_scatter | solution.py:310
  2588.7 128.7 %reduce-scatter.71.cloned.1.call-done = f32[96,768]{1,0:T(8,128)} async-done(((f32[3072,768]{1,0:T(8,128)}), f32[96,768]{1,0:T(8,128)}) %reduce-scatter.71.cloned.1.call-update) | async-done | bytes 294928 | tf_op jit(solution)/shard_map/reduce_scatter | solution.py:320
  2718.4 140.3 %reduce-scatter.65.cloned.1.call-done = f32[24,3072]{1,0:T(8,128)} async-done(((f32[768,3072]{1,0:T(8,128)}), f32[24,3072]{1,0:T(8,128)}) %reduce-scatter.65.cloned.1.call-update) | async-done | bytes 294928 | tf_op jit(solution)/shard_map/reduce_scatter | solution.py:318
  2871.3 127.8 %reduce-scatter.69.cloned.1.call-done = f32[96,768]{1,0:T(8,128)} async-done(((f32[3072,768]{1,0:T(8,128)}), f32[96,768]{1,0:T(8,128)}) %reduce-scatter.69.cloned.1.call-update) | async-done | bytes 294928 | tf_op jit(solution)/shard_map/reduce_scatter | solution.py:320
  3000.1 140.6 %reduce-scatter.63.cloned.1.call-done = f32[24,3072]{1,0:T(8,128)} async-done(((f32[768,3072]{1,0:T(8,128)}), f32[24,3072]{1,0:T(8,128)}) %reduce-scatter.63.cloned.1.call-update) | async-done | bytes 294928 | tf_op jit(solution)/shard_map/reduce_scatter | solution.py:318
  3153.2 127.9 %reduce-scatter.67.cloned.1.call-done = f32[96,768]{1,0:T(8,128)} async-done(((f32[3072,768]{1,0:T(8,128)}), f32[96,768]{1,0:T(8,128)}) %reduce-scatter.67.cloned.1.call-update) | async-done | bytes 294928 | tf_op jit(solution)/shard_map/reduce_scatter | solution.py:320
  3288.0 134.8 %reduce-scatter.61.cloned.1.call-done = f32[24,3072]{1,0:T(8,128)} async-done(((f32[768,3072]{1,0:T(8,128)}), f32[24,3072]{1,0:T(8,128)}) %reduce-scatter.61.cloned.1.call-update) | async-done | bytes 294928 | tf_op jit(solution)/shard_map/reduce_scatter | solution.py:318
  (1335 shorter events, 775.2 us)
Async XLA Ops:
  7.2 108.8 %all-gather.74.cloned.1.call-start = ((), (), s32[]{:S(2)}) async-start(), calls=%async_computation.41 | async-start | bytes 1253376 | tf_op jit(solution)/shard_map/all_gather | solution.py:194
  9.0 118.4 %all-gather.70.cloned.1.call-start = ((), (), s32[]{:S(2)}) async-start(), calls=%async_computation.39 | async-start | bytes 1253376 | tf_op jit(solution)/shard_map/all_gather | solution.py:192
  10.7 122.3 %all-gather.72.cloned.1.call-start = ((), (), s32[]{:S(2)}) async-start(), calls=%async_computation.40 | async-start | bytes 1253376 | tf_op jit(solution)/shard_map/all_gather | solution.py:193
  12.4 166.2 %all-gather.76.cloned.1.call-start = ((), (), s32[]{:S(2)}) async-start(), calls=%async_computation.42 | async-start | bytes 1253376 | tf_op jit(solution)/shard_map/all_gather | solution.py:195
  14.2 83.8 %copy-start.61 = (s32[1,256]{1,0:T(1,128)S(1)}, s32[1,256]{1,0:T(1,128)}, u32[]{:S(2)}) copy-start(s32[1,256]{1,0:T(1,128)} %param.38) | copy-start | bytes 3076
  14.2 83.8 %copy-start.140 = (s32[1,256]{1,0:T(1,128)S(1)}, s32[1,256]{1,0:T(1,128)}, u32[]{:S(2)}) copy-start(s32[1,256]{1,0:T(1,128)} %param.39) | copy-start | bytes 3076
  14.3 101.7 %copy-start = (bf16[1,256,768]{2,1,0:T(8,128)(2,1)S(1)}, bf16[1,256,768]{2,1,0:T(8,128)(2,1)}, u32[]{:S(2)}) copy-start(bf16[1,256,768]{2,1,0:T(8,128)(2,1)} %param.37) | copy-start | bytes 1179652
  14.3 213.2 %all-gather.78.cloned.1.call-start = ((), (), s32[]{:S(2)}) async-start(), calls=%async_computation.43 | async-start | bytes 5013504 | tf_op jit(solution)/shard_map/all_gather | solution.py:201
  16.5 265.5 %all-gather.80.cloned.1.call-start = ((), (), s32[]{:S(2)}) async-start(), calls=%async_computation.44 | async-start | bytes 5013504 | tf_op jit(solution)/shard_map/all_gather | solution.py:203
  17.5 303.7 %all-gather.86.cloned.1.call-start = ((), (), s32[]{:S(2)}) async-start(), calls=%async_computation.47 | async-start | bytes 1253376 | tf_op jit(solution)/shard_map/all_gather | solution.py:194
  18.3 342.5 %all-gather.84.cloned.1.call-start = ((), (), s32[]{:S(2)}) async-start(), calls=%async_computation.46 | async-start | bytes 1253376 | tf_op jit(solution)/shard_map/all_gather | solution.py:193
  19.0 381.4 %all-gather.82.cloned.1.call-start = ((), (), s32[]{:S(2)}) async-start(), calls=%async_computation.45 | async-start | bytes 1253376 | tf_op jit(solution)/shard_map/all_gather | solution.py:192
  19.7 420.1 %all-gather.88.cloned.1.call-start = ((), (), s32[]{:S(2)}) async-start(), calls=%async_computation.48 | async-start | bytes 1253376 | tf_op jit(solution)/shard_map/all_gather | solution.py:195
  20.3 474.7 %all-gather.90.cloned.1.call-start = ((), (), s32[]{:S(2)}) async-start(), calls=%async_computation.49 | async-start | bytes 5013504 | tf_op jit(solution)/shard_map/all_gather | solution.py:201
  21.1 527.9 %all-gather.92.cloned.1.call-start = ((), (), s32[]{:S(2)}) async-start(), calls=%async_computation.50 | async-start | bytes 5013504 | tf_op jit(solution)/shard_map/all_gather | solution.py:203
  21.6 566.6 %all-gather.96.cloned.1.call-start = ((), (), s32[]{:S(2)}) async-start(), calls=%async_computation.52 | async-start | bytes 1253376 | tf_op jit(solution)/shard_map/all_gather | solution.py:193
  22.4 605.3 %all-gather.98.cloned.1.call-start = ((), (), s32[]{:S(2)}) async-start(), calls=%async_computation.53 | async-start | bytes 1253376 | tf_op jit(solution)/shard_map/all_gather | solution.py:194
  23.0 644.1 %all-gather.94.cloned.1.call-start = ((), (), s32[]{:S(2)}) async-start(), calls=%async_computation.51 | async-start | bytes 1253376 | tf_op jit(solution)/shard_map/all_gather | solution.py:192
  23.6 683.1 %all-gather.100.cloned.1.call-start = ((), (), s32[]{:S(2)}) async-start(), calls=%async_computation.54 | async-start | bytes 1253376 | tf_op jit(solution)/shard_map/all_gather | solution.py:195
  24.1 737.5 %all-gather.102.cloned.1.call-start = ((), (), s32[]{:S(2)}) async-start(), calls=%async_computation.55 | async-start | bytes 5013504 | tf_op jit(solution)/shard_map/all_gather | solution.py:201
  24.7 790.9 %all-gather.104.cloned.1.call-start = ((), (), s32[]{:S(2)}) async-start(), calls=%async_computation.56 | async-start | bytes 5013504 | tf_op jit(solution)/shard_map/all_gather | solution.py:203
  25.3 990.1 %reduce-scatter.43.cloned.1.call-start = ((), (), s32[]{:S(2)}) async-start(), calls=%async_computation.24 | async-start | bytes 1179648 | tf_op jit(solution)/shard_map/reduce_scatter | solution.py:287
  102.9 179.1 %copy-start.68 = (f32[768]{0:T(1024)}, f32[768]{0:T(1024)S(1)}, u32[]{:S(2)}) copy-start(f32[768]{0:T(1024)S(1)} %convert_element_type.1018) | copy-start | bytes 9220
  178.6 117.5 %copy-start.17 = (bf16[12,1,512,64]{3,2,1,0:T(8,128)(2,1)}, bf16[12,1,512,64]{3,2,1,0:T(8,128)(2,1)S(1)}, u32[]{:S(2)}) copy-start(bf16[12,1,512,64]{3,2,1,0:T(8,128)(2,1)S(1)} %get-tuple-element.2184) | copy-start | bytes 2359300
  178.6 117.5 %copy-start.26 = (bf16[12,1,512,64]{3,2,1,0:T(8,128)(2,1)}, bf16[12,1,512,64]{3,2,1,0:T(8,128)(2,1)S(1)}, u32[]{:S(2)}) copy-start(bf16[12,1,512,64]{3,2,1,0:T(8,128)(2,1)S(1)} %get-tuple-element.2196) | copy-start | bytes 2359300
  298.9 101.5 %copy-start.3 = (bf16[256,768]{1,0:T(8,128)(2,1)}, bf16[256,768]{1,0:T(8,128)(2,1)S(1)}, u32[]{:S(2)}) copy-start(bf16[256,768]{1,0:T(8,128)(2,1)S(1)} %fusion.579) | copy-start | bytes 1179652
  434.6 128.6 %copy-start.18 = (bf16[12,1,512,64]{3,2,1,0:T(8,128)(2,1)}, bf16[12,1,512,64]{3,2,1,0:T(8,128)(2,1)S(1)}, u32[]{:S(2)}) copy-start(bf16[12,1,512,64]{3,2,1,0:T(8,128)(2,1)S(1)} %get-tuple-element.2186) | copy-start | bytes 2359300
  434.6 128.6 %copy-start.27 = (bf16[12,1,512,64]{3,2,1,0:T(8,128)(2,1)}, bf16[12,1,512,64]{3,2,1,0:T(8,128)(2,1)S(1)}, u32[]{:S(2)}) copy-start(bf16[12,1,512,64]{3,2,1,0:T(8,128)(2,1)S(1)} %get-tuple-element.2198) | copy-start | bytes 2359300
  434.6 114.4 %copy-start.75 = (f32[768]{0:T(1024)S(1)}, f32[768]{0:T(1024)}, u32[]{:S(2)}) copy-start(f32[768]{0:T(1024)} %convert_element_type.1028) | copy-start | bytes 9220
  563.2 78.2 %copy-start.118 = (f32[256]{0:T(256)}, f32[256]{0:T(256)S(1)}, u32[]{:S(2)}) copy-start(f32[256]{0:T(256)S(1)} %broadcast_multiply_fusion.20) | copy-start | bytes 3076
  566.0 101.2 %copy-start.5 = (bf16[256,768]{1,0:T(8,128)(2,1)}, bf16[256,768]{1,0:T(8,128)(2,1)S(1)}, u32[]{:S(2)}) copy-start(bf16[256,768]{1,0:T(8,128)(2,1)S(1)} %fusion.578) | copy-start | bytes 1179652
  690.8 124.8 %copy-start.70 = (f32[768]{0:T(1024)S(1)}, f32[768]{0:T(1024)}, u32[]{:S(2)}) copy-start(f32[768]{0:T(1024)} %convert_element_type.1036) | copy-start | bytes 9220
  962.6 54.8 %reduce-scatter.45.cloned.1.call-start = ((), (), s32[]{:S(2)}) async-start(), calls=%async_computation.25 | async-start | bytes 1179648 | tf_op jit(solution)/shard_map/reduce_scatter | solution.py:290
  998.3 173.5 %reduce-scatter.47.cloned.1.call-start = ((), (), s32[]{:S(2)}) async-start(), calls=%async_computation.26 | async-start | bytes 1179648 | tf_op jit(solution)/shard_map/reduce_scatter | solution.py:287
  1117.9 56.7 %reduce-scatter.49.cloned.1.call-start = ((), (), s32[]{:S(2)}) async-start(), calls=%async_computation.27 | async-start | bytes 1179648 | tf_op jit(solution)/shard_map/reduce_scatter | solution.py:290
  1154.3 169.7 %reduce-scatter.53.cloned.1.call-start = ((), (), s32[]{:S(2)}) async-start(), calls=%async_computation.29 | async-start | bytes 1179648 | tf_op jit(solution)/shard_map/reduce_scatter | solution.py:290
  1295.4 35.8 %reduce-scatter.51.cloned.1.call-start = ((), (), s32[]{:S(2)}) async-start(), calls=%async_computation.28 | async-start | bytes 1179648 | tf_op jit(solution)/shard_map/reduce_scatter | solution.py:287
  1296.0 139.6 %reduce-scatter.59.cloned.1.call-start = ((), (), s32[]{:S(2)}) async-start(), calls=%async_computation.32 | async-start | bytes 2433024 | tf_op jit(solution)/shard_map/reduce_scatter | solution.py:312
  1298.9 240.8 %reduce-scatter.77.cloned.1.call-start = ((), (), s32[]{:S(2)}) async-start(), calls=%async_computation.59 | async-start | bytes 2433024 | tf_op jit(solution)/shard_map/reduce_scatter | solution.py:309
  1302.1 340.8 %reduce-scatter.57.cloned.1.call-start = ((), (), s32[]{:S(2)}) async-start(), calls=%async_computation.31 | async-start | bytes 2433024 | tf_op jit(solution)/shard_map/reduce_scatter | solution.py:312
  1305.1 442.0 %reduce-scatter.89.cloned.1.call-start = ((), (), s32[]{:S(2)}) async-start(), calls=%async_computation.65 | async-start | bytes 2433024 | tf_op jit(solution)/shard_map/reduce_scatter | solution.py:311
  1307.2 543.3 %reduce-scatter.83.cloned.1.call-start = ((), (), s32[]{:S(2)}) async-start(), calls=%async_computation.62 | async-start | bytes 2433024 | tf_op jit(solution)/shard_map/reduce_scatter | solution.py:310
  1309.2 645.4 %reduce-scatter.75.cloned.1.call-start = ((), (), s32[]{:S(2)}) async-start(), calls=%async_computation.58 | async-start | bytes 2433024 | tf_op jit(solution)/shard_map/reduce_scatter | solution.py:309
  1311.4 746.6 %reduce-scatter.55.cloned.1.call-start = ((), (), s32[]{:S(2)}) async-start(), calls=%async_computation.30 | async-start | bytes 2433024 | tf_op jit(solution)/shard_map/reduce_scatter | solution.py:312
  1313.4 848.7 %reduce-scatter.87.cloned.1.call-start = ((), (), s32[]{:S(2)}) async-start(), calls=%async_computation.64 | async-start | bytes 2433024 | tf_op jit(solution)/shard_map/reduce_scatter | solution.py:311
  1315.8 949.5 %reduce-scatter.81.cloned.1.call-start = ((), (), s32[]{:S(2)}) async-start(), calls=%async_computation.61 | async-start | bytes 2433024 | tf_op jit(solution)/shard_map/reduce_scatter | solution.py:310
  1317.9 1051.7 %reduce-scatter.73.cloned.1.call-start = ((), (), s32[]{:S(2)}) async-start(), calls=%async_computation.57 | async-start | bytes 2433024 | tf_op jit(solution)/shard_map/reduce_scatter | solution.py:309
  1323.9 1149.0 %reduce-scatter.85.cloned.1.call-start = ((), (), s32[]{:S(2)}) async-start(), calls=%async_computation.63 | async-start | bytes 2433024 | tf_op jit(solution)/shard_map/reduce_scatter | solution.py:311
  1330.0 1247.0 %reduce-scatter.79.cloned.1.call-start = ((), (), s32[]{:S(2)}) async-start(), calls=%async_computation.60 | async-start | bytes 2433024 | tf_op jit(solution)/shard_map/reduce_scatter | solution.py:310
  1337.3 1380.1 %reduce-scatter.71.cloned.1.call-start = ((), (), s32[]{:S(2)}) async-start(), calls=%async_computation.38 | async-start | bytes 9732096 | tf_op jit(solution)/shard_map/reduce_scatter | solution.py:320
  1343.9 1514.8 %reduce-scatter.65.cloned.1.call-start = ((), (), s32[]{:S(2)}) async-start(), calls=%async_computation.35 | async-start | bytes 9732096 | tf_op jit(solution)/shard_map/reduce_scatter | solution.py:318
  1351.8 1647.3 %reduce-scatter.69.cloned.1.call-start = ((), (), s32[]{:S(2)}) async-start(), calls=%async_computation.37 | async-start | bytes 9732096 | tf_op jit(solution)/shard_map/reduce_scatter | solution.py:320
  1359.5 1781.2 %reduce-scatter.63.cloned.1.call-start = ((), (), s32[]{:S(2)}) async-start(), calls=%async_computation.34 | async-start | bytes 9732096 | tf_op jit(solution)/shard_map/reduce_scatter | solution.py:318
  1367.3 1913.9 %reduce-scatter.67.cloned.1.call-start = ((), (), s32[]{:S(2)}) async-start(), calls=%async_computation.36 | async-start | bytes 9732096 | tf_op jit(solution)/shard_map/reduce_scatter | solution.py:320
  1375.0 2047.8 %reduce-scatter.61.cloned.1.call-start = ((), (), s32[]{:S(2)}) async-start(), calls=%async_computation.33 | async-start | bytes 9732096 | tf_op jit(solution)/shard_map/reduce_scatter | solution.py:318
  1382.2 168.0 %copy-start.20 = (bf16[1,256,768]{1,2,0:T(8,128)(2,1)S(1)}, bf16[1,256,768]{1,2,0:T(8,128)(2,1)}, u32[]{:S(2)}) copy-start(bf16[1,256,768]{1,2,0:T(8,128)(2,1)} %reduce-scatter.53.cloned.1.call-done) | copy-start | bytes 1179652
  1387.5 592.3 %copy-start.43 = (bf16[1,256,768]{1,2,0:T(8,128)(2,1)S(1)}, bf16[1,256,768]{1,2,0:T(8,128)(2,1)}, u32[]{:S(2)}) copy-start(bf16[1,256,768]{1,2,0:T(8,128)(2,1)} %reduce-scatter.51.cloned.1.call-done) | copy-start | bytes 1179652
  1550.2 431.4 %copy-start.52 = (bf16[1,768,768]{2,1,0:T(8,128)(2,1)S(1)}, bf16[1,768,768]{2,1,0:T(8,128)(2,1)}, u32[]{:S(2)}) copy-start(bf16[1,768,768]{2,1,0:T(8,128)(2,1)} %all-gather.74.cloned.1.call-done) | copy-start | bytes 3538948
  1982.2 406.7 %copy-start.63 = (bf16[48,768]{1,0:T(8,128)(2,1)S(1)}, bf16[48,768]{1,0:T(8,128)(2,1)}, u32[]{:S(2)}) copy-start(bf16[48,768]{1,0:T(8,128)(2,1)} %all_gather.402) | copy-start | bytes 221188
  1982.2 406.7 %copy-start.66 = (bf16[48,768]{1,0:T(8,128)(2,1)S(1)}, bf16[48,768]{1,0:T(8,128)(2,1)}, u32[]{:S(2)}) copy-start(bf16[48,768]{1,0:T(8,128)(2,1)} %all_gather.401) | copy-start | bytes 221188
  1982.2 407.5 %copy-start.62 = (bf16[48,768]{1,0:T(8,128)(2,1)S(1)}, bf16[48,768]{1,0:T(8,128)(2,1)}, u32[]{:S(2)}) copy-start(bf16[48,768]{1,0:T(8,128)(2,1)} %all_gather.393) | copy-start | bytes 221188
  1982.3 407.5 %copy-start.67 = (bf16[48,768]{1,0:T(8,128)(2,1)S(1)}, bf16[48,768]{1,0:T(8,128)(2,1)}, u32[]{:S(2)}) copy-start(bf16[48,768]{1,0:T(8,128)(2,1)} %all_gather.392) | copy-start | bytes 221188
  1982.3 604.8 %copy-start.65 = (bf16[48,768]{1,0:T(8,128)(2,1)S(1)}, bf16[48,768]{1,0:T(8,128)(2,1)}, u32[]{:S(2)}) copy-start(bf16[48,768]{1,0:T(8,128)(2,1)} %all_gather.399) | copy-start | bytes 221188
  1982.3 605.6 %copy-start.64 = (bf16[48,768]{1,0:T(8,128)(2,1)S(1)}, bf16[48,768]{1,0:T(8,128)(2,1)}, u32[]{:S(2)}) copy-start(bf16[48,768]{1,0:T(8,128)(2,1)} %all_gather.396) | copy-start | bytes 221188
  (130 other events, 1417.0 us)
Sparse Core Ops, SparseCore 0:
  10.9 41.3 all-gather.73
  55.2 37.6 all-gather.69
  95.7 37.2 all-gather.71
  135.2 37.3 all-gather.75
  175.3 52.1 all-gather.77
  230.2 51.7 all-gather.79
  284.3 36.8 all-gather.85
  323.5 37.2 all-gather.83
  363.1 37.2 all-gather.81
  402.5 37.3 all-gather.87
  442.7 52.2 all-gather.89
  497.2 51.7 all-gather.91
  551.3 36.8 all-gather.95
  590.4 37.2 all-gather.97
  629.8 37.2 all-gather.93
  669.2 37.4 all-gather.99
  709.4 52.1 all-gather.101
  763.8 51.7 all-gather.103
  962.7 15.9 reduce-scatter.42
  998.4 16.0 reduce-scatter.44
  1118.0 16.0 reduce-scatter.46
  1154.4 16.0 reduce-scatter.48
  1295.5 16.0 reduce-scatter.52
  1313.8 17.4 reduce-scatter.50
  1336.5 99.0 reduce-scatter.58
  1441.6 98.0 reduce-scatter.76
  1544.8 98.0 reduce-scatter.56
  1649.1 98.0 reduce-scatter.88
  1752.4 97.9 reduce-scatter.82
  1856.4 98.0 reduce-scatter.74
  1959.8 98.0 reduce-scatter.54
  2064.1 98.0 reduce-scatter.86
  2167.3 98.0 reduce-scatter.80
  2271.5 98.0 reduce-scatter.72
  2374.8 97.9 reduce-scatter.84
  2478.9 98.0 reduce-scatter.78
  2582.7 134.6 reduce-scatter.70
  2724.3 134.3 reduce-scatter.64
  2864.4 134.5 reduce-scatter.68
  3006.0 134.5 reduce-scatter.62
  3146.5 134.5 reduce-scatter.66
  3288.1 134.5 reduce-scatter.60
where the time goes:
time: 3460 us; the launch traced here: 3440 us
  waiting for transfers between devices  2330 us (67%)
  matrix products  599 us (17%)
  blocking collectives  287 us (8%)
  local copies, waits for them, and re-layouts  103 us (3%)
  other arithmetic  85.7 us (2%)
    reduce_scatter x3, waiting for transfers between devices, body(): lax.psum_scatter(inner_weight_part, ('dp', 'seq'), scatter_dimension=0, t...  416 us
    reduce_scatter x3, waiting for transfers between devices, body(): lax.psum_scatter(outer_weight_part, ('dp', 'seq'), scatter_dimension=0, t...  384 us
    reduce_scatter x3, waiting for transfers between devices, body(): lax.psum_scatter(query_weight_part, ('dp', 'seq'), scatter_dimension=0, t...  310 us
    reduce_scatter x3, waiting for transfers between devices, body(): lax.psum_scatter(key_weight_part, ('dp', 'seq'), scatter_dimension=0, til...  308 us
    reduce_scatter x3, waiting for transfers between devices, body(): lax.psum_scatter(value_weight_part, ('dp', 'seq'), scatter_dimension=0, t...  289 us
    all_gather x3, waiting for transfers between devices, body(): lax.all_gather(outer_weight[layer_index], 'dp', axis=0, tiled=True)  162 us
    all_gather x3, waiting for transfers between devices, body(): lax.all_gather(inner_weight[layer_index], 'dp', axis=0, tiled=True)  148 us
    reduce_scatter x3, waiting for transfers between devices, body(): lax.psum_scatter(output_weight_part, ('dp', 'seq'), scatter_dimension=0,...  140 us
  transfers between devices with their start and end apart: 42, of which 34 were waited for; matrix products, arithmetic and copies ran while one was open for 12% of the time, Pallas kernels for 0%

commit v1 on v0

v1 whole, which is shorter than its diff:
```python
import functools

import jax
import jax.numpy as jnp
from jax import lax
from jax.experimental import pallas as pl
from jax.experimental.pallas import tpu as pltpu
from jax.sharding import PartitionSpec as P

HD = 64
SEGS = 4
BLOCKS = 16
EPS = 1e-06
MASKED = -1e30
AXES = ("dp", "seq")
F32 = jnp.float32
BF16 = jnp.bfloat16
MB = 1024 * 1024

QB, VB, OB, AG, AS, UB, FG, FS, IB = range(9)


def nn(left, right):
    return lax.dot_general(left, right, (((1,), (0,)), ((), ())), preferred_element_type=F32)


def nt(left, right):
    return lax.dot_general(left, right, (((1,), (1,)), ((), ())), preferred_element_type=F32)


def params(vmem):
    return pltpu.CompilerParams(vmem_limit_bytes=vmem * MB)


def cost(flops, us):
    return pl.CostEstimate(flops=flops, bytes_accessed=int(us * 3.0e6), transcendentals=0)


VMEM = pl.BlockSpec(memory_space=pltpu.VMEM)
SMEM = pl.BlockSpec(memory_space=pltpu.SMEM)
ANY = pl.BlockSpec(memory_space=pl.ANY)


def shape(dims, dtype):
    return jax.ShapeDtypeStruct(dims, dtype)


def block_at(pos_ref, shift, dx, dc, depth):
    z, x, c = pos_ref[0], pos_ref[1], pos_ref[2]
    zz = lax.rem(z + shift, depth)
    xx = x + dx - 2 * x * dx
    cc = c + dc - 2 * c * dc
    return (zz * 2 + xx) * 2 + cc


def half_at(pos_ref, dy):
    y = pos_ref[3]
    return y + dy - 2 * y * dy


def each_buffer():
    for dy in range(2):
        for dx in range(2):
            for dc in range(2):
                yield (dy * 2 + dx) * 2 + dc, dy, dx, dc


def fetch_columns(pos_ref, bufs, member, members, full_ref, column, sem):
    depth, rows, width = bufs[0].shape
    half = width // members
    for index, dy, dx, dc in each_buffer():
        for shift in range(depth):
            row = pl.multiple_of(block_at(pos_ref, shift, dx, dc, depth) * rows, 16)
            col = pl.multiple_of(column + half_at(pos_ref, dy) * half, 128)
            pltpu.make_async_copy(
                bufs[index].at[shift, :, pl.ds(member * half, half)],
                full_ref.at[pl.ds(row, rows), pl.ds(col, half)],
                sem,
            ).start()


def fetch_rows(pos_ref, bufs, full_ref, sem):
    depth, rows, width = bufs[0].shape
    for index, dy, dx, dc in each_buffer():
        for shift in range(depth):
            block = block_at(pos_ref, shift, dx, dc, depth) * 2 + half_at(pos_ref, dy)
            row = pl.multiple_of(block * rows, 16)
            pltpu.make_async_copy(
                bufs[index].at[shift], full_ref.at[pl.ds(row, rows), :], sem
            ).start()


def wait_full(full_ref, sem):
    pltpu.make_async_copy(full_ref, full_ref, sem).wait()


def export_rows(pos_ref, depth, wide_ref, out_ref):
    rows = out_ref.shape[3]
    for dc in range(2):
        for dx in range(2):
            for shift in range(depth):
                row = pl.multiple_of(block_at(pos_ref, shift, dx, dc, depth) * rows, 16)
                out_ref[dc, dx, shift] = wide_ref[pl.ds(row, rows), :]


def export_halves(pos_ref, depth, wide_ref, out_ref):
    rows = out_ref.shape[4]
    for dc in range(2):
        for dx in range(2):
            for dy in range(2):
                for shift in range(depth):
                    block = block_at(pos_ref, shift, dx, dc, depth) * 2 + half_at(pos_ref, dy)
                    row = pl.multiple_of(block * rows, 16)
                    out_ref[dc, dx, dy, shift] = wide_ref[pl.ds(row, rows), :]


def mean_of(values):
    return jnp.mean(values, axis=-1, keepdims=True)


def normalize(values):
    center = values - mean_of(values)
    inverse = lax.rsqrt(mean_of(center * center) + EPS)
    return center * inverse, inverse


def norm_back(normed, inverse, scaled):
    return inverse * (scaled - mean_of(scaled) - normed * mean_of(scaled * normed))


def colsum(values):
    return jnp.sum(values, axis=0, keepdims=True)


def row_of(vec_ref, index):
    return vec_ref[pl.ds(index, 1), :]


def attn_kernel(depth, *refs):
    pos_w, pos_g = refs[0], refs[1]
    x_ref, xp_ref, seg_ref, lab_ref, vec_ref = refs[2:7]
    bufs = refs[7:15]
    (h_ref, n1_ref, c1_ref, q_ref, k_ref, kt_ref, v_ref, p_ref, xt_ref, ot_ref, ht_ref) = refs[15:26]
    wq, wk, wv, wo, rows_ref, vt_ref, wide_ref, bias_ref, sems = refs[26:]
    tokens, width = x_ref.shape
    for member, full in enumerate((wq, wk, wv, wo)):
        fetch_columns(pos_w, bufs, member, 4, full, 0, sems.at[member])
    bias_ref[...] = jnp.where(lab_ref[...] == seg_ref[...], 0.0, MASKED)
    low = x_ref[...].astype(BF16)
    rows_ref[:tokens] = low
    rows_ref[tokens:] = xp_ref[...]
    wide_ref[...] = low.T
    export_rows(pos_g, depth, wide_ref, xt_ref)
    wait_full(wq, sems.at[0])
    query = (nn(low, wq[...]) + row_of(vec_ref, QB)).astype(BF16)
    q_ref[...] = (query.astype(F32) * HD ** (-0.5)).astype(BF16)
    wait_full(wk, sems.at[1])
    key = nn(rows_ref[...], wk[...]).astype(BF16)
    k_ref[...] = key
    kt_ref[...] = key.T
    wait_full(wv, sems.at[2])
    value = (nn(rows_ref[...], wv[...]) + row_of(vec_ref, VB)).astype(BF16)
    v_ref[...] = value
    vt_ref[...] = value.T

    def pair(index, carry):
        lane = pl.multiple_of(index * 128, 128)
        keys = k_ref[:, pl.ds(lane, 128)]
        queries = q_ref[:, pl.ds(lane, 128)]
        first = lax.broadcasted_iota(jnp.int32, queries.shape, 1) < HD
        for which in range(2):
            mine = jnp.where(first if which == 0 else ~first, queries, jnp.zeros_like(queries))
            scores = nt(keys, mine) + bias_ref[...]
            expos = jnp.exp(scores - jnp.max(scores, axis=0, keepdims=True))
            probs = (expos * (1.0 / jnp.sum(expos, axis=0, keepdims=True))).astype(BF16)
            p_ref[index * 2 + which] = probs
            row = pl.multiple_of(index * 128 + which * HD, HD)
            wide_ref[pl.ds(row, HD), :] = nn(vt_ref[pl.ds(row, HD), :], probs).astype(BF16)
        return carry

    lax.fori_loop(0, width // 128, pair, 0)
    export_rows(pos_g, depth, wide_ref, ot_ref)
    mixed = wide_ref[...].T
    wait_full(wo, sems.at[3])
    branch = nn(mixed, wo[...]) + row_of(vec_ref, OB)
    normed, inverse = normalize(x_ref[...] + branch)
    hidden = normed * row_of(vec_ref, AG) + row_of(vec_ref, AS)
    h_ref[...] = hidden
    n1_ref[...] = normed
    c1_ref[...] = jnp.broadcast_to(inverse, c1_ref.shape)
    wide_ref[...] = hidden.astype(BF16).T
    export_rows(pos_g, depth, wide_ref, ht_ref)


def attn_forward(depth, pos_w, pos_g, x, xp, seg, lab, vec, bufs):
    tokens, width = x.shape
    heads = width // HD
    export = shape((2, 2, depth, width // BLOCKS, tokens), BF16)
    return pl.pallas_call(
        functools.partial(attn_kernel, depth),
        out_shape=(
            shape((tokens, width), F32),
            shape((tokens, width), F32),
            shape((tokens, 128), F32),
            shape((tokens, width), BF16),
            shape((2 * tokens, width), BF16),
            shape((width, 2 * tokens), BF16),
            shape((2 * tokens, width), BF16),
            shape((heads, 2 * tokens, tokens), BF16),
            export,
            export,
            export,
        ),
        in_specs=[SMEM, SMEM] + [VMEM] * 5 + [ANY] * 8,
        out_specs=[VMEM] * 11,
        scratch_shapes=[pltpu.VMEM((width, width), BF16)] * 4
        + [
            pltpu.VMEM((2 * tokens, width), BF16),
            pltpu.VMEM((width, 2 * tokens), BF16),
            pltpu.VMEM((width, tokens), BF16),
            pltpu.VMEM((2 * tokens, tokens), F32),
            pltpu.SemaphoreType.DMA((4,)),
        ],
        compiler_params=params(40),
        cost_estimate=cost(2_200_000_000, 12),
        name="attn_forward",
    )(pos_w, pos_g, x, xp, seg, lab, vec, *bufs)


def ffn_kernel(depth, tile, *refs):
    pos_w, pos_g, h_ref, vec_ref = refs[:4]
    inner_bufs, outer_bufs = refs[4:12], refs[12:20]
    x_ref, xb_ref, n2_ref, c2_ref, gp_ref, gt_ref = refs[20:26]
    wi, wu, low_ref, acc_ref, wide_ref, sems = refs[26:]
    width, hidden = wi.shape
    fetch_columns(pos_w, inner_bufs, 0, 1, wi, 0, sems.at[0])
    fetch_rows(pos_w, outer_bufs, wu, sems.at[1])
    low_ref[...] = h_ref[...].astype(BF16)
    acc_ref[...] = jnp.zeros_like(acc_ref)
    wait_full(wi, sems.at[0])
    wait_full(wu, sems.at[1])
    per_row = width // tile

    def step(index, carry):
        lane = pl.multiple_of(index * tile, tile)
        bias = vec_ref[pl.ds(IB + lax.div(index, per_row), 1), :]
        part = lax.rem(index, per_row)
        chosen = bias[:, :tile]
        for other in range(1, per_row):
            chosen = jnp.where(part == other, bias[:, other * tile : (other + 1) * tile], chosen)
        pre = nn(low_ref[...], wi[:, pl.ds(lane, tile)]) + chosen
        phi = 0.5 * (1.0 + lax.erf(pre * 0.7071067811865476))
        dens = jnp.exp(-0.5 * pre * pre) * 0.3989422804014327
        gp_ref[:, pl.ds(lane, tile)] = (phi + pre * dens).astype(BF16)
        active = (pre * phi).astype(BF16)
        acc_ref[...] += nn(active, wu[pl.ds(lane, tile), :])
        wide_ref[pl.ds(lane, tile), :] = active.T
        return carry

    lax.fori_loop(0, hidden // tile, step, 0)
    export_halves(pos_g, depth, wide_ref, gt_ref)
    normed, inverse = normalize(h_ref[...] + (acc_ref[...] + row_of(vec_ref, UB)))
    result = normed * row_of(vec_ref, FG) + row_of(vec_ref, FS)
    x_ref[...] = result
    xb_ref[...] = result.astype(BF16)
    n2_ref[...] = normed
    c2_ref[...] = jnp.broadcast_to(inverse, c2_ref.shape)


def ffn_forward(depth, pos_w, pos_g, h, vec, inner_bufs, outer_bufs):
    tokens, width = h.shape
    hidden = outer_bufs[0].shape[1] * 2 * BLOCKS
    return pl.pallas_call(
        functools.partial(ffn_kernel, depth, 384),
        out_shape=(
            shape((tokens, width), F32),
            shape((tokens, width), BF16),
            shape((tokens, width), F32),
            shape((tokens, 128), F32),
            shape((tokens, hidden), BF16),
            shape((2, 2, 2, depth, hidden // BLOCKS // 2, tokens), BF16),
        ),
        in_specs=[SMEM, SMEM, VMEM, VMEM] + [ANY] * 16,
        out_specs=[VMEM] * 6,
        scratch_shapes=[
            pltpu.VMEM((width, hidden), BF16),
            pltpu.VMEM((hidden, width), BF16),
            pltpu.VMEM((tokens, width), BF16),
            pltpu.VMEM((tokens, width), F32),
            pltpu.VMEM((hidden, tokens), BF16),
            pltpu.SemaphoreType.DMA((2,)),
        ],
        compiler_params=params(40),
        cost_estimate=cost(2_400_000_000, 12),
        name="ffn_forward",
    )(pos_w, pos_g, h, vec, *inner_bufs, *outer_bufs)


def chain_kernel(tile, *refs):
    pos_w, dx_ref, n2_ref, c2_ref, gp_ref, n1_ref, c1_ref, vec_ref = refs[:8]
    inner_bufs, outer_bufs, attn_bufs = refs[8:16], refs[16:24], refs[24:32]
    dyl_ref, du_ref, da_ref, dal_ref, do_ref, sums_ref = refs[32:38]
    wi, wu, wo, acc_ref, sems = refs[38:]
    width, hidden = wi.shape
    fetch_rows(pos_w, outer_bufs, wu, sems.at[0])
    fetch_columns(pos_w, inner_bufs, 0, 1, wi, 0, sems.at[1])
    fetch_columns(pos_w, attn_bufs, 3, 4, wo, 0, sems.at[2])
    sums_ref[...] = jnp.zeros_like(sums_ref)
    grad = dx_ref[...].astype(F32)
    normed = n2_ref[...]
    sums_ref[pl.ds(FG, 1), :] = colsum(grad * normed)
    sums_ref[pl.ds(FS, 1), :] = colsum(grad)
    back = norm_back(normed, c2_ref[:, :1], grad * row_of(vec_ref, FG))
    low = back.astype(BF16)
    dyl_ref[...] = low
    sums_ref[pl.ds(UB, 1), :] = colsum(low.astype(F32))
    acc_ref[...] = back
    wait_full(wu, sems.at[0])
    wait_full(wi, sems.at[1])
    per_row = width // tile

    for index in range(hidden // tile):
        lane = index * tile
        part = nt(dyl_ref[...], wu[pl.ds(lane, tile), :])
        part = (part * gp_ref[:, pl.ds(lane, tile)].astype(F32)).astype(BF16)
        du_ref[:, pl.ds(lane, tile)] = part
        acc_ref[...] += nt(part, wi[:, pl.ds(lane, tile)])
        sums_ref[
            pl.ds(IB + index // per_row, 1), pl.ds(index % per_row * tile, tile)
        ] = colsum(part.astype(F32))

    grad = acc_ref[...]
    normed = n1_ref[...]
    sums_ref[pl.ds(AG, 1), :] = colsum(grad * normed)
    sums_ref[pl.ds(AS, 1), :] = colsum(grad)
    back = norm_back(normed, c1_ref[:, :1], grad * row_of(vec_ref, AG))
    da_ref[...] = back
    low = back.astype(BF16)
    dal_ref[...] = low
    sums_ref[pl.ds(OB, 1), :] = colsum(low.astype(F32))
    wait_full(wo, sems.at[2])
    do_ref[...] = nt(low, wo[...]).astype(BF16)


def chain_backward(pos_w, dx, n2, c2, gp, n1, c1, vec, inner_bufs, outer_bufs, attn_bufs):
    tokens, width = n2.shape
    hidden = gp.shape[1]
    return pl.pallas_call(
        functools.partial(chain_kernel, 384),
        out_shape=(
            shape((tokens, width), BF16),
            shape((tokens, hidden), BF16),
            shape((tokens, width), F32),
            shape((tokens, width), BF16),
            shape((tokens, width), BF16),
            shape((16, width), F32),
        ),
        in_specs=[SMEM] + [VMEM] * 7 + [ANY] * 24,
        out_specs=[VMEM] * 6,
        scratch_shapes=[
            pltpu.VMEM((width, hidden), BF16),
            pltpu.VMEM((hidden, width), BF16),
            pltpu.VMEM((width, width), BF16),
            pltpu.VMEM((tokens, width), F32),
            pltpu.SemaphoreType.DMA((3,)),
        ],
        compiler_params=params(40),
        cost_estimate=cost(2_700_000_000, 12),
        name="chain_backward",
    )(pos_w, dx, n2, c2, gp, n1, c1, vec, *inner_bufs, *outer_bufs, *attn_bufs)


def attn_back_kernel(q_ref, kt_ref, v_ref, p_ref, do_ref, dq_ref, dk_ref, dv_ref, sum_ref, wide_ref):
    tokens, width = q_ref.shape

    def pair(index, carry):
        lane = pl.multiple_of(index * 128, 128)
        values = v_ref[:, pl.ds(lane, 128)]
        queries = q_ref[:, pl.ds(lane, 128)]
        grads = do_ref[:, pl.ds(lane, 128)]
        first = lax.broadcasted_iota(jnp.int32, grads.shape, 1) < HD
        keys_back, values_back = [], []
        for which in range(2):
            mine = jnp.where(first if which == 0 else ~first, grads, jnp.zeros_like(grads))
            probs_low = p_ref[index * 2 + which]
            probs = probs_low.astype(F32)
            weighted = probs * nt(values, mine)
            back = weighted - probs * jnp.sum(weighted, axis=0, keepdims=True)
            low = back.astype(BF16)
            keys_back.append(nn(low, queries))
            values_back.append(nn(probs_low, grads))
            row = pl.multiple_of(index * 128 + which * HD, HD)
            wide_ref[pl.ds(row, HD), :] = nn(kt_ref[pl.ds(row, HD), :], low)
        split = lax.broadcasted_iota(jnp.int32, keys_back[0].shape, 1) < HD
        dk_ref[:, pl.ds(lane, 128)] = jnp.where(split, keys_back[0], keys_back[1]).astype(BF16)
        dv_ref[:, pl.ds(lane, 128)] = jnp.where(split, values_back[0], values_back[1]).astype(BF16)
        return carry

    lax.fori_loop(0, width // 128, pair, 0)
    low = (wide_ref[...].T * HD ** (-0.5)).astype(BF16)
    dq_ref[...] = low
    sum_ref[...] = jnp.broadcast_to(colsum(low.astype(F32)), sum_ref.shape)


def attn_backward(q, kt, v, p, do):
    tokens, width = q.shape
    return pl.pallas_call(
        attn_back_kernel,
        out_shape=(
            shape((tokens, width), BF16),
            shape((2 * tokens, width), BF16),
            shape((2 * tokens, width), BF16),
            shape((8, width), F32),
        ),
        in_specs=[VMEM] * 5,
        out_specs=[VMEM] * 4,
        scratch_shapes=[pltpu.VMEM((width, tokens), F32)],
        compiler_params=params(40),
        cost_estimate=cost(2_000_000_000, 10),
        name="attn_backward",
    )(q, kt, v, p, do)


def input_kernel(*refs):
    pos_w, da_ref, dq_ref, dk_ref, dv_ref, rk_ref, rv_ref = refs[:7]
    bufs = refs[7:15]
    dx_ref, tk_ref, tv_ref, sum_ref = refs[15:19]
    wq, wk, wv, sems = refs[19:]
    tokens, width = da_ref.shape
    for member, full in enumerate((wq, wk, wv)):
        fetch_columns(pos_w, bufs, member, 4, full, 0, sems.at[member])
    for total, own, other in ((tk_ref, dk_ref, rk_ref), (tv_ref, dv_ref, rv_ref)):
        total[:tokens] = (own[:tokens].astype(F32) + other[tokens:].astype(F32)).astype(BF16)
        total[tokens:] = (own[tokens:].astype(F32) + other[:tokens].astype(F32)).astype(BF16)
    sum_ref[...] = jnp.broadcast_to(colsum(tv_ref[:tokens].astype(F32)), sum_ref.shape)
    wait_full(wq, sems.at[0])
    dx = da_ref[...] + nt(dq_ref[...], wq[...])
    wait_full(wk, sems.at[1])
    dx += nt(tk_ref[:tokens], wk[...])
    wait_full(wv, sems.at[2])
    dx += nt(tv_ref[:tokens], wv[...])
    dx_ref[...] = dx


def input_backward(pos_w, da, dq, dk, dv, rk, rv, bufs):
    tokens, width = da.shape
    return pl.pallas_call(
        input_kernel,
        out_shape=(
            shape((tokens, width), F32),
            shape((2 * tokens, width), BF16),
            shape((2 * tokens, width), BF16),
            shape((8, width), F32),
        ),
        in_specs=[SMEM] + [VMEM] * 6 + [ANY] * 8,
        out_specs=[VMEM] * 4,
        scratch_shapes=[pltpu.VMEM((width, width), BF16)] * 3 + [pltpu.SemaphoreType.DMA((3,))],
        compiler_params=params(40),
        cost_estimate=cost(1_000_000_000, 6),
        name="input_backward",
    )(pos_w, da, dq, dk, dv, rk, rv, *bufs)


def inner_grad_kernel(tile, pos_ref, ta_ref, tb_ref, da_ref, db_ref, *outs):
    depth, rows, half = outs[0].shape
    tokens = ta_ref.shape[-1]
    left_a = ta_ref[0].reshape(2 * depth * rows, tokens)
    left_b = tb_ref[...].reshape(2 * depth * rows, tokens)
    for dy in range(2):
        start = half_at(pos_ref, dy) * half
        for index in range(half // tile):
            lane = pl.multiple_of(start + index * tile, 128)
            part = nn(left_a, da_ref[:, pl.ds(lane, tile)]) + nn(left_b, db_ref[:, pl.ds(lane, tile)])
            part = part.astype(BF16).reshape(2, depth, rows, tile)
            for dx in range(2):
                outs[dx * 2 + dy][:, :, pl.ds(index * tile, tile)] = part[dx]


def inner_grad(pos_g, ta, tb, da, db):
    _, _, depth, rows, tokens = ta.shape
    half = da.shape[1] // 2
    return pl.pallas_call(
        functools.partial(inner_grad_kernel, 384),
        out_shape=(shape((depth, rows, half), BF16),) * 4,
        in_specs=[SMEM] + [VMEM] * 4,
        out_specs=[VMEM] * 4,
        compiler_params=params(32),
        cost_estimate=cost(1_200_000_000, 4),
        name="inner_grad",
    )(pos_g, ta, tb, da, db)


def outer_grad_kernel(ta_ref, tb_ref, da_ref, db_ref, *outs):
    depth, rows, width = outs[0].shape
    tokens = ta_ref.shape[-1]
    for dx in range(2):
        for dy in range(2):
            left_a = ta_ref[0, dx, dy].reshape(depth * rows, tokens)
            left_b = tb_ref[dx, dy].reshape(depth * rows, tokens)
            part = nn(left_a, da_ref[...]) + nn(left_b, db_ref[...])
            outs[dx * 2 + dy][...] = part.astype(BF16).reshape(depth, rows, width)


def outer_grad(ta, tb, da, db):
    _, _, _, depth, rows, tokens = ta.shape
    width = da.shape[1]
    return pl.pallas_call(
        outer_grad_kernel,
        out_shape=(shape((depth, rows, width), BF16),) * 4,
        in_specs=[VMEM] * 4,
        out_specs=[VMEM] * 4,
        compiler_params=params(32),
        cost_estimate=cost(1_200_000_000, 4),
        name="outer_grad",
    )(ta, tb, da, db)


def attn_grad_kernel(pos_ref, xa_ref, xb_ref, oa_ref, ob_ref, qa_ref, qb_ref, k_ref, v_ref, da_ref, db_ref, *outs):
    depth, rows, wide = outs[0].shape
    half = wide // 4
    tokens = xa_ref.shape[-1]
    height = 2 * depth * rows
    x_a = xa_ref[0].reshape(height, tokens)
    x_b = xb_ref[...].reshape(height, tokens)
    o_a = oa_ref[0].reshape(height, tokens)
    o_b = ob_ref[...].reshape(height, tokens)
    for dy in range(2):
        lanes = pl.ds(pl.multiple_of(half_at(pos_ref, dy) * half, 128), half)
        parts = (
            nn(x_a, qa_ref[:, lanes]) + nn(x_b, qb_ref[:, lanes]),
            nn(x_a, k_ref[:tokens, lanes]) + nn(x_b, k_ref[tokens:, lanes]),
            nn(x_a, v_ref[:tokens, lanes]) + nn(x_b, v_ref[tokens:, lanes]),
            nn(o_a, da_ref[:, lanes]) + nn(o_b, db_ref[:, lanes]),
        )
        for member, part in enumerate(parts):
            part = part.astype(BF16).reshape(2, depth, rows, half)
            for dx in range(2):
                outs[dx * 2 + dy][:, :, member * half : (member + 1) * half] = part[dx]


def attn_grad(pos_g, xa, xb, oa, ob, qa, qb, tk, tv, da, db):
    _, _, depth, rows, tokens = xa.shape
    width = da.shape[1]
    return pl.pallas_call(
        attn_grad_kernel,
        out_shape=(shape((depth, rows, 2 * width), BF16),) * 4,
        in_specs=[SMEM] + [VMEM] * 10,
        out_specs=[VMEM] * 4,
        compiler_params=params(32),
        cost_estimate=cost(1_200_000_000, 4),
        name="attn_grad",
    )(pos_g, xa, xb, oa, ob, qa, qb, tk, tv, da, db)


def build(mesh):
    count = mesh.shape["dp"]
    depth = count // 4

    def flat(dp, seq):
        return dp * 2 + seq

    def pairs(source_of):
        out = []
        for dp in range(count):
            for seq in range(2):
                out.append((flat(*source_of(dp, seq)), flat(dp, seq)))
        return out

    swap_pairs = pairs(lambda dp, seq: (dp // 2 * 2 + seq, dp % 2))
    core_pairs = pairs(lambda dp, seq: (dp ^ 1, seq))
    x_pairs = pairs(lambda dp, seq: (dp ^ 2, seq))
    y_pairs = pairs(lambda dp, seq: (dp, 1 - seq))
    z_from = [pairs(lambda dp, seq, k=k: ((dp + 4 * k) % count, seq)) for k in range(depth)]
    z_to = [pairs(lambda dp, seq, k=k: ((dp - 4 * k) % count, seq)) for k in range(depth)]

    def move(value, perm):
        return lax.ppermute(value, AXES, perm)

    def move_all(values, perm):
        return [move(value, perm) for value in values]

    def gather_chunk(piece, x_first):
        zs = [piece] + [move(piece, z_from[k]) for k in range(1, depth)]
        base = jnp.stack(zs)
        near = move(base, x_pairs if x_first else y_pairs)
        far = move_all((base, near), y_pairs if x_first else x_pairs)
        if x_first:
            table = ((base, near), (far[0], far[1]))
        else:
            table = ((base, far[0]), (near, far[1]))
        bufs = []
        for dy in range(2):
            for dx in range(2):
                bufs.append(table[dy][dx])
                bufs.append(move(table[dy][dx], core_pairs))
        return bufs

    def add(left, right):
        return (left.astype(F32) + right.astype(F32)).astype(BF16)

    def reduce_chunk(outs, x_first):
        if x_first:
            got = move_all((outs[2], outs[3]), x_pairs)
            sums = [add(outs[0], got[0]), add(outs[1], got[1])]
            rest = add(sums[0], move(sums[1], y_pairs))
        else:
            got = move_all((outs[1], outs[3]), y_pairs)
            sums = [add(outs[0], got[0]), add(outs[2], got[1])]
            rest = add(sums[0], move(sums[1], x_pairs))
        total = rest[0].astype(F32)
        for k in range(1, depth):
            total = total + move(rest[k], z_to[k]).astype(F32)
        low = total.astype(BF16)
        return total, move(low, y_pairs).astype(F32)

    def reduce_small(value):
        for perm in (core_pairs, y_pairs, x_pairs):
            value = value + move(value, perm)
        return value + sum(move(value, z_from[k]) for k in range(1, depth))

    def spread_small(value):
        value = value + sum(move(value, z_from[k]) for k in range(1, depth))
        for perm in (x_pairs, core_pairs):
            value = value + move(value, perm)
        return value

    return dict(
        count=count,
        depth=depth,
        swap=swap_pairs,
        core=core_pairs,
        move=move,
        gather=gather_chunk,
        reduce=reduce_chunk,
        reduce_small=reduce_small,
        spread_small=spread_small,
    )


def body(
    net,
    tokens,
    segment_ids,
    padding,
    query_weight,
    key_weight,
    value_weight,
    output_weight,
    query_bias,
    value_bias,
    output_bias,
    attn_gain,
    attn_shift,
    inner_weight,
    inner_bias,
    outer_weight,
    outer_bias,
    ffn_gain,
    ffn_shift,
    upstream,
):
    layers, small, width = query_weight.shape
    hidden = inner_weight.shape[2]
    count = net["count"]
    move = net["move"]
    staged = count == BLOCKS and small % 16 == 0
    dp = lax.axis_index("dp").astype(jnp.int32)
    y = lax.axis_index("seq").astype(jnp.int32)
    core = lax.rem(dp, 2)
    if staged:
        depth = net["depth"]
        pos_g = jnp.stack([lax.div(dp, 4), lax.rem(lax.div(dp, 2), 2), core, y])
        pos_w = pos_g
    else:
        depth = BLOCKS // 4
        zero = jnp.zeros((), jnp.int32)
        pos_g = jnp.stack([zero, zero, core, zero])
        pos_w = jnp.stack([zero, zero, zero, zero])

    def half(value, axis):
        size = value.shape[axis] // 2
        return lax.dynamic_slice_in_dim(value, y * size, size, axis)

    labels = jnp.where(padding == 1, segment_ids, -1)
    small_own = move(jnp.concatenate([segment_ids, labels]), net["swap"])
    small_other = move(small_own, net["core"])
    seg = small_own[0:1]
    lab = jnp.concatenate([small_own[1], small_other[1]])[:, None]
    token_low = move(tokens[0], net["swap"])
    token_other = move(token_low, net["core"])
    grad_in = move(upstream[0], net["swap"])

    onehot = (jnp.arange(count, dtype=jnp.int32) == dp).astype(BF16)
    eight = jnp.stack(
        [query_bias, value_bias, output_bias, attn_gain, attn_shift, outer_bias, ffn_gain, ffn_shift],
        axis=1,
    )
    eight = (eight[:, :, None, :] * onehot[None, None, :, None]).reshape(layers, 8, width)
    wide = (inner_bias[:, None, :] * onehot[None, :, None]).reshape(layers, hidden // width, width)
    table = jnp.concatenate([eight, wide], axis=1)
    table = net["spread_small"](table) if staged else lax.psum(table, "dp")
    table = table.astype(F32)

    chunks = []
    for layer in range(layers):
        four = (query_weight[layer], key_weight[layer], value_weight[layer], output_weight[layer])
        if staged:
            pieces = (
                jnp.concatenate([half(value, 1) for value in four], axis=1),
                half(inner_weight[layer], 1),
                half(outer_weight[layer], 0),
            )
            chunks.append(
                [net["gather"](piece, (layer * 3 + index) % 2 == 1) for index, piece in enumerate(pieces)]
            )
        else:
            full = [lax.all_gather(value, "dp", axis=0, tiled=True) for value in four]
            inner = lax.all_gather(inner_weight[layer], "dp", axis=0, tiled=True)
            outer = lax.all_gather(outer_weight[layer], "dp", axis=0, tiled=True)
            rows = width // BLOCKS

            def cut(value, dy, dx, dc):
                value = value.reshape(depth, 2, 2, rows, 2, -1)
                return value[:, dx, dc, :, dy, :]

            lists = [[], [], []]
            for index, dy, dx, dc in each_buffer():
                lists[0].append(jnp.concatenate([cut(value, dy, dx, dc) for value in full], axis=2))
                lists[1].append(cut(inner, dy, dx, dc))
                lists[2].append(
                    outer.reshape(depth, 2, 2, 2, hidden // BLOCKS // 2, width)[:, dx, dc, dy]
                )
            chunks.append(lists)

    current = token_low.astype(F32)
    other = token_other
    kept = []
    for layer in range(layers):
        attn_bufs, inner_bufs, outer_bufs = chunks[layer]
        vec = table[layer]
        h, n1, c1, q, k, kt, v, p, xt, ot, ht = attn_forward(
            depth, pos_w, pos_g, current, other, seg, lab, vec, attn_bufs
        )
        current, low, n2, c2, gp, gt = ffn_forward(depth, pos_w, pos_g, h, vec, inner_bufs, outer_bufs)
        if layer + 1 < layers:
            other = move(low, net["core"])
        kept.append((n1, c1, q, kt, v, p, n2, c2, gp, xt, ot, ht, gt))
    hidden_out = move(low, net["swap"])[None]

    range_ids = jnp.arange(SEGS, dtype=jnp.int32)
    own = (small_own[1][None, :] == range_ids[:, None]).astype(F32)
    sums = jnp.dot(own, current, precision=lax.Precision.HIGHEST)
    sums = sums + move(sums, net["core"])
    counts = jnp.sum((lab[:, 0][None, :] == range_ids[:, None]).astype(F32), axis=1)
    pooled = move(sums / counts[:, None], net["swap"])[None]

    grad = grad_in
    collected = [None] * layers
    vectors = [None] * layers
    for layer in reversed(range(layers)):
        attn_bufs, inner_bufs, outer_bufs = chunks[layer]
        vec = table[layer]
        n1, c1, q, kt, v, p, n2, c2, gp, xt, ot, ht, gt = kept[layer]
        rxt, rot, rht, rgt = (move(value[1], net["core"]) for value in (xt, ot, ht, gt))
        dyl, du, da, dal, do, sums = chain_backward(
            pos_w, grad, n2, c2, gp, n1, c1, vec, inner_bufs, outer_bufs, attn_bufs
        )
        rdyl, rdu, rdal = (move(value, net["core"]) for value in (dyl, du, dal))
        outer_parts = outer_grad(gt, rgt, dyl, rdyl)
        dq, dk, dv, qsum = attn_backward(q, kt, v, p, do)
        rdq, rdk, rdv = (move(value, net["core"]) for value in (dq, dk, dv))
        inner_parts = inner_grad(pos_g, ht, rht, du, rdu)
        grad, tk, tv, vsum = input_backward(pos_w, da, dq, dk, dv, rdk, rdv, attn_bufs)
        attn_parts = attn_grad(pos_g, xt, rxt, ot, rot, dq, rdq, tk, tv, dal, rdal)
        vectors[layer] = jnp.concatenate([qsum[:1], vsum[:1], sums[2:12]], axis=0)
        parts = (outer_parts, inner_parts, attn_parts)
        if staged:
            results = [
                net["reduce"](part, (layer * 3 + index) % 2 == 1) for index, part in enumerate(parts)
            ]

            def sides(pair, axis):
                own, got = pair
                return jnp.where(
                    y == 0, jnp.concatenate([own, got], axis), jnp.concatenate([got, own], axis)
                )

            outer = sides(results[0], 0)
            inner = sides(results[1], 1)
            size = width // 2
            four = [
                sides(tuple(value[:, member * size : (member + 1) * size] for value in results[2]), 1)
                for member in range(4)
            ]
        else:
            def whole(outs, by_rows, member=None):
                out = jnp.stack(outs).reshape((2, 2) + outs[0].shape)
                if member is not None:
                    size = out.shape[-1] // 4
                    out = out[..., member * size : (member + 1) * size]
                if by_rows:
                    out = out.transpose(2, 0, 1, 3, 4)
                    out = out.reshape(depth * 2, 1, -1, out.shape[-1])
                else:
                    out = out.transpose(2, 0, 3, 1, 4)
                    out = out.reshape(depth * 2, 1, out.shape[2], -1)
                mine = (jnp.arange(2, dtype=jnp.int32) == core)[None, :, None, None]
                out = jnp.where(mine, out, jnp.zeros_like(out)).reshape(-1, out.shape[-1])
                out = lax.psum_scatter(out, "dp", scatter_dimension=0, tiled=True)
                return lax.psum(out.astype(F32), "seq")

            outer = whole(outer_parts, True)
            inner = whole(inner_parts, False)
            four = [whole(attn_parts, False, member) for member in range(4)]
        collected[layer] = four + [inner, outer]
    tokens_grad = move(grad.astype(BF16), net["swap"]).astype(F32)[None]
    table = jnp.stack(vectors)
    table = net["reduce_small"](table) if staged else lax.psum(table, AXES)
    eight = lax.dynamic_slice_in_dim(table[:, :8], dp * small, small, 2)
    wide = lax.dynamic_slice_in_dim(
        table[:, 8:].reshape(layers, hidden), dp * (hidden // count), hidden // count, 1
    )
    stacked = [jnp.stack([collected[layer][member] for layer in range(layers)]) for member in range(6)]
    return (
        hidden_out,
        pooled,
        tokens_grad,
        stacked[0],
        stacked[1],
        stacked[2],
        stacked[3],
        eight[:, QB],
        eight[:, VB],
        eight[:, OB],
        eight[:, AG],
        eight[:, AS],
        stacked[4],
        wide,
        stacked[5],
        eight[:, UB],
        eight[:, FG],
        eight[:, FS],
    )


def solution(mesh):
    cube = P(None, "dp", None)
    flat = P(None, "dp")
    acts = P("dp", "seq", None)
    ids = P("dp", "seq")
    return jax.shard_map(
        functools.partial(body, build(mesh)),
        mesh=mesh,
        in_specs=(acts, ids, ids, cube, cube, cube, cube, flat, flat, flat, flat, flat, cube, flat, cube)
        + (flat, flat, flat, acts),
        out_specs=(acts, P("dp", None, None), acts, cube, cube, cube, cube)
        + (flat, flat, flat, flat, flat, cube, flat, cube, flat, flat, flat),
        check_vma=False,
    )
```

time: 3460 us -> 961 us (0.28)
  waiting for transfers between devices: 2330 us -> 402 us
  matrix products: 599 us -> 0.38 us
  blocking collectives: 287 us -> 0 us
  Pallas kernels: 0 us -> 195 us
  starting transfers between devices: 2.11 us -> 194 us
  other arithmetic: 85.7 us -> 25.6 us
    reduce_scatter x24 -> x0, waiting for transfers between devices: 1850 us -> none  [the longest x3 416 us: body(): lax.psum_scatter(inner_weight_part, ('dp', 'seq'), scatter_dimension=0, t...]
    dot_general x379 -> x1, matrix products: 586 us -> 0.38 us  [body(): sums = jnp.dot(own, current, precision=lax.Precision.HIGHEST)]
    all_gather x18 -> x0, waiting for transfers between devices: 476 us -> none  [the longest x3 162 us: body(): lax.all_gather(outer_weight[layer_index], 'dp', axis=0, tiled=True)]
    ppermute x0 -> x205, waiting for transfers between devices: none -> 402 us  [move(): return lax.ppermute(value, AXES, perm)]
    pallas_call x0 -> x24, Pallas kernels: none -> 195 us  [the longest x3 45.4 us: ffn_forward(): pl.pallas_call(functools.partial(ffn_kernel, depth, 384), out_shape=(shap...]
    ppermute x0 -> x205, starting transfers between devices: none -> 194 us  [move(): return lax.ppermute(value, AXES, perm)]
    all_gather x25 -> x0, blocking collectives: 163 us -> none  [the longest x3 35.5 us: body(): lax.all_gather(key_low, 'seq', axis=1, tiled=True)]
    unnamed x3 -> x0, blocking collectives: 117 us -> none
  transfers between devices with their start and end apart: 42 -> 205, of which waited for: 34 -> 71; matrix products, arithmetic and copies ran while one was open for 12% -> 5% of each run, Pallas kernels for 0% -> 21%
where the time goes in v1:
time: 961 us; the launch traced here: 950 us
  waiting for transfers between devices  402 us (42%)
  Pallas kernels  195 us (20%)
  starting transfers between devices  194 us (20%)
  local copies, waits for them, and re-layouts  129 us (13%)
  other arithmetic  25.6 us (3%)
    ppermute x205, waiting for transfers between devices, move(): return lax.ppermute(value, AXES, perm)  402 us
    ppermute x205, starting transfers between devices, move(): return lax.ppermute(value, AXES, perm)  194 us
    unnamed x527, local copies, waits for them, and re-layouts  104 us
    pallas_call x3, Pallas kernels, ffn_forward(): pl.pallas_call(functools.partial(ffn_kernel, depth, 384), out_shape=(shap...  45.4 us
    pallas_call x3, Pallas kernels, chain_backward(): pl.pallas_call(functools.partial(chain_kernel, 384), out_shape=(shape((to...  45.4 us
    pallas_call x3, Pallas kernels, attn_forward(): pl.pallas_call(functools.partial(attn_kernel, depth), out_shape=(shape((t...  44.2 us
    pallas_call x3, Pallas kernels, attn_backward(): pl.pallas_call(attn_back_kernel, out_shape=(shape((tokens, width), BF16),...  21.3 us
  transfers between devices with their start and end apart: 205, of which 71 were waited for; matrix products, arithmetic and copies ran while one was open for 5% of the time, Pallas kernels for 21%

profile of v1, /device:TPU:0, one launch (start us, length us, event | category | flops | bytes accessed | tf_op | source)
XLA Modules:
  0.0 950.4 jit_solution(8156787150095409232)
XLA Ops:
  37.4 5.1 collective-permute-start.30
  46.2 6.7 collective-permute-done.20
  59.2 6.4 collective-permute-done.30
  65.6 4.8 collective-permute-start.51
  71.7 6.5 collective-permute-done.41
  78.3 4.9 collective-permute-start.61
  84.4 6.5 collective-permute-done.51
  90.9 4.9 collective-permute-start.72
  98.0 5.5 collective-permute-done.61
  103.5 5.0 collective-permute-start.82
  109.6 6.4 collective-permute-done.72
  122.8 6.0 collective-permute-done.82
  142.0 9.5 collective-permute-done.13.refs_9_.refs_26_
  155.1 9.0 collective-permute-done.23.refs_6_.refs_10_
  168.6 8.1 collective-permute-done.33.refs_14_.refs_18_
  181.4 8.1 collective-permute-done.44.refs_9_.refs_26_
  193.9 8.1 collective-permute-done.54.refs_6_.refs_10_
  207.0 7.7 collective-permute-done.64.refs_14_.refs_18_
  218.3 9.0 collective-permute-done.75.refs_9_.refs_26_
  232.5 7.4 collective-permute-done.85.refs_6_.refs_10_
  244.5 7.9 collective-permute-done.95.refs_14_.refs_18_
  259.8 7.8 collective-permute-done.17.refs_13_.refs_30_
  276.8 8.5 collective-permute-done.37.refs_18_.refs_22_
  286.0 4.1 collective-permute-done.48.refs_13_.refs_30_
  297.4 15.0 %attn_forward.3 = (f32[256,768]{1,0:T(8,128)S(1)}, f32[256,768]{1,0:T(8,128)S(1)}, f32[256,128]{1,0:T(8,128)S(1)}, bf16[256,768]{1,0:T(8,128)(2,1)S(1)}, bf16[51...) custom-call(s32[4]{0:T(128)S(1)} %pad_add_fusion.2.refs_0_.refs_1_.p, ...), custom_call_target="tpu_custom_call" | custom-call | flops 2200000000 | bytes 36000000 | tf_op jit(solution)/shard_map/attn_forward/pallas_call | solution.py:199
  318.4 14.6 %ffn_forward.3 = (f32[256,768]{1,0:T(8,128)S(1)}, bf16[256,768]{1,0:T(8,128)(2,1)S(1)}, f32[256,768]{1,0:T(8,128)S(1)}, f32[256,128]{1,0:T(8,128)S(1)}, bf16[256...) custom-call(s32[4]{0:T(128)S(1)} %pad_add_fusion.2.refs_0_.refs_1_.pos_ref, ...), custom_call_target="tpu_custom_call" | custom-call | flops 2400000000 | bytes 36000000 | tf_op jit(solution)/shard_map/ffn_forward/pallas_call | solution.py:273
  342.5 14.2 %attn_forward.4 = (f32[256,768]{1,0:T(8,128)S(1)}, f32[256,768]{1,0:T(8,128)S(1)}, f32[256,128]{1,0:T(8,128)S(1)}, bf16[256,768]{1,0:T(8,128)(2,1)S(1)}, bf16[51...) custom-call(s32[4]{0:T(128)S(1)} %pad_add_fusion.2.refs_0_.refs_1_.p, ...), custom_call_target="tpu_custom_call" | custom-call | flops 2200000000 | bytes 36000000 | tf_op jit(solution)/shard_map/attn_forward/pallas_call | solution.py:199
  374.0 16.5 %ffn_forward.4 = (f32[256,768]{1,0:T(8,128)S(1)}, bf16[256,768]{1,0:T(8,128)(2,1)}, f32[256,768]{1,0:T(8,128)S(1)}, f32[256,128]{1,0:T(8,128)S(1)}, bf16[256,307...) custom-call(s32[4]{0:T(128)S(1)} %pad_add_fusion.2.refs_0_.refs_1_.pos_ref, ...), custom_call_target="tpu_custom_call" | custom-call | flops 2400000000 | bytes 36000000 | tf_op jit(solution)/shard_map/ffn_forward/pallas_call | solution.py:273
  403.0 15.0 %attn_forward.5 = (f32[256,768]{1,0:T(8,128)S(1)}, f32[256,768]{1,0:T(8,128)S(1)}, f32[256,128]{1,0:T(8,128)S(1)}, bf16[256,768]{1,0:T(8,128)(2,1)S(1)}, bf16[51...) custom-call(s32[4]{0:T(128)S(1)} %pad_add_fusion.2.refs_0_.refs_1_.p, ...), custom_call_target="tpu_custom_call" | custom-call | flops 2200000000 | bytes 36000000 | tf_op jit(solution)/shard_map/attn_forward/pallas_call | solution.py:199
  426.2 4.5 collective-permute-start.104
  444.7 14.3 %ffn_forward.5 = (f32[256,768]{1,0:T(8,128)S(1)}, bf16[256,768]{1,0:T(8,128)(2,1)S(1)}, f32[256,768]{1,0:T(8,128)S(1)}, f32[256,128]{1,0:T(8,128)S(1)}, bf16[256...) custom-call(s32[4]{0:T(128)S(1)} %pad_add_fusion.2.refs_0_.refs_1_.pos_ref, ...), custom_call_target="tpu_custom_call" | custom-call | flops 2400000000 | bytes 36000000 | tf_op jit(solution)/shard_map/ffn_forward/pallas_call | solution.py:273
  467.7 14.6 %chain_backward.3 = (bf16[256,768]{1,0:T(8,128)(2,1)}, bf16[256,3072]{1,0:T(8,128)(2,1)}, f32[256,768]{1,0:T(8,128)}, bf16[256,768]{1,0:T(8,128)(2,1)}, bf16[256...) custom-call(s32[4]{0:T(128)S(1)} %pad_add_fusion.2.refs_0_.refs_1_.pos_ref, ...), custom_call_target="tpu_custom_call" | custom-call | flops 2700000000 | bytes 36000000 | tf_op jit(solution)/shard_map/chain_backward/pallas_call | solution.py:348
  486.4 7.0 attn_backward.3
  502.4 5.2 input_backward.3
  513.9 15.6 %chain_backward.4 = (bf16[256,768]{1,0:T(8,128)(2,1)S(1)}, bf16[256,3072]{1,0:T(8,128)(2,1)}, f32[256,768]{1,0:T(8,128)}, bf16[256,768]{1,0:T(8,128)(2,1)S(1)}, ...) custom-call(s32[4]{0:T(128)S(1)} %pad_add_fusion.2.refs_0_.refs_1_.pos_ref, f32[256,768]{1,0:T(8,128)} %copy-done.129, ...), custom_call_target="tpu_custom_call" | custom-call | flops 2700000000 | bytes 36000000 | tf_op jit(solution)/shard_map/chain_backward/pallas_call | solution.py:348
  532.8 7.4 attn_backward.4
  557.3 7.8 collective-permute-done.199
  566.9 4.2 input_backward.4
  574.3 15.3 %chain_backward.5 = (bf16[256,768]{1,0:T(8,128)(2,1)S(1)}, bf16[256,3072]{1,0:T(8,128)(2,1)}, f32[256,768]{1,0:T(8,128)}, bf16[256,768]{1,0:T(8,128)(2,1)S(1)}, ...) custom-call(s32[4]{0:T(128)S(1)} %pad_add_fusion.2.refs_0_.refs_1_.pos_ref, f32[256,768]{1,0:T(8,128)} %copy-done.130, ...), custom_call_target="tpu_custom_call" | custom-call | flops 2700000000 | bytes 36000000 | tf_op jit(solution)/shard_map/chain_backward/pallas_call | solution.py:348
  592.1 7.0 attn_backward.5
  610.5 5.0 collective-permute-done.138
  621.0 6.0 collective-permute-done.198
  645.4 6.1 collective-permute-done.202
  652.8 20.5 %collective-permute-done.172 = bf16[4,48,1536]{2,1,0:T(8,128)(2,1)S(1)} collective-permute-done((bf16[4,48,1536]{2,1,0:T(8,128)(2,1)S(1)}, bf16[4,48,1536]{2,1,0:T(8,128)(2,1)S(1)}, u32[]{:S(2)}, u32[]{:S(2)}) %collective-permute-start.172) | collective-permute-done | bytes 589856 | tf_op jit(solution)/shard_map/ppermute | solution.py:577
  687.1 9.6 %collective-permute-done.191 = bf16[4,96,768]{2,1,0:T(8,128)(2,1)S(1)} collective-permute-done((bf16[4,96,768]{2,1,0:T(8,128)(2,1)S(1)}, bf16[4,96,768]{2,1,0:T(8,128)(2,1)S(1)}, u32[]{:S(2)}, u32[]{:S(2)}) %collective-permute-start.191) | collective-permute-done | bytes 589856 | tf_op jit(solution)/shard_map/ppermute | solution.py:577
  698.1 4.9 input_backward.5
  716.3 6.6 collective-permute-done.193
  727.6 15.5 %collective-permute-done.146 = f32[3,12,768]{2,1,0:T(8,128)S(1)} collective-permute-done((f32[3,12,768]{2,1,0:T(8,128)S(1)}, f32[3,12,768]{2,1,0:T(8,128)S(1)}, u32[]{:S(2)}, u32[]{:S(2)}) %collective-permute-start.146) | collective-permute-done | bytes 110624 | tf_op jit(solution)/shard_map/ppermute | solution.py:577
  743.5 4.8 collective-permute-done.195
  748.6 4.8 collective-permute-done.147
  755.0 14.3 %collective-permute-done.173 = bf16[4,48,1536]{2,1,0:T(8,128)(2,1)S(1)} collective-permute-done((bf16[4,48,1536]{2,1,0:T(8,128)(2,1)S(1)}, bf16[4,48,1536]{2,1,0:T(8,128)(2,1)S(1)}, u32[]{:S(2)}, u32[]{:S(2)}) %collective-permute-start.173) | collective-permute-done | bytes 589856 | tf_op jit(solution)/shard_map/ppermute | solution.py:577
  775.9 4.0 collective-permute-done.149
  779.9 6.9 collective-permute-start.130
  800.0 9.2 collective-permute-done.175
  811.3 16.8 %collective-permute-done.117 = bf16[4,48,1536]{2,1,0:T(8,128)(2,1)S(1)} collective-permute-done((bf16[4,48,1536]{2,1,0:T(8,128)(2,1)S(1)}, bf16[4,48,1536]{2,1,0:T(8,128)(2,1)S(1)}, u32[]{:S(2)}, u32[]{:S(2)}) %collective-permute-start.117) | collective-permute-done | bytes 589856 | tf_op jit(solution)/shard_map/ppermute | solution.py:577
  828.6 12.2 %collective-permute-done.163 = bf16[4,48,1536]{2,1,0:T(8,128)(2,1)S(1)} collective-permute-done((bf16[4,48,1536]{2,1,0:T(8,128)(2,1)S(1)}, bf16[4,48,1536]{2,1,0:T(8,128)(2,1)S(1)}, u32[]{:S(2)}, u32[]{:S(2)}) %collective-permute-start.163) | collective-permute-done | bytes 589856 | tf_op jit(solution)/shard_map/ppermute | solution.py:577
  846.1 9.0 collective-permute-done.182
  863.0 5.0 collective-permute-done.184
  874.7 14.0 %collective-permute-done.186 = bf16[96,768]{1,0:T(8,128)(2,1)S(1)} collective-permute-done((bf16[96,768]{1,0:T(8,128)(2,1)S(1)}, bf16[96,768]{1,0:T(8,128)(2,1)S(1)}, u32[]{:S(2)}, u32[]{:S(2)}) %collective-permute-start.186) | collective-permute-done | bytes 147488 | tf_op jit(solution)/shard_map/ppermute | solution.py:577
  899.7 4.3 collective-permute-start.167
  904.0 4.6 collective-permute-done.120
  911.2 5.0 collective-permute-done.166
  922.8 5.4 collective-permute-done.155
  935.8 6.1 collective-permute-done.157
  (1072 shorter events, 403.7 us)
Async XLA Ops:
  37.4 28.2 %collective-permute-start.30 = (bf16[96,768]{1,0:T(8,128)(2,1)S(1)}, bf16[96,768]{1,0:T(8,128)(2,1)S(1)}, u32[]{:S(2)}, u32[]{:S(2)}) collective-permute-start(bf16[96,768]{1,0:T(8,128)(2,1)S(1)} %fusion.56), channel_id=1, source_target_pairs={{16,0},{17,1},{18,2},{19,3},{20,4},{21,5},{22,6},{23,7},{24,8},{25... | collective-permute-start | bytes 442376 | tf_op jit(solution)/shard_map/ppermute | solution.py:577
  54.5 23.8 %collective-permute-start.41 = (bf16[48,1536]{1,0:T(8,128)(2,1)S(1)}, bf16[48,1536]{1,0:T(8,128)(2,1)S(1)}, u32[]{:S(2)}, u32[]{:S(2)}) collective-permute-start(bf16[48,1536]{1,0:T(8,128)(2,1)S(1)} %get-tuple-element.363), channel_id=1, source_target_pairs={{16,0},{17,1},{18,2},{19,3},{20,4},{21,5},{22,6},{23,7},{24,8},{25... | collective-permute-start | bytes 442376 | tf_op jit(solution)/shard_map/ppermute | solution.py:577
  65.6 25.2 %collective-permute-start.51 = (bf16[48,1536]{1,0:T(8,128)(2,1)S(1)}, bf16[48,1536]{1,0:T(8,128)(2,1)S(1)}, u32[]{:S(2)}, u32[]{:S(2)}) collective-permute-start(bf16[48,1536]{1,0:T(8,128)(2,1)S(1)} %copy-done.248), channel_id=1, source_target_pairs={{16,0},{17,1},{18,2},{19,3},{20,4},{21,5},{22,6},{23,7},{24,8},{25... | collective-permute-start | bytes 442376 | tf_op jit(solution)/shard_map/ppermute | solution.py:577
  78.3 25.1 %collective-permute-start.61 = (bf16[96,768]{1,0:T(8,128)(2,1)S(1)}, bf16[96,768]{1,0:T(8,128)(2,1)S(1)}, u32[]{:S(2)}, u32[]{:S(2)}) collective-permute-start(bf16[96,768]{1,0:T(8,128)(2,1)S(1)} %fusion.54), channel_id=1, source_target_pairs={{16,0},{17,1},{18,2},{19,3},{20,4},{21,5},{22,6},{23,7},{24,8},{25... | collective-permute-start | bytes 442376 | tf_op jit(solution)/shard_map/ppermute | solution.py:577
  90.9 25.2 %collective-permute-start.72 = (bf16[48,1536]{1,0:T(8,128)(2,1)S(1)}, bf16[48,1536]{1,0:T(8,128)(2,1)S(1)}, u32[]{:S(2)}, u32[]{:S(2)}) collective-permute-start(bf16[48,1536]{1,0:T(8,128)(2,1)S(1)} %get-tuple-element.358), channel_id=1, source_target_pairs={{16,0},{17,1},{18,2},{19,3},{20,4},{21,5},{22,6},{23,7},{24,8},{25... | collective-permute-start | bytes 442376 | tf_op jit(solution)/shard_map/ppermute | solution.py:577
  103.5 25.3 %collective-permute-start.82 = (bf16[48,1536]{1,0:T(8,128)(2,1)S(1)}, bf16[48,1536]{1,0:T(8,128)(2,1)S(1)}, u32[]{:S(2)}, u32[]{:S(2)}) collective-permute-start(bf16[48,1536]{1,0:T(8,128)(2,1)S(1)} %copy-done.247), channel_id=1, source_target_pairs={{16,0},{17,1},{18,2},{19,3},{20,4},{21,5},{22,6},{23,7},{24,8},{25... | collective-permute-start | bytes 442376 | tf_op jit(solution)/shard_map/ppermute | solution.py:577
  138.6 25.5 %collective-permute-start.23 = (bf16[4,48,1536]{2,1,0:T(8,128)(2,1)S(1)}, bf16[4,48,1536]{2,1,0:T(8,128)(2,1)S(1)}, u32[]{:S(2)}, u32[]{:S(2)}) collective-permute-start(bf16[4,48,1536]{2,1,0:T(8,128)(2,1)S(1)} %pad_maximum_fusion.3.refs_4_.refs_8_), channel_id=1, source_target_pairs={{4,0},{5,1},{6,2},{7,3},{0,4},{1,5},{2,6},{3,7},{12,8},{13,9},{14,... | collective-permute-start | bytes 1769480 | tf_op jit(solution)/shard_map/ppermute | solution.py:577
  138.8 28.4 %collective-permute-start.25 = (bf16[4,48,1536]{2,1,0:T(8,128)(2,1)S(1)}, bf16[4,48,1536]{2,1,0:T(8,128)(2,1)S(1)}, u32[]{:S(2)}, u32[]{:S(2)}) collective-permute-start(bf16[4,48,1536]{2,1,0:T(8,128)(2,1)S(1)} %pad_maximum_fusion.3.refs_4_.refs_8_), channel_id=1, source_target_pairs={{1,0},{0,1},{3,2},{2,3},{5,4},{4,5},{7,6},{6,7},{9,8},{8,9},{11,10... | collective-permute-start | bytes 1769480 | tf_op jit(solution)/shard_map/ppermute | solution.py:577
  154.6 25.4 %collective-permute-start.35 = (bf16[4,96,768]{2,1,0:T(8,128)(2,1)S(1)}, bf16[4,96,768]{2,1,0:T(8,128)(2,1)}, u32[]{:S(2)}, u32[]{:S(2)}) collective-permute-start(bf16[4,96,768]{2,1,0:T(8,128)(2,1)S(1)} %pad_maximum_fusion.4.refs_12_.refs_16_), channel_id=1, source_target_pairs={{1,0},{0,1},{3,2},{2,3},{5,4},{4,5},{7,6},{6,7},{9,8},{8,9},{11,10... | collective-permute-start | bytes 1769480 | tf_op jit(solution)/shard_map/ppermute | solution.py:577
  168.2 24.4 %collective-permute-start.46 = (bf16[4,48,1536]{2,1,0:T(8,128)(2,1)S(1)}, bf16[4,48,1536]{2,1,0:T(8,128)(2,1)}, u32[]{:S(2)}, u32[]{:S(2)}) collective-permute-start(bf16[4,48,1536]{2,1,0:T(8,128)(2,1)S(1)} %pad_maximum_fusion.5.refs_7_.refs_24_), channel_id=1, source_target_pairs={{1,0},{0,1},{3,2},{2,3},{5,4},{4,5},{7,6},{6,7},{9,8},{8,9},{11,10... | collective-permute-start | bytes 1769480 | tf_op jit(solution)/shard_map/ppermute | solution.py:577
  180.9 24.3 %collective-permute-start.56 = (bf16[4,48,1536]{2,1,0:T(8,128)(2,1)S(1)}, bf16[4,48,1536]{2,1,0:T(8,128)(2,1)S(1)}, u32[]{:S(2)}, u32[]{:S(2)}) collective-permute-start(bf16[4,48,1536]{2,1,0:T(8,128)(2,1)S(1)} %pad_maximum_fusion.6.refs_4_.refs_8_), channel_id=1, source_target_pairs={{1,0},{0,1},{3,2},{2,3},{5,4},{4,5},{7,6},{6,7},{9,8},{8,9},{11,10... | collective-permute-start | bytes 1769480 | tf_op jit(solution)/shard_map/ppermute | solution.py:577
  193.5 24.3 %collective-permute-start.66 = (bf16[4,96,768]{2,1,0:T(8,128)(2,1)S(1)}, bf16[4,96,768]{2,1,0:T(8,128)(2,1)S(1)}, u32[]{:S(2)}, u32[]{:S(2)}) collective-permute-start(bf16[4,96,768]{2,1,0:T(8,128)(2,1)S(1)} %pad_maximum_fusion.7.refs_12_.refs_16_), channel_id=1, source_target_pairs={{1,0},{0,1},{3,2},{2,3},{5,4},{4,5},{7,6},{6,7},{9,8},{8,9},{11,10... | collective-permute-start | bytes 1769480 | tf_op jit(solution)/shard_map/ppermute | solution.py:577
  206.8 23.6 %collective-permute-start.77 = (bf16[4,48,1536]{2,1,0:T(8,128)(2,1)S(1)}, bf16[4,48,1536]{2,1,0:T(8,128)(2,1)S(1)}, u32[]{:S(2)}, u32[]{:S(2)}) collective-permute-start(bf16[4,48,1536]{2,1,0:T(8,128)(2,1)S(1)} %pad_maximum_fusion.8.refs_7_.refs_24_), channel_id=1, source_target_pairs={{1,0},{0,1},{3,2},{2,3},{5,4},{4,5},{7,6},{6,7},{9,8},{8,9},{11,10... | collective-permute-start | bytes 1769480 | tf_op jit(solution)/shard_map/ppermute | solution.py:577
  217.8 25.4 %collective-permute-start.87 = (bf16[4,48,1536]{2,1,0:T(8,128)(2,1)S(1)}, bf16[4,48,1536]{2,1,0:T(8,128)(2,1)}, u32[]{:S(2)}, u32[]{:S(2)}) collective-permute-start(bf16[4,48,1536]{2,1,0:T(8,128)(2,1)S(1)} %pad_maximum_fusion.9.refs_4_.refs_8_), channel_id=1, source_target_pairs={{1,0},{0,1},{3,2},{2,3},{5,4},{4,5},{7,6},{6,7},{9,8},{8,9},{11,10... | collective-permute-start | bytes 1769480 | tf_op jit(solution)/shard_map/ppermute | solution.py:577
  231.3 23.6 %collective-permute-start.97 = (bf16[4,96,768]{2,1,0:T(8,128)(2,1)S(1)}, bf16[4,96,768]{2,1,0:T(8,128)(2,1)}, u32[]{:S(2)}, u32[]{:S(2)}) collective-permute-start(bf16[4,96,768]{2,1,0:T(8,128)(2,1)S(1)} %pad_maximum_fusion.10.refs_12_.refs_16_), channel_id=1, source_target_pairs={{1,0},{0,1},{3,2},{2,3},{5,4},{4,5},{7,6},{6,7},{9,8},{8,9},{11,10... | collective-permute-start | bytes 1769480 | tf_op jit(solution)/shard_map/ppermute | solution.py:577
  285.4 31.2 %collective-permute-start.55 = (bf16[4,48,1536]{2,1,0:T(8,128)(2,1)}, bf16[4,48,1536]{2,1,0:T(8,128)(2,1)S(1)}, u32[]{:S(2)}, u32[]{:S(2)}) collective-permute-start(bf16[4,48,1536]{2,1,0:T(8,128)(2,1)} %copy-done.64), channel_id=1, source_target_pairs={{2,0},{3,1},{0,2},{1,3},{6,4},{7,5},{4,6},{5,7},{10,8},{11,9},{8,1... | collective-permute-start | bytes 1769480 | tf_op jit(solution)/shard_map/ppermute | solution.py:577
  285.4 31.8 %collective-permute-start.57 = (bf16[4,48,1536]{2,1,0:T(8,128)(2,1)}, bf16[4,48,1536]{2,1,0:T(8,128)(2,1)S(1)}, u32[]{:S(2)}, u32[]{:S(2)}) collective-permute-start(bf16[4,48,1536]{2,1,0:T(8,128)(2,1)} %copy-done.67), channel_id=1, source_target_pairs={{2,0},{3,1},{0,2},{1,3},{6,4},{7,5},{4,6},{5,7},{10,8},{11,9},{8,1... | collective-permute-start | bytes 1769480 | tf_op jit(solution)/shard_map/ppermute | solution.py:577
  285.9 31.8 %collective-permute-start.28 = (bf16[4,48,1536]{2,1,0:T(8,128)(2,1)}, bf16[4,48,1536]{2,1,0:T(8,128)(2,1)S(1)}, u32[]{:S(2)}, u32[]{:S(2)}) collective-permute-start(bf16[4,48,1536]{2,1,0:T(8,128)(2,1)} %copy-done.58), channel_id=1, source_target_pairs={{2,0},{3,1},{0,2},{1,3},{6,4},{7,5},{4,6},{5,7},{10,8},{11,9},{8,1... | collective-permute-start | bytes 1769480 | tf_op jit(solution)/shard_map/ppermute | solution.py:577
  290.0 27.8 %collective-permute-start.38 = (bf16[4,96,768]{2,1,0:T(8,128)(2,1)}, bf16[4,96,768]{2,1,0:T(8,128)(2,1)S(1)}, u32[]{:S(2)}, u32[]{:S(2)}) collective-permute-start(bf16[4,96,768]{2,1,0:T(8,128)(2,1)} %collective-permute-done.37.refs_18_.refs_22_), channel_id=1, source_target_pairs={{2,0},{3,1},{0,2},{1,3},{6,4},{7,5},{4,6},{5,7},{10,8},{11,9},{8,1... | collective-permute-start | bytes 1769480 | tf_op jit(solution)/shard_map/ppermute | solution.py:577
  292.1 44.6 %collective-permute-start.58 = (bf16[4,48,1536]{2,1,0:T(8,128)(2,1)}, bf16[4,48,1536]{2,1,0:T(8,128)(2,1)}, u32[]{:S(2)}, u32[]{:S(2)}) collective-permute-start(bf16[4,48,1536]{2,1,0:T(8,128)(2,1)} %copy-done.67), channel_id=1, source_target_pairs={{4,0},{5,1},{6,2},{7,3},{0,4},{1,5},{2,6},{3,7},{12,8},{13,9},{14,... | collective-permute-start | bytes 1769480 | tf_op jit(solution)/shard_map/ppermute | solution.py:577
  337.5 26.6 %collective-permute-start.76 = (bf16[4,48,1536]{2,1,0:T(8,128)(2,1)S(1)}, bf16[4,48,1536]{2,1,0:T(8,128)(2,1)S(1)}, u32[]{:S(2)}, u32[]{:S(2)}) collective-permute-start(bf16[4,48,1536]{2,1,0:T(8,128)(2,1)S(1)} %copy-done.26), channel_id=1, source_target_pairs={{2,0},{3,1},{0,2},{1,3},{6,4},{7,5},{4,6},{5,7},{10,8},{11,9},{8,1... | collective-permute-start | bytes 1769480 | tf_op jit(solution)/shard_map/ppermute | solution.py:577
  338.8 25.6 %collective-permute-start.79 = (bf16[4,48,1536]{2,1,0:T(8,128)(2,1)S(1)}, bf16[4,48,1536]{2,1,0:T(8,128)(2,1)S(1)}, u32[]{:S(2)}, u32[]{:S(2)}) collective-permute-start(bf16[4,48,1536]{2,1,0:T(8,128)(2,1)S(1)} %copy-done.28), channel_id=1, source_target_pairs={{4,0},{5,1},{6,2},{7,3},{0,4},{1,5},{2,6},{3,7},{12,8},{13,9},{14,... | collective-permute-start | bytes 1769480 | tf_op jit(solution)/shard_map/ppermute | solution.py:577
  340.3 25.9 %collective-permute-start.59 = (bf16[4,48,1536]{2,1,0:T(8,128)(2,1)}, bf16[4,48,1536]{2,1,0:T(8,128)(2,1)}, u32[]{:S(2)}, u32[]{:S(2)}) collective-permute-start(bf16[4,48,1536]{2,1,0:T(8,128)(2,1)} %collective-permute-done.58.refs_10_.refs_14_), channel_id=1, source_target_pairs={{2,0},{3,1},{0,2},{1,3},{6,4},{7,5},{4,6},{5,7},{10,8},{11,9},{8,1... | collective-permute-start | bytes 1769480 | tf_op jit(solution)/shard_map/ppermute | solution.py:577
  340.3 26.2 %collective-permute-start.69 = (bf16[4,96,768]{2,1,0:T(8,128)(2,1)}, bf16[4,96,768]{2,1,0:T(8,128)(2,1)}, u32[]{:S(2)}, u32[]{:S(2)}) collective-permute-start(bf16[4,96,768]{2,1,0:T(8,128)(2,1)} %collective-permute-done.68.refs_18_.refs_22_), channel_id=1, source_target_pairs={{2,0},{3,1},{0,2},{1,3},{6,4},{7,5},{4,6},{5,7},{10,8},{11,9},{8,1... | collective-permute-start | bytes 1769480 | tf_op jit(solution)/shard_map/ppermute | solution.py:577
  341.5 51.5 %collective-permute-start.78 = (bf16[4,48,1536]{2,1,0:T(8,128)(2,1)S(1)}, bf16[4,48,1536]{2,1,0:T(8,128)(2,1)S(1)}, u32[]{:S(2)}, u32[]{:S(2)}) collective-permute-start(bf16[4,48,1536]{2,1,0:T(8,128)(2,1)S(1)} %copy-done.28), channel_id=1, source_target_pairs={{2,0},{3,1},{0,2},{1,3},{6,4},{7,5},{4,6},{5,7},{10,8},{11,9},{8,1... | collective-permute-start | bytes 1769480 | tf_op jit(solution)/shard_map/ppermute | solution.py:577
  364.1 33.0 %collective-permute-start.86 = (bf16[4,48,1536]{2,1,0:T(8,128)(2,1)}, bf16[4,48,1536]{2,1,0:T(8,128)(2,1)S(1)}, u32[]{:S(2)}, u32[]{:S(2)}) collective-permute-start(bf16[4,48,1536]{2,1,0:T(8,128)(2,1)} %copy-done.88), channel_id=1, source_target_pairs={{2,0},{3,1},{0,2},{1,3},{6,4},{7,5},{4,6},{5,7},{10,8},{11,9},{8,1... | collective-permute-start | bytes 1769480 | tf_op jit(solution)/shard_map/ppermute | solution.py:577
  364.4 32.7 %collective-permute-start.89 = (bf16[4,48,1536]{2,1,0:T(8,128)(2,1)}, bf16[4,48,1536]{2,1,0:T(8,128)(2,1)}, u32[]{:S(2)}, u32[]{:S(2)}) collective-permute-start(bf16[4,48,1536]{2,1,0:T(8,128)(2,1)} %copy-done.88), channel_id=1, source_target_pairs={{1,0},{0,1},{3,2},{2,3},{5,4},{4,5},{7,6},{6,7},{9,8},{8,9},{11,10... | collective-permute-start | bytes 1769480 | tf_op jit(solution)/shard_map/ppermute | solution.py:577
  366.2 31.4 %collective-permute-start.99 = (bf16[4,96,768]{2,1,0:T(8,128)(2,1)}, bf16[4,96,768]{2,1,0:T(8,128)(2,1)}, u32[]{:S(2)}, u32[]{:S(2)}) collective-permute-start(bf16[4,96,768]{2,1,0:T(8,128)(2,1)} %collective-permute-done.97.refs_16_.refs_20_), channel_id=1, source_target_pairs={{4,0},{5,1},{6,2},{7,3},{0,4},{1,5},{2,6},{3,7},{12,8},{13,9},{14,... | collective-permute-start | bytes 1769480 | tf_op jit(solution)/shard_map/ppermute | solution.py:577
  366.5 31.2 %collective-permute-start.80 = (bf16[4,48,1536]{2,1,0:T(8,128)(2,1)S(1)}, bf16[4,48,1536]{2,1,0:T(8,128)(2,1)S(1)}, u32[]{:S(2)}, u32[]{:S(2)}) collective-permute-start(bf16[4,48,1536]{2,1,0:T(8,128)(2,1)S(1)} %collective-permute-done.79.refs_13_.refs_30_), channel_id=1, source_target_pairs={{2,0},{3,1},{0,2},{1,3},{6,4},{7,5},{4,6},{5,7},{10,8},{11,9},{8,1... | collective-permute-start | bytes 1769480 | tf_op jit(solution)/shard_map/ppermute | solution.py:577
  397.0 34.5 %collective-permute-start.98 = (bf16[4,96,768]{2,1,0:T(8,128)(2,1)}, bf16[4,96,768]{2,1,0:T(8,128)(2,1)S(1)}, u32[]{:S(2)}, u32[]{:S(2)}) collective-permute-start(bf16[4,96,768]{2,1,0:T(8,128)(2,1)} %collective-permute-done.97.refs_16_.refs_20_), channel_id=1, source_target_pairs={{2,0},{3,1},{0,2},{1,3},{6,4},{7,5},{4,6},{5,7},{10,8},{11,9},{8,1... | collective-permute-start | bytes 1769480 | tf_op jit(solution)/shard_map/ppermute | solution.py:577
  397.1 28.3 %collective-permute-start.88 = (bf16[4,48,1536]{2,1,0:T(8,128)(2,1)}, bf16[4,48,1536]{2,1,0:T(8,128)(2,1)S(1)}, u32[]{:S(2)}, u32[]{:S(2)}) collective-permute-start(bf16[4,48,1536]{2,1,0:T(8,128)(2,1)} %collective-permute-done.87.refs_8_.refs_12_), channel_id=1, source_target_pairs={{2,0},{3,1},{0,2},{1,3},{6,4},{7,5},{4,6},{5,7},{10,8},{11,9},{8,1... | collective-permute-start | bytes 1769480 | tf_op jit(solution)/shard_map/ppermute | solution.py:577
  397.6 33.1 %collective-permute-start.96 = (bf16[4,96,768]{2,1,0:T(8,128)(2,1)}, bf16[4,96,768]{2,1,0:T(8,128)(2,1)S(1)}, u32[]{:S(2)}, u32[]{:S(2)}) collective-permute-start(bf16[4,96,768]{2,1,0:T(8,128)(2,1)} %collective-permute-done.95.refs_14_.refs_18_), channel_id=1, source_target_pairs={{2,0},{3,1},{0,2},{1,3},{6,4},{7,5},{4,6},{5,7},{10,8},{11,9},{8,1... | collective-permute-start | bytes 1769480 | tf_op jit(solution)/shard_map/ppermute | solution.py:577
  397.6 34.7 %collective-permute-start.90 = (bf16[4,48,1536]{2,1,0:T(8,128)(2,1)}, bf16[4,48,1536]{2,1,0:T(8,128)(2,1)S(1)}, u32[]{:S(2)}, u32[]{:S(2)}) collective-permute-start(bf16[4,48,1536]{2,1,0:T(8,128)(2,1)} %collective-permute-done.89.refs_10_.refs_14_), channel_id=1, source_target_pairs={{2,0},{3,1},{0,2},{1,3},{6,4},{7,5},{4,6},{5,7},{10,8},{11,9},{8,1... | collective-permute-start | bytes 1769480 | tf_op jit(solution)/shard_map/ppermute | solution.py:577
  398.1 35.1 %collective-permute-start.100 = (bf16[4,96,768]{2,1,0:T(8,128)(2,1)}, bf16[4,96,768]{2,1,0:T(8,128)(2,1)S(1)}, u32[]{:S(2)}, u32[]{:S(2)}) collective-permute-start(bf16[4,96,768]{2,1,0:T(8,128)(2,1)} %collective-permute-done.99.refs_18_.refs_22_), channel_id=1, source_target_pairs={{2,0},{3,1},{0,2},{1,3},{6,4},{7,5},{4,6},{5,7},{10,8},{11,9},{8,1... | collective-permute-start | bytes 1769480 | tf_op jit(solution)/shard_map/ppermute | solution.py:577
  426.2 36.1 %collective-permute-start.104 = (bf16[256,768]{1,0:T(8,128)(2,1)}, bf16[256,768]{1,0:T(8,128)(2,1)}, u32[]{:S(2)}, u32[]{:S(2)}) collective-permute-start(bf16[256,768]{1,0:T(8,128)(2,1)} %bitcast.69), channel_id=1, source_target_pairs={{0,0},{2,1},{1,2},{3,3},{4,4},{6,5},{5,6},{7,7},{8,8},{10,9},{9,10... | collective-permute-start | bytes 1179656 | tf_op jit(solution)/shard_map/ppermute | solution.py:577
  460.3 39.4 %collective-permute-start.101 = (bf16[256,768]{1,0:T(8,128)(2,1)S(1)}, bf16[256,768]{1,0:T(8,128)(2,1)S(1)}, u32[]{:S(2)}, u32[]{:S(2)}) collective-permute-start(bf16[256,768]{1,0:T(8,128)(2,1)S(1)} %get-tuple-element.151), channel_id=1, source_target_pairs={{0,0},{2,1},{1,2},{3,3},{4,4},{6,5},{5,6},{7,7},{8,8},{10,9},{9,10... | collective-permute-start | bytes 1179656 | tf_op jit(solution)/shard_map/ppermute | solution.py:577
  461.5 32.7 %collective-permute-start.102 = (f32[4,768]{1,0:T(4,128)S(1)}, f32[4,768]{1,0:T(4,128)S(1)}, u32[]{:S(2)}, u32[]{:S(2)}) collective-permute-start(f32[4,768]{1,0:T(4,128)S(1)} %fusion.30), channel_id=1, source_target_pairs={{2,0},{3,1},{0,2},{1,3},{6,4},{7,5},{4,6},{5,7},{10,8},{11,9},{8,1... | collective-permute-start | bytes 36872 | tf_op jit(solution)/shard_map/ppermute | solution.py:577
  500.5 40.8 %collective-permute-start.196 = (bf16[2,2,4,96,256]{4,3,2,1,0:T(8,128)(2,1)}, bf16[2,2,4,96,256]{4,3,2,1,0:T(8,128)(2,1)S(1)}, u32[]{:S(2)}, u32[]{:S(2)}) collective-permute-start(bf16[2,2,4,96,256]{4,3,2,1,0:T(8,128)(2,1)} %slice_bitcast_fusion), channel_id=1, source_target_pairs={{2,0},{3,1},{0,2},{1,3},{6,4},{7,5},{4,6},{5,7},{10,8},{11,9},{8,1... | collective-permute-start | bytes 2359304 | tf_op jit(solution)/shard_map/ppermute | solution.py:577
  502.3 47.0 %collective-permute-start.187 = (bf16[2,2,4,96,256]{4,3,2,1,0:T(8,128)(2,1)}, bf16[2,2,4,96,256]{4,3,2,1,0:T(8,128)(2,1)}, u32[]{:S(2)}, u32[]{:S(2)}) collective-permute-start(bf16[2,2,4,96,256]{4,3,2,1,0:T(8,128)(2,1)} %slice_bitcast_fusion.1), channel_id=1, source_target_pairs={{2,0},{3,1},{0,2},{1,3},{6,4},{7,5},{4,6},{5,7},{10,8},{11,9},{8,1... | collective-permute-start | bytes 2359304 | tf_op jit(solution)/shard_map/ppermute | solution.py:577
  507.6 32.6 %collective-permute-start.197 = (bf16[256,768]{1,0:T(8,128)(2,1)}, bf16[256,768]{1,0:T(8,128)(2,1)S(1)}, u32[]{:S(2)}, u32[]{:S(2)}) collective-permute-start(bf16[256,768]{1,0:T(8,128)(2,1)} %get-tuple-element.265.da_ref), channel_id=1, source_target_pairs={{2,0},{3,1},{0,2},{1,3},{6,4},{7,5},{4,6},{5,7},{10,8},{11,9},{8,1... | collective-permute-start | bytes 1179656 | tf_op jit(solution)/shard_map/ppermute | solution.py:577
  513.7 41.2 %collective-permute-start.139 = (bf16[4,48,1536]{2,1,0:T(8,128)(2,1)}, bf16[4,48,1536]{2,1,0:T(8,128)(2,1)}, u32[]{:S(2)}, u32[]{:S(2)}) collective-permute-start(bf16[4,48,1536]{2,1,0:T(8,128)(2,1)} %get-tuple-element.224), channel_id=1, source_target_pairs={{1,0},{0,1},{3,2},{2,3},{5,4},{4,5},{7,6},{6,7},{9,8},{8,9},{11,10... | collective-permute-start | bytes 1769480 | tf_op jit(solution)/shard_map/ppermute | solution.py:577
  540.9 60.1 %collective-permute-start.170 = (bf16[256,3072]{1,0:T(8,128)(2,1)}, bf16[256,3072]{1,0:T(8,128)(2,1)}, u32[]{:S(2)}, u32[]{:S(2)}) collective-permute-start(bf16[256,3072]{1,0:T(8,128)(2,1)} %get-tuple-element.247.da_ref), channel_id=1, source_target_pairs={{2,0},{3,1},{0,2},{1,3},{6,4},{7,5},{4,6},{5,7},{10,8},{11,9},{8,1... | collective-permute-start | bytes 4718600 | tf_op jit(solution)/shard_map/ppermute | solution.py:577
  542.1 23.9 %collective-permute-start.107 = (bf16[512,768]{1,0:T(8,128)(2,1)S(1)}, bf16[512,768]{1,0:T(8,128)(2,1)S(1)}, u32[]{:S(2)}, u32[]{:S(2)}) collective-permute-start(bf16[512,768]{1,0:T(8,128)(2,1)S(1)} %get-tuple-element.180.refs_3_), channel_id=1, source_target_pairs={{2,0},{3,1},{0,2},{1,3},{6,4},{7,5},{4,6},{5,7},{10,8},{11,9},{8,1... | collective-permute-start | bytes 2359304 | tf_op jit(solution)/shard_map/ppermute | solution.py:577
  566.1 33.1 %collective-permute-start.169 = (bf16[2,4,48,256]{3,2,1,0:T(8,128)(2,1)}, bf16[2,4,48,256]{3,2,1,0:T(8,128)(2,1)}, u32[]{:S(2)}, u32[]{:S(2)}) collective-permute-start(bf16[2,4,48,256]{3,2,1,0:T(8,128)(2,1)} %slice_bitcast_fusion.3), channel_id=1, source_target_pairs={{2,0},{3,1},{0,2},{1,3},{6,4},{7,5},{4,6},{5,7},{10,8},{11,9},{8,1... | collective-permute-start | bytes 589832 | tf_op jit(solution)/shard_map/ppermute | solution.py:577
  566.6 38.5 %collective-permute-start.125 = (bf16[256,768]{1,0:T(8,128)(2,1)S(1)}, bf16[256,768]{1,0:T(8,128)(2,1)S(1)}, u32[]{:S(2)}, u32[]{:S(2)}) collective-permute-start(bf16[256,768]{1,0:T(8,128)(2,1)S(1)} %get-tuple-element.179.refs_2_.qa_ref), channel_id=1, source_target_pairs={{2,0},{3,1},{0,2},{1,3},{6,4},{7,5},{4,6},{5,7},{10,8},{11,9},{8,1... | collective-permute-start | bytes 1179656 | tf_op jit(solution)/shard_map/ppermute | solution.py:577
  571.9 33.3 %collective-permute-start.126 = (bf16[256,768]{1,0:T(8,128)(2,1)S(1)}, bf16[256,768]{1,0:T(8,128)(2,1)S(1)}, u32[]{:S(2)}, u32[]{:S(2)}) collective-permute-start(bf16[256,768]{1,0:T(8,128)(2,1)S(1)} %copy-done.196), channel_id=1, source_target_pairs={{2,0},{3,1},{0,2},{1,3},{6,4},{7,5},{4,6},{5,7},{10,8},{11,9},{8,1... | collective-permute-start | bytes 1179656 | tf_op jit(solution)/shard_map/ppermute | solution.py:577
  572.4 36.3 %collective-permute-start.190 = (bf16[4,96,768]{2,1,0:T(8,128)(2,1)}, bf16[4,96,768]{2,1,0:T(8,128)(2,1)S(1)}, u32[]{:S(2)}, u32[]{:S(2)}) collective-permute-start(bf16[4,96,768]{2,1,0:T(8,128)(2,1)} %get-tuple-element.263), channel_id=1, source_target_pairs={{4,0},{5,1},{6,2},{7,3},{0,4},{1,5},{2,6},{3,7},{12,8},{13,9},{14,... | collective-permute-start | bytes 1769480 | tf_op jit(solution)/shard_map/ppermute | solution.py:577
  605.1 26.0 %collective-permute-start.178 = (bf16[2,2,4,96,256]{4,3,2,1,0:T(8,128)(2,1)S(1)}, bf16[2,2,4,96,256]{4,3,2,1,0:T(8,128)(2,1)S(1)}, u32[]{:S(2)}, u32[]{:S(2)}) collective-permute-start(bf16[2,2,4,96,256]{4,3,2,1,0:T(8,128)(2,1)S(1)} %copy-done.228), channel_id=1, source_target_pairs={{2,0},{3,1},{0,2},{1,3},{6,4},{7,5},{4,6},{5,7},{10,8},{11,9},{8,1... | collective-permute-start | bytes 2359304 | tf_op jit(solution)/shard_map/ppermute | solution.py:577
  632.3 71.3 %collective-permute-start.161 = (bf16[256,3072]{1,0:T(8,128)(2,1)S(1)}, bf16[256,3072]{1,0:T(8,128)(2,1)S(1)}, u32[]{:S(2)}, u32[]{:S(2)}) collective-permute-start(bf16[256,3072]{1,0:T(8,128)(2,1)S(1)} %copy-done.182), channel_id=1, source_target_pairs={{2,0},{3,1},{0,2},{1,3},{6,4},{7,5},{4,6},{5,7},{10,8},{11,9},{8,1... | collective-permute-start | bytes 4718600 | tf_op jit(solution)/shard_map/ppermute | solution.py:577
  642.2 44.8 %collective-permute-start.189 = (bf16[4,96,768]{2,1,0:T(8,128)(2,1)S(1)}, bf16[4,96,768]{2,1,0:T(8,128)(2,1)S(1)}, u32[]{:S(2)}, u32[]{:S(2)}) collective-permute-start(bf16[4,96,768]{2,1,0:T(8,128)(2,1)S(1)} %copy-done.190), channel_id=1, source_target_pairs={{4,0},{5,1},{6,2},{7,3},{0,4},{1,5},{2,6},{3,7},{12,8},{13,9},{14,... | collective-permute-start | bytes 1769480 | tf_op jit(solution)/shard_map/ppermute | solution.py:577
  651.5 45.5 %collective-permute-start.109 = (bf16[512,768]{1,0:T(8,128)(2,1)S(1)}, bf16[512,768]{1,0:T(8,128)(2,1)S(1)}, u32[]{:S(2)}, u32[]{:S(2)}) collective-permute-start(bf16[512,768]{1,0:T(8,128)(2,1)S(1)} %get-tuple-element.195.refs_3_), channel_id=1, source_target_pairs={{2,0},{3,1},{0,2},{1,3},{6,4},{7,5},{4,6},{5,7},{10,8},{11,9},{8,1... | collective-permute-start | bytes 2359304 | tf_op jit(solution)/shard_map/ppermute | solution.py:577
  652.4 45.1 %collective-permute-start.110 = (bf16[512,768]{1,0:T(8,128)(2,1)S(1)}, bf16[512,768]{1,0:T(8,128)(2,1)S(1)}, u32[]{:S(2)}, u32[]{:S(2)}) collective-permute-start(bf16[512,768]{1,0:T(8,128)(2,1)S(1)} %get-tuple-element.196.refs_4_), channel_id=1, source_target_pairs={{2,0},{3,1},{0,2},{1,3},{6,4},{7,5},{4,6},{5,7},{10,8},{11,9},{8,1... | collective-permute-start | bytes 2359304 | tf_op jit(solution)/shard_map/ppermute | solution.py:577
  697.0 173.3 %collective-permute-start.151 = (bf16[2,4,48,256]{3,2,1,0:T(8,128)(2,1)}, bf16[2,4,48,256]{3,2,1,0:T(8,128)(2,1)S(1)}, u32[]{:S(2)}, u32[]{:S(2)}) collective-permute-start(bf16[2,4,48,256]{3,2,1,0:T(8,128)(2,1)} %slice_bitcast_fusion.5), channel_id=1, source_target_pairs={{2,0},{3,1},{0,2},{1,3},{6,4},{7,5},{4,6},{5,7},{10,8},{11,9},{8,1... | collective-permute-start | bytes 589832 | tf_op jit(solution)/shard_map/ppermute | solution.py:577
  716.3 37.1 %collective-permute-start.127 = (bf16[4,48,1536]{2,1,0:T(8,128)(2,1)S(1)}, bf16[4,48,1536]{2,1,0:T(8,128)(2,1)S(1)}, u32[]{:S(2)}, u32[]{:S(2)}) collective-permute-start(bf16[4,48,1536]{2,1,0:T(8,128)(2,1)S(1)} %get-tuple-element.213), channel_id=1, source_target_pairs={{4,0},{5,1},{6,2},{7,3},{0,4},{1,5},{2,6},{3,7},{12,8},{13,9},{14,... | collective-permute-start | bytes 1769480 | tf_op jit(solution)/shard_map/ppermute | solution.py:577
  722.9 31.9 %collective-permute-start.171 = (bf16[4,48,1536]{2,1,0:T(8,128)(2,1)S(1)}, bf16[4,48,1536]{2,1,0:T(8,128)(2,1)S(1)}, u32[]{:S(2)}, u32[]{:S(2)}) collective-permute-start(bf16[4,48,1536]{2,1,0:T(8,128)(2,1)S(1)} %get-tuple-element.249), channel_id=1, source_target_pairs={{4,0},{5,1},{6,2},{7,3},{0,4},{1,5},{2,6},{3,7},{12,8},{13,9},{14,... | collective-permute-start | bytes 1769480 | tf_op jit(solution)/shard_map/ppermute | solution.py:577
  725.2 28.6 %collective-permute-start.129 = (bf16[4,48,1536]{2,1,0:T(8,128)(2,1)S(1)}, bf16[4,48,1536]{2,1,0:T(8,128)(2,1)S(1)}, u32[]{:S(2)}, u32[]{:S(2)}) collective-permute-start(bf16[4,48,1536]{2,1,0:T(8,128)(2,1)S(1)} %add_convert_fusion.22), channel_id=1, source_target_pairs={{1,0},{0,1},{3,2},{2,3},{5,4},{4,5},{7,6},{6,7},{9,8},{8,9},{11,10... | collective-permute-start | bytes 1769480 | tf_op jit(solution)/shard_map/ppermute | solution.py:577
  753.4 117.4 %collective-permute-start.152 = (bf16[256,3072]{1,0:T(8,128)(2,1)S(1)}, bf16[256,3072]{1,0:T(8,128)(2,1)S(1)}, u32[]{:S(2)}, u32[]{:S(2)}) collective-permute-start(bf16[256,3072]{1,0:T(8,128)(2,1)S(1)} %copy-done.181), channel_id=1, source_target_pairs={{2,0},{3,1},{0,2},{1,3},{6,4},{7,5},{4,6},{5,7},{10,8},{11,9},{8,1... | collective-permute-start | bytes 4718600 | tf_op jit(solution)/shard_map/ppermute | solution.py:577
  799.5 46.6 %collective-permute-start.180 = (bf16[4,96,768]{2,1,0:T(8,128)(2,1)S(1)}, bf16[4,96,768]{2,1,0:T(8,128)(2,1)S(1)}, u32[]{:S(2)}, u32[]{:S(2)}) collective-permute-start(bf16[4,96,768]{2,1,0:T(8,128)(2,1)S(1)} %get-tuple-element.255), channel_id=1, source_target_pairs={{1,0},{0,1},{3,2},{2,3},{5,4},{4,5},{7,6},{6,7},{9,8},{8,9},{11,10... | collective-permute-start | bytes 1769480 | tf_op jit(solution)/shard_map/ppermute | solution.py:577
  809.4 31.4 %collective-permute-start.163 = (bf16[4,48,1536]{2,1,0:T(8,128)(2,1)S(1)}, bf16[4,48,1536]{2,1,0:T(8,128)(2,1)S(1)}, u32[]{:S(2)}, u32[]{:S(2)}) collective-permute-start(bf16[4,48,1536]{2,1,0:T(8,128)(2,1)S(1)} %get-tuple-element.245), channel_id=1, source_target_pairs={{1,0},{0,1},{3,2},{2,3},{5,4},{4,5},{7,6},{6,7},{9,8},{8,9},{11,10... | collective-permute-start | bytes 1769480 | tf_op jit(solution)/shard_map/ppermute | solution.py:577
  863.0 27.5 %collective-permute-start.116 = (bf16[4,48,1536]{2,1,0:T(8,128)(2,1)S(1)}, bf16[4,48,1536]{2,1,0:T(8,128)(2,1)S(1)}, u32[]{:S(2)}, u32[]{:S(2)}) collective-permute-start(bf16[4,48,1536]{2,1,0:T(8,128)(2,1)S(1)} %get-tuple-element.204), channel_id=1, source_target_pairs={{1,0},{0,1},{3,2},{2,3},{5,4},{4,5},{7,6},{6,7},{9,8},{8,9},{11,10... | collective-permute-start | bytes 1769480 | tf_op jit(solution)/shard_map/ppermute | solution.py:577
  868.0 27.3 %collective-permute-start.162 = (bf16[4,48,1536]{2,1,0:T(8,128)(2,1)S(1)}, bf16[4,48,1536]{2,1,0:T(8,128)(2,1)S(1)}, u32[]{:S(2)}, u32[]{:S(2)}) collective-permute-start(bf16[4,48,1536]{2,1,0:T(8,128)(2,1)S(1)} %get-tuple-element.243), channel_id=1, source_target_pairs={{1,0},{0,1},{3,2},{2,3},{5,4},{4,5},{7,6},{6,7},{9,8},{8,9},{11,10... | collective-permute-start | bytes 1769480 | tf_op jit(solution)/shard_map/ppermute | solution.py:577
  870.8 28.4 %collective-permute-start.164 = (bf16[4,48,1536]{2,1,0:T(8,128)(2,1)S(1)}, bf16[4,48,1536]{2,1,0:T(8,128)(2,1)S(1)}, u32[]{:S(2)}, u32[]{:S(2)}) collective-permute-start(bf16[4,48,1536]{2,1,0:T(8,128)(2,1)S(1)} %add_convert_fusion.13), channel_id=1, source_target_pairs={{4,0},{5,1},{6,2},{7,3},{0,4},{1,5},{2,6},{3,7},{12,8},{13,9},{14,... | collective-permute-start | bytes 1769480 | tf_op jit(solution)/shard_map/ppermute | solution.py:577
  888.7 28.8 %collective-permute-start.154 = (bf16[4,48,1536]{2,1,0:T(8,128)(2,1)S(1)}, bf16[4,48,1536]{2,1,0:T(8,128)(2,1)S(1)}, u32[]{:S(2)}, u32[]{:S(2)}) collective-permute-start(bf16[4,48,1536]{2,1,0:T(8,128)(2,1)S(1)} %get-tuple-element.239), channel_id=1, source_target_pairs={{4,0},{5,1},{6,2},{7,3},{0,4},{1,5},{2,6},{3,7},{12,8},{13,9},{14,... | collective-permute-start | bytes 1769480 | tf_op jit(solution)/shard_map/ppermute | solution.py:577
  890.4 32.4 %collective-permute-start.153 = (bf16[4,48,1536]{2,1,0:T(8,128)(2,1)S(1)}, bf16[4,48,1536]{2,1,0:T(8,128)(2,1)S(1)}, u32[]{:S(2)}, u32[]{:S(2)}) collective-permute-start(bf16[4,48,1536]{2,1,0:T(8,128)(2,1)S(1)} %get-tuple-element.237), channel_id=1, source_target_pairs={{4,0},{5,1},{6,2},{7,3},{0,4},{1,5},{2,6},{3,7},{12,8},{13,9},{14,... | collective-permute-start | bytes 1769480 | tf_op jit(solution)/shard_map/ppermute | solution.py:577
  (395 other events, 4691.6 us)

commit v2 on v1

v2 whole, which is shorter than its diff:
```python
import functools

import jax
import jax.numpy as jnp
from jax import lax
from jax.experimental import pallas as pl
from jax.experimental.pallas import tpu as pltpu
from jax.sharding import PartitionSpec as P

HD = 64
SEGS = 4
BLOCKS = 16
ZS = 4
LAG = 1
VMEM_MB = 24
EPS = 1e-06
MASKED = -1e30
AXES = ("dp", "seq")
F32 = jnp.float32
BF16 = jnp.bfloat16
MB = 1024 * 1024

QB, VB, OB, AG, AS, UB, FG, FS, IB = range(9)


def nn(left, right):
    return lax.dot_general(left, right, (((1,), (0,)), ((), ())), preferred_element_type=F32)


def nt(left, right):
    return lax.dot_general(left, right, (((1,), (1,)), ((), ())), preferred_element_type=F32)


def params(vmem):
    return pltpu.CompilerParams(vmem_limit_bytes=vmem * MB)


def cost():
    return pl.CostEstimate(flops=1, bytes_accessed=1, transcendentals=0)


def load(source, target, sem):
    pltpu.make_async_copy(source, target, sem).start()


VMEM = pl.BlockSpec(memory_space=pltpu.VMEM)
SMEM = pl.BlockSpec(memory_space=pltpu.SMEM)
ANY = pl.BlockSpec(memory_space=pl.ANY)
HBM = pl.BlockSpec(memory_space=pltpu.HBM)


def shape(dims, dtype):
    return jax.ShapeDtypeStruct(dims, dtype)


def flip(value, bit):
    return value + bit - 2 * value * bit


def block_at(pos_ref, k, dx, dc):
    z, x, c = pos_ref[0], pos_ref[1], pos_ref[2]
    low = lax.rem(z, 2)
    zz = flip(lax.div(z, 2), k // 2) * 2 + flip(low, k % 2)
    return (zz * 2 + flip(x, dx)) * 2 + flip(c, dc)


def half_at(pos_ref, dy):
    return flip(pos_ref[3], dy)


UNITS = (
    (0, 0, 0),
    (0, 1, 0),
    (0, 0, 1),
    (0, 1, 1),
    (1, 0, 0),
    (1, 0, 1),
    (1, 1, 0),
    (1, 1, 1),
)


def each_piece(bufs):
    for dc in range(2):
        for unit, (part, dy, dx) in enumerate(UNITS):
            for k in range(ZS):
                yield bufs[dc].at[unit * ZS + k], part, dy, dx, dc, k


def fetch_member(pos_ref, bufs, member, full_ref, sem):
    _, rows, width = bufs[0].shape
    half = width // 2
    for piece, part, dy, dx, dc, k in each_piece(bufs):
        if part != member // 2:
            continue
        row = pl.multiple_of(block_at(pos_ref, k, dx, dc) * rows, 16)
        col = pl.multiple_of(half_at(pos_ref, dy) * half, 128)
        pltpu.make_async_copy(
            piece.at[:, pl.ds(member % 2 * half, half)],
            full_ref.at[pl.ds(row, rows), pl.ds(col, half)],
            sem,
        ).start()


def fetch_columns(pos_ref, bufs, full_ref, sem):
    _, rows, width = bufs[0].shape
    for piece, part, dy, dx, dc, k in each_piece(bufs):
        row = pl.multiple_of(block_at(pos_ref, k, dx, dc) * rows, 16)
        col = pl.multiple_of((half_at(pos_ref, dy) * 2 + part) * width, 128)
        pltpu.make_async_copy(
            piece, full_ref.at[pl.ds(row, rows), pl.ds(col, width)], sem
        ).start()


def fetch_rows(pos_ref, bufs, full_ref, sem):
    _, rows, width = bufs[0].shape
    for piece, part, dy, dx, dc, k in each_piece(bufs):
        block = block_at(pos_ref, k, dx, dc) * 2 + half_at(pos_ref, dy)
        row = pl.multiple_of((block * 2 + part) * rows, 16)
        pltpu.make_async_copy(piece, full_ref.at[pl.ds(row, rows), :], sem).start()


def wait_full(full_ref, sem):
    pltpu.make_async_copy(full_ref, full_ref, sem).wait()


def export_rows(pos_ref, wide_ref, outs, index):
    rows = outs[0].shape[3]
    for dc in range(2):
        for dx in range(2):
            for k in range(ZS):
                row = pl.multiple_of(block_at(pos_ref, k, dx, dc) * rows, 16)
                outs[dc][index, dx, k] = wide_ref[pl.ds(row, rows), :]


def export_halves(pos_ref, wide_ref, outs):
    rows = outs[0].shape[4]
    for dc in range(2):
        for dx in range(2):
            for dy in range(2):
                for k in range(ZS):
                    block = block_at(pos_ref, k, dx, dc) * 2 + half_at(pos_ref, dy)
                    for part in range(2):
                        row = pl.multiple_of((block * 2 + part) * rows, 16)
                        outs[dc][dx, dy, part, k] = wide_ref[pl.ds(row, rows), :]


def mean_of(values):
    return jnp.mean(values, axis=-1, keepdims=True)


def normalize(values):
    center = values - mean_of(values)
    inverse = lax.rsqrt(mean_of(center * center) + EPS)
    return center * inverse, inverse


def norm_back(normed, inverse, scaled):
    return inverse * (scaled - mean_of(scaled) - normed * mean_of(scaled * normed))


def colsum(values):
    return jnp.sum(values, axis=0, keepdims=True)


def row_of(vec_ref, index):
    return vec_ref[pl.ds(index, 1), :]


def attn_kernel(*refs):
    pos_w, pos_g = refs[0], refs[1]
    x_ref, xp_ref, seg_ref, lab_ref, vec_ref = refs[2:7]
    bufs = refs[7:9]
    h_ref = refs[9]
    kept = refs[10:18]
    wq, wk, wv, wo, rows_ref, vt_ref, wide_ref, bias_ref, k_ref = refs[18:27]
    held = refs[27:35]
    n1_ref, c1_ref, q_ref, kt_ref, v_ref, p_ref = held[:6]
    exports = held[6:]
    sems, store_sems = refs[35:]

    def store(index):
        load(held[index], kept[index], store_sems.at[index])

    tokens, width = x_ref.shape
    for member, full in enumerate((wq, wk, wv, wo)):
        fetch_member(pos_w, bufs, member, full, sems.at[member])
    bias_ref[...] = jnp.where(lab_ref[...] == seg_ref[...], 0.0, MASKED)
    low = x_ref[...].astype(BF16)
    rows_ref[:tokens] = low
    rows_ref[tokens:] = xp_ref[...]
    wide_ref[...] = low.T
    export_rows(pos_g, wide_ref, exports, 0)
    wait_full(wq, sems.at[0])
    query = (nn(low, wq[...]) + row_of(vec_ref, QB)).astype(BF16)
    q_ref[...] = (query.astype(F32) * HD ** (-0.5)).astype(BF16)
    wait_full(wk, sems.at[1])
    key = nn(rows_ref[...], wk[...]).astype(BF16)
    k_ref[...] = key
    kt_ref[...] = key.T
    store(2)
    store(3)
    wait_full(wv, sems.at[2])
    value = (nn(rows_ref[...], wv[...]) + row_of(vec_ref, VB)).astype(BF16)
    v_ref[...] = value
    vt_ref[...] = value.T
    store(4)

    def pair(index, carry):
        lane = pl.multiple_of(index * 128, 128)
        keys = k_ref[:, pl.ds(lane, 128)]
        queries = q_ref[:, pl.ds(lane, 128)]
        first = lax.broadcasted_iota(jnp.int32, queries.shape, 1) < HD
        for which in range(2):
            mine = jnp.where(first if which == 0 else ~first, queries, jnp.zeros_like(queries))
            scores = nt(keys, mine) + bias_ref[...]
            expos = jnp.exp(scores - jnp.max(scores, axis=0, keepdims=True))
            probs = (expos * (1.0 / jnp.sum(expos, axis=0, keepdims=True))).astype(BF16)
            p_ref[index * 2 + which] = probs
            row = pl.multiple_of(index * 128 + which * HD, HD)
            wide_ref[pl.ds(row, HD), :] = nn(vt_ref[pl.ds(row, HD), :], probs).astype(BF16)
        both = pl.ds(index * 2, 2)
        load(p_ref.at[both], kept[5].at[both], store_sems.at[5])
        return carry

    lax.fori_loop(0, width // 128, pair, 0)
    export_rows(pos_g, wide_ref, exports, 1)
    mixed = wide_ref[...].T
    wait_full(wo, sems.at[3])
    branch = nn(mixed, wo[...]) + row_of(vec_ref, OB)
    normed, inverse = normalize(x_ref[...] + branch)
    hidden = normed * row_of(vec_ref, AG) + row_of(vec_ref, AS)
    h_ref[...] = hidden
    n1_ref[...] = normed
    c1_ref[...] = jnp.broadcast_to(inverse, c1_ref.shape)
    wide_ref[...] = hidden.astype(BF16).T
    export_rows(pos_g, wide_ref, exports, 2)
    for index in (0, 1, 6, 7):
        store(index)
    for index in range(8):
        wait_full(held[index], store_sems.at[index])


def attn_forward(pos_w, pos_g, x, xp, seg, lab, vec, bufs):
    tokens, width = x.shape
    heads = width // HD
    export = shape((3, 2, ZS, width // BLOCKS, tokens), BF16)
    kept = (
        shape((tokens, width), F32),
        shape((tokens, 128), F32),
        shape((tokens, width), BF16),
        shape((width, 2 * tokens), BF16),
        shape((2 * tokens, width), BF16),
        shape((heads, 2 * tokens, tokens), BF16),
        export,
        export,
    )
    return pl.pallas_call(
        attn_kernel,
        out_shape=(shape((tokens, width), F32),) + kept,
        in_specs=[SMEM, SMEM] + [VMEM] * 5 + [ANY] * 2,
        out_specs=[VMEM] + [HBM] * 8,
        scratch_shapes=[pltpu.VMEM((width, width), BF16)] * 4
        + [
            pltpu.VMEM((2 * tokens, width), BF16),
            pltpu.VMEM((width, 2 * tokens), BF16),
            pltpu.VMEM((width, tokens), BF16),
            pltpu.VMEM((2 * tokens, tokens), F32),
            pltpu.VMEM((2 * tokens, width), BF16),
        ]
        + [pltpu.VMEM(each.shape, each.dtype) for each in kept]
        + [pltpu.SemaphoreType.DMA((4,)), pltpu.SemaphoreType.DMA((8,))],
        compiler_params=params(VMEM_MB),
        cost_estimate=cost(),
        name="attn_forward",
    )(pos_w, pos_g, x, xp, seg, lab, vec, *bufs)


def ffn_kernel(tile, *refs):
    pos_w, pos_g, h_ref, vec_ref = refs[:4]
    inner_bufs, outer_bufs = refs[4:6], refs[6:8]
    x_ref, xb_ref = refs[8:10]
    kept = refs[10:15]
    wi, wu, low_ref, acc_ref, wide_ref = refs[15:20]
    held = refs[20:25]
    n2_ref, c2_ref, gp_ref = held[:3]
    exports = held[3:]
    sems, store_sems = refs[25:]

    def store(index):
        load(held[index], kept[index], store_sems.at[index])

    width, hidden = wi.shape
    fetch_columns(pos_w, inner_bufs, wi, sems.at[0])
    fetch_rows(pos_w, outer_bufs, wu, sems.at[1])
    low_ref[...] = h_ref[...].astype(BF16)
    acc_ref[...] = jnp.zeros_like(acc_ref)
    wait_full(wi, sems.at[0])
    wait_full(wu, sems.at[1])
    per_row = width // tile

    def step(index, carry):
        lane = pl.multiple_of(index * tile, tile)
        bias = vec_ref[pl.ds(IB + lax.div(index, per_row), 1), :]
        part = lax.rem(index, per_row)
        chosen = bias[:, :tile]
        for other in range(1, per_row):
            chosen = jnp.where(part == other, bias[:, other * tile : (other + 1) * tile], chosen)
        pre = nn(low_ref[...], wi[:, pl.ds(lane, tile)]) + chosen
        phi = 0.5 * (1.0 + lax.erf(pre * 0.7071067811865476))
        dens = jnp.exp(-0.5 * pre * pre) * 0.3989422804014327
        gp_ref[:, pl.ds(lane, tile)] = (phi + pre * dens).astype(BF16)
        active = (pre * phi).astype(BF16)
        acc_ref[...] += nn(active, wu[pl.ds(lane, tile), :])
        wide_ref[pl.ds(lane, tile), :] = active.T
        return carry

    lax.fori_loop(0, hidden // tile, step, 0)
    store(2)
    export_halves(pos_g, wide_ref, exports)
    store(3)
    store(4)
    normed, inverse = normalize(h_ref[...] + (acc_ref[...] + row_of(vec_ref, UB)))
    result = normed * row_of(vec_ref, FG) + row_of(vec_ref, FS)
    x_ref[...] = result
    xb_ref[...] = result.astype(BF16)
    n2_ref[...] = normed
    c2_ref[...] = jnp.broadcast_to(inverse, c2_ref.shape)
    store(0)
    store(1)
    for index in range(5):
        wait_full(held[index], store_sems.at[index])


def ffn_forward(pos_w, pos_g, h, vec, inner_bufs, outer_bufs):
    tokens, width = h.shape
    hidden = outer_bufs[0].shape[1] * 4 * BLOCKS
    export = shape((2, 2, 2, ZS, hidden // BLOCKS // 4, tokens), BF16)
    kept = (
        shape((tokens, width), F32),
        shape((tokens, 128), F32),
        shape((tokens, hidden), BF16),
        export,
        export,
    )
    return pl.pallas_call(
        functools.partial(ffn_kernel, 384),
        out_shape=(shape((tokens, width), F32), shape((tokens, width), BF16)) + kept,
        in_specs=[SMEM, SMEM, VMEM, VMEM] + [ANY] * 4,
        out_specs=[VMEM] * 2 + [HBM] * 5,
        scratch_shapes=[
            pltpu.VMEM((width, hidden), BF16),
            pltpu.VMEM((hidden, width), BF16),
            pltpu.VMEM((tokens, width), BF16),
            pltpu.VMEM((tokens, width), F32),
            pltpu.VMEM((hidden, tokens), BF16),
        ]
        + [pltpu.VMEM(each.shape, each.dtype) for each in kept]
        + [pltpu.SemaphoreType.DMA((2,)), pltpu.SemaphoreType.DMA((5,))],
        compiler_params=params(VMEM_MB),
        cost_estimate=cost(),
        name="ffn_forward",
    )(pos_w, pos_g, h, vec, *inner_bufs, *outer_bufs)


def chain_kernel(tile, *refs):
    pos_w, dx_ref = refs[:2]
    sources, vec_ref = refs[2:7], refs[7]
    inner_bufs, outer_bufs, attn_bufs = refs[8:10], refs[10:12], refs[12:14]
    pack_ref, da_ref, do_ref, sums_ref = refs[14:18]
    wi, wu, wo, acc_ref = refs[18:22]
    held = refs[22:27]
    n2_ref, c2_ref, gp_ref, n1_ref, c1_ref = held
    sems, load_sems = refs[27:]
    width, hidden = wi.shape
    for index in range(5):
        load(sources[index], held[index], load_sems.at[index])
    dyl_ref = pack_ref.at[:, pl.ds(0, width)]
    du_ref = pack_ref.at[:, pl.ds(width, hidden)]
    dal_ref = pack_ref.at[:, pl.ds(width + hidden, width)]
    fetch_rows(pos_w, outer_bufs, wu, sems.at[0])
    fetch_columns(pos_w, inner_bufs, wi, sems.at[1])
    fetch_member(pos_w, attn_bufs, 3, wo, sems.at[2])
    sums_ref[...] = jnp.zeros_like(sums_ref)
    grad = dx_ref[...].astype(F32)
    wait_full(n2_ref, load_sems.at[0])
    wait_full(c2_ref, load_sems.at[1])
    normed = n2_ref[...]
    sums_ref[pl.ds(FG, 1), :] = colsum(grad * normed)
    sums_ref[pl.ds(FS, 1), :] = colsum(grad)
    back = norm_back(normed, c2_ref[:, :1], grad * row_of(vec_ref, FG))
    low = back.astype(BF16)
    dyl_ref[...] = low
    sums_ref[pl.ds(UB, 1), :] = colsum(low.astype(F32))
    acc_ref[...] = back
    wait_full(gp_ref, load_sems.at[2])
    wait_full(wu, sems.at[0])
    wait_full(wi, sems.at[1])
    per_row = width // tile

    for index in range(hidden // tile):
        lane = index * tile
        part = nt(dyl_ref[...], wu[pl.ds(lane, tile), :])
        part = (part * gp_ref[:, pl.ds(lane, tile)].astype(F32)).astype(BF16)
        du_ref[:, pl.ds(lane, tile)] = part
        acc_ref[...] += nt(part, wi[:, pl.ds(lane, tile)])
        sums_ref[
            pl.ds(IB + index // per_row, 1), pl.ds(index % per_row * tile, tile)
        ] = colsum(part.astype(F32))

    grad = acc_ref[...]
    wait_full(n1_ref, load_sems.at[3])
    wait_full(c1_ref, load_sems.at[4])
    normed = n1_ref[...]
    sums_ref[pl.ds(AG, 1), :] = colsum(grad * normed)
    sums_ref[pl.ds(AS, 1), :] = colsum(grad)
    back = norm_back(normed, c1_ref[:, :1], grad * row_of(vec_ref, AG))
    da_ref[...] = back
    low = back.astype(BF16)
    dal_ref[...] = low
    sums_ref[pl.ds(OB, 1), :] = colsum(low.astype(F32))
    wait_full(wo, sems.at[2])
    do_ref[...] = nt(low, wo[...]).astype(BF16)


def chain_backward(pos_w, dx, n2, c2, gp, n1, c1, vec, inner_bufs, outer_bufs, attn_bufs):
    tokens, width = n2.shape
    hidden = gp.shape[1]
    return pl.pallas_call(
        functools.partial(chain_kernel, 384),
        out_shape=(
            shape((tokens, 2 * width + hidden), BF16),
            shape((tokens, width), F32),
            shape((tokens, width), BF16),
            shape((16, width), F32),
        ),
        in_specs=[SMEM, VMEM] + [HBM] * 5 + [VMEM] + [ANY] * 6,
        out_specs=[VMEM] * 4,
        scratch_shapes=[
            pltpu.VMEM((width, hidden), BF16),
            pltpu.VMEM((hidden, width), BF16),
            pltpu.VMEM((width, width), BF16),
            pltpu.VMEM((tokens, width), F32),
        ]
        + [pltpu.VMEM(each.shape, each.dtype) for each in (n2, c2, gp, n1, c1)]
        + [pltpu.SemaphoreType.DMA((3,)), pltpu.SemaphoreType.DMA((5,))],
        compiler_params=params(VMEM_MB),
        cost_estimate=cost(),
        name="chain_backward",
    )(pos_w, dx, n2, c2, gp, n1, c1, vec, *inner_bufs, *outer_bufs, *attn_bufs)


def attn_back_kernel(*refs):
    sources, do_ref, pack_ref, sum_ref, wide_ref = refs[:4], refs[4], refs[5], refs[6], refs[7]
    held, sems, pair_sems = refs[8:12], refs[12], refs[13]
    q_ref, kt_ref, v_ref, p_ref = held
    tokens, width = q_ref.shape
    for index in range(3):
        load(sources[index], held[index], sems.at[index])
    for index in range(width // 128):
        both = pl.ds(index * 2, 2)
        load(sources[3].at[both], p_ref.at[both], pair_sems.at[index])
    for index in range(3):
        wait_full(held[index], sems.at[index])

    def pair(index, carry):
        lane = pl.multiple_of(index * 128, 128)
        values = v_ref[:, pl.ds(lane, 128)]
        queries = q_ref[:, pl.ds(lane, 128)]
        grads = do_ref[:, pl.ds(lane, 128)]
        first = lax.broadcasted_iota(jnp.int32, grads.shape, 1) < HD
        keys_back, values_back = [], []
        wait_full(p_ref.at[pl.ds(index * 2, 2)], pair_sems.at[index])
        for which in range(2):
            mine = jnp.where(first if which == 0 else ~first, grads, jnp.zeros_like(grads))
            probs_low = p_ref[index * 2 + which]
            probs = probs_low.astype(F32)
            weighted = probs * nt(values, mine)
            back = weighted - probs * jnp.sum(weighted, axis=0, keepdims=True)
            low = back.astype(BF16)
            keys_back.append(nn(low, queries))
            values_back.append(nn(probs_low, grads))
            row = pl.multiple_of(index * 128 + which * HD, HD)
            wide_ref[pl.ds(row, HD), :] = nn(kt_ref[pl.ds(row, HD), :], low)
        split = lax.broadcasted_iota(jnp.int32, keys_back[0].shape, 1) < HD
        for at, back in ((1, keys_back), (3, values_back)):
            low = jnp.where(split, back[0], back[1]).astype(BF16)
            pack_ref[at, :, pl.ds(lane, 128)] = low[:tokens]
            pack_ref[at + 1, :, pl.ds(lane, 128)] = low[tokens:]
        return carry

    lax.fori_loop(0, width // 128, pair, 0)
    low = (wide_ref[...].T * HD ** (-0.5)).astype(BF16)
    pack_ref[0] = low
    sum_ref[...] = jnp.broadcast_to(colsum(low.astype(F32)), sum_ref.shape)


def attn_backward(q, kt, v, p, do):
    tokens, width = q.shape
    return pl.pallas_call(
        attn_back_kernel,
        out_shape=(
            shape((5, tokens, width), BF16),
            shape((8, width), F32),
        ),
        in_specs=[HBM] * 4 + [VMEM],
        out_specs=[VMEM] * 2,
        scratch_shapes=[pltpu.VMEM((width, tokens), F32)]
        + [pltpu.VMEM(each.shape, each.dtype) for each in (q, kt, v, p)]
        + [pltpu.SemaphoreType.DMA((3,)), pltpu.SemaphoreType.DMA((width // 128,))],
        compiler_params=params(VMEM_MB),
        cost_estimate=cost(),
        name="attn_backward",
    )(q, kt, v, p, do)


def input_kernel(*refs):
    pos_w, da_ref, pack_ref, got_ref = refs[:4]
    bufs = refs[4:6]
    dx_ref, total_ref, sum_ref = refs[6:9]
    wq, wk, wv, sems = refs[9:]
    tokens, width = da_ref.shape
    for member, full in enumerate((wq, wk, wv)):
        fetch_member(pos_w, bufs, member, full, sems.at[member])
    for at, (mine, theirs) in enumerate(((1, 2), (2, 1), (3, 4), (4, 3))):
        total_ref[at] = (pack_ref[mine].astype(F32) + got_ref[theirs].astype(F32)).astype(BF16)
    sum_ref[...] = jnp.broadcast_to(colsum(total_ref[2].astype(F32)), sum_ref.shape)
    wait_full(wq, sems.at[0])
    dx = da_ref[...] + nt(pack_ref[0], wq[...])
    wait_full(wk, sems.at[1])
    dx += nt(total_ref[0], wk[...])
    wait_full(wv, sems.at[2])
    dx += nt(total_ref[2], wv[...])
    dx_ref[...] = dx


def input_backward(pos_w, da, pack, got, bufs):
    tokens, width = da.shape
    return pl.pallas_call(
        input_kernel,
        out_shape=(
            shape((tokens, width), F32),
            shape((4, tokens, width), BF16),
            shape((8, width), F32),
        ),
        in_specs=[SMEM] + [VMEM] * 3 + [ANY] * 2,
        out_specs=[VMEM] * 3,
        scratch_shapes=[pltpu.VMEM((width, width), BF16)] * 3 + [pltpu.SemaphoreType.DMA((3,))],
        compiler_params=params(VMEM_MB),
        cost_estimate=cost(),
        name="input_backward",
    )(pos_w, da, pack, got, *bufs)


def place(outs, part, dy, value):
    a_keep, a_send, b_keep, b_send = outs
    if part == 0:
        a_keep[dy] = value[0]
        a_send[dy] = value[1]
    else:
        (b_send if dy else b_keep)[...] = value


def grad_shapes(rows, width):
    return (shape((2, ZS, rows, width), BF16),) * 4


def inner_grad_kernel(pos_ref, ta_ref, tb_ref, da_ref, db_ref, *refs):
    outs, left, sems = refs[:4], refs[4], refs[5]
    _, _, rows, width = outs[0].shape
    tokens = ta_ref.shape[-1]
    for side, source in enumerate((ta_ref, tb_ref)):
        load(source.at[2], left.at[side], sems.at[side])
    for side in range(2):
        wait_full(left.at[side], sems.at[side])
    left_a = left[0].reshape(2 * ZS * rows, tokens)
    left_b = left[1].reshape(2 * ZS * rows, tokens)
    for dy in range(2):
        for part in range(2):
            lanes = pl.ds(pl.multiple_of((half_at(pos_ref, dy) * 2 + part) * width + width, 128), width)
            value = nn(left_a, da_ref[:, lanes]) + nn(left_b, db_ref[:, lanes])
            place(outs, part, dy, value.astype(BF16).reshape(2, ZS, rows, width))


def inner_grad(pos_g, ta, tb, da, db):
    rows = ta.shape[3]
    return pl.pallas_call(
        inner_grad_kernel,
        out_shape=grad_shapes(rows, rows * BLOCKS),
        in_specs=[SMEM] + [HBM] * 2 + [VMEM] * 2,
        out_specs=[VMEM] * 4,
        scratch_shapes=[pltpu.VMEM((2,) + ta.shape[1:], BF16), pltpu.SemaphoreType.DMA((2,))],
        compiler_params=params(VMEM_MB),
        cost_estimate=cost(),
        name="inner_grad",
    )(pos_g, ta, tb, da, db)


def outer_grad_kernel(ta_ref, tb_ref, da_ref, db_ref, *refs):
    outs, left, sems = refs[:4], refs[4], refs[5]
    _, _, rows, width = outs[0].shape
    tokens = ta_ref.shape[-1]
    for side, source in enumerate((ta_ref, tb_ref)):
        load(source, left.at[side], sems.at[side])
    for side in range(2):
        wait_full(left.at[side], sems.at[side])
    for dy in range(2):
        for part in range(2):
            values = []
            for dx in range(2):
                left_a = left[0, dx, dy, part].reshape(ZS * rows, tokens)
                left_b = left[1, dx, dy, part].reshape(ZS * rows, tokens)
                value = nn(left_a, da_ref[:, :width]) + nn(left_b, db_ref[:, :width])
                values.append(value.astype(BF16).reshape(ZS, rows, width))
            place(outs, part, dy, jnp.stack(values))


def outer_grad(ta, tb, da, db, width):
    rows = ta.shape[4]
    return pl.pallas_call(
        outer_grad_kernel,
        out_shape=grad_shapes(rows, width),
        in_specs=[HBM] * 2 + [VMEM] * 2,
        out_specs=[VMEM] * 4,
        scratch_shapes=[pltpu.VMEM((2,) + ta.shape, BF16), pltpu.SemaphoreType.DMA((2,))],
        compiler_params=params(VMEM_MB),
        cost_estimate=cost(),
        name="outer_grad",
    )(ta, tb, da, db)


def attn_grad_kernel(pos_ref, xa_ref, xb_ref, qa_ref, qb_ref, total_ref, da_ref, db_ref, *refs):
    outs, left, sems = refs[:4], refs[4], refs[5]
    for side, source in enumerate((xa_ref, xb_ref)):
        load(source.at[pl.ds(0, 2)], left.at[side], sems.at[side])
    for side in range(2):
        wait_full(left.at[side], sems.at[side])
    _, _, rows, width = outs[0].shape
    half = width // 2
    tokens = xa_ref.shape[-1]
    height = 2 * ZS * rows
    x_a = left[0, 0].reshape(height, tokens)
    x_b = left[1, 0].reshape(height, tokens)
    o_a = left[0, 1].reshape(height, tokens)
    o_b = left[1, 1].reshape(height, tokens)
    last = da_ref.shape[1] - width
    for dy in range(2):
        start = half_at(pos_ref, dy) * half
        lanes = pl.ds(pl.multiple_of(start, 128), half)
        tail = pl.ds(pl.multiple_of(start + last, 128), half)
        members = (
            nn(x_a, qa_ref[0, :, lanes]) + nn(x_b, qb_ref[0, :, lanes]),
            nn(x_a, total_ref[0, :, lanes]) + nn(x_b, total_ref[1, :, lanes]),
            nn(x_a, total_ref[2, :, lanes]) + nn(x_b, total_ref[3, :, lanes]),
            nn(o_a, da_ref[:, tail]) + nn(o_b, db_ref[:, tail]),
        )
        for part in range(2):
            value = jnp.concatenate(members[part * 2 : part * 2 + 2], axis=1)
            place(outs, part, dy, value.astype(BF16).reshape(2, ZS, rows, width))


def attn_grad(pos_g, xa, xb, qa, qb, total, da, db):
    rows = xa.shape[3]
    return pl.pallas_call(
        attn_grad_kernel,
        out_shape=grad_shapes(rows, rows * BLOCKS),
        in_specs=[SMEM] + [HBM] * 2 + [VMEM] * 5,
        out_specs=[VMEM] * 4,
        scratch_shapes=[pltpu.VMEM((2, 2) + xa.shape[1:], BF16), pltpu.SemaphoreType.DMA((2,))],
        compiler_params=params(VMEM_MB),
        cost_estimate=cost(),
        name="attn_grad",
    )(pos_g, xa, xb, qa, qb, total, da, db)


def copy_kernel(plan, inputs, *refs):
    ins, outs, sems = refs[:inputs], refs[inputs:-1], refs[-1]
    copies = []
    for index, (out, to, source, at, size) in enumerate(plan):
        copies.append(
            pltpu.make_async_copy(
                ins[source].at[pl.ds(at, size)], outs[out].at[pl.ds(to, size)], sems.at[index]
            )
        )
    for each in copies:
        each.start()
    for each in copies:
        each.wait()


def copy_blocks(plan, inputs, sizes, name):
    piece = inputs[0].shape[1:]
    return pl.pallas_call(
        functools.partial(copy_kernel, plan, len(inputs)),
        out_shape=tuple(shape((size,) + piece, BF16) for size in sizes),
        in_specs=[ANY] * len(inputs),
        out_specs=[VMEM] * len(sizes),
        scratch_shapes=[pltpu.SemaphoreType.DMA((len(plan),))],
        compiler_params=params(VMEM_MB),
        cost_estimate=cost(),
        name=name,
    )(*inputs)


def pack_kernel(group, pos_ref, *refs):
    four, inner, outer = refs[:4], refs[4], refs[5]
    out, sem = refs[6], refs[7]
    rows, width = out.shape[1:]
    half = width // 2
    y = pos_ref[3]
    for j, chunk in enumerate(group):
        layer, kind = chunk // 3, chunk % 3
        for part in range(2):
            to = out.at[2 * j + part]
            if kind == 0:
                for side in range(2):
                    pltpu.make_async_copy(
                        four[2 * part + side].at[layer, :, pl.ds(pl.multiple_of(y * half, 128), half)],
                        to.at[:, pl.ds(side * half, half)],
                        sem,
                    ).start()
            elif kind == 1:
                lane = pl.multiple_of((2 * y + part) * width, 128)
                pltpu.make_async_copy(inner.at[layer, :, pl.ds(lane, width)], to, sem).start()
            else:
                row = pl.multiple_of((2 * y + part) * rows, 16)
                pltpu.make_async_copy(outer.at[layer, pl.ds(row, rows)], to, sem).start()
    wait_full(out, sem)


def pack_pieces(group, pos, weights):
    _, rows, width = weights[0].shape
    return pl.pallas_call(
        functools.partial(pack_kernel, group),
        out_shape=shape((2 * len(group), rows, width), BF16),
        in_specs=[SMEM] + [HBM] * 6,
        out_specs=VMEM,
        scratch_shapes=[pltpu.SemaphoreType.DMA],
        compiler_params=params(VMEM_MB),
        cost_estimate=cost(),
        name="pack",
    )(pos, *weights)


def table_kernel(at_ref, *refs):
    vectors, out = refs[:-1], refs[-1]
    width = out.shape[2]
    for index, vector in enumerate(vectors):
        size = vector.shape[1]
        start = at_ref[0] * size
        for piece in range(max(1, out.shape[1] - IB if index == IB else 1)):
            lanes = lax.broadcasted_iota(jnp.int32, (size, width), 1) + piece * width
            spot = lax.broadcasted_iota(jnp.int32, (size, width), 0) + start
            chosen = (lanes == spot).astype(F32).astype(BF16)
            out[:, index + piece, :] = nn(vector[...], chosen)


def vector_table(at, vectors, width):
    layers, last = vectors[-1].shape[0], vectors[-1].shape[1]
    rows = IB + last // vectors[0].shape[1]
    return pl.pallas_call(
        table_kernel,
        out_shape=shape((layers, rows, width), F32),
        in_specs=[SMEM] + [VMEM] * len(vectors),
        out_specs=VMEM,
        compiler_params=params(VMEM_MB),
        cost_estimate=cost(),
        name="vector_table",
    )(at, *vectors)


def finish_kernel(kind, offsets, pos_ref, *refs):
    layers = len(offsets)
    owns, gots = refs[:layers], refs[layers : 2 * layers]
    outs, buf, sems = refs[2 * layers : -2], refs[-2], refs[-1]
    rows, width = buf.shape[2:]
    half = width // 2
    y = pos_ref[3]
    copies = []
    for layer in range(layers):
        copies.append(
            pltpu.make_async_copy(
                gots[layer].at[pl.ds(offsets[layer], 2)], buf.at[layer], sems.at[layer]
            )
        )
        copies[-1].start()
    for side in range(2):
        yy = y if side == 0 else 1 - y
        if side:
            for each in copies:
                each.wait()
        for layer in range(layers):
            for part in range(2):
                value = buf[layer, part].astype(F32) if side else owns[layer][part]
                if kind == 0:
                    lanes = pl.ds(pl.multiple_of(yy * half, 128), half)
                    for member in range(2):
                        outs[2 * part + member][layer, :, lanes] = value[
                            :, member * half : (member + 1) * half
                        ]
                elif kind == 1:
                    lane = pl.multiple_of((2 * yy + part) * width, 128)
                    outs[0][layer, :, pl.ds(lane, width)] = value
                else:
                    row = pl.multiple_of((2 * yy + part) * rows, 16)
                    outs[0][layer, pl.ds(row, rows), :] = value


def finish(kind, pos, results):
    layers = len(results)
    _, rows, width = results[0][0].shape
    outs = {
        0: (shape((layers, rows, width), F32),) * 4,
        1: (shape((layers, rows, 4 * width), F32),),
        2: (shape((layers, 4 * rows, width), F32),),
    }[kind]
    return pl.pallas_call(
        functools.partial(finish_kernel, kind, tuple(value[2] for value in results)),
        out_shape=outs,
        in_specs=[SMEM] + [VMEM] * layers + [ANY] * layers,
        out_specs=[VMEM] * len(outs),
        scratch_shapes=[
            pltpu.VMEM((layers, 2, rows, width), BF16),
            pltpu.SemaphoreType.DMA((layers,)),
        ],
        compiler_params=params(VMEM_MB),
        cost_estimate=cost(),
        name="finish",
    )(pos, *[value[0] for value in results], *[value[1] for value in results])


def sum_kernel(config, *refs):
    fresh, first, second, third, fourth = config
    refs = list(refs)

    def take(count):
        out = refs[:count]
        del refs[:count]
        return out

    sends = take(2) if fresh else None
    got_x, got_y = take(2) if first or second else (None, None)
    keeps = take(2) if first else None
    rests = take(2) if second else None
    pairs = take(2) if third else None
    lasts = take(2) if fourth else None
    to_x, to_y = take(2) if fresh or first or fourth else (None, None)
    at = 0
    if fresh:
        for out, send in ((to_x, sends[0]), (to_y, sends[1])):
            for half in range(2):
                out[half * ZS : (half + 1) * ZS] = send[half]
        at = 2 * ZS
    got = 0
    if first:
        outs = take(2)
        for keep, come, rest, send in (
            (keeps[0], got_x, outs[0], to_y),
            (keeps[1], got_y, outs[1], to_x),
        ):
            rest[...] = (keep[0].astype(F32) + come[:ZS].astype(F32)).astype(BF16)
            send[at : at + ZS] = (keep[1].astype(F32) + come[ZS : 2 * ZS].astype(F32)).astype(BF16)
        got = 2 * ZS
        at += ZS
    if second:
        hold, go = take(2)
        for part, (rest, come) in enumerate(((rests[0], got_y), (rests[1], got_x))):
            for k in range(ZS):
                value = rest[k].astype(F32) + come[got + k].astype(F32)
                (go if k % 2 else hold)[k // 2, part] = value.astype(BF16)
    if third:
        hold, go = take(2)
        hold[...] = pairs[0][0].astype(F32) + pairs[1][0].astype(F32)
        go[...] = (pairs[0][1].astype(F32) + pairs[1][1].astype(F32)).astype(BF16)
    if fourth:
        (total,) = take(1)
        value = lasts[0][...] + lasts[1][...].astype(F32)
        total[...] = value
        to_y[at : at + 2] = value.astype(BF16)


def sum_round(fresh, got_x, got_y, first, second, third, fourth):
    config = tuple(value is not None for value in (fresh, first, second, third, fourth))
    sample = fresh or first or second or third or fourth
    rows, width = sample[-1].shape[-2:]
    inputs, outputs = [], []
    if fresh is not None:
        inputs += [fresh[1], fresh[3]]
    if first is not None or second is not None:
        inputs += [got_x, got_y]
    for value in (first, second, third, fourth):
        if value is not None:
            inputs += list(value)
    going = 2 * ZS * config[0] + ZS * config[1]
    if config[0] or config[1] or config[4]:
        size_y = going + 2 * config[4]
        outputs += [shape((max(going, 1), rows, width), BF16), shape((size_y, rows, width), BF16)]
    if config[1]:
        outputs += [shape((ZS, rows, width), BF16)] * 2
    if config[2]:
        outputs += [shape((2, 2, rows, width), BF16)] * 2
    if config[3]:
        outputs += [shape((2, rows, width), F32), shape((2, rows, width), BF16)]
    if config[4]:
        outputs += [shape((2, rows, width), F32)]
    outs = list(
        pl.pallas_call(
            functools.partial(sum_kernel, config),
            out_shape=tuple(outputs),
            in_specs=[VMEM] * len(inputs),
            out_specs=[VMEM] * len(outputs),
            compiler_params=params(VMEM_MB),
            cost_estimate=cost(),
            name="sum_round",
        )(*inputs)
    )

    def take(wanted, count):
        if not wanted:
            return None
        out = tuple(outs[:count])
        del outs[:count]
        return out

    sends = take(config[0] or config[1] or config[4], 2)
    return sends, going, take(config[1], 2), take(config[2], 2), take(config[3], 2), take(config[4], 1)


def fence(values):
    return lax.optimization_barrier(values)


def build(mesh):
    count = mesh.shape["dp"]

    def flat(dp, seq):
        return dp * 2 + seq

    def pairs(source_of):
        out = []
        for dp in range(count):
            for seq in range(2):
                out.append((flat(*source_of(dp, seq)), flat(dp, seq)))
        return out

    swap_pairs = pairs(lambda dp, seq: (dp // 2 * 2 + seq, dp % 2))
    core_pairs = pairs(lambda dp, seq: (dp ^ 1, seq))
    x_pairs = pairs(lambda dp, seq: (dp ^ 2, seq))
    y_pairs = pairs(lambda dp, seq: (dp, 1 - seq))
    z_pairs = [pairs(lambda dp, seq, k=k: ((dp // 4 ^ k) * 4 + dp % 4, seq)) for k in (1, 2)]

    def move(value, perm):
        return lax.ppermute(value, AXES, perm)

    return dict(
        count=count,
        swap=swap_pairs,
        core=core_pairs,
        x=x_pairs,
        y=y_pairs,
        z1=z_pairs[0],
        z2=z_pairs[1],
        move=move,
    )


def body(
    net,
    tokens,
    segment_ids,
    padding,
    query_weight,
    key_weight,
    value_weight,
    output_weight,
    query_bias,
    value_bias,
    output_bias,
    attn_gain,
    attn_shift,
    inner_weight,
    inner_bias,
    outer_weight,
    outer_bias,
    ffn_gain,
    ffn_shift,
    upstream,
):
    layers, small, width = query_weight.shape
    hidden = inner_weight.shape[2]
    count = net["count"]
    move = net["move"]
    staged = count == BLOCKS and small % 16 == 0
    dp = lax.axis_index("dp").astype(jnp.int32)
    y = lax.axis_index("seq").astype(jnp.int32)
    core = lax.rem(dp, 2)
    if staged:
        pos_g = jnp.stack([lax.div(dp, 4), lax.rem(lax.div(dp, 2), 2), core, y])
        pos_w = pos_g
    else:
        zero = jnp.zeros((), jnp.int32)
        pos_g = jnp.stack([zero, zero, core, zero])
        pos_w = jnp.stack([zero, zero, zero, zero])

    labels = jnp.where(padding == 1, segment_ids, -1)
    small_own = move(jnp.concatenate([segment_ids, labels]), net["swap"])
    token_low = move(tokens[0], net["swap"])

    vector_args = [query_bias, value_bias, output_bias, attn_gain, attn_shift, outer_bias]
    vector_args += [ffn_gain, ffn_shift, inner_bias]
    table = vector_table(dp[None], vector_args, width)
    if staged:
        table = table + move(table, net["x"])
    else:
        table = lax.psum(table, "dp")

    raw = (query_weight, key_weight, value_weight, output_weight, inner_weight, outer_weight)
    chunks = []
    for layer in range(layers):
        four = (query_weight[layer], key_weight[layer], value_weight[layer], output_weight[layer])
        if not staged:
            full = [lax.all_gather(value, "dp", axis=0, tiled=True) for value in four]
            inner = lax.all_gather(inner_weight[layer], "dp", axis=0, tiled=True)
            outer = lax.all_gather(outer_weight[layer], "dp", axis=0, tiled=True)
            rows = width // BLOCKS

            def cut(value, dy, dx, dc):
                value = value.reshape(ZS, 2, 2, rows, 2, -1)
                return value[:, dx, dc, :, dy, :]

            lists = [[[], []], [[], []], [[], []]]
            for dc in range(2):
                for part, dy, dx in UNITS:
                    lists[0][dc].append(
                        jnp.concatenate([cut(value, dy, dx, dc) for value in full[part * 2 : part * 2 + 2]], axis=2)
                    )
                    lists[1][dc].append(cut(inner, dy, dx, dc)[..., part * width : (part + 1) * width])
                    lists[2][dc].append(
                        outer.reshape(ZS, 2, 2, 2, 2, hidden // BLOCKS // 4, width)[:, dx, dc, dy, part]
                    )
            chunks.extend(tuple(jnp.concatenate(side) for side in value) for value in lists)

    total_chunks = 3 * layers
    groups = []
    if staged:
        edges = [0, 1, 2] + list(range(3, total_chunks + 1, 3))
        groups = [range(low, high) for low, high in zip(edges[:-1], edges[1:])]
    where_of = {i: (g, i - group[0]) for g, group in enumerate(groups) for i in group}
    stage_z = [None] * len(groups)

    def start_z2(g):
        own = pack_pieces(groups[g], pos_g, raw)
        stage_z[g] = (own, move(own, net["z2"]))

    def start_z1(g):
        own, come = stage_z[g]
        size = own.shape[0]
        both = copy_blocks([(0, 0, 0, 0, size), (0, size, 1, 0, size)], (own, come), [2 * size], "gather_z")[0]
        stage_z[g] = (both, move(both, net["z1"]))

    if staged:
        start_z2(0)
        stage_z[0], raw, table, small_own, token_low = fence(
            (stage_z[0], raw, table, small_own, token_low)
        )
        start_z1(0)
        start_z2(1)
        table = table + move(table, net["core"])
    small_other = move(small_own, net["core"])
    token_other = move(token_low, net["core"])
    if staged:
        stage_z[:2], raw, table, small_own, small_other, token_low, token_other, upstream = fence(
            (stage_z[:2], raw, table, small_own, small_other, token_low, token_other, upstream)
        )
    seg = small_own[0:1]
    lab = jnp.concatenate([small_own[1], small_other[1]])[:, None]
    current = token_low.astype(F32)
    other = token_other
    kept = [None] * layers
    todo = []
    for layer in range(layers):
        todo.append(("attn", layer, 3 * layer))
        todo.append(("ffn", layer, 3 * layer + 2))
    low = None
    attn_out = None
    arrived = 0 if staged else total_chunks

    def compute():
        nonlocal current, other, low, attn_out
        if not todo or todo[0][2] >= arrived:
            return
        kind, layer, _ = todo.pop(0)
        if kind == "attn":
            attn_out = attn_forward(
                pos_w, pos_g, current, other, seg, lab, table[layer], chunks[3 * layer]
            )
            return
        h, n1, c1, q, kt, v, p, xoh, far_xoh = attn_out
        current, low, n2, c2, gp, gt, far_gt = ffn_forward(
            pos_w, pos_g, h, table[layer], chunks[3 * layer + 1], chunks[3 * layer + 2]
        )
        if layer + 1 < layers:
            other = move(low, net["core"])
        kept[layer] = (n1, c1, q, kt, v, p, n2, c2, gp, xoh, gt) + (
            move(far_xoh, net["core"]),
            move(far_gt, net["core"]),
        )

    if staged:
        sent, got = {}, {}
        zplan = {
            -LAG: [(1, 1), (2, 2)],
            -LAG + 1: [(1, 2), (2, 3)],
            -LAG + 2: [(1, 3)],
            -LAG + 3: [(2, 4)],
            -LAG + 4: [(1, 4)],
        }
        spread = [net["z2"], net["z1"]]
        for r in range(-LAG, total_chunks + LAG):
            inputs, plan = [], []
            sizes = [0, 0]
            use = lambda value: (inputs.append(value), len(inputs) - 1)[1]
            fresh = r + LAG < total_chunks
            if fresh:
                g, j = where_of[r + LAG]
                n = len(groups[g])
                mine, theirs = use(stage_z[g][0]), use(stage_z[g][1])
                for out, part in ((0, 1), (1, 0)):
                    for k, (source, slot) in enumerate(((mine, 0), (theirs, 0), (mine, 1), (theirs, 1))):
                        plan.append((out, k, source, (slot * n + j) * 2 + part, 1))
                    sizes[out] = ZS
            before = r - LAG
            home = 0 <= before < total_chunks
            if before >= -LAG and (r < total_chunks or home):
                sx, sy = use(sent[before][0]), use(sent[before][1])
                rx, ry = use(got[before][0]), use(got[before][1])
                first = ZS if before + LAG < total_chunks else 0
                if r < total_chunks:
                    for out, send, come in ((0, sy, ry), (1, sx, rx)):
                        plan.append((out, sizes[out], send, 0, ZS))
                        plan.append((out, sizes[out] + ZS, come, 0, ZS))
                        sizes[out] += 2 * ZS
                if home:
                    sizes.append(8 * ZS)
                    slot = 2
                    for at, (send, come) in enumerate(((sx, rx), (sy, ry))):
                        plan.append((slot, at * 4 * ZS, send, first, 2 * ZS))
                        plan.append((slot, at * 4 * ZS + 2 * ZS, come, first, 2 * ZS))
            live = [index for index, size in enumerate(sizes) if size]
            outs = copy_blocks(
                [(live.index(each[0]),) + each[1:] for each in plan],
                inputs,
                [sizes[index] for index in live],
                "gather_round",
            )
            outs = dict(zip(live, outs))
            if 0 in outs:
                sent[r] = (outs[0], outs[1])
                got[r] = (move(outs[0], net["x"]), move(outs[1], net["y"]))
            core_pair = None
            if home:
                core_pair = (outs[2], move(outs[2], net["core"]))
            for stage, g in zplan.get(r, ()):
                if g < len(groups):
                    (start_z2 if stage == 2 else start_z1)(g)
            if spread:
                table = table + move(table, spread.pop(0))
            if r == total_chunks - 2:
                upstream = move(upstream[0], net["swap"])
            compute()
            ready = r + 1 - LAG
            state = (got.get(ready), core_pair, stage_z, current, other, attn_out, raw, table, upstream)
            state = fence(state)
            if ready in got:
                got[ready] = state[0]
            if home:
                chunks.append(state[1])
                arrived += 1
            stage_z, current, other, attn_out, raw, table, upstream = (list(state[2]),) + tuple(state[3:])
    while todo:
        compute()
    range_ids = jnp.arange(SEGS, dtype=jnp.int32)
    own = (small_own[1][None, :] == range_ids[:, None]).astype(F32)
    sums = jnp.dot(own, current, precision=lax.Precision.HIGHEST)
    pool_sums = sums
    counts = jnp.sum((lab[:, 0][None, :] == range_ids[:, None]).astype(F32), axis=1)
    loose = {}
    if staged:
        loose["hidden"] = move(low, net["swap"])
        loose["pool"] = pool_sums + move(pool_sums, net["core"])

    grad = upstream if staged else move(upstream[0], net["swap"])
    parts = []
    vectors = [None] * layers
    rounds = []
    ends = []

    def side_work():
        step = len(rounds)
        last = total_chunks
        if step == 0:
            loose["pooled"] = move(loose.pop("pool") / counts[:, None], net["swap"])
        if step == last - 2:
            loose["table"] = jnp.stack(vectors)
            loose["table"] = loose["table"] + move(loose["table"], net["core"])
        order = {last - 1: "z1", last: "z2", last + 1: "x", last + 2: "y"}
        if step in order:
            loose["table"] = loose["table"] + move(loose["table"], net[order[step]])
        if step == last:
            loose["grad"] = move(loose.pop("grad").astype(BF16), net["swap"])

    def settle(state):
        nonlocal loose
        state, loose = fence((state, loose))
        return state

    def advance(fresh, state):
        nonlocal loose
        if not staged:
            if fresh is not None:
                parts.append(fresh)
            return state
        side_work()
        s = len(rounds)
        past = rounds[s - LAG] if s >= LAG else {}
        pick = lambda key: past.get(key)
        has_home = pick("first") is not None or pick("second") is not None
        sends, going, first, second, third, fourth = sum_round(
            fresh,
            pick("got_x") if has_home else None,
            pick("got_y") if has_home else None,
            pick("first"),
            pick("second"),
            pick("third"),
            pick("fourth"),
        )
        now = {}
        if fresh is not None:
            now["first"] = (fresh[0], fresh[2])
        if first is not None:
            now["second"] = first
        if sends is not None:
            if going:
                now["got_x"] = move(sends[0], net["x"])
            now["got_y"] = move(sends[1], net["y"])
        if second is not None:
            now["third"] = (second[0], move(second[1], net["z1"]))
        if third is not None:
            now["fourth"] = (third[0], move(third[1], net["z2"]))
        if fourth is not None:
            now["total"] = fourth[0]
            ends.append(going)
        rounds.append(now)
        ready = s + 1 - LAG
        if ready < 0:
            state, loose = fence((state, loose))
            return state
        rounds[ready], state, loose = fence((rounds[ready], state, loose))
        return state

    ready = None
    for layer in reversed(range(layers)):
        attn_bufs, inner_bufs, outer_bufs = chunks[3 * layer : 3 * layer + 3]
        vec = table[layer]
        n1, c1, q, kt, v, p, n2, c2, gp, xoh, gt, far_xoh, far_gt = kept[layer]
        pack, da, do, sums = chain_backward(
            pos_w, grad, n2, c2, gp, n1, c1, vec, inner_bufs, outer_bufs, attn_bufs
        )
        if layer + 1 < layers:
            attn_parts = attn_grad(*attn_args)
            (pack, da, do, sums), attn_parts = advance(ready, ((pack, da, do, sums), attn_parts))
            ready = attn_parts
        got_pack = move(pack, net["core"])
        back, qsum = attn_backward(q, kt, v, p, do)
        outer_parts = outer_grad(gt, far_gt, pack, got_pack, width)
        state = (back, qsum, outer_parts, pack, got_pack, da)
        back, qsum, outer_parts, pack, got_pack, da = (
            advance(ready, state) if ready is not None else settle(state)
        )
        got_back = move(back, net["core"])
        inner_parts = inner_grad(pos_g, xoh, far_xoh, pack, got_pack)
        grad, total, vsum = input_backward(pos_w, da, back, got_back, attn_bufs)
        state = (grad, total, vsum, inner_parts, back, got_back)
        grad, total, vsum, inner_parts, back, got_back = advance(outer_parts, state)
        ready = inner_parts
        attn_args = (pos_g, xoh, far_xoh, back, got_back, total, pack, got_pack)
        vectors[layer] = jnp.concatenate([qsum[:1], vsum[:1], sums[2:12]], axis=0)
    loose["grad"] = grad
    attn_parts = attn_grad(*attn_args)
    attn_parts = advance(ready, attn_parts)
    advance(attn_parts, None)
    results = []
    if staged:
        for _ in range(4 * LAG):
            advance(None, None)
        for s, now in enumerate(rounds):
            if "total" in now:
                results.append((now["total"], now["got_y"], ends[len(results)]))

    if staged:
        stacked = []
        for kind, first in ((0, 2), (1, 1), (2, 0)):
            stacked += list(finish(kind, pos_g, results[first::3][::-1]))
        hidden_out, pooled, tokens_grad, table = (
            loose[key] for key in ("hidden", "pooled", "grad", "table")
        )
    else:
        collected = [None] * layers
        for place_at, layer in enumerate(reversed(range(layers))):
            outer_parts, inner_parts, attn_parts = parts[3 * place_at : 3 * place_at + 3]

            def spread(outs):
                a_keep, a_send, b_keep, b_send = outs
                a = jnp.stack([a_keep, a_send])
                b = jnp.stack([b_keep, b_send], axis=1)
                return jnp.stack([a, b], axis=2)

            def total(out):
                out = out.reshape(ZS * 2, 1, out.shape[2], out.shape[3])
                mine = (jnp.arange(2, dtype=jnp.int32) == core)[None, :, None, None]
                out = jnp.where(mine, out, jnp.zeros_like(out)).reshape(-1, out.shape[-1])
                out = lax.psum_scatter(out, "dp", scatter_dimension=0, tiled=True)
                return lax.psum(out.astype(F32), "seq")

            outer = spread(outer_parts).transpose(3, 0, 1, 2, 4, 5)
            outer = total(outer.reshape(ZS, 2, -1, width))
            inner = spread(inner_parts).transpose(3, 0, 4, 1, 2, 5)
            inner = total(inner.reshape(ZS, 2, inner.shape[2], -1))
            attn = spread(attn_parts)
            attn = attn.reshape(attn.shape[:5] + (2, width // 2)).transpose(2, 5, 3, 0, 4, 1, 6)
            attn = attn.reshape(4, ZS, 2, attn.shape[4], width)
            four = [total(attn[index]) for index in range(4)]
            collected[layer] = four + [inner, outer]
        stacked = [
            jnp.stack([collected[layer][member] for layer in range(layers)]) for member in range(6)
        ]
        hidden_out = move(low, net["swap"])
        pooled = move((pool_sums + move(pool_sums, net["core"])) / counts[:, None], net["swap"])
        tokens_grad = move(grad.astype(BF16), net["swap"])
        table = lax.psum(jnp.stack(vectors), AXES)
    eight = lax.dynamic_slice_in_dim(table[:, :8], dp * small, small, 2)
    wide = lax.dynamic_slice_in_dim(
        table[:, 8:].reshape(layers, hidden), dp * (hidden // count), hidden // count, 1
    )
    return (
        hidden_out[None],
        pooled[None],
        tokens_grad.astype(F32)[None],
        stacked[0],
        stacked[1],
        stacked[2],
        stacked[3],
        eight[:, QB],
        eight[:, VB],
        eight[:, OB],
        eight[:, AG],
        eight[:, AS],
        stacked[4],
        wide,
        stacked[5],
        eight[:, UB],
        eight[:, FG],
        eight[:, FS],
    )


def solution(mesh):
    cube = P(None, "dp", None)
    flat = P(None, "dp")
    acts = P("dp", "seq", None)
    ids = P("dp", "seq")
    return jax.shard_map(
        functools.partial(body, build(mesh)),
        mesh=mesh,
        in_specs=(acts, ids, ids, cube, cube, cube, cube, flat, flat, flat, flat, flat, cube, flat, cube)
        + (flat, flat, flat, acts),
        out_specs=(acts, P("dp", None, None), acts, cube, cube, cube, cube)
        + (flat, flat, flat, flat, flat, cube, flat, cube, flat, flat, flat),
        check_vma=False,
    )
```

time: 961 us -> 649 us (0.68)
  waiting for transfers between devices: 402 us -> 216 us
  starting transfers between devices: 194 us -> 115 us
  local copies, waits for them, and re-layouts: 129 us -> 52.1 us
  Pallas kernels: 195 us -> 248 us
  other arithmetic: 25.6 us -> 3.74 us
    ppermute x205 -> x112, waiting for transfers between devices: 402 us -> 216 us  [move(): return lax.ppermute(value, AXES, perm)]
    ppermute x205 -> x112, starting transfers between devices: 194 us -> 115 us  [move(): return lax.ppermute(value, AXES, perm)]
    unnamed x527 -> x338, local copies, waits for them, and re-layouts: 104 us -> 47.5 us
    pallas_call x18 -> x56, Pallas kernels: 136 us -> 183 us  [the longest x3 50.4 us: ffn_forward(): pl.pallas_call(functools.partial(ffn_kernel, 384), out_shape=(shape((toke...]
    squeeze x21 -> x5, local copies, waits for them, and re-layouts: 14 us -> 0.83 us  [compute(): table[layer]]
  transfers between devices with their start and end apart: 205 -> 112, of which waited for: 71 -> 47; matrix products, arithmetic and copies ran while one was open for 5% -> 1% of each run, Pallas kernels for 21% -> 29%
where the time goes in v2:
time: 649 us; the launch traced here: 638 us
  Pallas kernels  248 us (38%)
  waiting for transfers between devices  216 us (33%)
  starting transfers between devices  115 us (18%)
  local copies, waits for them, and re-layouts  52.1 us (8%)
    ppermute x112, waiting for transfers between devices, move(): return lax.ppermute(value, AXES, perm)  216 us
    ppermute x112, starting transfers between devices, move(): return lax.ppermute(value, AXES, perm)  115 us
    pallas_call x3, Pallas kernels, ffn_forward(): pl.pallas_call(functools.partial(ffn_kernel, 384), out_shape=(shape((toke...  50.4 us
    pallas_call x3, Pallas kernels, chain_backward(): pl.pallas_call(functools.partial(chain_kernel, 384), out_shape=(shape((to...  49.8 us
    unnamed x338, local copies, waits for them, and re-layouts  47.5 us
    pallas_call x3, Pallas kernels, attn_forward(): pl.pallas_call(attn_kernel, out_shape=(shape((tokens, width), F32),) + ke...  44.6 us
    pallas_call x3, Pallas kernels, attn_backward(): pl.pallas_call(attn_back_kernel, out_shape=(shape((5, tokens, width), BF1...  23.3 us
    pallas_call x16, Pallas kernels, copy_blocks(): pl.pallas_call(functools.partial(copy_kernel, plan, len(inputs)), out_sha...  22.6 us
  transfers between devices with their start and end apart: 112, of which 47 were waited for; matrix products, arithmetic and copies ran while one was open for 1% of the time, Pallas kernels for 29%

profile of v2, /device:TPU:0, one launch (start us, length us, event | category | flops | bytes accessed | tf_op | source)
XLA Modules:
  0.0 638.3 jit_solution(15714533441115199057)
XLA Ops:
  9.3 4.1 collective-permute-start
  16.1 3.9 collective-permute-done.1
  24.3 2.5 collective-permute-start.5
  28.3 5.1 collective-permute-done.5.refs_1_
  34.7 2.7 collective-permute-start.11
  44.9 11.3 %collective-permute-done.13 = f32[3,12,768]{2,1,0:T(8,128)S(1)} collective-permute-done((f32[3,12,768]{2,1,0:T(8,128)S(1)}, f32[3,12,768]{2,1,0:T(8,128)S(1)}, u32[]{:S(2)}, u32[]{:S(2)}) %collective-permute-start.13) | collective-permute-done | bytes 110624 | tf_op jit(solution)/shard_map/ppermute | solution.py:953
  62.9 17.7 %collective-permute-done.18 = f32[3,12,768]{2,1,0:T(8,128)S(1)} collective-permute-done((f32[3,12,768]{2,1,0:T(8,128)S(1)}, f32[3,12,768]{2,1,0:T(8,128)S(1)}, u32[]{:S(2)}, u32[]{:S(2)}) %collective-permute-start.18) | collective-permute-done | bytes 110624 | tf_op jit(solution)/shard_map/ppermute | solution.py:953
  86.0 19.7 %collective-permute-done.22.refs_1_ = bf16[12,48,768]{2,1,0:T(8,128)(2,1)S(1)} collective-permute-done((bf16[12,48,768]{2,1,0:T(8,128)(2,1)S(1)}, bf16[12,48,768]{2,1,0:T(8,128)(2,1)S(1)}, u32[]{:S(2)}, u32[]{:S(2)}) %collective-permute-start.22) | collective-permute-done | bytes 884768 | tf_op jit(solution)/shard_map/ppermute | solution.py:953
  108.7 3.6 gather_round.14
  115.7 2.1 collective-permute-start.26
  122.6 14.9 %attn_forward.3 = (f32[256,768]{1,0:T(8,128)S(1)}, f32[256,768]{1,0:T(8,128)S(1)}, f32[256,128]{1,0:T(8,128)S(1)}, bf16[256,768]{1,0:T(8,128)(2,1)S(1)}, bf16[76...) custom-call(s32[4]{0:T(128)S(1)} %pad_add_fusion.2.pos_ref.refs_0_.r, ...), custom_call_target="tpu_custom_call" | custom-call | flops 1 | bytes 1 | tf_op jit(solution)/shard_map/attn_forward/pallas_call | solution.py:258
  140.7 3.9 gather_round.15
  150.1 17.8 %collective-permute-done.30.refs_1_ = bf16[12,48,768]{2,1,0:T(8,128)(2,1)S(1)} collective-permute-done((bf16[12,48,768]{2,1,0:T(8,128)(2,1)S(1)}, bf16[12,48,768]{2,1,0:T(8,128)(2,1)S(1)}, u32[]{:S(2)}, u32[]{:S(2)}) %collective-permute-start.30) | collective-permute-done | bytes 884768 | tf_op jit(solution)/shard_map/ppermute | solution.py:953
  173.2 16.5 %ffn_forward.3 = (f32[256,768]{1,0:T(8,128)S(1)}, bf16[256,768]{1,0:T(8,128)(2,1)S(1)}, f32[256,768]{1,0:T(8,128)S(1)}, f32[256,128]{1,0:T(8,128)S(1)}, bf16[256...) custom-call(s32[4]{0:T(128)S(1)} %pad_add_fusion.2.pos_ref.refs_0_.re, ...), custom_call_target="tpu_custom_call" | custom-call | flops 1 | bytes 1 | tf_op jit(solution)/shard_map/ffn_forward/pallas_call | solution.py:346
  198.4 14.9 %attn_forward.4 = (f32[256,768]{1,0:T(8,128)S(1)}, f32[256,768]{1,0:T(8,128)S(1)}, f32[256,128]{1,0:T(8,128)S(1)}, bf16[256,768]{1,0:T(8,128)(2,1)S(1)}, bf16[76...) custom-call(s32[4]{0:T(128)S(1)} %pad_add_fusion.2.pos_ref.refs_0_.r, ...), custom_call_target="tpu_custom_call" | custom-call | flops 1 | bytes 1 | tf_op jit(solution)/shard_map/attn_forward/pallas_call | solution.py:258
  222.3 20.0 %collective-permute-done.38.refs_4_ = bf16[12,48,768]{2,1,0:T(8,128)(2,1)S(1)} collective-permute-done((bf16[12,48,768]{2,1,0:T(8,128)(2,1)S(1)}, bf16[12,48,768]{2,1,0:T(8,128)(2,1)S(1)}, u32[]{:S(2)}, u32[]{:S(2)}) %collective-permute-start.38) | collective-permute-done | bytes 884768 | tf_op jit(solution)/shard_map/ppermute | solution.py:953
  247.5 17.0 %ffn_forward.4 = (f32[256,768]{1,0:T(8,128)S(1)}, bf16[256,768]{1,0:T(8,128)(2,1)S(1)}, f32[256,768]{1,0:T(8,128)S(1)}, f32[256,128]{1,0:T(8,128)S(1)}, bf16[256...) custom-call(s32[4]{0:T(128)S(1)} %pad_add_fusion.2.pos_ref.refs_0_.re, ...), custom_call_target="tpu_custom_call" | custom-call | flops 1 | bytes 1 | tf_op jit(solution)/shard_map/ffn_forward/pallas_call | solution.py:346
  268.5 7.6 %collective-permute-start.48 = (bf16[32,48,768]{2,1,0:T(8,128)(2,1)S(1)}, bf16[32,48,768]{2,1,0:T(8,128)(2,1)S(1)}, u32[]{:S(2)}, u32[]{:S(2)}) collective-permute-start(bf16[32,48,768]{2,1,0:T(8,128)(2,1)S(1)} %get-tuple-element.902.refs_4_.refs_8_), channel_id=1, source_target_pairs={{2,0},{3,1},{0,2},{1,3},{6,4},{7,5},{4,6},{5,7},{10,8},{11,9},{8,1... | collective-permute-start | bytes 7077896 | tf_op jit(solution)/shard_map/ppermute | solution.py:953
  276.6 14.9 %attn_forward.5 = (f32[256,768]{1,0:T(8,128)S(1)}, f32[256,768]{1,0:T(8,128)S(1)}, f32[256,128]{1,0:T(8,128)S(1)}, bf16[256,768]{1,0:T(8,128)(2,1)S(1)}, bf16[76...) custom-call(s32[4]{0:T(128)S(1)} %pad_add_fusion.2.pos_ref.refs_0_.r, ...), custom_call_target="tpu_custom_call" | custom-call | flops 1 | bytes 1 | tf_op jit(solution)/shard_map/attn_forward/pallas_call | solution.py:258
  294.6 4.5 collective-permute-done.49.refs_7_.refs_11_
  299.8 17.0 %ffn_forward.5 = (f32[256,768]{1,0:T(8,128)S(1)}, bf16[256,768]{1,0:T(8,128)(2,1)S(1)}, f32[256,768]{1,0:T(8,128)S(1)}, f32[256,128]{1,0:T(8,128)S(1)}, bf16[256...) custom-call(s32[4]{0:T(128)S(1)} %pad_add_fusion.2.pos_ref.refs_0_.re, ...), custom_call_target="tpu_custom_call" | custom-call | flops 1 | bytes 1 | tf_op jit(solution)/shard_map/ffn_forward/pallas_call | solution.py:346
  318.4 16.9 %chain_backward.3 = (bf16[256,4608]{1,0:T(8,128)(2,1)S(1)}, f32[256,768]{1,0:T(8,128)S(1)}, bf16[256,768]{1,0:T(8,128)(2,1)S(1)}, f32[16,768]{1,0:T(8,128)S(1)}) custom-call(s32[4]{0:T(128)S(1)} %pad_add_fusion.2.pos_ref.refs_0_.refs_1_, bf16[256,768]{1,0:T(8,128)(2,1)S(1)} %collective-permute-done.45.refs_1_, f32[256,768]{1,0:T(8,128)S(1)} %get-tuple-element.906.refs_2_, ...), custom_call_target="tpu_custom_call" | custom-call | flops 1 | bytes 1 | tf_op jit(solution)/shard_map/chain_backward/pallas_call | solution.py:429
  337.0 3.3 collective-permute-start.53
  342.2 7.8 %attn_backward.3 = (bf16[5,256,768]{2,1,0:T(8,128)(2,1)S(1)}, f32[8,768]{1,0:T(8,128)S(1)}) custom-call(bf16[256,768]{1,0:T(8,128)(2,1)S(1)} %get-tuple-element.895.refs_0_, bf16[768,512]{1,0:T(8,128)(2,1)S(1)} %copy-done.81, bf16[512,768]{1,0:T(8,128)(2,1)S(1)} %copy-done.83, bf16[12,512,256]{2,1,0:T(8,128)(2,1)S(1)} %copy-done.42, ...), custom_call_target="tpu_custom_call" | custom-call | flops 1 | bytes 1 | tf_op jit(solution)/shard_map/attn_backward/pallas_call | solution.py:500
  356.5 2.9 inner_grad.3
  360.3 5.0 input_backward.3
  365.3 2.3 collective-permute-done.54.refs_2_
  372.1 16.9 %chain_backward.4 = (bf16[256,4608]{1,0:T(8,128)(2,1)S(1)}, f32[256,768]{1,0:T(8,128)S(1)}, bf16[256,768]{1,0:T(8,128)(2,1)S(1)}, f32[16,768]{1,0:T(8,128)S(1)}) custom-call(s32[4]{0:T(128)S(1)} %pad_add_fusion.2.pos_ref.refs_0_.refs_1_, f32[256,768]{1,0:T(8,128)S(1)} %get-tuple-element.957.refs_1_, f32[256,768]{1,0:T(8,128)S(1)} %copy-done.67, ...), custom_call_target="tpu_custom_call" | custom-call | flops 1 | bytes 1 | tf_op jit(solution)/shard_map/chain_backward/pallas_call | solution.py:429
  389.0 2.8 attn_grad.3
  397.4 7.8 %attn_backward.4 = (bf16[5,256,768]{2,1,0:T(8,128)(2,1)S(1)}, f32[8,768]{1,0:T(8,128)S(1)}) custom-call(bf16[256,768]{1,0:T(8,128)(2,1)S(1)} %copy-done.95, bf16[768,512]{1,0:T(8,128)(2,1)S(1)} %copy-done.77, bf16[512,768]{1,0:T(8,128)(2,1)S(1)} %copy-done.79, bf16[12,512,256]{2,1,0:T(8,128)(2,1)S(1)} %copy-done.40, ...), custom_call_target="tpu_custom_call" | custom-call | flops 1 | bytes 1 | tf_op jit(solution)/shard_map/attn_backward/pallas_call | solution.py:500
  406.8 7.7 %collective-permute-done.61.refs_2_ = bf16[12,48,768]{2,1,0:T(8,128)(2,1)S(1)} collective-permute-done((bf16[12,48,768]{2,1,0:T(8,128)(2,1)S(1)}, bf16[12,48,768]{2,1,0:T(8,128)(2,1)S(1)}, u32[]{:S(2)}, u32[]{:S(2)}) %collective-permute-start.61) | collective-permute-done | bytes 884768 | tf_op jit(solution)/shard_map/ppermute | solution.py:953
  420.7 2.1 collective-permute-start.66
  422.9 2.5 inner_grad.4
  426.2 5.2 input_backward.4
  431.4 7.2 %collective-permute-done.67.refs_2_ = bf16[12,48,768]{2,1,0:T(8,128)(2,1)S(1)} collective-permute-done((bf16[12,48,768]{2,1,0:T(8,128)(2,1)S(1)}, bf16[12,48,768]{2,1,0:T(8,128)(2,1)S(1)}, u32[]{:S(2)}, u32[]{:S(2)}) %collective-permute-start.67) | collective-permute-done | bytes 884768 | tf_op jit(solution)/shard_map/ppermute | solution.py:953
  446.7 16.0 %chain_backward.5 = (bf16[256,4608]{1,0:T(8,128)(2,1)S(1)}, f32[256,768]{1,0:T(8,128)S(1)}, bf16[256,768]{1,0:T(8,128)(2,1)S(1)}, f32[16,768]{1,0:T(8,128)S(1)}) custom-call(s32[4]{0:T(128)S(1)} %pad_add_fusion.2.pos_ref.refs_0_.refs_1_, f32[256,768]{1,0:T(8,128)S(1)} %get-tuple-element.1059.refs_1_, f32[256,768]{1,0:T(8,128)S(1)} %copy-done.63, ...), custom_call_target="tpu_custom_call" | custom-call | flops 1 | bytes 1 | tf_op jit(solution)/shard_map/chain_backward/pallas_call | solution.py:429
  462.8 3.2 attn_grad.4
  473.3 2.1 collective-permute-start.76
  475.4 7.8 %attn_backward.5 = (bf16[5,256,768]{2,1,0:T(8,128)(2,1)S(1)}, f32[8,768]{1,0:T(8,128)S(1)}) custom-call(bf16[256,768]{1,0:T(8,128)(2,1)S(1)} %copy-done.93, bf16[768,512]{1,0:T(8,128)(2,1)S(1)} %copy-done.73, bf16[512,768]{1,0:T(8,128)(2,1)S(1)} %copy-done.75, bf16[12,512,256]{2,1,0:T(8,128)(2,1)S(1)} %copy-done.38, bf16[256,768]{1,0:T(8,128)(2,1)S(1)} %copy-done.97), custom_call_target="tpu_custom_call" | custom-call | flops 1 | bytes 1 | tf_op jit(solution)/shard_map/attn_backward/pallas_call | solution.py:500
  484.8 8.3 %collective-permute-done.77.refs_2_ = bf16[12,48,768]{2,1,0:T(8,128)(2,1)S(1)} collective-permute-done((bf16[12,48,768]{2,1,0:T(8,128)(2,1)S(1)}, bf16[12,48,768]{2,1,0:T(8,128)(2,1)S(1)}, u32[]{:S(2)}, u32[]{:S(2)}) %collective-permute-start.77) | collective-permute-done | bytes 884768 | tf_op jit(solution)/shard_map/ppermute | solution.py:953
  493.1 2.5 collective-permute-done.78.refs_3_.refs_5_
  500.5 2.1 collective-permute-start.82
  502.5 2.5 inner_grad.5
  505.0 5.2 input_backward.5
  510.8 8.5 %collective-permute-done.83.refs_2_ = bf16[12,48,768]{2,1,0:T(8,128)(2,1)S(1)} collective-permute-done((bf16[12,48,768]{2,1,0:T(8,128)(2,1)S(1)}, bf16[12,48,768]{2,1,0:T(8,128)(2,1)S(1)}, u32[]{:S(2)}, u32[]{:S(2)}) %collective-permute-start.83) | collective-permute-done | bytes 884768 | tf_op jit(solution)/shard_map/ppermute | solution.py:953
  519.3 3.0 collective-permute-done.84.refs_3_.refs_5_
  529.0 2.8 attn_grad.5
  531.9 6.4 %collective-permute-done.88.refs_11_ = bf16[2,48,768]{2,1,0:T(8,128)(2,1)S(1)} collective-permute-done((bf16[2,48,768]{2,1,0:T(8,128)(2,1)S(1)}, bf16[2,48,768]{2,1,0:T(8,128)(2,1)S(1)}, u32[]{:S(2)}, u32[]{:S(2)}) %collective-permute-start.88) | collective-permute-done | bytes 147488 | tf_op jit(solution)/shard_map/ppermute | solution.py:953
  539.1 5.3 collective-permute-done.89.refs_2_
  544.4 3.0 collective-permute-done.90.refs_3_.refs_4_
  553.0 9.0 %collective-permute-done.97 = f32[3,12,768]{2,1,0:T(8,128)S(1)} collective-permute-done((f32[3,12,768]{2,1,0:T(8,128)S(1)}, f32[3,12,768]{2,1,0:T(8,128)S(1)}, u32[]{:S(2)}, u32[]{:S(2)}) %collective-permute-start.97) | collective-permute-done | bytes 110624 | tf_op jit(solution)/shard_map/ppermute | solution.py:953
  562.1 6.2 collective-permute-done.94.refs_0_
  568.2 3.0 collective-permute-done.95.refs_1_.refs_4_
  575.9 7.4 %collective-permute-done.103 = f32[3,12,768]{2,1,0:T(8,128)S(1)} collective-permute-done((f32[3,12,768]{2,1,0:T(8,128)S(1)}, f32[3,12,768]{2,1,0:T(8,128)S(1)}, u32[]{:S(2)}, u32[]{:S(2)}) %collective-permute-start.103) | collective-permute-done | bytes 110624 | tf_op jit(solution)/shard_map/ppermute | solution.py:953
  583.3 3.4 collective-permute-start.98
  586.7 6.7 %collective-permute-done.98.refs_7_ = bf16[2,48,768]{2,1,0:T(8,128)(2,1)S(1)} collective-permute-done((bf16[2,48,768]{2,1,0:T(8,128)(2,1)S(1)}, bf16[2,48,768]{2,1,0:T(8,128)(2,1)S(1)}, u32[]{:S(2)}, u32[]{:S(2)}) %collective-permute-start.98) | collective-permute-done | bytes 147488 | tf_op jit(solution)/shard_map/ppermute | solution.py:953
  595.2 5.4 collective-permute-start.105
  601.7 4.0 collective-permute-done.107
  605.7 2.3 collective-permute-done.106.refs_1_
  609.4 2.0 collective-permute-start.110
  611.4 6.7 %collective-permute-done.110 = f32[3,12,768]{2,1,0:T(8,128)S(1)} collective-permute-done((f32[3,12,768]{2,1,0:T(8,128)S(1)}, f32[3,12,768]{2,1,0:T(8,128)S(1)}, u32[]{:S(2)}, u32[]{:S(2)}) %collective-permute-start.110) | collective-permute-done | bytes 110624 | tf_op jit(solution)/shard_map/ppermute | solution.py:953
  622.5 2.5 finish.5
  625.2 2.5 finish.4
  634.1 2.7 finish.3
  (605 shorter events, 181.1 us)
Async XLA Ops:
  0.8 19.3 %collective-permute-start.3 = (bf16[256,768]{1,0:T(8,128)(2,1)}, bf16[256,768]{1,0:T(8,128)(2,1)S(1)}, u32[]{:S(2)}, u32[]{:S(2)}) collective-permute-start(bf16[256,768]{1,0:T(8,128)(2,1)} %bitcast.80), channel_id=1, source_target_pairs={{0,0},{2,1},{1,2},{3,3},{4,4},{6,5},{5,6},{7,7},{8,8},{10,9},{9,10... | collective-permute-start | bytes 1179656 | tf_op jit(solution)/shard_map/ppermute | solution.py:953
  34.7 21.6 %collective-permute-start.11 = (bf16[4,48,768]{2,1,0:T(8,128)(2,1)S(1)}, bf16[4,48,768]{2,1,0:T(8,128)(2,1)S(1)}, u32[]{:S(2)}, u32[]{:S(2)}) collective-permute-start(bf16[4,48,768]{2,1,0:T(8,128)(2,1)S(1)} %gather_z.6.refs_0_), channel_id=1, source_target_pairs={{8,0},{9,1},{10,2},{11,3},{12,4},{13,5},{14,6},{15,7},{0,8},{1,9},... | collective-permute-start | bytes 884744 | tf_op jit(solution)/shard_map/ppermute | solution.py:953
  38.2 18.1 %collective-permute-start.10 = (bf16[4,48,768]{2,1,0:T(8,128)(2,1)S(1)}, bf16[4,48,768]{2,1,0:T(8,128)(2,1)S(1)}, u32[]{:S(2)}, u32[]{:S(2)}) collective-permute-start(bf16[4,48,768]{2,1,0:T(8,128)(2,1)S(1)} %get-tuple-element.672.refs_3_), channel_id=1, source_target_pairs={{1,0},{0,1},{3,2},{2,3},{5,4},{4,5},{7,6},{6,7},{9,8},{8,9},{11,10... | collective-permute-start | bytes 884744 | tf_op jit(solution)/shard_map/ppermute | solution.py:953
  38.7 17.6 %collective-permute-start.9 = (bf16[4,48,768]{2,1,0:T(8,128)(2,1)S(1)}, bf16[4,48,768]{2,1,0:T(8,128)(2,1)S(1)}, u32[]{:S(2)}, u32[]{:S(2)}) collective-permute-start(bf16[4,48,768]{2,1,0:T(8,128)(2,1)S(1)} %get-tuple-element.671.refs_2_), channel_id=1, source_target_pairs={{4,0},{5,1},{6,2},{7,3},{0,4},{1,5},{2,6},{3,7},{12,8},{13,9},{14,... | collective-permute-start | bytes 884744 | tf_op jit(solution)/shard_map/ppermute | solution.py:953
  41.0 15.3 %collective-permute-start.12 = (bf16[2,48,768]{2,1,0:T(8,128)(2,1)S(1)}, bf16[2,48,768]{2,1,0:T(8,128)(2,1)S(1)}, u32[]{:S(2)}, u32[]{:S(2)}) collective-permute-start(bf16[2,48,768]{2,1,0:T(8,128)(2,1)S(1)} %pack.7.refs_0_), channel_id=1, source_target_pairs={{16,0},{17,1},{18,2},{19,3},{20,4},{21,5},{22,6},{23,7},{24,8},{25... | collective-permute-start | bytes 442376 | tf_op jit(solution)/shard_map/ppermute | solution.py:953
  57.5 23.9 %collective-permute-start.14 = (bf16[12,48,768]{2,1,0:T(8,128)(2,1)S(1)}, bf16[12,48,768]{2,1,0:T(8,128)(2,1)S(1)}, u32[]{:S(2)}, u32[]{:S(2)}) collective-permute-start(bf16[12,48,768]{2,1,0:T(8,128)(2,1)S(1)} %get-tuple-element.689.refs_2_), channel_id=1, source_target_pairs={{4,0},{5,1},{6,2},{7,3},{0,4},{1,5},{2,6},{3,7},{12,8},{13,9},{14,... | collective-permute-start | bytes 2654216 | tf_op jit(solution)/shard_map/ppermute | solution.py:953
  58.1 23.3 %collective-permute-start.15 = (bf16[12,48,768]{2,1,0:T(8,128)(2,1)S(1)}, bf16[12,48,768]{2,1,0:T(8,128)(2,1)S(1)}, u32[]{:S(2)}, u32[]{:S(2)}) collective-permute-start(bf16[12,48,768]{2,1,0:T(8,128)(2,1)S(1)} %get-tuple-element.690.refs_3_), channel_id=1, source_target_pairs={{1,0},{0,1},{3,2},{2,3},{5,4},{4,5},{7,6},{6,7},{9,8},{8,9},{11,10... | collective-permute-start | bytes 2654216 | tf_op jit(solution)/shard_map/ppermute | solution.py:953
  60.3 21.0 %collective-permute-start.17 = (bf16[6,48,768]{2,1,0:T(8,128)(2,1)S(1)}, bf16[6,48,768]{2,1,0:T(8,128)(2,1)S(1)}, u32[]{:S(2)}, u32[]{:S(2)}) collective-permute-start(bf16[6,48,768]{2,1,0:T(8,128)(2,1)S(1)} %pack.8.refs_0_), channel_id=1, source_target_pairs={{16,0},{17,1},{18,2},{19,3},{20,4},{21,5},{22,6},{23,7},{24,8},{25... | collective-permute-start | bytes 1327112 | tf_op jit(solution)/shard_map/ppermute | solution.py:953
  60.8 20.5 %collective-permute-start.16 = (bf16[4,48,768]{2,1,0:T(8,128)(2,1)S(1)}, bf16[4,48,768]{2,1,0:T(8,128)(2,1)S(1)}, u32[]{:S(2)}, u32[]{:S(2)}) collective-permute-start(bf16[4,48,768]{2,1,0:T(8,128)(2,1)S(1)} %gather_z.7.refs_0_), channel_id=1, source_target_pairs={{8,0},{9,1},{10,2},{11,3},{12,4},{13,5},{14,6},{15,7},{0,8},{1,9},... | collective-permute-start | bytes 884744 | tf_op jit(solution)/shard_map/ppermute | solution.py:953
  62.7 18.0 %collective-permute-start.18 = (f32[3,12,768]{2,1,0:T(8,128)S(1)}, f32[3,12,768]{2,1,0:T(8,128)S(1)}, u32[]{:S(2)}, u32[]{:S(2)}) collective-permute-start(f32[3,12,768]{2,1,0:T(8,128)S(1)} %add.38), channel_id=1, source_target_pairs={{8,0},{9,1},{10,2},{11,3},{12,4},{13,5},{14,6},{15,7},{0,8},{1,9},... | collective-permute-start | bytes 331784 | tf_op jit(solution)/shard_map/ppermute | solution.py:953
  83.0 24.2 %collective-permute-start.21 = (bf16[32,48,768]{2,1,0:T(8,128)(2,1)S(1)}, bf16[32,48,768]{2,1,0:T(8,128)(2,1)S(1)}, u32[]{:S(2)}, u32[]{:S(2)}) collective-permute-start(bf16[32,48,768]{2,1,0:T(8,128)(2,1)S(1)} %get-tuple-element.740.refs_7_.refs_12_.refs_4_), channel_id=1, source_target_pairs={{2,0},{3,1},{0,2},{1,3},{6,4},{7,5},{4,6},{5,7},{10,8},{11,9},{8,1... | collective-permute-start | bytes 7077896 | tf_op jit(solution)/shard_map/ppermute | solution.py:953
  83.6 22.1 %collective-permute-start.22 = (bf16[12,48,768]{2,1,0:T(8,128)(2,1)S(1)}, bf16[12,48,768]{2,1,0:T(8,128)(2,1)S(1)}, u32[]{:S(2)}, u32[]{:S(2)}) collective-permute-start(bf16[12,48,768]{2,1,0:T(8,128)(2,1)S(1)} %gather_z.8.refs_0_), channel_id=1, source_target_pairs={{8,0},{9,1},{10,2},{11,3},{12,4},{13,5},{14,6},{15,7},{0,8},{1,9},... | collective-permute-start | bytes 2654216 | tf_op jit(solution)/shard_map/ppermute | solution.py:953
  83.7 22.1 %collective-permute-start.19 = (bf16[12,48,768]{2,1,0:T(8,128)(2,1)S(1)}, bf16[12,48,768]{2,1,0:T(8,128)(2,1)S(1)}, u32[]{:S(2)}, u32[]{:S(2)}) collective-permute-start(bf16[12,48,768]{2,1,0:T(8,128)(2,1)S(1)} %get-tuple-element.707.refs_2_), channel_id=1, source_target_pairs={{4,0},{5,1},{6,2},{7,3},{0,4},{1,5},{2,6},{3,7},{12,8},{13,9},{14,... | collective-permute-start | bytes 2654216 | tf_op jit(solution)/shard_map/ppermute | solution.py:953
  85.4 21.8 %collective-permute-start.20 = (bf16[12,48,768]{2,1,0:T(8,128)(2,1)S(1)}, bf16[12,48,768]{2,1,0:T(8,128)(2,1)S(1)}, u32[]{:S(2)}, u32[]{:S(2)}) collective-permute-start(bf16[12,48,768]{2,1,0:T(8,128)(2,1)S(1)} %get-tuple-element.708.refs_3_), channel_id=1, source_target_pairs={{1,0},{0,1},{3,2},{2,3},{5,4},{4,5},{7,6},{6,7},{9,8},{8,9},{11,10... | collective-permute-start | bytes 2654216 | tf_op jit(solution)/shard_map/ppermute | solution.py:953
  113.2 27.5 %collective-permute-start.25 = (bf16[32,48,768]{2,1,0:T(8,128)(2,1)}, bf16[32,48,768]{2,1,0:T(8,128)(2,1)}, u32[]{:S(2)}, u32[]{:S(2)}) collective-permute-start(bf16[32,48,768]{2,1,0:T(8,128)(2,1)} %get-tuple-element.783.refs_4_.refs_8_), channel_id=1, source_target_pairs={{2,0},{3,1},{0,2},{1,3},{6,4},{7,5},{4,6},{5,7},{10,8},{11,9},{8,1... | collective-permute-start | bytes 7077896 | tf_op jit(solution)/shard_map/ppermute | solution.py:953
  113.2 27.4 %collective-permute-start.23 = (bf16[12,48,768]{2,1,0:T(8,128)(2,1)}, bf16[12,48,768]{2,1,0:T(8,128)(2,1)}, u32[]{:S(2)}, u32[]{:S(2)}) collective-permute-start(bf16[12,48,768]{2,1,0:T(8,128)(2,1)} %get-tuple-element.726.refs_2_), channel_id=1, source_target_pairs={{4,0},{5,1},{6,2},{7,3},{0,4},{1,5},{2,6},{3,7},{12,8},{13,9},{14,... | collective-permute-start | bytes 2654216 | tf_op jit(solution)/shard_map/ppermute | solution.py:953
  113.6 27.1 %collective-permute-start.24 = (bf16[12,48,768]{2,1,0:T(8,128)(2,1)}, bf16[12,48,768]{2,1,0:T(8,128)(2,1)}, u32[]{:S(2)}, u32[]{:S(2)}) collective-permute-start(bf16[12,48,768]{2,1,0:T(8,128)(2,1)} %get-tuple-element.727.refs_3_), channel_id=1, source_target_pairs={{1,0},{0,1},{3,2},{2,3},{5,4},{4,5},{7,6},{6,7},{9,8},{8,9},{11,10... | collective-permute-start | bytes 2654216 | tf_op jit(solution)/shard_map/ppermute | solution.py:953
  115.7 24.9 %collective-permute-start.26 = (bf16[6,48,768]{2,1,0:T(8,128)(2,1)}, bf16[6,48,768]{2,1,0:T(8,128)(2,1)}, u32[]{:S(2)}, u32[]{:S(2)}) collective-permute-start(bf16[6,48,768]{2,1,0:T(8,128)(2,1)} %pack.9.refs_0_), channel_id=1, source_target_pairs={{16,0},{17,1},{18,2},{19,3},{20,4},{21,5},{22,6},{23,7},{24,8},{25... | collective-permute-start | bytes 1327112 | tf_op jit(solution)/shard_map/ppermute | solution.py:953
  144.6 24.7 %collective-permute-start.29 = (bf16[32,48,768]{2,1,0:T(8,128)(2,1)S(1)}, bf16[32,48,768]{2,1,0:T(8,128)(2,1)S(1)}, u32[]{:S(2)}, u32[]{:S(2)}) collective-permute-start(bf16[32,48,768]{2,1,0:T(8,128)(2,1)S(1)} %get-tuple-element.785.refs_6_.refs_10_), channel_id=1, source_target_pairs={{2,0},{3,1},{0,2},{1,3},{6,4},{7,5},{4,6},{5,7},{10,8},{11,9},{8,1... | collective-permute-start | bytes 7077896 | tf_op jit(solution)/shard_map/ppermute | solution.py:953
  146.5 21.5 %collective-permute-start.30 = (bf16[12,48,768]{2,1,0:T(8,128)(2,1)S(1)}, bf16[12,48,768]{2,1,0:T(8,128)(2,1)S(1)}, u32[]{:S(2)}, u32[]{:S(2)}) collective-permute-start(bf16[12,48,768]{2,1,0:T(8,128)(2,1)S(1)} %gather_z.9.refs_0_), channel_id=1, source_target_pairs={{8,0},{9,1},{10,2},{11,3},{12,4},{13,5},{14,6},{15,7},{0,8},{1,9},... | collective-permute-start | bytes 2654216 | tf_op jit(solution)/shard_map/ppermute | solution.py:953
  147.0 21.1 %collective-permute-start.27 = (bf16[12,48,768]{2,1,0:T(8,128)(2,1)S(1)}, bf16[12,48,768]{2,1,0:T(8,128)(2,1)S(1)}, u32[]{:S(2)}, u32[]{:S(2)}) collective-permute-start(bf16[12,48,768]{2,1,0:T(8,128)(2,1)S(1)} %get-tuple-element.756.refs_2_), channel_id=1, source_target_pairs={{4,0},{5,1},{6,2},{7,3},{0,4},{1,5},{2,6},{3,7},{12,8},{13,9},{14,... | collective-permute-start | bytes 2654216 | tf_op jit(solution)/shard_map/ppermute | solution.py:953
  148.5 20.8 %collective-permute-start.28 = (bf16[12,48,768]{2,1,0:T(8,128)(2,1)S(1)}, bf16[12,48,768]{2,1,0:T(8,128)(2,1)S(1)}, u32[]{:S(2)}, u32[]{:S(2)}) collective-permute-start(bf16[12,48,768]{2,1,0:T(8,128)(2,1)S(1)} %get-tuple-element.757.refs_3_), channel_id=1, source_target_pairs={{1,0},{0,1},{3,2},{2,3},{5,4},{4,5},{7,6},{6,7},{9,8},{8,9},{11,10... | collective-permute-start | bytes 2654216 | tf_op jit(solution)/shard_map/ppermute | solution.py:953
  171.0 22.4 %collective-permute-start.33 = (bf16[32,48,768]{2,1,0:T(8,128)(2,1)S(1)}, bf16[32,48,768]{2,1,0:T(8,128)(2,1)S(1)}, u32[]{:S(2)}, u32[]{:S(2)}) collective-permute-start(bf16[32,48,768]{2,1,0:T(8,128)(2,1)S(1)} %get-tuple-element.808.refs_7_.refs_12_.refs_4_), channel_id=1, source_target_pairs={{2,0},{3,1},{0,2},{1,3},{6,4},{7,5},{4,6},{5,7},{10,8},{11,9},{8,1... | collective-permute-start | bytes 7077896 | tf_op jit(solution)/shard_map/ppermute | solution.py:953
  171.0 22.2 %collective-permute-start.31 = (bf16[12,48,768]{2,1,0:T(8,128)(2,1)S(1)}, bf16[12,48,768]{2,1,0:T(8,128)(2,1)S(1)}, u32[]{:S(2)}, u32[]{:S(2)}) collective-permute-start(bf16[12,48,768]{2,1,0:T(8,128)(2,1)S(1)} %get-tuple-element.776.refs_2_), channel_id=1, source_target_pairs={{4,0},{5,1},{6,2},{7,3},{0,4},{1,5},{2,6},{3,7},{12,8},{13,9},{14,... | collective-permute-start | bytes 2654216 | tf_op jit(solution)/shard_map/ppermute | solution.py:953
  171.6 21.7 %collective-permute-start.32 = (bf16[12,48,768]{2,1,0:T(8,128)(2,1)S(1)}, bf16[12,48,768]{2,1,0:T(8,128)(2,1)S(1)}, u32[]{:S(2)}, u32[]{:S(2)}) collective-permute-start(bf16[12,48,768]{2,1,0:T(8,128)(2,1)S(1)} %get-tuple-element.777.refs_3_), channel_id=1, source_target_pairs={{1,0},{0,1},{3,2},{2,3},{5,4},{4,5},{7,6},{6,7},{9,8},{8,9},{11,10... | collective-permute-start | bytes 2654216 | tf_op jit(solution)/shard_map/ppermute | solution.py:953
  195.0 23.4 %collective-permute-start.37 = (bf16[32,48,768]{2,1,0:T(8,128)(2,1)S(1)}, bf16[32,48,768]{2,1,0:T(8,128)(2,1)S(1)}, u32[]{:S(2)}, u32[]{:S(2)}) collective-permute-start(bf16[32,48,768]{2,1,0:T(8,128)(2,1)S(1)} %get-tuple-element.847.refs_4_.refs_8_), channel_id=1, source_target_pairs={{2,0},{3,1},{0,2},{1,3},{6,4},{7,5},{4,6},{5,7},{10,8},{11,9},{8,1... | collective-permute-start | bytes 7077896 | tf_op jit(solution)/shard_map/ppermute | solution.py:953
  195.1 22.2 %collective-permute-start.35 = (bf16[12,48,768]{2,1,0:T(8,128)(2,1)S(1)}, bf16[12,48,768]{2,1,0:T(8,128)(2,1)S(1)}, u32[]{:S(2)}, u32[]{:S(2)}) collective-permute-start(bf16[12,48,768]{2,1,0:T(8,128)(2,1)S(1)} %get-tuple-element.802.refs_2_), channel_id=1, source_target_pairs={{4,0},{5,1},{6,2},{7,3},{0,4},{1,5},{2,6},{3,7},{12,8},{13,9},{14,... | collective-permute-start | bytes 2654216 | tf_op jit(solution)/shard_map/ppermute | solution.py:953
  196.8 21.6 %collective-permute-start.36 = (bf16[12,48,768]{2,1,0:T(8,128)(2,1)S(1)}, bf16[12,48,768]{2,1,0:T(8,128)(2,1)S(1)}, u32[]{:S(2)}, u32[]{:S(2)}) collective-permute-start(bf16[12,48,768]{2,1,0:T(8,128)(2,1)S(1)} %get-tuple-element.803.refs_3_), channel_id=1, source_target_pairs={{1,0},{0,1},{3,2},{2,3},{5,4},{4,5},{7,6},{6,7},{9,8},{8,9},{11,10... | collective-permute-start | bytes 2654216 | tf_op jit(solution)/shard_map/ppermute | solution.py:953
  220.1 22.4 %collective-permute-start.40 = (bf16[32,48,768]{2,1,0:T(8,128)(2,1)S(1)}, bf16[32,48,768]{2,1,0:T(8,128)(2,1)S(1)}, u32[]{:S(2)}, u32[]{:S(2)}) collective-permute-start(bf16[32,48,768]{2,1,0:T(8,128)(2,1)S(1)} %get-tuple-element.849.refs_6_.refs_10_), channel_id=1, source_target_pairs={{2,0},{3,1},{0,2},{1,3},{6,4},{7,5},{4,6},{5,7},{10,8},{11,9},{8,1... | collective-permute-start | bytes 7077896 | tf_op jit(solution)/shard_map/ppermute | solution.py:953
  220.2 22.1 %collective-permute-start.38 = (bf16[12,48,768]{2,1,0:T(8,128)(2,1)S(1)}, bf16[12,48,768]{2,1,0:T(8,128)(2,1)S(1)}, u32[]{:S(2)}, u32[]{:S(2)}) collective-permute-start(bf16[12,48,768]{2,1,0:T(8,128)(2,1)S(1)} %get-tuple-element.824.refs_2_), channel_id=1, source_target_pairs={{4,0},{5,1},{6,2},{7,3},{0,4},{1,5},{2,6},{3,7},{12,8},{13,9},{14,... | collective-permute-start | bytes 2654216 | tf_op jit(solution)/shard_map/ppermute | solution.py:953
  220.7 21.7 %collective-permute-start.39 = (bf16[12,48,768]{2,1,0:T(8,128)(2,1)S(1)}, bf16[12,48,768]{2,1,0:T(8,128)(2,1)S(1)}, u32[]{:S(2)}, u32[]{:S(2)}) collective-permute-start(bf16[12,48,768]{2,1,0:T(8,128)(2,1)S(1)} %get-tuple-element.825.refs_3_), channel_id=1, source_target_pairs={{1,0},{0,1},{3,2},{2,3},{5,4},{4,5},{7,6},{6,7},{9,8},{8,9},{11,10... | collective-permute-start | bytes 2654216 | tf_op jit(solution)/shard_map/ppermute | solution.py:953
  244.1 23.4 %collective-permute-start.43 = (bf16[32,48,768]{2,1,0:T(8,128)(2,1)S(1)}, bf16[32,48,768]{2,1,0:T(8,128)(2,1)S(1)}, u32[]{:S(2)}, u32[]{:S(2)}) collective-permute-start(bf16[32,48,768]{2,1,0:T(8,128)(2,1)S(1)} %get-tuple-element.870.refs_7_.refs_12_.refs_4_), channel_id=1, source_target_pairs={{2,0},{3,1},{0,2},{1,3},{6,4},{7,5},{4,6},{5,7},{10,8},{11,9},{8,1... | collective-permute-start | bytes 7077896 | tf_op jit(solution)/shard_map/ppermute | solution.py:953
  244.2 23.0 %collective-permute-start.41 = (bf16[12,48,768]{2,1,0:T(8,128)(2,1)S(1)}, bf16[12,48,768]{2,1,0:T(8,128)(2,1)S(1)}, u32[]{:S(2)}, u32[]{:S(2)}) collective-permute-start(bf16[12,48,768]{2,1,0:T(8,128)(2,1)S(1)} %get-tuple-element.842.refs_0_), channel_id=1, source_target_pairs={{4,0},{5,1},{6,2},{7,3},{0,4},{1,5},{2,6},{3,7},{12,8},{13,9},{14,... | collective-permute-start | bytes 2654216 | tf_op jit(solution)/shard_map/ppermute | solution.py:953
  245.8 21.7 %collective-permute-start.42 = (bf16[12,48,768]{2,1,0:T(8,128)(2,1)S(1)}, bf16[12,48,768]{2,1,0:T(8,128)(2,1)S(1)}, u32[]{:S(2)}, u32[]{:S(2)}) collective-permute-start(bf16[12,48,768]{2,1,0:T(8,128)(2,1)S(1)} %get-tuple-element.843.refs_1_), channel_id=1, source_target_pairs={{1,0},{0,1},{3,2},{2,3},{5,4},{4,5},{7,6},{6,7},{9,8},{8,9},{11,10... | collective-permute-start | bytes 2654216 | tf_op jit(solution)/shard_map/ppermute | solution.py:953
  268.5 24.8 %collective-permute-start.48 = (bf16[32,48,768]{2,1,0:T(8,128)(2,1)S(1)}, bf16[32,48,768]{2,1,0:T(8,128)(2,1)S(1)}, u32[]{:S(2)}, u32[]{:S(2)}) collective-permute-start(bf16[32,48,768]{2,1,0:T(8,128)(2,1)S(1)} %get-tuple-element.902.refs_4_.refs_8_), channel_id=1, source_target_pairs={{2,0},{3,1},{0,2},{1,3},{6,4},{7,5},{4,6},{5,7},{10,8},{11,9},{8,1... | collective-permute-start | bytes 7077896 | tf_op jit(solution)/shard_map/ppermute | solution.py:953
  276.1 17.1 %collective-permute-start.46 = (bf16[8,48,768]{2,1,0:T(8,128)(2,1)S(1)}, bf16[8,48,768]{2,1,0:T(8,128)(2,1)S(1)}, u32[]{:S(2)}, u32[]{:S(2)}) collective-permute-start(bf16[8,48,768]{2,1,0:T(8,128)(2,1)S(1)} %get-tuple-element.864.refs_0_), channel_id=1, source_target_pairs={{4,0},{5,1},{6,2},{7,3},{0,4},{1,5},{2,6},{3,7},{12,8},{13,9},{14,... | collective-permute-start | bytes 1769480 | tf_op jit(solution)/shard_map/ppermute | solution.py:953
  276.5 16.8 %collective-permute-start.47 = (bf16[8,48,768]{2,1,0:T(8,128)(2,1)S(1)}, bf16[8,48,768]{2,1,0:T(8,128)(2,1)S(1)}, u32[]{:S(2)}, u32[]{:S(2)}) collective-permute-start(bf16[8,48,768]{2,1,0:T(8,128)(2,1)S(1)} %get-tuple-element.865.refs_1_), channel_id=1, source_target_pairs={{1,0},{0,1},{3,2},{2,3},{5,4},{4,5},{7,6},{6,7},{9,8},{8,9},{11,10... | collective-permute-start | bytes 1769480 | tf_op jit(solution)/shard_map/ppermute | solution.py:953
  335.3 14.7 %collective-permute-start.51 = (bf16[256,4608]{1,0:T(8,128)(2,1)S(1)}, bf16[256,4608]{1,0:T(8,128)(2,1)S(1)}, u32[]{:S(2)}, u32[]{:S(2)}) collective-permute-start(bf16[256,4608]{1,0:T(8,128)(2,1)S(1)} %get-tuple-element.937.da_ref), channel_id=1, source_target_pairs={{2,0},{3,1},{0,2},{1,3},{6,4},{7,5},{4,6},{5,7},{10,8},{11,9},{8,1... | collective-permute-start | bytes 7077896 | tf_op jit(solution)/shard_map/ppermute | solution.py:953
  335.9 15.7 %collective-permute-start.52 = (bf16[256,768]{1,0:T(8,128)(2,1)S(1)}, bf16[256,768]{1,0:T(8,128)(2,1)S(1)}, u32[]{:S(2)}, u32[]{:S(2)}) collective-permute-start(bf16[256,768]{1,0:T(8,128)(2,1)S(1)} %get-tuple-element.922), channel_id=1, source_target_pairs={{0,0},{2,1},{1,2},{3,3},{4,4},{6,5},{5,6},{7,7},{8,8},{10,9},{9,10... | collective-permute-start | bytes 1179656 | tf_op jit(solution)/shard_map/ppermute | solution.py:953
  352.3 15.4 %collective-permute-start.54 = (bf16[8,48,768]{2,1,0:T(8,128)(2,1)S(1)}, bf16[8,48,768]{2,1,0:T(8,128)(2,1)S(1)}, u32[]{:S(2)}, u32[]{:S(2)}) collective-permute-start(bf16[8,48,768]{2,1,0:T(8,128)(2,1)S(1)} %get-tuple-element.928), channel_id=1, source_target_pairs={{4,0},{5,1},{6,2},{7,3},{0,4},{1,5},{2,6},{3,7},{12,8},{13,9},{14,... | collective-permute-start | bytes 1769480 | tf_op jit(solution)/shard_map/ppermute | solution.py:953
  354.0 15.0 %collective-permute-start.55 = (bf16[8,48,768]{2,1,0:T(8,128)(2,1)S(1)}, bf16[8,48,768]{2,1,0:T(8,128)(2,1)S(1)}, u32[]{:S(2)}, u32[]{:S(2)}) collective-permute-start(bf16[8,48,768]{2,1,0:T(8,128)(2,1)S(1)} %get-tuple-element.929), channel_id=1, source_target_pairs={{1,0},{0,1},{3,2},{2,3},{5,4},{4,5},{7,6},{6,7},{9,8},{8,9},{11,10... | collective-permute-start | bytes 1769480 | tf_op jit(solution)/shard_map/ppermute | solution.py:953
  369.4 22.4 %collective-permute-start.59 = (bf16[12,48,768]{2,1,0:T(8,128)(2,1)S(1)}, bf16[12,48,768]{2,1,0:T(8,128)(2,1)S(1)}, u32[]{:S(2)}, u32[]{:S(2)}) collective-permute-start(bf16[12,48,768]{2,1,0:T(8,128)(2,1)S(1)} %get-tuple-element.953), channel_id=1, source_target_pairs={{4,0},{5,1},{6,2},{7,3},{0,4},{1,5},{2,6},{3,7},{12,8},{13,9},{14,... | collective-permute-start | bytes 2654216 | tf_op jit(solution)/shard_map/ppermute | solution.py:953
  369.9 22.0 %collective-permute-start.60 = (bf16[12,48,768]{2,1,0:T(8,128)(2,1)S(1)}, bf16[12,48,768]{2,1,0:T(8,128)(2,1)S(1)}, u32[]{:S(2)}, u32[]{:S(2)}) collective-permute-start(bf16[12,48,768]{2,1,0:T(8,128)(2,1)S(1)} %get-tuple-element.954), channel_id=1, source_target_pairs={{1,0},{0,1},{3,2},{2,3},{5,4},{4,5},{7,6},{6,7},{9,8},{8,9},{11,10... | collective-permute-start | bytes 2654216 | tf_op jit(solution)/shard_map/ppermute | solution.py:953
  392.4 22.1 %collective-permute-start.61 = (bf16[12,48,768]{2,1,0:T(8,128)(2,1)S(1)}, bf16[12,48,768]{2,1,0:T(8,128)(2,1)S(1)}, u32[]{:S(2)}, u32[]{:S(2)}) collective-permute-start(bf16[12,48,768]{2,1,0:T(8,128)(2,1)S(1)} %get-tuple-element.984), channel_id=1, source_target_pairs={{4,0},{5,1},{6,2},{7,3},{0,4},{1,5},{2,6},{3,7},{12,8},{13,9},{14,... | collective-permute-start | bytes 2654216 | tf_op jit(solution)/shard_map/ppermute | solution.py:953
  394.2 21.8 %collective-permute-start.62 = (bf16[12,48,768]{2,1,0:T(8,128)(2,1)S(1)}, bf16[12,48,768]{2,1,0:T(8,128)(2,1)S(1)}, u32[]{:S(2)}, u32[]{:S(2)}) collective-permute-start(bf16[12,48,768]{2,1,0:T(8,128)(2,1)S(1)} %get-tuple-element.985), channel_id=1, source_target_pairs={{1,0},{0,1},{3,2},{2,3},{5,4},{4,5},{7,6},{6,7},{9,8},{8,9},{11,10... | collective-permute-start | bytes 2654216 | tf_op jit(solution)/shard_map/ppermute | solution.py:953
  416.5 22.1 %collective-permute-start.67 = (bf16[12,48,768]{2,1,0:T(8,128)(2,1)S(1)}, bf16[12,48,768]{2,1,0:T(8,128)(2,1)S(1)}, u32[]{:S(2)}, u32[]{:S(2)}) collective-permute-start(bf16[12,48,768]{2,1,0:T(8,128)(2,1)S(1)} %get-tuple-element.1017), channel_id=1, source_target_pairs={{4,0},{5,1},{6,2},{7,3},{0,4},{1,5},{2,6},{3,7},{12,8},{13,9},{14,... | collective-permute-start | bytes 2654216 | tf_op jit(solution)/shard_map/ppermute | solution.py:953
  416.9 21.8 %collective-permute-start.68 = (bf16[12,48,768]{2,1,0:T(8,128)(2,1)S(1)}, bf16[12,48,768]{2,1,0:T(8,128)(2,1)S(1)}, u32[]{:S(2)}, u32[]{:S(2)}) collective-permute-start(bf16[12,48,768]{2,1,0:T(8,128)(2,1)S(1)} %get-tuple-element.1018), channel_id=1, source_target_pairs={{1,0},{0,1},{3,2},{2,3},{5,4},{4,5},{7,6},{6,7},{9,8},{8,9},{11,10... | collective-permute-start | bytes 2654216 | tf_op jit(solution)/shard_map/ppermute | solution.py:953
  440.9 26.7 %collective-permute-start.74 = (bf16[14,48,768]{2,1,0:T(8,128)(2,1)S(1)}, bf16[14,48,768]{2,1,0:T(8,128)(2,1)S(1)}, u32[]{:S(2)}, u32[]{:S(2)}) collective-permute-start(bf16[14,48,768]{2,1,0:T(8,128)(2,1)S(1)} %get-tuple-element.1053), channel_id=1, source_target_pairs={{1,0},{0,1},{3,2},{2,3},{5,4},{4,5},{7,6},{6,7},{9,8},{8,9},{11,10... | collective-permute-start | bytes 3096584 | tf_op jit(solution)/shard_map/ppermute | solution.py:953
  442.5 24.2 %collective-permute-start.73 = (bf16[12,48,768]{2,1,0:T(8,128)(2,1)}, bf16[12,48,768]{2,1,0:T(8,128)(2,1)S(1)}, u32[]{:S(2)}, u32[]{:S(2)}) collective-permute-start(bf16[12,48,768]{2,1,0:T(8,128)(2,1)} %get-tuple-element.1052), channel_id=1, source_target_pairs={{4,0},{5,1},{6,2},{7,3},{0,4},{1,5},{2,6},{3,7},{12,8},{13,9},{14,... | collective-permute-start | bytes 2654216 | tf_op jit(solution)/shard_map/ppermute | solution.py:953
  444.1 21.8 %collective-permute-start.75 = (bf16[2,2,48,768]{3,2,1,0:T(8,128)(2,1)}, bf16[2,2,48,768]{3,2,1,0:T(8,128)(2,1)S(1)}, u32[]{:S(2)}, u32[]{:S(2)}) collective-permute-start(bf16[2,2,48,768]{3,2,1,0:T(8,128)(2,1)} %get-tuple-element.1057), channel_id=1, source_target_pairs={{8,0},{9,1},{10,2},{11,3},{12,4},{13,5},{14,6},{15,7},{0,8},{1,9},... | collective-permute-start | bytes 884744 | tf_op jit(solution)/shard_map/ppermute | solution.py:953
  445.8 20.2 %collective-permute-start.72 = (bf16[2,48,768]{2,1,0:T(8,128)(2,1)S(1)}, bf16[2,48,768]{2,1,0:T(8,128)(2,1)S(1)}, u32[]{:S(2)}, u32[]{:S(2)}) collective-permute-start(bf16[2,48,768]{2,1,0:T(8,128)(2,1)S(1)} %get-tuple-element.1051), channel_id=1, source_target_pairs={{16,0},{17,1},{18,2},{19,3},{20,4},{21,5},{22,6},{23,7},{24,8},{25... | collective-permute-start | bytes 442376 | tf_op jit(solution)/shard_map/ppermute | solution.py:953
  467.6 15.6 %collective-permute-start.81 = (bf16[256,4608]{1,0:T(8,128)(2,1)S(1)}, bf16[256,4608]{1,0:T(8,128)(2,1)S(1)}, u32[]{:S(2)}, u32[]{:S(2)}) collective-permute-start(bf16[256,4608]{1,0:T(8,128)(2,1)S(1)} %get-tuple-element.1140.da_ref), channel_id=1, source_target_pairs={{2,0},{3,1},{0,2},{1,3},{6,4},{7,5},{4,6},{5,7},{10,8},{11,9},{8,1... | collective-permute-start | bytes 7077896 | tf_op jit(solution)/shard_map/ppermute | solution.py:953
  470.5 25.1 %collective-permute-start.78 = (bf16[14,48,768]{2,1,0:T(8,128)(2,1)S(1)}, bf16[14,48,768]{2,1,0:T(8,128)(2,1)S(1)}, u32[]{:S(2)}, u32[]{:S(2)}) collective-permute-start(bf16[14,48,768]{2,1,0:T(8,128)(2,1)S(1)} %get-tuple-element.1093), channel_id=1, source_target_pairs={{1,0},{0,1},{3,2},{2,3},{5,4},{4,5},{7,6},{6,7},{9,8},{8,9},{11,10... | collective-permute-start | bytes 3096584 | tf_op jit(solution)/shard_map/ppermute | solution.py:953
  471.1 22.0 %collective-permute-start.77 = (bf16[12,48,768]{2,1,0:T(8,128)(2,1)S(1)}, bf16[12,48,768]{2,1,0:T(8,128)(2,1)S(1)}, u32[]{:S(2)}, u32[]{:S(2)}) collective-permute-start(bf16[12,48,768]{2,1,0:T(8,128)(2,1)S(1)} %get-tuple-element.1092), channel_id=1, source_target_pairs={{4,0},{5,1},{6,2},{7,3},{0,4},{1,5},{2,6},{3,7},{12,8},{13,9},{14,... | collective-permute-start | bytes 2654216 | tf_op jit(solution)/shard_map/ppermute | solution.py:953
  497.3 24.9 %collective-permute-start.84 = (bf16[14,48,768]{2,1,0:T(8,128)(2,1)S(1)}, bf16[14,48,768]{2,1,0:T(8,128)(2,1)S(1)}, u32[]{:S(2)}, u32[]{:S(2)}) collective-permute-start(bf16[14,48,768]{2,1,0:T(8,128)(2,1)S(1)} %get-tuple-element.1129), channel_id=1, source_target_pairs={{1,0},{0,1},{3,2},{2,3},{5,4},{4,5},{7,6},{6,7},{9,8},{8,9},{11,10... | collective-permute-start | bytes 3096584 | tf_op jit(solution)/shard_map/ppermute | solution.py:953
  497.8 21.5 %collective-permute-start.83 = (bf16[12,48,768]{2,1,0:T(8,128)(2,1)S(1)}, bf16[12,48,768]{2,1,0:T(8,128)(2,1)S(1)}, u32[]{:S(2)}, u32[]{:S(2)}) collective-permute-start(bf16[12,48,768]{2,1,0:T(8,128)(2,1)S(1)} %get-tuple-element.1128), channel_id=1, source_target_pairs={{4,0},{5,1},{6,2},{7,3},{0,4},{1,5},{2,6},{3,7},{12,8},{13,9},{14,... | collective-permute-start | bytes 2654216 | tf_op jit(solution)/shard_map/ppermute | solution.py:953
  523.3 24.1 %collective-permute-start.90 = (bf16[14,48,768]{2,1,0:T(8,128)(2,1)S(1)}, bf16[14,48,768]{2,1,0:T(8,128)(2,1)S(1)}, u32[]{:S(2)}, u32[]{:S(2)}) collective-permute-start(bf16[14,48,768]{2,1,0:T(8,128)(2,1)S(1)} %get-tuple-element.1165), channel_id=1, source_target_pairs={{1,0},{0,1},{3,2},{2,3},{5,4},{4,5},{7,6},{6,7},{9,8},{8,9},{11,10... | collective-permute-start | bytes 3096584 | tf_op jit(solution)/shard_map/ppermute | solution.py:953
  523.7 20.7 %collective-permute-start.89 = (bf16[12,48,768]{2,1,0:T(8,128)(2,1)S(1)}, bf16[12,48,768]{2,1,0:T(8,128)(2,1)S(1)}, u32[]{:S(2)}, u32[]{:S(2)}) collective-permute-start(bf16[12,48,768]{2,1,0:T(8,128)(2,1)S(1)} %get-tuple-element.1164), channel_id=1, source_target_pairs={{4,0},{5,1},{6,2},{7,3},{0,4},{1,5},{2,6},{3,7},{12,8},{13,9},{14,... | collective-permute-start | bytes 2654216 | tf_op jit(solution)/shard_map/ppermute | solution.py:953
  548.0 23.3 %collective-permute-start.95 = (bf16[14,48,768]{2,1,0:T(8,128)(2,1)S(1)}, bf16[14,48,768]{2,1,0:T(8,128)(2,1)S(1)}, u32[]{:S(2)}, u32[]{:S(2)}) collective-permute-start(bf16[14,48,768]{2,1,0:T(8,128)(2,1)S(1)} %get-tuple-element.1207), channel_id=1, source_target_pairs={{1,0},{0,1},{3,2},{2,3},{5,4},{4,5},{7,6},{6,7},{9,8},{8,9},{11,10... | collective-permute-start | bytes 3096584 | tf_op jit(solution)/shard_map/ppermute | solution.py:953
  548.5 19.7 %collective-permute-start.94 = (bf16[12,48,768]{2,1,0:T(8,128)(2,1)S(1)}, bf16[12,48,768]{2,1,0:T(8,128)(2,1)S(1)}, u32[]{:S(2)}, u32[]{:S(2)}) collective-permute-start(bf16[12,48,768]{2,1,0:T(8,128)(2,1)S(1)} %get-tuple-element.1206), channel_id=1, source_target_pairs={{4,0},{5,1},{6,2},{7,3},{0,4},{1,5},{2,6},{3,7},{12,8},{13,9},{14,... | collective-permute-start | bytes 2654216 | tf_op jit(solution)/shard_map/ppermute | solution.py:953
  571.7 21.7 %collective-permute-start.100 = (bf16[6,48,768]{2,1,0:T(8,128)(2,1)S(1)}, bf16[6,48,768]{2,1,0:T(8,128)(2,1)S(1)}, u32[]{:S(2)}, u32[]{:S(2)}) collective-permute-start(bf16[6,48,768]{2,1,0:T(8,128)(2,1)S(1)} %get-tuple-element.1230), channel_id=1, source_target_pairs={{1,0},{0,1},{3,2},{2,3},{5,4},{4,5},{7,6},{6,7},{9,8},{8,9},{11,10... | collective-permute-start | bytes 1327112 | tf_op jit(solution)/shard_map/ppermute | solution.py:953
  572.3 21.1 %collective-permute-start.102 = (bf16[256,768]{1,0:T(8,128)(2,1)S(1)}, bf16[256,768]{1,0:T(8,128)(2,1)S(1)}, u32[]{:S(2)}, u32[]{:S(2)}) collective-permute-start(bf16[256,768]{1,0:T(8,128)(2,1)S(1)} %convert_element_type.13), channel_id=1, source_target_pairs={{0,0},{2,1},{1,2},{3,3},{4,4},{6,5},{5,6},{7,7},{8,8},{10,9},{9,10... | collective-permute-start | bytes 1179656 | tf_op jit(solution)/shard_map/ppermute | solution.py:953
  573.0 20.4 %collective-permute-start.101 = (bf16[2,2,48,768]{3,2,1,0:T(8,128)(2,1)S(1)}, bf16[2,2,48,768]{3,2,1,0:T(8,128)(2,1)S(1)}, u32[]{:S(2)}, u32[]{:S(2)}) collective-permute-start(bf16[2,2,48,768]{3,2,1,0:T(8,128)(2,1)S(1)} %get-tuple-element.1234), channel_id=1, source_target_pairs={{8,0},{9,1},{10,2},{11,3},{12,4},{13,5},{14,6},{15,7},{0,8},{1,9},... | collective-permute-start | bytes 884744 | tf_op jit(solution)/shard_map/ppermute | solution.py:953
  574.7 18.7 %collective-permute-start.99 = (bf16[4,48,768]{2,1,0:T(8,128)(2,1)S(1)}, bf16[4,48,768]{2,1,0:T(8,128)(2,1)S(1)}, u32[]{:S(2)}, u32[]{:S(2)}) collective-permute-start(bf16[4,48,768]{2,1,0:T(8,128)(2,1)S(1)} %get-tuple-element.1229), channel_id=1, source_target_pairs={{4,0},{5,1},{6,2},{7,3},{0,4},{1,5},{2,6},{3,7},{12,8},{13,9},{14,... | collective-permute-start | bytes 884744 | tf_op jit(solution)/shard_map/ppermute | solution.py:953
  (212 other events, 1725.7 us)

commit v3 on v2

--- a/solution.py
+++ b/solution.py
@@ -80,44 +80,51 @@
 )
 
 
-def each_piece(bufs):
+def each_unit(pos_ref, bufs):
     for dc in range(2):
         for unit, (part, dy, dx) in enumerate(UNITS):
-            for k in range(ZS):
-                yield bufs[dc].at[unit * ZS + k], part, dy, dx, dc, k
+            at = flip(pos_ref[1], dx) * 2 + flip(pos_ref[2], dc)
+            yield bufs[dc].at[pl.ds(unit * ZS, ZS)], part, dy, at
 
 
 def fetch_member(pos_ref, bufs, member, full_ref, sem):
-    _, rows, width = bufs[0].shape
-    half = width // 2
-    for piece, part, dy, dx, dc, k in each_piece(bufs):
-        if part != member // 2:
-            continue
-        row = pl.multiple_of(block_at(pos_ref, k, dx, dc) * rows, 16)
-        col = pl.multiple_of(half_at(pos_ref, dy) * half, 128)
-        pltpu.make_async_copy(
-            piece.at[:, pl.ds(member % 2 * half, half)],
-            full_ref.at[pl.ds(row, rows), pl.ds(col, half)],
-            sem,
-        ).start()
+    half = full_ref.shape[3] // 2
+    for unit, part, dy, at in each_unit(pos_ref, bufs):
+        if part == member // 2:
+            col = pl.multiple_of(half_at(pos_ref, dy) * half, 128)
+            load(
+                unit.at[:, :, pl.ds(member % 2 * half, half)],
+                full_ref.at[:, at, :, pl.ds(col, half)],
+                sem,
+            )
 
 
 def fetch_columns(pos_ref, bufs, full_ref, sem):
-    _, rows, width = bufs[0].shape
-    for piece, part, dy, dx, dc, k in each_piece(bufs):
-        row = pl.multiple_of(block_at(pos_ref, k, dx, dc) * rows, 16)
+    width = full_ref.shape[3] // 4
+    for unit, part, dy, at in each_unit(pos_ref, bufs):
         col = pl.multiple_of((half_at(pos_ref, dy) * 2 + part) * width, 128)
-        pltpu.make_async_copy(
-            piece, full_ref.at[pl.ds(row, rows), pl.ds(col, width)], sem
-        ).start()
+        load(unit, full_ref.at[:, at, :, pl.ds(col, width)], sem)
 
 
 def fetch_rows(pos_ref, bufs, full_ref, sem):
-    _, rows, width = bufs[0].shape
-    for piece, part, dy, dx, dc, k in each_piece(bufs):
-        block = block_at(pos_ref, k, dx, dc) * 2 + half_at(pos_ref, dy)
-        row = pl.multiple_of((block * 2 + part) * rows, 16)
-        pltpu.make_async_copy(piece, full_ref.at[pl.ds(row, rows), :], sem).start()
+    for unit, part, dy, at in each_unit(pos_ref, bufs):
+        load(unit, full_ref.at[:, at, half_at(pos_ref, dy) * 2 + part], sem)
+
+
+def flat(values):
+    return values.reshape(-1, values.shape[-1])
+
+
+def square(width):
+    return pltpu.VMEM((ZS, BLOCKS // ZS, width // BLOCKS, width), BF16)
+
+
+def wide_matrix(width, hidden):
+    return pltpu.VMEM((ZS, BLOCKS // ZS, width // BLOCKS, hidden), BF16)
+
+
+def tall_matrix(hidden, width):
+    return pltpu.VMEM((ZS, BLOCKS // ZS, 4, hidden // BLOCKS // 4, width), BF16)
 
 
 def wait_full(full_ref, sem):
@@ -192,16 +199,16 @@
     wide_ref[...] = low.T
     export_rows(pos_g, wide_ref, exports, 0)
     wait_full(wq, sems.at[0])
-    query = (nn(low, wq[...]) + row_of(vec_ref, QB)).astype(BF16)
+    query = (nn(low, flat(wq[...])) + row_of(vec_ref, QB)).astype(BF16)
     q_ref[...] = (query.astype(F32) * HD ** (-0.5)).astype(BF16)
     wait_full(wk, sems.at[1])
-    key = nn(rows_ref[...], wk[...]).astype(BF16)
+    key = nn(rows_ref[...], flat(wk[...])).astype(BF16)
     k_ref[...] = key
     kt_ref[...] = key.T
     store(2)
     store(3)
     wait_full(wv, sems.at[2])
-    value = (nn(rows_ref[...], wv[...]) + row_of(vec_ref, VB)).astype(BF16)
+    value = (nn(rows_ref[...], flat(wv[...])) + row_of(vec_ref, VB)).astype(BF16)
     v_ref[...] = value
     vt_ref[...] = value.T
     store(4)
@@ -227,7 +234,7 @@
     export_rows(pos_g, wide_ref, exports, 1)
     mixed = wide_ref[...].T
     wait_full(wo, sems.at[3])
-    branch = nn(mixed, wo[...]) + row_of(vec_ref, OB)
+    branch = nn(mixed, flat(wo[...])) + row_of(vec_ref, OB)
     normed, inverse = normalize(x_ref[...] + branch)
     hidden = normed * row_of(vec_ref, AG) + row_of(vec_ref, AS)
     h_ref[...] = hidden
@@ -260,7 +267,7 @@
         out_shape=(shape((tokens, width), F32),) + kept,
         in_specs=[SMEM, SMEM] + [VMEM] * 5 + [ANY] * 2,
         out_specs=[VMEM] + [HBM] * 8,
-        scratch_shapes=[pltpu.VMEM((width, width), BF16)] * 4
+        scratch_shapes=[square(width)] * 4
         + [
             pltpu.VMEM((2 * tokens, width), BF16),
             pltpu.VMEM((width, 2 * tokens), BF16),
@@ -276,141 +283,175 @@
     )(pos_w, pos_g, x, xp, seg, lab, vec, *bufs)
 
 
-def ffn_kernel(tile, *refs):
+def head_back(grad, normed, inverse, gain, low_ref, back_ref, sums_ref):
+    sums_ref[...] = jnp.zeros_like(sums_ref)
+    sums_ref[pl.ds(0, 1), :] = colsum(grad * normed)
+    sums_ref[pl.ds(1, 1), :] = colsum(grad)
+    back = norm_back(normed, inverse, grad * gain)
+    low = back.astype(BF16)
+    low_ref[...] = low
+    back_ref[...] = back
+    sums_ref[pl.ds(2, 1), :] = colsum(low.astype(F32))
+
+
+def head_shapes(tokens, width):
+    return (
+        shape((tokens, width), BF16),
+        shape((tokens, width), F32),
+        shape((8, width), F32),
+    )
+
+
+def inner_kernel(tile, *refs):
     pos_w, pos_g, h_ref, vec_ref = refs[:4]
-    inner_bufs, outer_bufs = refs[4:6], refs[6:8]
-    x_ref, xb_ref = refs[8:10]
-    kept = refs[10:15]
-    wi, wu, low_ref, acc_ref, wide_ref = refs[15:20]
-    held = refs[20:25]
-    n2_ref, c2_ref, gp_ref = held[:3]
-    exports = held[3:]
-    sems, store_sems = refs[25:]
-
-    def store(index):
-        load(held[index], kept[index], store_sems.at[index])
-
-    width, hidden = wi.shape
-    fetch_columns(pos_w, inner_bufs, wi, sems.at[0])
-    fetch_rows(pos_w, outer_bufs, wu, sems.at[1])
+    bufs, active_ref, kept = refs[4:6], refs[6], refs[7:10]
+    wi, low_ref, wide_ref = refs[10:13]
+    held = refs[13:16]
+    gp_ref, exports = held[0], held[1:]
+    sem, store_sems = refs[16:]
+    width, hidden = h_ref.shape[1], wi.shape[3]
+    fetch_columns(pos_w, bufs, wi, sem)
     low_ref[...] = h_ref[...].astype(BF16)
-    acc_ref[...] = jnp.zeros_like(acc_ref)
-    wait_full(wi, sems.at[0])
-    wait_full(wu, sems.at[1])
+    wait_full(wi, sem)
     per_row = width // tile
 
     def step(index, carry):
-        lane = pl.multiple_of(index * tile, tile)
+        lanes = pl.ds(pl.multiple_of(index * tile, tile), tile)
         bias = vec_ref[pl.ds(IB + lax.div(index, per_row), 1), :]
         part = lax.rem(index, per_row)
         chosen = bias[:, :tile]
         for other in range(1, per_row):
             chosen = jnp.where(part == other, bias[:, other * tile : (other + 1) * tile], chosen)
-        pre = nn(low_ref[...], wi[:, pl.ds(lane, tile)]) + chosen
+        pre = nn(low_ref[...], flat(wi[:, :, :, lanes])) + chosen
         phi = 0.5 * (1.0 + lax.erf(pre * 0.7071067811865476))
         dens = jnp.exp(-0.5 * pre * pre) * 0.3989422804014327
-        gp_ref[:, pl.ds(lane, tile)] = (phi + pre * dens).astype(BF16)
+        gp_ref[:, lanes] = (phi + pre * dens).astype(BF16)
         active = (pre * phi).astype(BF16)
-        acc_ref[...] += nn(active, wu[pl.ds(lane, tile), :])
-        wide_ref[pl.ds(lane, tile), :] = active.T
+        active_ref[:, lanes] = active
+        wide_ref[lanes, :] = active.T
         return carry
 
     lax.fori_loop(0, hidden // tile, step, 0)
-    store(2)
+    load(held[0], kept[0], store_sems.at[0])
     export_halves(pos_g, wide_ref, exports)
-    store(3)
-    store(4)
-    normed, inverse = normalize(h_ref[...] + (acc_ref[...] + row_of(vec_ref, UB)))
-    result = normed * row_of(vec_ref, FG) + row_of(vec_ref, FS)
-    x_ref[...] = result
-    xb_ref[...] = result.astype(BF16)
-    n2_ref[...] = normed
-    c2_ref[...] = jnp.broadcast_to(inverse, c2_ref.shape)
-    store(0)
-    store(1)
-    for index in range(5):
+    for index in (1, 2):
+        load(held[index], kept[index], store_sems.at[index])
+    for index in range(3):
         wait_full(held[index], store_sems.at[index])
 
 
-def ffn_forward(pos_w, pos_g, h, vec, inner_bufs, outer_bufs):
+def inner_forward(pos_w, pos_g, h, vec, bufs):
     tokens, width = h.shape
-    hidden = outer_bufs[0].shape[1] * 4 * BLOCKS
+    hidden = bufs[0].shape[2] * 4
     export = shape((2, 2, 2, ZS, hidden // BLOCKS // 4, tokens), BF16)
-    kept = (
-        shape((tokens, width), F32),
-        shape((tokens, 128), F32),
-        shape((tokens, hidden), BF16),
-        export,
-        export,
-    )
+    kept = (shape((tokens, hidden), BF16), export, export)
     return pl.pallas_call(
-        functools.partial(ffn_kernel, 384),
-        out_shape=(shape((tokens, width), F32), shape((tokens, width), BF16)) + kept,
-        in_specs=[SMEM, SMEM, VMEM, VMEM] + [ANY] * 4,
-        out_specs=[VMEM] * 2 + [HBM] * 5,
+        functools.partial(inner_kernel, 384),
+        out_shape=(shape((tokens, hidden), BF16),) + kept,
+        in_specs=[SMEM, SMEM, VMEM, VMEM] + [ANY] * 2,
+        out_specs=[VMEM] + [HBM] * 3,
         scratch_shapes=[
-            pltpu.VMEM((width, hidden), BF16),
-            pltpu.VMEM((hidden, width), BF16),
+            wide_matrix(width, hidden),
             pltpu.VMEM((tokens, width), BF16),
-            pltpu.VMEM((tokens, width), F32),
             pltpu.VMEM((hidden, tokens), BF16),
         ]
         + [pltpu.VMEM(each.shape, each.dtype) for each in kept]
-        + [pltpu.SemaphoreType.DMA((2,)), pltpu.SemaphoreType.DMA((5,))],
+        + [pltpu.SemaphoreType.DMA, pltpu.SemaphoreType.DMA((3,))],
         compiler_params=params(VMEM_MB),
         cost_estimate=cost(),
-        name="ffn_forward",
-    )(pos_w, pos_g, h, vec, *inner_bufs, *outer_bufs)
-
-
-def chain_kernel(tile, *refs):
-    pos_w, dx_ref = refs[:2]
-    sources, vec_ref = refs[2:7], refs[7]
-    inner_bufs, outer_bufs, attn_bufs = refs[8:10], refs[10:12], refs[12:14]
-    pack_ref, da_ref, do_ref, sums_ref = refs[14:18]
-    wi, wu, wo, acc_ref = refs[18:22]
-    held = refs[22:27]
-    n2_ref, c2_ref, gp_ref, n1_ref, c1_ref = held
-    sems, load_sems = refs[27:]
-    width, hidden = wi.shape
-    for index in range(5):
+        name="inner_forward",
+    )(pos_w, pos_g, h, vec, *bufs)
+
+
+def outer_kernel(last, *refs):
+    pos_w, h_ref, active_ref, vec_ref = refs[:4]
+    grad_ref = refs[4] if last else None
+    refs = refs[4 + last :]
+    bufs = refs[:2]
+    outs, wu, acc_ref, sem = refs[2:-3], refs[-3], refs[-2], refs[-1]
+    fetch_rows(pos_w, bufs, wu, sem)
+    acc_ref[...] = h_ref[...] + row_of(vec_ref, UB)
+    wait_full(wu, sem)
+    tile = active_ref.shape[1] // ZS
+    for z in range(ZS):
+        acc_ref[...] += nn(active_ref[:, pl.ds(z * tile, tile)], flat(wu[z]))
+    normed, inverse = normalize(acc_ref[...])
+    result = normed * row_of(vec_ref, FG) + row_of(vec_ref, FS)
+    outs[0][...] = result
+    outs[1][...] = result.astype(BF16)
+    if last:
+        head_back(
+            grad_ref[...].astype(F32), normed, inverse, row_of(vec_ref, FG), outs[2], outs[3], outs[4]
+        )
+    else:
+        outs[2][...] = normed
+        outs[3][...] = jnp.broadcast_to(inverse, outs[3].shape)
+
+
+def outer_forward(pos_w, h, active, vec, bufs, grad):
+    tokens, width = h.shape
+    hidden = active.shape[1]
+    last = grad is not None
+    outs = (shape((tokens, width), F32), shape((tokens, width), BF16))
+    if last:
+        outs += head_shapes(tokens, width)
+    else:
+        outs += (shape((tokens, width), F32), shape((tokens, 128), F32))
+    return pl.pallas_call(
+        functools.partial(outer_kernel, int(last)),
+        out_shape=outs,
+        in_specs=[SMEM] + [VMEM] * (3 + last) + [ANY] * 2,
+        out_specs=[VMEM] * len(outs),
+        scratch_shapes=[
+            tall_matrix(hidden, width),
+            pltpu.VMEM((tokens, width), F32),
+            pltpu.SemaphoreType.DMA,
+        ],
+        compiler_params=params(VMEM_MB),
+        cost_estimate=cost(),
+        name="outer_forward",
+    )(pos_w, h, active, vec, *((grad,) if last else ()), *bufs)
+
+
+def chain_kernel(tile, waits, *refs):
+    pos_w, dyl_ref, dy_ref = refs[:3]
+    sources, vec_ref = refs[3:6], refs[6]
+    inner_bufs, outer_bufs, attn_bufs = refs[7:9], refs[9:11], refs[11:13]
+    refs = refs[13 + waits :]
+    pack_ref, da_ref, do_ref, sums_ref = refs[:4]
+    wi, wu, wo, acc_ref = refs[4:8]
+    held = refs[8:11]
+    gp_ref, n1_ref, c1_ref = held
+    sems, load_sems = refs[11:]
+    width, hidden = dy_ref.shape[1], wi.shape[3]
+    for index in range(3):
         load(sources[index], held[index], load_sems.at[index])
-    dyl_ref = pack_ref.at[:, pl.ds(0, width)]
-    du_ref = pack_ref.at[:, pl.ds(width, hidden)]
-    dal_ref = pack_ref.at[:, pl.ds(width + hidden, width)]
+    du_ref = pack_ref.at[:, pl.ds(0, hidden)]
+    dal_ref = pack_ref.at[:, pl.ds(hidden, width)]
     fetch_rows(pos_w, outer_bufs, wu, sems.at[0])
     fetch_columns(pos_w, inner_bufs, wi, sems.at[1])
     fetch_member(pos_w, attn_bufs, 3, wo, sems.at[2])
     sums_ref[...] = jnp.zeros_like(sums_ref)
-    grad = dx_ref[...].astype(F32)
-    wait_full(n2_ref, load_sems.at[0])
-    wait_full(c2_ref, load_sems.at[1])
-    normed = n2_ref[...]
-    sums_ref[pl.ds(FG, 1), :] = colsum(grad * normed)
-    sums_ref[pl.ds(FS, 1), :] = colsum(grad)
-    back = norm_back(normed, c2_ref[:, :1], grad * row_of(vec_ref, FG))
-    low = back.astype(BF16)
-    dyl_ref[...] = low
-    sums_ref[pl.ds(UB, 1), :] = colsum(low.astype(F32))
-    acc_ref[...] = back
-    wait_full(gp_ref, load_sems.at[2])
+    acc_ref[...] = dy_ref[...]
+    wait_full(gp_ref, load_sems.at[0])
     wait_full(wu, sems.at[0])
     wait_full(wi, sems.at[1])
     per_row = width // tile
 
     for index in range(hidden // tile):
         lane = index * tile
-        part = nt(dyl_ref[...], wu[pl.ds(lane, tile), :])
+        rows = wu[index * ZS * tile // hidden, pl.ds(lane % (hidden // ZS) * BLOCKS // hidden, tile * BLOCKS // hidden)]
+        part = nt(dyl_ref[...], flat(rows))
         part = (part * gp_ref[:, pl.ds(lane, tile)].astype(F32)).astype(BF16)
         du_ref[:, pl.ds(lane, tile)] = part
-        acc_ref[...] += nt(part, wi[:, pl.ds(lane, tile)])
+        acc_ref[...] += nt(part, flat(wi[:, :, :, pl.ds(lane, tile)]))
         sums_ref[
             pl.ds(IB + index // per_row, 1), pl.ds(index % per_row * tile, tile)
         ] = colsum(part.astype(F32))
 
     grad = acc_ref[...]
-    wait_full(n1_ref, load_sems.at[3])
-    wait_full(c1_ref, load_sems.at[4])
+    wait_full(n1_ref, load_sems.at[1])
+    wait_full(c1_ref, load_sems.at[2])
     normed = n1_ref[...]
     sums_ref[pl.ds(AG, 1), :] = colsum(grad * normed)
     sums_ref[pl.ds(AS, 1), :] = colsum(grad)
@@ -420,34 +461,34 @@
     dal_ref[...] = low
     sums_ref[pl.ds(OB, 1), :] = colsum(low.astype(F32))
     wait_full(wo, sems.at[2])
-    do_ref[...] = nt(low, wo[...]).astype(BF16)
-
-
-def chain_backward(pos_w, dx, n2, c2, gp, n1, c1, vec, inner_bufs, outer_bufs, attn_bufs):
-    tokens, width = n2.shape
+    do_ref[...] = nt(low, flat(wo[...])).astype(BF16)
+
+
+def chain_backward(pos_w, dyl, dy, gp, n1, c1, vec, inner_bufs, outer_bufs, attn_bufs, after=()):
+    tokens, width = n1.shape
     hidden = gp.shape[1]
     return pl.pallas_call(
-        functools.partial(chain_kernel, 384),
+        functools.partial(chain_kernel, 384, len(after)),
         out_shape=(
-            shape((tokens, 2 * width + hidden), BF16),
+            shape((tokens, hidden + width), BF16),
             shape((tokens, width), F32),
             shape((tokens, width), BF16),
             shape((16, width), F32),
         ),
-        in_specs=[SMEM, VMEM] + [HBM] * 5 + [VMEM] + [ANY] * 6,
+        in_specs=[SMEM] + [VMEM] * 2 + [HBM] * 3 + [VMEM] + [ANY] * (6 + len(after)),
         out_specs=[VMEM] * 4,
         scratch_shapes=[
-            pltpu.VMEM((width, hidden), BF16),
-            pltpu.VMEM((hidden, width), BF16),
-            pltpu.VMEM((width, width), BF16),
+            wide_matrix(width, hidden),
+            tall_matrix(hidden, width),
+            square(width),
             pltpu.VMEM((tokens, width), F32),
         ]
-        + [pltpu.VMEM(each.shape, each.dtype) for each in (n2, c2, gp, n1, c1)]
-        + [pltpu.SemaphoreType.DMA((3,)), pltpu.SemaphoreType.DMA((5,))],
+        + [pltpu.VMEM(each.shape, each.dtype) for each in (gp, n1, c1)]
+        + [pltpu.SemaphoreType.DMA((3,)), pltpu.SemaphoreType.DMA((3,))],
         compiler_params=params(VMEM_MB),
         cost_estimate=cost(),
         name="chain_backward",
-    )(pos_w, dx, n2, c2, gp, n1, c1, vec, *inner_bufs, *outer_bufs, *attn_bufs)
+    )(pos_w, dyl, dy, gp, n1, c1, vec, *inner_bufs, *outer_bufs, *attn_bufs, *after)
 
 
 def attn_back_kernel(*refs):
@@ -514,11 +555,16 @@
     )(q, kt, v, p, do)
 
 
-def input_kernel(*refs):
+def input_kernel(first, *refs):
     pos_w, da_ref, pack_ref, got_ref = refs[:4]
     bufs = refs[4:6]
-    dx_ref, total_ref, sum_ref = refs[6:9]
-    wq, wk, wv, sems = refs[9:]
+    refs = refs[6:]
+    if not first:
+        n2_ref, c2_ref, vec_ref = refs[:3]
+        refs = refs[3:]
+    total_ref, sum_ref = refs[:2]
+    heads = refs[2:-4]
+    wq, wk, wv, sems = refs[-4:]
     tokens, width = da_ref.shape
     for member, full in enumerate((wq, wk, wv)):
         fetch_member(pos_w, bufs, member, full, sems.at[member])
@@ -526,30 +572,32 @@
         total_ref[at] = (pack_ref[mine].astype(F32) + got_ref[theirs].astype(F32)).astype(BF16)
     sum_ref[...] = jnp.broadcast_to(colsum(total_ref[2].astype(F32)), sum_ref.shape)
     wait_full(wq, sems.at[0])
-    dx = da_ref[...] + nt(pack_ref[0], wq[...])
+    dx = da_ref[...] + nt(pack_ref[0], flat(wq[...]))
     wait_full(wk, sems.at[1])
-    dx += nt(total_ref[0], wk[...])
+    dx += nt(total_ref[0], flat(wk[...]))
     wait_full(wv, sems.at[2])
-    dx += nt(total_ref[2], wv[...])
-    dx_ref[...] = dx
-
-
-def input_backward(pos_w, da, pack, got, bufs):
+    dx += nt(total_ref[2], flat(wv[...]))
+    if first:
+        heads[0][...] = dx.astype(BF16)
+    else:
+        head_back(dx, n2_ref[...], c2_ref[:, :1], row_of(vec_ref, FG), *heads)
+
+
+def input_backward(pos_w, da, pack, got, bufs, below):
     tokens, width = da.shape
+    first = below is None
+    outs = (shape((4, tokens, width), BF16), shape((8, width), F32))
+    outs += (shape((tokens, width), BF16),) if first else head_shapes(tokens, width)
     return pl.pallas_call(
-        input_kernel,
-        out_shape=(
-            shape((tokens, width), F32),
-            shape((4, tokens, width), BF16),
-            shape((8, width), F32),
-        ),
-        in_specs=[SMEM] + [VMEM] * 3 + [ANY] * 2,
-        out_specs=[VMEM] * 3,
-        scratch_shapes=[pltpu.VMEM((width, width), BF16)] * 3 + [pltpu.SemaphoreType.DMA((3,))],
+        functools.partial(input_kernel, first),
+        out_shape=outs,
+        in_specs=[SMEM] + [VMEM] * 3 + [ANY] * 2 + ([] if first else [VMEM] * 3),
+        out_specs=[VMEM] * len(outs),
+        scratch_shapes=[square(width)] * 3 + [pltpu.SemaphoreType.DMA((3,))],
         compiler_params=params(VMEM_MB),
         cost_estimate=cost(),
         name="input_backward",
-    )(pos_w, da, pack, got, *bufs)
+    )(pos_w, da, pack, got, *bufs, *(() if first else below))
 
 
 def place(outs, part, dy, value):
@@ -577,7 +625,7 @@
     left_b = left[1].reshape(2 * ZS * rows, tokens)
     for dy in range(2):
         for part in range(2):
-            lanes = pl.ds(pl.multiple_of((half_at(pos_ref, dy) * 2 + part) * width + width, 128), width)
+            lanes = pl.ds(pl.multiple_of((half_at(pos_ref, dy) * 2 + part) * width, 128), width)
             value = nn(left_a, da_ref[:, lanes]) + nn(left_b, db_ref[:, lanes])
             place(outs, part, dy, value.astype(BF16).reshape(2, ZS, rows, width))
 
@@ -610,13 +658,13 @@
             for dx in range(2):
                 left_a = left[0, dx, dy, part].reshape(ZS * rows, tokens)
                 left_b = left[1, dx, dy, part].reshape(ZS * rows, tokens)
-                value = nn(left_a, da_ref[:, :width]) + nn(left_b, db_ref[:, :width])
+                value = nn(left_a, da_ref[...]) + nn(left_b, db_ref[...])
                 values.append(value.astype(BF16).reshape(ZS, rows, width))
             place(outs, part, dy, jnp.stack(values))
 
 
-def outer_grad(ta, tb, da, db, width):
-    rows = ta.shape[4]
+def outer_grad(ta, tb, da, db):
+    rows, width = ta.shape[4], da.shape[1]
     return pl.pallas_call(
         outer_grad_kernel,
         out_shape=grad_shapes(rows, width),
@@ -673,10 +721,13 @@
     )(pos_g, xa, xb, qa, qb, total, da, db)
 
 
-def copy_kernel(plan, inputs, *refs):
+def copy_kernel(plan, inputs, pos_ref, *refs):
     ins, outs, sems = refs[:inputs], refs[inputs:-1], refs[-1]
     copies = []
-    for index, (out, to, source, at, size) in enumerate(plan):
+    for index, (out, to, source, at, size, by_z) in enumerate(plan):
+        if by_z:
+            z = pos_ref[0]
+            to = flip(lax.div(z, 2), to // 2) * 2 + flip(lax.rem(z, 2), to % 2)
         copies.append(
             pltpu.make_async_copy(
                 ins[source].at[pl.ds(at, size)], outs[out].at[pl.ds(to, size)], sems.at[index]
@@ -688,18 +739,18 @@
         each.wait()
 
 
-def copy_blocks(plan, inputs, sizes, name):
+def copy_blocks(pos, plan, inputs, sizes, name):
     piece = inputs[0].shape[1:]
     return pl.pallas_call(
         functools.partial(copy_kernel, plan, len(inputs)),
         out_shape=tuple(shape((size,) + piece, BF16) for size in sizes),
-        in_specs=[ANY] * len(inputs),
+        in_specs=[SMEM] + [ANY] * len(inputs),
         out_specs=[VMEM] * len(sizes),
         scratch_shapes=[pltpu.SemaphoreType.DMA((len(plan),))],
         compiler_params=params(VMEM_MB),
         cost_estimate=cost(),
         name=name,
-    )(*inputs)
+    )(pos, *inputs)
 
 
 def pack_kernel(group, pos_ref, *refs):
@@ -791,7 +842,7 @@
                 each.wait()
         for layer in range(layers):
             for part in range(2):
-                value = buf[layer, part].astype(F32) if side else owns[layer][part]
+                value = (buf[layer, part] if side else owns[layer][part].astype(BF16)).astype(F32)
                 if kind == 0:
                     lanes = pl.ds(pl.multiple_of(yy * half, 128), half)
                     for member in range(2):
@@ -830,7 +881,7 @@
 
 
 def sum_kernel(config, *refs):
-    fresh, first, second, third, fourth = config
+    fresh, first, second, third, fourth, small = config
     refs = list(refs)
 
     def take(count):
@@ -844,6 +895,7 @@
     rests = take(2) if second else None
     pairs = take(2) if third else None
     lasts = take(2) if fourth else None
+    tables = take(2 if small == 1 else 1) if small else None
     to_x, to_y = take(2) if fresh or first or fourth else (None, None)
     at = 0
     if fresh:
@@ -863,24 +915,34 @@
         got = 2 * ZS
         at += ZS
     if second:
-        hold, go = take(2)
+        hold, to_z1 = take(2)
         for part, (rest, come) in enumerate(((rests[0], got_y), (rests[1], got_x))):
             for k in range(ZS):
                 value = rest[k].astype(F32) + come[got + k].astype(F32)
-                (go if k % 2 else hold)[k // 2, part] = value.astype(BF16)
+                (to_z1 if k % 2 else hold)[k // 2 * 2 + part] = value.astype(BF16)
     if third:
-        hold, go = take(2)
-        hold[...] = pairs[0][0].astype(F32) + pairs[1][0].astype(F32)
-        go[...] = (pairs[0][1].astype(F32) + pairs[1][1].astype(F32)).astype(BF16)
+        hold, to_z2 = take(2)
+        for part in range(2):
+            hold[part] = pairs[0][part].astype(F32) + pairs[1][part].astype(F32)
+            value = pairs[0][2 + part].astype(F32) + pairs[1][2 + part].astype(F32)
+            to_z2[part] = value.astype(BF16)
     if fourth:
         (total,) = take(1)
-        value = lasts[0][...] + lasts[1][...].astype(F32)
+        value = lasts[0][...] + lasts[1][:2].astype(F32)
         total[...] = value
         to_y[at : at + 2] = value.astype(BF16)
-
-
-def sum_round(fresh, got_x, got_y, first, second, third, fourth):
-    config = tuple(value is not None for value in (fresh, first, second, third, fourth))
+    if small:
+        come = (None, None, got_x, pairs and pairs[1], lasts and lasts[1])[small]
+        come = tables[1][...] if small == 1 else come[come.shape[0] - 1]
+        value = tables[0][...] + come.astype(F32)
+        refs[0][...] = value
+        to = (None, to_x, to_z1 if second else None, to_z2 if third else None, to_y)[small]
+        to[to.shape[0] - 1] = value.astype(BF16)
+
+
+def sum_round(fresh, got_x, got_y, first, second, third, fourth, small):
+    stage, table = small
+    config = tuple(value is not None for value in (fresh, first, second, third, fourth)) + (stage,)
     sample = fresh or first or second or third or fourth
     rows, width = sample[-1].shape[-2:]
     inputs, outputs = [], []
@@ -888,21 +950,23 @@
         inputs += [fresh[1], fresh[3]]
     if first is not None or second is not None:
         inputs += [got_x, got_y]
-    for value in (first, second, third, fourth):
+    for value in (first, second, third, fourth, table):
         if value is not None:
             inputs += list(value)
     going = 2 * ZS * config[0] + ZS * config[1]
     if config[0] or config[1] or config[4]:
-        size_y = going + 2 * config[4]
-        outputs += [shape((max(going, 1), rows, width), BF16), shape((size_y, rows, width), BF16)]
+        size_x, size_y = max(going, 1) + (stage == 1), going + 2 * config[4] + (stage == 4)
+        outputs += [shape((size_x, rows, width), BF16), shape((size_y, rows, width), BF16)]
     if config[1]:
         outputs += [shape((ZS, rows, width), BF16)] * 2
     if config[2]:
-        outputs += [shape((2, 2, rows, width), BF16)] * 2
+        outputs += [shape((4, rows, width), BF16), shape((4 + (stage == 2), rows, width), BF16)]
     if config[3]:
-        outputs += [shape((2, rows, width), F32), shape((2, rows, width), BF16)]
+        outputs += [shape((2, rows, width), F32), shape((2 + (stage == 3), rows, width), BF16)]
     if config[4]:
         outputs += [shape((2, rows, width), F32)]
+    if config[5]:
+        outputs += [shape(table[0].shape, F32)]
     outs = list(
         pl.pallas_call(
             functools.partial(sum_kernel, config),
@@ -923,7 +987,70 @@
         return out
 
     sends = take(config[0] or config[1] or config[4], 2)
-    return sends, going, take(config[1], 2), take(config[2], 2), take(config[3], 2), take(config[4], 1)
+    return (
+        sends,
+        going,
+        take(config[1], 2),
+        take(config[2], 2),
+        take(config[3], 2),
+        take(config[4], 1),
+        take(stage > 0, 1),
+    )
+
+
+def collect_kernel(*refs):
+    out = refs[-1]
+    for layer in range(out.shape[0]):
+        query_ref, value_ref, head_ref, chain_ref = refs[4 * layer : 4 * layer + 4]
+        out[layer] = chain_ref[...]
+        out[layer, pl.ds(QB, 1), :] = query_ref[:1]
+        out[layer, pl.ds(VB, 1), :] = value_ref[:1]
+        for at, index in enumerate((FG, FS, UB)):
+            out[layer, pl.ds(index, 1), :] = head_ref[at : at + 1]
+
+
+def collect(vectors, rows):
+    flat = [value for layer in vectors for value in layer]
+    width = flat[0].shape[1]
+    return pl.pallas_call(
+        collect_kernel,
+        out_shape=shape((len(vectors), rows, width), F32),
+        in_specs=[VMEM] * len(flat),
+        out_specs=VMEM,
+        compiler_params=params(VMEM_MB),
+        cost_estimate=cost(),
+        name="collect",
+    )(*flat)
+
+
+def vectors_kernel(last, at_ref, table_ref, got_ref, *outs):
+    layers, width = outs[0].shape[0], table_ref.shape[1]
+    at = at_ref[0]
+    for index, out in enumerate(outs):
+        size = out.shape[1]
+        start = at * size
+        shift = lax.rem(width - lax.rem(start, width), width)
+        for layer in range(layers):
+            spot = pl.ds(layer * 16 + index + lax.div(start, width), 1)
+            value = table_ref[spot, :]
+            if last is not None:
+                value = value.astype(BF16).astype(F32) + got_ref[spot, :]
+            value = jnp.broadcast_to(value, (8, width))
+            out[pl.ds(layer, 1), :] = pltpu.roll(value, shift, 1)[:1, :size]
+
+
+def own_vectors(at, table, got, layers, size, wide):
+    sizes = [size] * IB + [wide]
+    last = None if got is None else 0
+    return pl.pallas_call(
+        functools.partial(vectors_kernel, last),
+        out_shape=tuple(shape((layers, each), F32) for each in sizes),
+        in_specs=[SMEM, VMEM, VMEM],
+        out_specs=[VMEM] * len(sizes),
+        compiler_params=params(VMEM_MB),
+        cost_estimate=cost(),
+        name="own_vectors",
+    )(at, table, table if got is None else got)
 
 
 def fence(values):
@@ -990,7 +1117,7 @@
     hidden = inner_weight.shape[2]
     count = net["count"]
     move = net["move"]
-    staged = count == BLOCKS and small % 16 == 0
+    staged = count == BLOCKS and small == 16 * layers
     dp = lax.axis_index("dp").astype(jnp.int32)
     y = lax.axis_index("seq").astype(jnp.int32)
     core = lax.rem(dp, 2)
@@ -1055,7 +1182,13 @@
     def start_z1(g):
         own, come = stage_z[g]
         size = own.shape[0]
-        both = copy_blocks([(0, 0, 0, 0, size), (0, size, 1, 0, size)], (own, come), [2 * size], "gather_z")[0]
+        both = copy_blocks(
+            pos_g,
+            [(0, 0, 0, 0, size, False), (0, size, 1, 0, size, False)],
+            (own, come),
+            [2 * size],
+            "gather_z",
+        )[0]
         stage_z[g] = (both, move(both, net["z1"]))
 
     if staged:
@@ -1080,32 +1213,42 @@
     todo = []
     for layer in range(layers):
         todo.append(("attn", layer, 3 * layer))
-        todo.append(("ffn", layer, 3 * layer + 2))
+        todo.append(("inner", layer, 3 * layer + 1))
+        todo.append(("outer", layer, 3 * layer + 2))
     low = None
     attn_out = None
     arrived = 0 if staged else total_chunks
 
+    mid = None
+
     def compute():
-        nonlocal current, other, low, attn_out
+        nonlocal current, other, low, attn_out, mid, head
         if not todo or todo[0][2] >= arrived:
             return
         kind, layer, _ = todo.pop(0)
+        vec = table[layer]
         if kind == "attn":
-            attn_out = attn_forward(
-                pos_w, pos_g, current, other, seg, lab, table[layer], chunks[3 * layer]
-            )
+            attn_out = attn_forward(pos_w, pos_g, current, other, seg, lab, vec, chunks[3 * layer])
             return
         h, n1, c1, q, kt, v, p, xoh, far_xoh = attn_out
-        current, low, n2, c2, gp, gt, far_gt = ffn_forward(
-            pos_w, pos_g, h, table[layer], chunks[3 * layer + 1], chunks[3 * layer + 2]
+        if kind == "inner":
+            active, gp, gt, far_gt = inner_forward(pos_w, pos_g, h, vec, chunks[3 * layer + 1])
+            mid = (active, gp, gt, move(far_gt, net["core"]), move(far_xoh, net["core"]))
+            return
+        active, gp, gt, far_gt, far_xoh = mid
+        last = layer + 1 == layers
+        current, low, *rest = outer_forward(
+            pos_w, h, active, vec, chunks[3 * layer + 2], upstream if last else None
         )
-        if layer + 1 < layers:
+        if last:
+            head, rest = rest, (None, None)
+        else:
             other = move(low, net["core"])
-        kept[layer] = (n1, c1, q, kt, v, p, n2, c2, gp, xoh, gt) + (
-            move(far_xoh, net["core"]),
-            move(far_gt, net["core"]),
-        )
-
+        kept[layer] = (n1, c1, q, kt, v, p, *rest, gp, xoh, gt, far_xoh, far_gt)
+
+    head = None
+    if not staged:
+        upstream = move(upstream[0], net["swap"])
     if staged:
         sent, got = {}, {}
         zplan = {
@@ -1127,7 +1270,7 @@
                 mine, theirs = use(stage_z[g][0]), use(stage_z[g][1])
                 for out, part in ((0, 1), (1, 0)):
                     for k, (source, slot) in enumerate(((mine, 0), (theirs, 0), (mine, 1), (theirs, 1))):
-                        plan.append((out, k, source, (slot * n + j) * 2 + part, 1))
+                        plan.append((out, k, source, (slot * n + j) * 2 + part, 1, True))
                     sizes[out] = ZS
             before = r - LAG
             home = 0 <= before < total_chunks
@@ -1137,17 +1280,18 @@
                 first = ZS if before + LAG < total_chunks else 0
                 if r < total_chunks:
                     for out, send, come in ((0, sy, ry), (1, sx, rx)):
-                        plan.append((out, sizes[out], send, 0, ZS))
-                        plan.append((out, sizes[out] + ZS, come, 0, ZS))
+                        plan.append((out, sizes[out], send, 0, ZS, False))
+                        plan.append((out, sizes[out] + ZS, come, 0, ZS, False))
                         sizes[out] += 2 * ZS
                 if home:
                     sizes.append(8 * ZS)
                     slot = 2
                     for at, (send, come) in enumerate(((sx, rx), (sy, ry))):
-                        plan.append((slot, at * 4 * ZS, send, first, 2 * ZS))
-                        plan.append((slot, at * 4 * ZS + 2 * ZS, come, first, 2 * ZS))
+                        plan.append((slot, at * 4 * ZS, send, first, 2 * ZS, False))
+                        plan.append((slot, at * 4 * ZS + 2 * ZS, come, first, 2 * ZS, False))
             live = [index for index, size in enumerate(sizes) if size]
             outs = copy_blocks(
+                pos_g,
                 [(live.index(each[0]),) + each[1:] for each in plan],
                 inputs,
                 [sizes[index] for index in live],
@@ -1165,18 +1309,18 @@
                     (start_z2 if stage == 2 else start_z1)(g)
             if spread:
                 table = table + move(table, spread.pop(0))
-            if r == total_chunks - 2:
+            if r == total_chunks - 1:
                 upstream = move(upstream[0], net["swap"])
             compute()
             ready = r + 1 - LAG
-            state = (got.get(ready), core_pair, stage_z, current, other, attn_out, raw, table, upstream)
+            state = (got.get(ready), core_pair, stage_z, current, other, attn_out, raw, table, upstream, mid)
             state = fence(state)
             if ready in got:
                 got[ready] = state[0]
             if home:
                 chunks.append(state[1])
                 arrived += 1
-            stage_z, current, other, attn_out, raw, table, upstream = (list(state[2]),) + tuple(state[3:])
+            stage_z, current, other, attn_out, raw, table, upstream, mid = (list(state[2]),) + tuple(state[3:])
     while todo:
         compute()
     range_ids = jnp.arange(SEGS, dtype=jnp.int32)
@@ -1189,43 +1333,34 @@
         loose["hidden"] = move(low, net["swap"])
         loose["pool"] = pool_sums + move(pool_sums, net["core"])
 
-    grad = upstream if staged else move(upstream[0], net["swap"])
     parts = []
     vectors = [None] * layers
     rounds = []
     ends = []
+    table_stage = 1
 
     def side_work():
         step = len(rounds)
         last = total_chunks
         if step == 0:
             loose["pooled"] = move(loose.pop("pool") / counts[:, None], net["swap"])
-        if step == last - 2:
-            loose["table"] = jnp.stack(vectors)
-            loose["table"] = loose["table"] + move(loose["table"], net["core"])
-        order = {last - 1: "z1", last: "z2", last + 1: "x", last + 2: "y"}
-        if step in order:
-            loose["table"] = loose["table"] + move(loose["table"], net[order[step]])
-        if step == last:
-            loose["grad"] = move(loose.pop("grad").astype(BF16), net["swap"])
+        if step == last + 2:
+            loose["grad"] = move(loose.pop("grad"), net["swap"])
 
     def settle(state):
-        nonlocal loose
-        state, loose = fence((state, loose))
-        return state
+        return fence(state)
 
     def advance(fresh, state):
-        nonlocal loose
         if not staged:
             if fresh is not None:
                 parts.append(fresh)
-            return state
+            return state(()) if callable(state) else state
         side_work()
         s = len(rounds)
         past = rounds[s - LAG] if s >= LAG else {}
         pick = lambda key: past.get(key)
         has_home = pick("first") is not None or pick("second") is not None
-        sends, going, first, second, third, fourth = sum_round(
+        sends, going, first, second, third, fourth, small = sum_round(
             fresh,
             pick("got_x") if has_home else None,
             pick("got_y") if has_home else None,
@@ -1233,6 +1368,7 @@
             pick("second"),
             pick("third"),
             pick("fourth"),
+            loose.pop("small", (0, None)),
         )
         now = {}
         if fresh is not None:
@@ -1250,44 +1386,62 @@
         if fourth is not None:
             now["total"] = fourth[0]
             ends.append(going)
+        if "vectors" in loose:
+            small = loose.pop("vectors").reshape(-1, width)
+            loose["small"] = (1, (small, move(small, net["core"])))
+        elif small is not None:
+            nonlocal table_stage
+            table_stage += 1
+            loose["small"] = (table_stage, small)
+        if callable(state):
+            state = state(sends)
         rounds.append(now)
         ready = s + 1 - LAG
         if ready < 0:
-            state, loose = fence((state, loose))
-            return state
-        rounds[ready], state, loose = fence((rounds[ready], state, loose))
+            return fence(state)
+        rounds[ready], state = fence((rounds[ready], state))
         return state
 
-    ready = None
+    top = layers - 1
+    attn_parts = None
+    dyl, dy, head_sums = head
     for layer in reversed(range(layers)):
         attn_bufs, inner_bufs, outer_bufs = chunks[3 * layer : 3 * layer + 3]
-        vec = table[layer]
         n1, c1, q, kt, v, p, n2, c2, gp, xoh, gt, far_xoh, far_gt = kept[layer]
-        pack, da, do, sums = chain_backward(
-            pos_w, grad, n2, c2, gp, n1, c1, vec, inner_bufs, outer_bufs, attn_bufs
-        )
-        if layer + 1 < layers:
-            attn_parts = attn_grad(*attn_args)
-            (pack, da, do, sums), attn_parts = advance(ready, ((pack, da, do, sums), attn_parts))
-            ready = attn_parts
-        got_pack = move(pack, net["core"])
-        back, qsum = attn_backward(q, kt, v, p, do)
-        outer_parts = outer_grad(gt, far_gt, pack, got_pack, width)
-        state = (back, qsum, outer_parts, pack, got_pack, da)
-        back, qsum, outer_parts, pack, got_pack, da = (
-            advance(ready, state) if ready is not None else settle(state)
-        )
+        got_dyl = move(dyl, net["core"])
+        chain_args = (pos_w, dyl, dy, gp, n1, c1, table[layer], inner_bufs, outer_bufs, attn_bufs)
+        if layer == top:
+            outer_parts = settle(outer_grad(gt, far_gt, dyl, got_dyl))
+
+            def first_chain(sends):
+                pack, da, do, sums = chain_backward(*chain_args, after=sends)
+                got_pack = move(pack, net["core"])
+                inner_parts = inner_grad(pos_g, xoh, far_xoh, pack, got_pack)
+                return pack, da, do, sums, got_pack, inner_parts
+
+            pack, da, do, sums, got_pack, inner_parts = advance(outer_parts, first_chain)
+            back, qsum = attn_backward(q, kt, v, p, do)
+        else:
+            pack, da, do, sums = chain_backward(*chain_args)
+            outer_parts = outer_grad(gt, far_gt, dyl, got_dyl)
+            state = advance(attn_parts, (pack, da, do, sums, outer_parts))
+            pack, da, do, sums, outer_parts = state
+            got_pack = move(pack, net["core"])
+            back, qsum = attn_backward(q, kt, v, p, do)
+            inner_parts = inner_grad(pos_g, xoh, far_xoh, pack, got_pack)
+            state = advance(outer_parts, (back, qsum, got_pack, inner_parts))
+            back, qsum, got_pack, inner_parts = state
         got_back = move(back, net["core"])
-        inner_parts = inner_grad(pos_g, xoh, far_xoh, pack, got_pack)
-        grad, total, vsum = input_backward(pos_w, da, back, got_back, attn_bufs)
-        state = (grad, total, vsum, inner_parts, back, got_back)
-        grad, total, vsum, inner_parts, back, got_back = advance(outer_parts, state)
-        ready = inner_parts
-        attn_args = (pos_g, xoh, far_xoh, back, got_back, total, pack, got_pack)
-        vectors[layer] = jnp.concatenate([qsum[:1], vsum[:1], sums[2:12]], axis=0)
-    loose["grad"] = grad
-    attn_parts = attn_grad(*attn_args)
-    attn_parts = advance(ready, attn_parts)
+        below = None if layer == 0 else (kept[layer - 1][6], kept[layer - 1][7], table[layer - 1])
+        total, vsum, *head = input_backward(pos_w, da, back, got_back, attn_bufs, below)
+        attn_parts = attn_grad(pos_g, xoh, far_xoh, back, got_back, total, pack, got_pack)
+        vectors[layer] = (qsum, vsum, head_sums, sums)
+        attn_parts, head, vectors[layer] = advance(inner_parts, (attn_parts, head, vectors[layer]))
+        if layer:
+            dyl, dy, head_sums = head
+    grad = head[0]
+    vectors = collect(vectors, 16)
+    loose["vectors"], loose["grad"] = vectors, grad
     advance(attn_parts, None)
     results = []
     if staged:
@@ -1301,9 +1455,9 @@
         stacked = []
         for kind, first in ((0, 2), (1, 1), (2, 0)):
             stacked += list(finish(kind, pos_g, results[first::3][::-1]))
-        hidden_out, pooled, tokens_grad, table = (
-            loose[key] for key in ("hidden", "pooled", "grad", "table")
-        )
+        hidden_out, pooled, tokens_grad = (loose[key] for key in ("hidden", "pooled", "grad"))
+        vectors = loose["small"][1][0]
+        got_vectors = rounds[-1]["got_y"][-1].astype(F32)
     else:
         collected = [None] * layers
         for place_at, layer in enumerate(reversed(range(layers))):
@@ -1336,12 +1490,10 @@
         ]
         hidden_out = move(low, net["swap"])
         pooled = move((pool_sums + move(pool_sums, net["core"])) / counts[:, None], net["swap"])
-        tokens_grad = move(grad.astype(BF16), net["swap"])
-        table = lax.psum(jnp.stack(vectors), AXES)
-    eight = lax.dynamic_slice_in_dim(table[:, :8], dp * small, small, 2)
-    wide = lax.dynamic_slice_in_dim(
-        table[:, 8:].reshape(layers, hidden), dp * (hidden // count), hidden // count, 1
-    )
+        tokens_grad = move(grad, net["swap"])
+        vectors = lax.psum(vectors, AXES).reshape(-1, width)
+        got_vectors = None
+    own = own_vectors(dp[None], vectors, got_vectors, layers, small, hidden // count)
     return (
         hidden_out[None],
         pooled[None],
@@ -1350,17 +1502,17 @@
         stacked[1],
         stacked[2],
         stacked[3],
-        eight[:, QB],
-        eight[:, VB],
-        eight[:, OB],
-        eight[:, AG],
-        eight[:, AS],
+        own[QB],
+        own[VB],
+        own[OB],
+        own[AG],
+        own[AS],
         stacked[4],
-        wide,
+        own[IB],
         stacked[5],
-        eight[:, UB],
-        eight[:, FG],
-        eight[:, FS],
+        own[UB],
+        own[FG],
+        own[FS],
     )
 
 

time: 649 us -> 615 us (0.948)
  Pallas kernels: 248 us -> 200 us
  waiting for transfers between devices: 216 us -> 257 us
  local copies, waits for them, and re-layouts: 52.1 us -> 30.1 us
    pallas_call x9 -> x14, Pallas kernels: 115 us -> 66.6 us  [the longest x3 24.8 us: chain_backward(): pl.pallas_call(functools.partial(chain_kernel, 384, len(after)), out_shap...]
    ppermute x112 -> x111, waiting for transfers between devices: 216 us -> 257 us  [move(): return lax.ppermute(value, AXES, perm)]
    unnamed x338 -> x264, local copies, waits for them, and re-layouts: 47.5 us -> 29.1 us
    pallas_call x16, Pallas kernels: 22.6 us -> 29.7 us  [copy_blocks(): pl.pallas_call(functools.partial(copy_kernel, plan, len(inputs)), out_sha...]
    ppermute x112 -> x111, starting transfers between devices: 115 us -> 113 us  [move(): return lax.ppermute(value, AXES, perm)]
  transfers between devices with their start and end apart: 112 -> 111, of which waited for: 47 -> 60; matrix products, arithmetic and copies ran while one was open for 1% -> 1% of each run, Pallas kernels for 29% -> 25%
where the time goes in v3:
time: 615 us; the launch traced here: 606 us
  waiting for transfers between devices  257 us (42%)
  Pallas kernels  200 us (33%)
  starting transfers between devices  113 us (18%)
  local copies, waits for them, and re-layouts  30.1 us (5%)
    ppermute x111, waiting for transfers between devices, move(): return lax.ppermute(value, AXES, perm)  257 us
    ppermute x111, starting transfers between devices, move(): return lax.ppermute(value, AXES, perm)  113 us
    pallas_call x3, Pallas kernels, attn_forward(): pl.pallas_call(attn_kernel, out_shape=(shape((tokens, width), F32),) + ke...  39.7 us
    pallas_call x16, Pallas kernels, copy_blocks(): pl.pallas_call(functools.partial(copy_kernel, plan, len(inputs)), out_sha...  29.7 us
    unnamed x264, local copies, waits for them, and re-layouts  29.1 us
    pallas_call x3, Pallas kernels, chain_backward(): pl.pallas_call(functools.partial(chain_kernel, 384, len(after)), out_shap...  24.8 us
    pallas_call x3, Pallas kernels, attn_backward(): pl.pallas_call(attn_back_kernel, out_shape=(shape((5, tokens, width), BF1...  23.3 us
    pallas_call x3, Pallas kernels, inner_forward(): pl.pallas_call(functools.partial(inner_kernel, 384), out_shape=(shape((to...  19.4 us
  transfers between devices with their start and end apart: 111, of which 60 were waited for; matrix products, arithmetic and copies ran while one was open for 1% of the time, Pallas kernels for 25%

profile of v3, /device:TPU:0, one launch (start us, length us, event | category | flops | bytes accessed | tf_op | source)
XLA Modules:
  0.0 605.7 jit_solution(16667010313668718899)
XLA Ops:
  9.3 4.1 collective-permute-start
  16.1 3.9 collective-permute-done.1
  24.9 2.5 collective-permute-start.5
  28.8 5.1 collective-permute-done.5.refs_1_
  35.8 2.7 collective-permute-start.11
  46.6 11.2 %collective-permute-done.13 = f32[3,12,768]{2,1,0:T(8,128)S(1)} collective-permute-done((f32[3,12,768]{2,1,0:T(8,128)S(1)}, f32[3,12,768]{2,1,0:T(8,128)S(1)}, u32[]{:S(2)}, u32[]{:S(2)}) %collective-permute-start.13) | collective-permute-done | bytes 110624 | tf_op jit(solution)/shard_map/ppermute | solution.py:1080
  65.7 18.0 %collective-permute-done.18 = f32[3,12,768]{2,1,0:T(8,128)S(1)} collective-permute-done((f32[3,12,768]{2,1,0:T(8,128)S(1)}, f32[3,12,768]{2,1,0:T(8,128)S(1)}, u32[]{:S(2)}, u32[]{:S(2)}) %collective-permute-start.18) | collective-permute-done | bytes 110624 | tf_op jit(solution)/shard_map/ppermute | solution.py:1080
  84.4 2.2 gather_round.13
  89.9 19.9 %collective-permute-done.22.refs_1_ = bf16[12,48,768]{2,1,0:T(8,128)(2,1)S(1)} collective-permute-done((bf16[12,48,768]{2,1,0:T(8,128)(2,1)S(1)}, bf16[12,48,768]{2,1,0:T(8,128)(2,1)S(1)}, u32[]{:S(2)}, u32[]{:S(2)}) %collective-permute-start.22) | collective-permute-done | bytes 884768 | tf_op jit(solution)/shard_map/ppermute | solution.py:1080
  112.7 4.2 gather_round.14
  120.2 2.3 collective-permute-start.26
  127.3 13.2 %attn_forward.3 = (f32[256,768]{1,0:T(8,128)S(1)}, f32[256,768]{1,0:T(8,128)S(1)}, f32[256,128]{1,0:T(8,128)S(1)}, bf16[256,768]{1,0:T(8,128)(2,1)S(1)}, bf16[76...) custom-call(s32[4]{0:T(128)S(1)} %pad_add_fusion.2.pos_ref.refs_0_.r, ...), custom_call_target="tpu_custom_call" | custom-call | flops 1 | bytes 1 | tf_op jit(solution)/shard_map/attn_forward/pallas_call | solution.py:265
  143.1 3.4 gather_round.15
  152.3 7.7 %inner_forward.3 = (bf16[256,3072]{1,0:T(8,128)(2,1)S(1)}, bf16[256,3072]{1,0:T(8,128)(2,1)S(1)}, bf16[2,2,2,4,48,256]{5,4,3,2,1,0:T(8,128)(2,1)S(1)}, bf16[2,2,2,4,48,256]{5,4,3,2,1,0:T(8,128)(2,1)S(1)}) custom-call(s32[4]{0:T(128)S(1)} %pad_add_fusion.2.pos_ref.refs_0_.refs_1_, s32[4]{0:T(128)S(1)} %pad_add_fusion.2.pos_ref.refs_0_.refs_1_, ...), custom_call_target="tpu_custom_call" | custom-call | flops 1 | bytes 1 | tf_op jit(solution)/shard_map/inner_forward/pallas_call | solution.py:348
  160.9 2.3 collective-permute-done.31.tb_ref
  164.1 6.4 %collective-permute-done.30.refs_1_ = bf16[12,48,768]{2,1,0:T(8,128)(2,1)S(1)} collective-permute-done((bf16[12,48,768]{2,1,0:T(8,128)(2,1)S(1)}, bf16[12,48,768]{2,1,0:T(8,128)(2,1)S(1)}, u32[]{:S(2)}, u32[]{:S(2)}) %collective-permute-start.30) | collective-permute-done | bytes 884768 | tf_op jit(solution)/shard_map/ppermute | solution.py:1080
  176.4 3.3 outer_forward.3
  181.5 14.9 %collective-permute-done.33.refs_4_ = bf16[12,48,768]{2,1,0:T(8,128)(2,1)S(1)} collective-permute-done((bf16[12,48,768]{2,1,0:T(8,128)(2,1)S(1)}, bf16[12,48,768]{2,1,0:T(8,128)(2,1)S(1)}, u32[]{:S(2)}, u32[]{:S(2)}) %collective-permute-start.33) | collective-permute-done | bytes 884768 | tf_op jit(solution)/shard_map/ppermute | solution.py:1080
  202.2 13.2 %attn_forward.4 = (f32[256,768]{1,0:T(8,128)S(1)}, f32[256,768]{1,0:T(8,128)S(1)}, f32[256,128]{1,0:T(8,128)S(1)}, bf16[256,768]{1,0:T(8,128)(2,1)S(1)}, bf16[76...) custom-call(s32[4]{0:T(128)S(1)} %pad_add_fusion.2.pos_ref.refs_0_.r, ...), custom_call_target="tpu_custom_call" | custom-call | flops 1 | bytes 1 | tf_op jit(solution)/shard_map/attn_forward/pallas_call | solution.py:265
  217.1 3.7 collective-permute-done.37.refs_4_
  226.6 5.9 inner_forward.4
  233.1 2.6 collective-permute-done.44.tb_ref.xb_ref
  236.7 10.0 %collective-permute-done.40.refs_4_ = bf16[12,48,768]{2,1,0:T(8,128)(2,1)S(1)} collective-permute-done((bf16[12,48,768]{2,1,0:T(8,128)(2,1)S(1)}, bf16[12,48,768]{2,1,0:T(8,128)(2,1)S(1)}, u32[]{:S(2)}, u32[]{:S(2)}) %collective-permute-start.40) | collective-permute-done | bytes 884768 | tf_op jit(solution)/shard_map/ppermute | solution.py:1080
  252.4 2.8 outer_forward.4
  257.1 14.0 %collective-permute-done.45.refs_2_ = bf16[12,48,768]{2,1,0:T(8,128)(2,1)S(1)} collective-permute-done((bf16[12,48,768]{2,1,0:T(8,128)(2,1)S(1)}, bf16[12,48,768]{2,1,0:T(8,128)(2,1)S(1)}, u32[]{:S(2)}, u32[]{:S(2)}) %collective-permute-start.45) | collective-permute-done | bytes 884768 | tf_op jit(solution)/shard_map/ppermute | solution.py:1080
  276.7 13.4 %attn_forward.5 = (f32[256,768]{1,0:T(8,128)S(1)}, f32[256,768]{1,0:T(8,128)S(1)}, f32[256,128]{1,0:T(8,128)S(1)}, bf16[256,768]{1,0:T(8,128)(2,1)S(1)}, bf16[76...) custom-call(s32[4]{0:T(128)S(1)} %pad_add_fusion.2.pos_ref.refs_0_.r, ...), custom_call_target="tpu_custom_call" | custom-call | flops 1 | bytes 1 | tf_op jit(solution)/shard_map/attn_forward/pallas_call | solution.py:265
  295.7 5.9 inner_forward.5
  302.5 2.7 collective-permute-done.55.tb_ref.xb_ref
  305.2 3.2 outer_forward.5
  315.4 7.9 %chain_backward.3 = (bf16[256,3840]{1,0:T(8,128)(2,1)S(1)}, f32[256,768]{1,0:T(8,128)S(1)}, bf16[256,768]{1,0:T(8,128)(2,1)S(1)}, f32[16,768]{1,0:T(8,128)S(1)}) custom-call(s32[4]{0:T(128)S(1)} %pad_add_fusion.2.pos_ref.refs_0_.refs_1_, bf16[256,768]{1,0:T(8,128)(2,1)S(1)} %get-tuple-element.916.da_ref.refs_1_, f32[256,768]{1,0:T(8,128)S(1)} %get-tuple-element.923.refs_2_, ...), custom_call_target="tpu_custom_call" | custom-call | flops 1 | bytes 1 | tf_op jit(solution)/shard_map/chain_backward/pallas_call | solution.py:470
  328.3 2.5 inner_grad.3
  330.8 9.3 %collective-permute-done.60.refs_2_ = bf16[8,48,768]{2,1,0:T(8,128)(2,1)S(1)} collective-permute-done((bf16[8,48,768]{2,1,0:T(8,128)(2,1)S(1)}, bf16[8,48,768]{2,1,0:T(8,128)(2,1)S(1)}, u32[]{:S(2)}, u32[]{:S(2)}) %collective-permute-start.60) | collective-permute-done | bytes 589856 | tf_op jit(solution)/shard_map/ppermute | solution.py:1080
  341.5 7.8 %attn_backward.3 = (bf16[5,256,768]{2,1,0:T(8,128)(2,1)S(1)}, f32[8,768]{1,0:T(8,128)S(1)}) custom-call(bf16[256,768]{1,0:T(8,128)(2,1)S(1)} %copy-done.103, bf16[768,512]{1,0:T(8,128)(2,1)S(1)} %copy-done.77, bf16[512,768]{1,0:T(8,128)(2,1)S(1)} %copy-done.79, bf16[12,512,256]{2,1,0:T(8,128)(2,1)S(1)} %copy-done.38, ...), custom_call_target="tpu_custom_call" | custom-call | flops 1 | bytes 1 | tf_op jit(solution)/shard_map/attn_backward/pallas_call | solution.py:541
  353.4 4.1 input_backward.3
  358.4 3.2 attn_grad.3
  362.4 9.5 %collective-permute-done.63.refs_2_ = bf16[12,48,768]{2,1,0:T(8,128)(2,1)S(1)} collective-permute-done((bf16[12,48,768]{2,1,0:T(8,128)(2,1)S(1)}, bf16[12,48,768]{2,1,0:T(8,128)(2,1)S(1)}, u32[]{:S(2)}, u32[]{:S(2)}) %collective-permute-start.63) | collective-permute-done | bytes 884768 | tf_op jit(solution)/shard_map/ppermute | solution.py:1080
  377.3 7.7 %chain_backward.4 = (bf16[256,3840]{1,0:T(8,128)(2,1)S(1)}, f32[256,768]{1,0:T(8,128)S(1)}, bf16[256,768]{1,0:T(8,128)(2,1)S(1)}, f32[16,768]{1,0:T(8,128)S(1)}) custom-call(s32[4]{0:T(128)S(1)} %pad_add_fusion.2.pos_ref.refs_0_.refs_1_, bf16[256,768]{1,0:T(8,128)(2,1)S(1)} %get-tuple-element.988.refs_1_.da_ref, f32[256,768]{1,0:T(8,128)S(1)} %copy-done.57, ...), custom_call_target="tpu_custom_call" | custom-call | flops 1 | bytes 1 | tf_op jit(solution)/shard_map/chain_backward/pallas_call | solution.py:470
  386.6 7.1 %collective-permute-done.66.refs_2_ = bf16[12,48,768]{2,1,0:T(8,128)(2,1)S(1)} collective-permute-done((bf16[12,48,768]{2,1,0:T(8,128)(2,1)S(1)}, bf16[12,48,768]{2,1,0:T(8,128)(2,1)S(1)}, u32[]{:S(2)}, u32[]{:S(2)}) %collective-permute-start.66) | collective-permute-done | bytes 884768 | tf_op jit(solution)/shard_map/ppermute | solution.py:1080
  399.9 7.8 %attn_backward.4 = (bf16[5,256,768]{2,1,0:T(8,128)(2,1)S(1)}, f32[8,768]{1,0:T(8,128)S(1)}) custom-call(bf16[256,768]{1,0:T(8,128)(2,1)S(1)} %copy-done.101, bf16[768,512]{1,0:T(8,128)(2,1)S(1)} %copy-done.73, bf16[512,768]{1,0:T(8,128)(2,1)S(1)} %copy-done.75, bf16[12,512,256]{2,1,0:T(8,128)(2,1)S(1)} %copy-done.36, ...), custom_call_target="tpu_custom_call" | custom-call | flops 1 | bytes 1 | tf_op jit(solution)/shard_map/attn_backward/pallas_call | solution.py:541
  407.7 2.6 inner_grad.4
  410.4 7.3 %collective-permute-done.71.refs_2_ = bf16[12,48,768]{2,1,0:T(8,128)(2,1)S(1)} collective-permute-done((bf16[12,48,768]{2,1,0:T(8,128)(2,1)S(1)}, bf16[12,48,768]{2,1,0:T(8,128)(2,1)S(1)}, u32[]{:S(2)}, u32[]{:S(2)}) %collective-permute-start.71) | collective-permute-done | bytes 884768 | tf_op jit(solution)/shard_map/ppermute | solution.py:1080
  423.7 4.0 input_backward.4
  427.8 2.8 attn_grad.4
  433.5 8.4 %collective-permute-done.76.refs_2_ = bf16[12,48,768]{2,1,0:T(8,128)(2,1)S(1)} collective-permute-done((bf16[12,48,768]{2,1,0:T(8,128)(2,1)S(1)}, bf16[12,48,768]{2,1,0:T(8,128)(2,1)S(1)}, u32[]{:S(2)}, u32[]{:S(2)}) %collective-permute-start.76) | collective-permute-done | bytes 884768 | tf_op jit(solution)/shard_map/ppermute | solution.py:1080
  449.6 9.3 %chain_backward.5 = (bf16[256,3840]{1,0:T(8,128)(2,1)S(1)}, f32[256,768]{1,0:T(8,128)S(1)}, bf16[256,768]{1,0:T(8,128)(2,1)S(1)}, f32[16,768]{1,0:T(8,128)S(1)}) custom-call(s32[4]{0:T(128)S(1)} %pad_add_fusion.2.pos_ref.refs_0_.refs_1_, bf16[256,768]{1,0:T(8,128)(2,1)S(1)} %get-tuple-element.1089.refs_1_.da_ref, ...), custom_call_target="tpu_custom_call" | custom-call | flops 1 | bytes 1 | tf_op jit(solution)/shard_map/chain_backward/pallas_call | solution.py:470
  460.6 6.4 %collective-permute-done.81.refs_2_ = bf16[12,48,768]{2,1,0:T(8,128)(2,1)S(1)} collective-permute-done((bf16[12,48,768]{2,1,0:T(8,128)(2,1)S(1)}, bf16[12,48,768]{2,1,0:T(8,128)(2,1)S(1)}, u32[]{:S(2)}, u32[]{:S(2)}) %collective-permute-start.81) | collective-permute-done | bytes 884768 | tf_op jit(solution)/shard_map/ppermute | solution.py:1080
  474.8 7.8 %attn_backward.5 = (bf16[5,256,768]{2,1,0:T(8,128)(2,1)S(1)}, f32[8,768]{1,0:T(8,128)S(1)}) custom-call(bf16[256,768]{1,0:T(8,128)(2,1)S(1)} %copy-done.99, bf16[768,512]{1,0:T(8,128)(2,1)S(1)} %copy-done.69, bf16[512,768]{1,0:T(8,128)(2,1)S(1)} %copy-done.71, bf16[12,512,256]{2,1,0:T(8,128)(2,1)S(1)} %copy-done.34, ...), custom_call_target="tpu_custom_call" | custom-call | flops 1 | bytes 1 | tf_op jit(solution)/shard_map/attn_backward/pallas_call | solution.py:541
  482.6 2.5 inner_grad.5
  485.1 7.8 %collective-permute-done.86.refs_2_ = bf16[12,48,768]{2,1,0:T(8,128)(2,1)S(1)} collective-permute-done((bf16[12,48,768]{2,1,0:T(8,128)(2,1)S(1)}, bf16[12,48,768]{2,1,0:T(8,128)(2,1)S(1)}, u32[]{:S(2)}, u32[]{:S(2)}) %collective-permute-start.86) | collective-permute-done | bytes 884768 | tf_op jit(solution)/shard_map/ppermute | solution.py:1080
  500.7 4.0 input_backward.5
  504.6 2.8 attn_grad.5
  507.4 2.2 collective-permute-done.90.refs_11_
  510.5 8.4 %collective-permute-done.91.refs_2_ = bf16[12,48,768]{2,1,0:T(8,128)(2,1)S(1)} collective-permute-done((bf16[12,48,768]{2,1,0:T(8,128)(2,1)S(1)}, bf16[12,48,768]{2,1,0:T(8,128)(2,1)S(1)}, u32[]{:S(2)}, u32[]{:S(2)}) %collective-permute-start.91) | collective-permute-done | bytes 884768 | tf_op jit(solution)/shard_map/ppermute | solution.py:1080
  526.7 8.1 %collective-permute-done.96.refs_9_ = bf16[2,48,768]{2,1,0:T(8,128)(2,1)S(1)} collective-permute-done((bf16[2,48,768]{2,1,0:T(8,128)(2,1)S(1)}, bf16[2,48,768]{2,1,0:T(8,128)(2,1)S(1)}, u32[]{:S(2)}, u32[]{:S(2)}) %collective-permute-start.96) | collective-permute-done | bytes 147488 | tf_op jit(solution)/shard_map/ppermute | solution.py:1080
  535.6 8.4 %collective-permute-done.97.refs_0_ = bf16[12,48,768]{2,1,0:T(8,128)(2,1)S(1)} collective-permute-done((bf16[12,48,768]{2,1,0:T(8,128)(2,1)S(1)}, bf16[12,48,768]{2,1,0:T(8,128)(2,1)S(1)}, u32[]{:S(2)}, u32[]{:S(2)}) %collective-permute-start.97) | collective-permute-done | bytes 884768 | tf_op jit(solution)/shard_map/ppermute | solution.py:1080
  551.6 7.3 %collective-permute-done.101.refs_7_ = bf16[2,48,768]{2,1,0:T(8,128)(2,1)S(1)} collective-permute-done((bf16[2,48,768]{2,1,0:T(8,128)(2,1)S(1)}, bf16[2,48,768]{2,1,0:T(8,128)(2,1)S(1)}, u32[]{:S(2)}, u32[]{:S(2)}) %collective-permute-start.101) | collective-permute-done | bytes 147488 | tf_op jit(solution)/shard_map/ppermute | solution.py:1080
  564.6 4.8 collective-permute-start.106
  570.3 4.4 collective-permute-start.57
  574.8 3.6 collective-permute-done.106.refs_3_
  580.3 4.1 collective-permute-done.109.refs_3_
  584.4 8.1 %collective-permute-done.108.refs_1_ = bf16[3,48,768]{2,1,0:T(8,128)(2,1)S(1)} collective-permute-done((bf16[3,48,768]{2,1,0:T(8,128)(2,1)S(1)}, bf16[3,48,768]{2,1,0:T(8,128)(2,1)S(1)}, u32[]{:S(2)}, u32[]{:S(2)}) %collective-permute-start.108) | collective-permute-done | bytes 221216 | tf_op jit(solution)/shard_map/ppermute | solution.py:1080
  594.4 2.5 finish.5
  596.9 2.5 finish.4
  601.5 2.4 finish.3
  (515 shorter events, 199.0 us)
Async XLA Ops:
  0.8 19.3 %collective-permute-start.3 = (bf16[256,768]{1,0:T(8,128)(2,1)}, bf16[256,768]{1,0:T(8,128)(2,1)S(1)}, u32[]{:S(2)}, u32[]{:S(2)}) collective-permute-start(bf16[256,768]{1,0:T(8,128)(2,1)} %bitcast.50), channel_id=1, source_target_pairs={{0,0},{2,1},{1,2},{3,3},{4,4},{6,5},{5,6},{7,7},{8,8},{10,9},{9,10... | collective-permute-start | bytes 1179656 | tf_op jit(solution)/shard_map/ppermute | solution.py:1080
  20.1 14.7 %collective-permute-start.8 = (bf16[256,768]{1,0:T(8,128)(2,1)S(1)}, bf16[256,768]{1,0:T(8,128)(2,1)S(1)}, u32[]{:S(2)}, u32[]{:S(2)}) collective-permute-start(bf16[256,768]{1,0:T(8,128)(2,1)S(1)} %collective-permute-done.3), channel_id=1, source_target_pairs={{2,0},{3,1},{0,2},{1,3},{6,4},{7,5},{4,6},{5,7},{10,8},{11,9},{8,1... | collective-permute-start | bytes 1179656 | tf_op jit(solution)/shard_map/ppermute | solution.py:1080
  35.8 22.1 %collective-permute-start.11 = (bf16[4,48,768]{2,1,0:T(8,128)(2,1)S(1)}, bf16[4,48,768]{2,1,0:T(8,128)(2,1)S(1)}, u32[]{:S(2)}, u32[]{:S(2)}) collective-permute-start(bf16[4,48,768]{2,1,0:T(8,128)(2,1)S(1)} %gather_z.6.refs_0_), channel_id=1, source_target_pairs={{8,0},{9,1},{10,2},{11,3},{12,4},{13,5},{14,6},{15,7},{0,8},{1,9},... | collective-permute-start | bytes 884744 | tf_op jit(solution)/shard_map/ppermute | solution.py:1080
  39.9 18.0 %collective-permute-start.9 = (bf16[4,48,768]{2,1,0:T(8,128)(2,1)S(1)}, bf16[4,48,768]{2,1,0:T(8,128)(2,1)S(1)}, u32[]{:S(2)}, u32[]{:S(2)}) collective-permute-start(bf16[4,48,768]{2,1,0:T(8,128)(2,1)S(1)} %get-tuple-element.660.refs_2_), channel_id=1, source_target_pairs={{4,0},{5,1},{6,2},{7,3},{0,4},{1,5},{2,6},{3,7},{12,8},{13,9},{14,... | collective-permute-start | bytes 884744 | tf_op jit(solution)/shard_map/ppermute | solution.py:1080
  41.4 16.5 %collective-permute-start.10 = (bf16[4,48,768]{2,1,0:T(8,128)(2,1)S(1)}, bf16[4,48,768]{2,1,0:T(8,128)(2,1)S(1)}, u32[]{:S(2)}, u32[]{:S(2)}) collective-permute-start(bf16[4,48,768]{2,1,0:T(8,128)(2,1)S(1)} %get-tuple-element.661.refs_3_), channel_id=1, source_target_pairs={{1,0},{0,1},{3,2},{2,3},{5,4},{4,5},{7,6},{6,7},{9,8},{8,9},{11,10... | collective-permute-start | bytes 884744 | tf_op jit(solution)/shard_map/ppermute | solution.py:1080
  42.7 15.2 %collective-permute-start.12 = (bf16[2,48,768]{2,1,0:T(8,128)(2,1)S(1)}, bf16[2,48,768]{2,1,0:T(8,128)(2,1)S(1)}, u32[]{:S(2)}, u32[]{:S(2)}) collective-permute-start(bf16[2,48,768]{2,1,0:T(8,128)(2,1)S(1)} %pack.7.refs_0_), channel_id=1, source_target_pairs={{16,0},{17,1},{18,2},{19,3},{20,4},{21,5},{22,6},{23,7},{24,8},{25... | collective-permute-start | bytes 442376 | tf_op jit(solution)/shard_map/ppermute | solution.py:1080
  59.6 24.8 %collective-permute-start.14 = (bf16[12,48,768]{2,1,0:T(8,128)(2,1)S(1)}, bf16[12,48,768]{2,1,0:T(8,128)(2,1)S(1)}, u32[]{:S(2)}, u32[]{:S(2)}) collective-permute-start(bf16[12,48,768]{2,1,0:T(8,128)(2,1)S(1)} %get-tuple-element.678.refs_2_), channel_id=1, source_target_pairs={{4,0},{5,1},{6,2},{7,3},{0,4},{1,5},{2,6},{3,7},{12,8},{13,9},{14,... | collective-permute-start | bytes 2654216 | tf_op jit(solution)/shard_map/ppermute | solution.py:1080
  60.3 24.0 %collective-permute-start.15 = (bf16[12,48,768]{2,1,0:T(8,128)(2,1)S(1)}, bf16[12,48,768]{2,1,0:T(8,128)(2,1)S(1)}, u32[]{:S(2)}, u32[]{:S(2)}) collective-permute-start(bf16[12,48,768]{2,1,0:T(8,128)(2,1)S(1)} %get-tuple-element.679.refs_3_), channel_id=1, source_target_pairs={{1,0},{0,1},{3,2},{2,3},{5,4},{4,5},{7,6},{6,7},{9,8},{8,9},{11,10... | collective-permute-start | bytes 2654216 | tf_op jit(solution)/shard_map/ppermute | solution.py:1080
  62.6 21.8 %collective-permute-start.17 = (bf16[6,48,768]{2,1,0:T(8,128)(2,1)S(1)}, bf16[6,48,768]{2,1,0:T(8,128)(2,1)S(1)}, u32[]{:S(2)}, u32[]{:S(2)}) collective-permute-start(bf16[6,48,768]{2,1,0:T(8,128)(2,1)S(1)} %pack.8.refs_0_), channel_id=1, source_target_pairs={{16,0},{17,1},{18,2},{19,3},{20,4},{21,5},{22,6},{23,7},{24,8},{25... | collective-permute-start | bytes 1327112 | tf_op jit(solution)/shard_map/ppermute | solution.py:1080
  63.6 20.7 %collective-permute-start.16 = (bf16[4,48,768]{2,1,0:T(8,128)(2,1)S(1)}, bf16[4,48,768]{2,1,0:T(8,128)(2,1)S(1)}, u32[]{:S(2)}, u32[]{:S(2)}) collective-permute-start(bf16[4,48,768]{2,1,0:T(8,128)(2,1)S(1)} %gather_z.7.refs_0_), channel_id=1, source_target_pairs={{8,0},{9,1},{10,2},{11,3},{12,4},{13,5},{14,6},{15,7},{0,8},{1,9},... | collective-permute-start | bytes 884744 | tf_op jit(solution)/shard_map/ppermute | solution.py:1080
  65.5 18.2 %collective-permute-start.18 = (f32[3,12,768]{2,1,0:T(8,128)S(1)}, f32[3,12,768]{2,1,0:T(8,128)S(1)}, u32[]{:S(2)}, u32[]{:S(2)}) collective-permute-start(f32[3,12,768]{2,1,0:T(8,128)S(1)} %add.17), channel_id=1, source_target_pairs={{8,0},{9,1},{10,2},{11,3},{12,4},{13,5},{14,6},{15,7},{0,8},{1,9},... | collective-permute-start | bytes 331784 | tf_op jit(solution)/shard_map/ppermute | solution.py:1080
  86.6 24.7 %collective-permute-start.21 = (bf16[32,48,768]{2,1,0:T(8,128)(2,1)S(1)}, bf16[32,48,768]{2,1,0:T(8,128)(2,1)S(1)}, u32[]{:S(2)}, u32[]{:S(2)}) collective-permute-start(bf16[32,48,768]{2,1,0:T(8,128)(2,1)S(1)} %get-tuple-element.729.refs_7_.refs_11_.refs_4_), channel_id=1, source_target_pairs={{2,0},{3,1},{0,2},{1,3},{6,4},{7,5},{4,6},{5,7},{10,8},{11,9},{8,1... | collective-permute-start | bytes 7077896 | tf_op jit(solution)/shard_map/ppermute | solution.py:1080
  87.7 22.1 %collective-permute-start.22 = (bf16[12,48,768]{2,1,0:T(8,128)(2,1)S(1)}, bf16[12,48,768]{2,1,0:T(8,128)(2,1)S(1)}, u32[]{:S(2)}, u32[]{:S(2)}) collective-permute-start(bf16[12,48,768]{2,1,0:T(8,128)(2,1)S(1)} %gather_z.8.refs_0_), channel_id=1, source_target_pairs={{8,0},{9,1},{10,2},{11,3},{12,4},{13,5},{14,6},{15,7},{0,8},{1,9},... | collective-permute-start | bytes 2654216 | tf_op jit(solution)/shard_map/ppermute | solution.py:1080
  87.8 22.1 %collective-permute-start.19 = (bf16[12,48,768]{2,1,0:T(8,128)(2,1)S(1)}, bf16[12,48,768]{2,1,0:T(8,128)(2,1)S(1)}, u32[]{:S(2)}, u32[]{:S(2)}) collective-permute-start(bf16[12,48,768]{2,1,0:T(8,128)(2,1)S(1)} %get-tuple-element.696.refs_2_), channel_id=1, source_target_pairs={{4,0},{5,1},{6,2},{7,3},{0,4},{1,5},{2,6},{3,7},{12,8},{13,9},{14,... | collective-permute-start | bytes 2654216 | tf_op jit(solution)/shard_map/ppermute | solution.py:1080
  89.6 21.8 %collective-permute-start.20 = (bf16[12,48,768]{2,1,0:T(8,128)(2,1)S(1)}, bf16[12,48,768]{2,1,0:T(8,128)(2,1)S(1)}, u32[]{:S(2)}, u32[]{:S(2)}) collective-permute-start(bf16[12,48,768]{2,1,0:T(8,128)(2,1)S(1)} %get-tuple-element.697.refs_3_), channel_id=1, source_target_pairs={{1,0},{0,1},{3,2},{2,3},{5,4},{4,5},{7,6},{6,7},{9,8},{8,9},{11,10... | collective-permute-start | bytes 2654216 | tf_op jit(solution)/shard_map/ppermute | solution.py:1080
  117.9 25.1 %collective-permute-start.25 = (bf16[32,48,768]{2,1,0:T(8,128)(2,1)}, bf16[32,48,768]{2,1,0:T(8,128)(2,1)}, u32[]{:S(2)}, u32[]{:S(2)}) collective-permute-start(bf16[32,48,768]{2,1,0:T(8,128)(2,1)} %get-tuple-element.761.refs_4_.refs_7_), channel_id=1, source_target_pairs={{2,0},{3,1},{0,2},{1,3},{6,4},{7,5},{4,6},{5,7},{10,8},{11,9},{8,1... | collective-permute-start | bytes 7077896 | tf_op jit(solution)/shard_map/ppermute | solution.py:1080
  117.9 25.1 %collective-permute-start.23 = (bf16[12,48,768]{2,1,0:T(8,128)(2,1)}, bf16[12,48,768]{2,1,0:T(8,128)(2,1)}, u32[]{:S(2)}, u32[]{:S(2)}) collective-permute-start(bf16[12,48,768]{2,1,0:T(8,128)(2,1)} %get-tuple-element.715.refs_2_), channel_id=1, source_target_pairs={{4,0},{5,1},{6,2},{7,3},{0,4},{1,5},{2,6},{3,7},{12,8},{13,9},{14,... | collective-permute-start | bytes 2654216 | tf_op jit(solution)/shard_map/ppermute | solution.py:1080
  118.3 24.8 %collective-permute-start.24 = (bf16[12,48,768]{2,1,0:T(8,128)(2,1)}, bf16[12,48,768]{2,1,0:T(8,128)(2,1)}, u32[]{:S(2)}, u32[]{:S(2)}) collective-permute-start(bf16[12,48,768]{2,1,0:T(8,128)(2,1)} %get-tuple-element.716.refs_3_), channel_id=1, source_target_pairs={{1,0},{0,1},{3,2},{2,3},{5,4},{4,5},{7,6},{6,7},{9,8},{8,9},{11,10... | collective-permute-start | bytes 2654216 | tf_op jit(solution)/shard_map/ppermute | solution.py:1080
  120.2 22.8 %collective-permute-start.26 = (bf16[6,48,768]{2,1,0:T(8,128)(2,1)}, bf16[6,48,768]{2,1,0:T(8,128)(2,1)}, u32[]{:S(2)}, u32[]{:S(2)}) collective-permute-start(bf16[6,48,768]{2,1,0:T(8,128)(2,1)} %pack.9.refs_0_), channel_id=1, source_target_pairs={{16,0},{17,1},{18,2},{19,3},{20,4},{21,5},{22,6},{23,7},{24,8},{25... | collective-permute-start | bytes 1327112 | tf_op jit(solution)/shard_map/ppermute | solution.py:1080
  146.5 25.5 %collective-permute-start.29 = (bf16[32,48,768]{2,1,0:T(8,128)(2,1)S(1)}, bf16[32,48,768]{2,1,0:T(8,128)(2,1)S(1)}, u32[]{:S(2)}, u32[]{:S(2)}) collective-permute-start(bf16[32,48,768]{2,1,0:T(8,128)(2,1)S(1)} %get-tuple-element.779.refs_4_.refs_9_), channel_id=1, source_target_pairs={{2,0},{3,1},{0,2},{1,3},{6,4},{7,5},{4,6},{5,7},{10,8},{11,9},{8,1... | collective-permute-start | bytes 7077896 | tf_op jit(solution)/shard_map/ppermute | solution.py:1080
  146.6 14.3 %collective-permute-start.32 = (bf16[3,2,4,48,256]{4,3,2,1,0:T(8,128)(2,1)S(1)}, bf16[3,2,4,48,256]{4,3,2,1,0:T(8,128)(2,1)S(1)}, u32[]{:S(2)}, u32[]{:S(2)}) collective-permute-start(bf16[3,2,4,48,256]{4,3,2,1,0:T(8,128)(2,1)S(1)} %get-tuple-element.758), channel_id=1, source_target_pairs={{2,0},{3,1},{0,2},{1,3},{6,4},{7,5},{4,6},{5,7},{10,8},{11,9},{8,1... | collective-permute-start | bytes 1769480 | tf_op jit(solution)/shard_map/ppermute | solution.py:1080
  148.8 21.7 %collective-permute-start.30 = (bf16[12,48,768]{2,1,0:T(8,128)(2,1)S(1)}, bf16[12,48,768]{2,1,0:T(8,128)(2,1)S(1)}, u32[]{:S(2)}, u32[]{:S(2)}) collective-permute-start(bf16[12,48,768]{2,1,0:T(8,128)(2,1)S(1)} %gather_z.9.refs_0_), channel_id=1, source_target_pairs={{8,0},{9,1},{10,2},{11,3},{12,4},{13,5},{14,6},{15,7},{0,8},{1,9},... | collective-permute-start | bytes 2654216 | tf_op jit(solution)/shard_map/ppermute | solution.py:1080
  148.9 21.7 %collective-permute-start.27 = (bf16[12,48,768]{2,1,0:T(8,128)(2,1)S(1)}, bf16[12,48,768]{2,1,0:T(8,128)(2,1)S(1)}, u32[]{:S(2)}, u32[]{:S(2)}) collective-permute-start(bf16[12,48,768]{2,1,0:T(8,128)(2,1)S(1)} %get-tuple-element.745.refs_2_), channel_id=1, source_target_pairs={{4,0},{5,1},{6,2},{7,3},{0,4},{1,5},{2,6},{3,7},{12,8},{13,9},{14,... | collective-permute-start | bytes 2654216 | tf_op jit(solution)/shard_map/ppermute | solution.py:1080
  150.6 21.4 %collective-permute-start.28 = (bf16[12,48,768]{2,1,0:T(8,128)(2,1)S(1)}, bf16[12,48,768]{2,1,0:T(8,128)(2,1)S(1)}, u32[]{:S(2)}, u32[]{:S(2)}) collective-permute-start(bf16[12,48,768]{2,1,0:T(8,128)(2,1)S(1)} %get-tuple-element.746.refs_3_), channel_id=1, source_target_pairs={{1,0},{0,1},{3,2},{2,3},{5,4},{4,5},{7,6},{6,7},{9,8},{8,9},{11,10... | collective-permute-start | bytes 2654216 | tf_op jit(solution)/shard_map/ppermute | solution.py:1080
  174.2 22.2 %collective-permute-start.35 = (bf16[32,48,768]{2,1,0:T(8,128)(2,1)S(1)}, bf16[32,48,768]{2,1,0:T(8,128)(2,1)S(1)}, u32[]{:S(2)}, u32[]{:S(2)}) collective-permute-start(bf16[32,48,768]{2,1,0:T(8,128)(2,1)S(1)} %get-tuple-element.805.refs_7_.refs_11_.refs_4_), channel_id=1, source_target_pairs={{2,0},{3,1},{0,2},{1,3},{6,4},{7,5},{4,6},{5,7},{10,8},{11,9},{8,1... | collective-permute-start | bytes 7077896 | tf_op jit(solution)/shard_map/ppermute | solution.py:1080
  174.3 22.1 %collective-permute-start.33 = (bf16[12,48,768]{2,1,0:T(8,128)(2,1)S(1)}, bf16[12,48,768]{2,1,0:T(8,128)(2,1)S(1)}, u32[]{:S(2)}, u32[]{:S(2)}) collective-permute-start(bf16[12,48,768]{2,1,0:T(8,128)(2,1)S(1)} %get-tuple-element.771.refs_2_), channel_id=1, source_target_pairs={{4,0},{5,1},{6,2},{7,3},{0,4},{1,5},{2,6},{3,7},{12,8},{13,9},{14,... | collective-permute-start | bytes 2654216 | tf_op jit(solution)/shard_map/ppermute | solution.py:1080
  174.7 21.7 %collective-permute-start.34 = (bf16[12,48,768]{2,1,0:T(8,128)(2,1)S(1)}, bf16[12,48,768]{2,1,0:T(8,128)(2,1)S(1)}, u32[]{:S(2)}, u32[]{:S(2)}) collective-permute-start(bf16[12,48,768]{2,1,0:T(8,128)(2,1)S(1)} %get-tuple-element.772.refs_3_), channel_id=1, source_target_pairs={{1,0},{0,1},{3,2},{2,3},{5,4},{4,5},{7,6},{6,7},{9,8},{8,9},{11,10... | collective-permute-start | bytes 2654216 | tf_op jit(solution)/shard_map/ppermute | solution.py:1080
  198.7 23.5 %collective-permute-start.39 = (bf16[32,48,768]{2,1,0:T(8,128)(2,1)S(1)}, bf16[32,48,768]{2,1,0:T(8,128)(2,1)S(1)}, u32[]{:S(2)}, u32[]{:S(2)}) collective-permute-start(bf16[32,48,768]{2,1,0:T(8,128)(2,1)S(1)} %get-tuple-element.835.refs_4_.refs_7_), channel_id=1, source_target_pairs={{2,0},{3,1},{0,2},{1,3},{6,4},{7,5},{4,6},{5,7},{10,8},{11,9},{8,1... | collective-permute-start | bytes 7077896 | tf_op jit(solution)/shard_map/ppermute | solution.py:1080
  198.8 22.1 %collective-permute-start.37 = (bf16[12,48,768]{2,1,0:T(8,128)(2,1)S(1)}, bf16[12,48,768]{2,1,0:T(8,128)(2,1)S(1)}, u32[]{:S(2)}, u32[]{:S(2)}) collective-permute-start(bf16[12,48,768]{2,1,0:T(8,128)(2,1)S(1)} %get-tuple-element.799.refs_2_), channel_id=1, source_target_pairs={{4,0},{5,1},{6,2},{7,3},{0,4},{1,5},{2,6},{3,7},{12,8},{13,9},{14,... | collective-permute-start | bytes 2654216 | tf_op jit(solution)/shard_map/ppermute | solution.py:1080
  200.5 21.7 %collective-permute-start.38 = (bf16[12,48,768]{2,1,0:T(8,128)(2,1)S(1)}, bf16[12,48,768]{2,1,0:T(8,128)(2,1)S(1)}, u32[]{:S(2)}, u32[]{:S(2)}) collective-permute-start(bf16[12,48,768]{2,1,0:T(8,128)(2,1)S(1)} %get-tuple-element.800.refs_3_), channel_id=1, source_target_pairs={{1,0},{0,1},{3,2},{2,3},{5,4},{4,5},{7,6},{6,7},{9,8},{8,9},{11,10... | collective-permute-start | bytes 2654216 | tf_op jit(solution)/shard_map/ppermute | solution.py:1080
  224.5 22.2 %collective-permute-start.42 = (bf16[32,48,768]{2,1,0:T(8,128)(2,1)S(1)}, bf16[32,48,768]{2,1,0:T(8,128)(2,1)S(1)}, u32[]{:S(2)}, u32[]{:S(2)}) collective-permute-start(bf16[32,48,768]{2,1,0:T(8,128)(2,1)S(1)} %get-tuple-element.851.refs_4_.refs_9_), channel_id=1, source_target_pairs={{2,0},{3,1},{0,2},{1,3},{6,4},{7,5},{4,6},{5,7},{10,8},{11,9},{8,1... | collective-permute-start | bytes 7077896 | tf_op jit(solution)/shard_map/ppermute | solution.py:1080
  224.6 22.1 %collective-permute-start.40 = (bf16[12,48,768]{2,1,0:T(8,128)(2,1)S(1)}, bf16[12,48,768]{2,1,0:T(8,128)(2,1)S(1)}, u32[]{:S(2)}, u32[]{:S(2)}) collective-permute-start(bf16[12,48,768]{2,1,0:T(8,128)(2,1)S(1)} %get-tuple-element.821.refs_2_), channel_id=1, source_target_pairs={{4,0},{5,1},{6,2},{7,3},{0,4},{1,5},{2,6},{3,7},{12,8},{13,9},{14,... | collective-permute-start | bytes 2654216 | tf_op jit(solution)/shard_map/ppermute | solution.py:1080
  225.0 21.7 %collective-permute-start.41 = (bf16[12,48,768]{2,1,0:T(8,128)(2,1)S(1)}, bf16[12,48,768]{2,1,0:T(8,128)(2,1)S(1)}, u32[]{:S(2)}, u32[]{:S(2)}) collective-permute-start(bf16[12,48,768]{2,1,0:T(8,128)(2,1)S(1)} %get-tuple-element.822.refs_3_), channel_id=1, source_target_pairs={{1,0},{0,1},{3,2},{2,3},{5,4},{4,5},{7,6},{6,7},{9,8},{8,9},{11,10... | collective-permute-start | bytes 2654216 | tf_op jit(solution)/shard_map/ppermute | solution.py:1080
  249.0 23.5 %collective-permute-start.47 = (bf16[32,48,768]{2,1,0:T(8,128)(2,1)S(1)}, bf16[32,48,768]{2,1,0:T(8,128)(2,1)S(1)}, u32[]{:S(2)}, u32[]{:S(2)}) collective-permute-start(bf16[32,48,768]{2,1,0:T(8,128)(2,1)S(1)} %get-tuple-element.875.refs_7_.refs_11_.refs_4_), channel_id=1, source_target_pairs={{2,0},{3,1},{0,2},{1,3},{6,4},{7,5},{4,6},{5,7},{10,8},{11,9},{8,1... | collective-permute-start | bytes 7077896 | tf_op jit(solution)/shard_map/ppermute | solution.py:1080
  249.0 22.1 %collective-permute-start.45 = (bf16[12,48,768]{2,1,0:T(8,128)(2,1)S(1)}, bf16[12,48,768]{2,1,0:T(8,128)(2,1)S(1)}, u32[]{:S(2)}, u32[]{:S(2)}) collective-permute-start(bf16[12,48,768]{2,1,0:T(8,128)(2,1)S(1)} %get-tuple-element.845.refs_0_), channel_id=1, source_target_pairs={{4,0},{5,1},{6,2},{7,3},{0,4},{1,5},{2,6},{3,7},{12,8},{13,9},{14,... | collective-permute-start | bytes 2654216 | tf_op jit(solution)/shard_map/ppermute | solution.py:1080
  250.8 21.7 %collective-permute-start.46 = (bf16[12,48,768]{2,1,0:T(8,128)(2,1)S(1)}, bf16[12,48,768]{2,1,0:T(8,128)(2,1)S(1)}, u32[]{:S(2)}, u32[]{:S(2)}) collective-permute-start(bf16[12,48,768]{2,1,0:T(8,128)(2,1)S(1)} %get-tuple-element.846.refs_1_), channel_id=1, source_target_pairs={{1,0},{0,1},{3,2},{2,3},{5,4},{4,5},{7,6},{6,7},{9,8},{8,9},{11,10... | collective-permute-start | bytes 2654216 | tf_op jit(solution)/shard_map/ppermute | solution.py:1080
  273.9 18.8 %collective-permute-start.51 = (bf16[32,48,768]{2,1,0:T(8,128)(2,1)S(1)}, bf16[32,48,768]{2,1,0:T(8,128)(2,1)S(1)}, u32[]{:S(2)}, u32[]{:S(2)}) collective-permute-start(bf16[32,48,768]{2,1,0:T(8,128)(2,1)S(1)} %get-tuple-element.900.refs_4_.refs_7_), channel_id=1, source_target_pairs={{2,0},{3,1},{0,2},{1,3},{6,4},{7,5},{4,6},{5,7},{10,8},{11,9},{8,1... | collective-permute-start | bytes 7077896 | tf_op jit(solution)/shard_map/ppermute | solution.py:1080
  273.9 18.7 %collective-permute-start.49 = (bf16[8,48,768]{2,1,0:T(8,128)(2,1)S(1)}, bf16[8,48,768]{2,1,0:T(8,128)(2,1)S(1)}, u32[]{:S(2)}, u32[]{:S(2)}) collective-permute-start(bf16[8,48,768]{2,1,0:T(8,128)(2,1)S(1)} %get-tuple-element.869.refs_0_), channel_id=1, source_target_pairs={{4,0},{5,1},{6,2},{7,3},{0,4},{1,5},{2,6},{3,7},{12,8},{13,9},{14,... | collective-permute-start | bytes 1769480 | tf_op jit(solution)/shard_map/ppermute | solution.py:1080
  274.4 18.3 %collective-permute-start.50 = (bf16[8,48,768]{2,1,0:T(8,128)(2,1)S(1)}, bf16[8,48,768]{2,1,0:T(8,128)(2,1)S(1)}, u32[]{:S(2)}, u32[]{:S(2)}) collective-permute-start(bf16[8,48,768]{2,1,0:T(8,128)(2,1)S(1)} %get-tuple-element.870.refs_1_), channel_id=1, source_target_pairs={{1,0},{0,1},{3,2},{2,3},{5,4},{4,5},{7,6},{6,7},{9,8},{8,9},{11,10... | collective-permute-start | bytes 1769480 | tf_op jit(solution)/shard_map/ppermute | solution.py:1080
  276.0 16.6 %collective-permute-start.52 = (bf16[256,768]{1,0:T(8,128)(2,1)S(1)}, bf16[256,768]{1,0:T(8,128)(2,1)S(1)}, u32[]{:S(2)}, u32[]{:S(2)}) collective-permute-start(bf16[256,768]{1,0:T(8,128)(2,1)S(1)} %bitcast.51), channel_id=1, source_target_pairs={{0,0},{2,1},{1,2},{3,3},{4,4},{6,5},{5,6},{7,7},{8,8},{10,9},{9,10... | collective-permute-start | bytes 1179656 | tf_op jit(solution)/shard_map/ppermute | solution.py:1080
  324.7 15.4 %collective-permute-start.60 = (bf16[8,48,768]{2,1,0:T(8,128)(2,1)S(1)}, bf16[8,48,768]{2,1,0:T(8,128)(2,1)S(1)}, u32[]{:S(2)}, u32[]{:S(2)}) collective-permute-start(bf16[8,48,768]{2,1,0:T(8,128)(2,1)S(1)} %get-tuple-element.921.refs_13_), channel_id=1, source_target_pairs={{4,0},{5,1},{6,2},{7,3},{0,4},{1,5},{2,6},{3,7},{12,8},{13,9},{14,... | collective-permute-start | bytes 1769480 | tf_op jit(solution)/shard_map/ppermute | solution.py:1080
  326.4 15.1 %collective-permute-start.61 = (bf16[8,48,768]{2,1,0:T(8,128)(2,1)S(1)}, bf16[8,48,768]{2,1,0:T(8,128)(2,1)S(1)}, u32[]{:S(2)}, u32[]{:S(2)}) collective-permute-start(bf16[8,48,768]{2,1,0:T(8,128)(2,1)S(1)} %get-tuple-element.922.refs_14_), channel_id=1, source_target_pairs={{1,0},{0,1},{3,2},{2,3},{5,4},{4,5},{7,6},{6,7},{9,8},{8,9},{11,10... | collective-permute-start | bytes 1769480 | tf_op jit(solution)/shard_map/ppermute | solution.py:1080
  349.8 22.1 %collective-permute-start.63 = (bf16[12,48,768]{2,1,0:T(8,128)(2,1)S(1)}, bf16[12,48,768]{2,1,0:T(8,128)(2,1)S(1)}, u32[]{:S(2)}, u32[]{:S(2)}) collective-permute-start(bf16[12,48,768]{2,1,0:T(8,128)(2,1)S(1)} %get-tuple-element.945), channel_id=1, source_target_pairs={{4,0},{5,1},{6,2},{7,3},{0,4},{1,5},{2,6},{3,7},{12,8},{13,9},{14,... | collective-permute-start | bytes 2654216 | tf_op jit(solution)/shard_map/ppermute | solution.py:1080
  350.2 21.8 %collective-permute-start.64 = (bf16[12,48,768]{2,1,0:T(8,128)(2,1)S(1)}, bf16[12,48,768]{2,1,0:T(8,128)(2,1)S(1)}, u32[]{:S(2)}, u32[]{:S(2)}) collective-permute-start(bf16[12,48,768]{2,1,0:T(8,128)(2,1)S(1)} %get-tuple-element.946), channel_id=1, source_target_pairs={{1,0},{0,1},{3,2},{2,3},{5,4},{4,5},{7,6},{6,7},{9,8},{8,9},{11,10... | collective-permute-start | bytes 2654216 | tf_op jit(solution)/shard_map/ppermute | solution.py:1080
  372.5 21.2 %collective-permute-start.66 = (bf16[12,48,768]{2,1,0:T(8,128)(2,1)S(1)}, bf16[12,48,768]{2,1,0:T(8,128)(2,1)S(1)}, u32[]{:S(2)}, u32[]{:S(2)}) collective-permute-start(bf16[12,48,768]{2,1,0:T(8,128)(2,1)S(1)} %get-tuple-element.982), channel_id=1, source_target_pairs={{4,0},{5,1},{6,2},{7,3},{0,4},{1,5},{2,6},{3,7},{12,8},{13,9},{14,... | collective-permute-start | bytes 2654216 | tf_op jit(solution)/shard_map/ppermute | solution.py:1080
  374.2 20.6 %collective-permute-start.67 = (bf16[12,48,768]{2,1,0:T(8,128)(2,1)S(1)}, bf16[12,48,768]{2,1,0:T(8,128)(2,1)S(1)}, u32[]{:S(2)}, u32[]{:S(2)}) collective-permute-start(bf16[12,48,768]{2,1,0:T(8,128)(2,1)S(1)} %get-tuple-element.983), channel_id=1, source_target_pairs={{1,0},{0,1},{3,2},{2,3},{5,4},{4,5},{7,6},{6,7},{9,8},{8,9},{11,10... | collective-permute-start | bytes 2654216 | tf_op jit(solution)/shard_map/ppermute | solution.py:1080
  395.6 22.1 %collective-permute-start.71 = (bf16[12,48,768]{2,1,0:T(8,128)(2,1)S(1)}, bf16[12,48,768]{2,1,0:T(8,128)(2,1)S(1)}, u32[]{:S(2)}, u32[]{:S(2)}) collective-permute-start(bf16[12,48,768]{2,1,0:T(8,128)(2,1)S(1)} %get-tuple-element.1012), channel_id=1, source_target_pairs={{4,0},{5,1},{6,2},{7,3},{0,4},{1,5},{2,6},{3,7},{12,8},{13,9},{14,... | collective-permute-start | bytes 2654216 | tf_op jit(solution)/shard_map/ppermute | solution.py:1080
  396.3 21.7 %collective-permute-start.72 = (bf16[12,48,768]{2,1,0:T(8,128)(2,1)S(1)}, bf16[12,48,768]{2,1,0:T(8,128)(2,1)S(1)}, u32[]{:S(2)}, u32[]{:S(2)}) collective-permute-start(bf16[12,48,768]{2,1,0:T(8,128)(2,1)S(1)} %get-tuple-element.1013), channel_id=1, source_target_pairs={{1,0},{0,1},{3,2},{2,3},{5,4},{4,5},{7,6},{6,7},{9,8},{8,9},{11,10... | collective-permute-start | bytes 2654216 | tf_op jit(solution)/shard_map/ppermute | solution.py:1080
  418.6 25.3 %collective-permute-start.77 = (bf16[14,48,768]{2,1,0:T(8,128)(2,1)S(1)}, bf16[14,48,768]{2,1,0:T(8,128)(2,1)S(1)}, u32[]{:S(2)}, u32[]{:S(2)}) collective-permute-start(bf16[14,48,768]{2,1,0:T(8,128)(2,1)S(1)} %get-tuple-element.1043), channel_id=1, source_target_pairs={{1,0},{0,1},{3,2},{2,3},{5,4},{4,5},{7,6},{6,7},{9,8},{8,9},{11,10... | collective-permute-start | bytes 3096584 | tf_op jit(solution)/shard_map/ppermute | solution.py:1080
  420.1 21.8 %collective-permute-start.76 = (bf16[12,48,768]{2,1,0:T(8,128)(2,1)S(1)}, bf16[12,48,768]{2,1,0:T(8,128)(2,1)S(1)}, u32[]{:S(2)}, u32[]{:S(2)}) collective-permute-start(bf16[12,48,768]{2,1,0:T(8,128)(2,1)S(1)} %get-tuple-element.1042), channel_id=1, source_target_pairs={{4,0},{5,1},{6,2},{7,3},{0,4},{1,5},{2,6},{3,7},{12,8},{13,9},{14,... | collective-permute-start | bytes 2654216 | tf_op jit(solution)/shard_map/ppermute | solution.py:1080
  444.5 24.5 %collective-permute-start.82 = (bf16[14,48,768]{2,1,0:T(8,128)(2,1)S(1)}, bf16[14,48,768]{2,1,0:T(8,128)(2,1)S(1)}, u32[]{:S(2)}, u32[]{:S(2)}) collective-permute-start(bf16[14,48,768]{2,1,0:T(8,128)(2,1)S(1)} %get-tuple-element.1083), channel_id=1, source_target_pairs={{1,0},{0,1},{3,2},{2,3},{5,4},{4,5},{7,6},{6,7},{9,8},{8,9},{11,10... | collective-permute-start | bytes 3096584 | tf_op jit(solution)/shard_map/ppermute | solution.py:1080
  446.0 21.0 %collective-permute-start.81 = (bf16[12,48,768]{2,1,0:T(8,128)(2,1)S(1)}, bf16[12,48,768]{2,1,0:T(8,128)(2,1)S(1)}, u32[]{:S(2)}, u32[]{:S(2)}) collective-permute-start(bf16[12,48,768]{2,1,0:T(8,128)(2,1)S(1)} %get-tuple-element.1082), channel_id=1, source_target_pairs={{4,0},{5,1},{6,2},{7,3},{0,4},{1,5},{2,6},{3,7},{12,8},{13,9},{14,... | collective-permute-start | bytes 2654216 | tf_op jit(solution)/shard_map/ppermute | solution.py:1080
  469.0 13.6 %collective-permute-start.89 = (bf16[256,3840]{1,0:T(8,128)(2,1)S(1)}, bf16[256,3840]{1,0:T(8,128)(2,1)S(1)}, u32[]{:S(2)}, u32[]{:S(2)}) collective-permute-start(bf16[256,3840]{1,0:T(8,128)(2,1)S(1)} %get-tuple-element.1125.da_ref), channel_id=1, source_target_pairs={{2,0},{3,1},{0,2},{1,3},{6,4},{7,5},{4,6},{5,7},{10,8},{11,9},{8,1... | collective-permute-start | bytes 5898248 | tf_op jit(solution)/shard_map/ppermute | solution.py:1080
  469.7 25.3 %collective-permute-start.87 = (bf16[14,48,768]{2,1,0:T(8,128)(2,1)S(1)}, bf16[14,48,768]{2,1,0:T(8,128)(2,1)S(1)}, u32[]{:S(2)}, u32[]{:S(2)}) collective-permute-start(bf16[14,48,768]{2,1,0:T(8,128)(2,1)S(1)} %get-tuple-element.1116), channel_id=1, source_target_pairs={{1,0},{0,1},{3,2},{2,3},{5,4},{4,5},{7,6},{6,7},{9,8},{8,9},{11,10... | collective-permute-start | bytes 3096584 | tf_op jit(solution)/shard_map/ppermute | solution.py:1080
  471.2 21.8 %collective-permute-start.86 = (bf16[12,48,768]{2,1,0:T(8,128)(2,1)S(1)}, bf16[12,48,768]{2,1,0:T(8,128)(2,1)S(1)}, u32[]{:S(2)}, u32[]{:S(2)}) collective-permute-start(bf16[12,48,768]{2,1,0:T(8,128)(2,1)S(1)} %get-tuple-element.1115), channel_id=1, source_target_pairs={{4,0},{5,1},{6,2},{7,3},{0,4},{1,5},{2,6},{3,7},{12,8},{13,9},{14,... | collective-permute-start | bytes 2654216 | tf_op jit(solution)/shard_map/ppermute | solution.py:1080
  495.6 25.3 %collective-permute-start.92 = (bf16[14,48,768]{2,1,0:T(8,128)(2,1)S(1)}, bf16[14,48,768]{2,1,0:T(8,128)(2,1)S(1)}, u32[]{:S(2)}, u32[]{:S(2)}) collective-permute-start(bf16[14,48,768]{2,1,0:T(8,128)(2,1)S(1)} %get-tuple-element.1147), channel_id=1, source_target_pairs={{1,0},{0,1},{3,2},{2,3},{5,4},{4,5},{7,6},{6,7},{9,8},{8,9},{11,10... | collective-permute-start | bytes 3096584 | tf_op jit(solution)/shard_map/ppermute | solution.py:1080
  497.0 21.8 %collective-permute-start.91 = (bf16[12,48,768]{2,1,0:T(8,128)(2,1)S(1)}, bf16[12,48,768]{2,1,0:T(8,128)(2,1)S(1)}, u32[]{:S(2)}, u32[]{:S(2)}) collective-permute-start(bf16[12,48,768]{2,1,0:T(8,128)(2,1)S(1)} %get-tuple-element.1146), channel_id=1, source_target_pairs={{4,0},{5,1},{6,2},{7,3},{0,4},{1,5},{2,6},{3,7},{12,8},{13,9},{14,... | collective-permute-start | bytes 2654216 | tf_op jit(solution)/shard_map/ppermute | solution.py:1080
  521.5 24.5 %collective-permute-start.98 = (bf16[14,48,768]{2,1,0:T(8,128)(2,1)S(1)}, bf16[14,48,768]{2,1,0:T(8,128)(2,1)S(1)}, u32[]{:S(2)}, u32[]{:S(2)}) collective-permute-start(bf16[14,48,768]{2,1,0:T(8,128)(2,1)S(1)} %get-tuple-element.1184), channel_id=1, source_target_pairs={{1,0},{0,1},{3,2},{2,3},{5,4},{4,5},{7,6},{6,7},{9,8},{8,9},{11,10... | collective-permute-start | bytes 3096584 | tf_op jit(solution)/shard_map/ppermute | solution.py:1080
  522.9 21.0 %collective-permute-start.97 = (bf16[12,48,768]{2,1,0:T(8,128)(2,1)S(1)}, bf16[12,48,768]{2,1,0:T(8,128)(2,1)S(1)}, u32[]{:S(2)}, u32[]{:S(2)}) collective-permute-start(bf16[12,48,768]{2,1,0:T(8,128)(2,1)S(1)} %get-tuple-element.1183), channel_id=1, source_target_pairs={{4,0},{5,1},{6,2},{7,3},{0,4},{1,5},{2,6},{3,7},{12,8},{13,9},{14,... | collective-permute-start | bytes 2654216 | tf_op jit(solution)/shard_map/ppermute | solution.py:1080
  526.6 19.4 %collective-permute-start.100 = (f32[48,768]{1,0:T(8,128)S(1)}, f32[48,768]{1,0:T(8,128)S(1)}, u32[]{:S(2)}, u32[]{:S(2)}) collective-permute-start(f32[48,768]{1,0:T(8,128)S(1)} %bitcast.42), channel_id=1, source_target_pairs={{2,0},{3,1},{0,2},{1,3},{6,4},{7,5},{4,6},{5,7},{10,8},{11,9},{8,1... | collective-permute-start | bytes 442376 | tf_op jit(solution)/shard_map/ppermute | solution.py:1080
  560.6 17.8 %collective-permute-start.107 = (bf16[5,48,768]{2,1,0:T(8,128)(2,1)S(1)}, bf16[5,48,768]{2,1,0:T(8,128)(2,1)S(1)}, u32[]{:S(2)}, u32[]{:S(2)}) collective-permute-start(bf16[5,48,768]{2,1,0:T(8,128)(2,1)S(1)} %get-tuple-element.1234), channel_id=1, source_target_pairs={{8,0},{9,1},{10,2},{11,3},{12,4},{13,5},{14,6},{15,7},{0,8},{1,9},... | collective-permute-start | bytes 1105928 | tf_op jit(solution)/shard_map/ppermute | solution.py:1080
  562.5 17.8 %collective-permute-start.56 = (bf16[256,768]{1,0:T(8,128)(2,1)S(1)}, bf16[256,768]{1,0:T(8,128)(2,1)S(1)}, u32[]{:S(2)}, u32[]{:S(2)}) collective-permute-start(bf16[256,768]{1,0:T(8,128)(2,1)S(1)} %copy-done.126), channel_id=1, source_target_pairs={{0,0},{2,1},{1,2},{3,3},{4,4},{6,5},{5,6},{7,7},{8,8},{10,9},{9,10... | collective-permute-start | bytes 1179656 | tf_op jit(solution)/shard_map/ppermute | solution.py:1080
  563.1 30.4 %collective-permute-start.95 = (bf16[256,768]{1,0:T(8,128)(2,1)S(1)}, bf16[256,768]{1,0:T(8,128)(2,1)S(1)}, u32[]{:S(2)}, u32[]{:S(2)}) collective-permute-start(bf16[256,768]{1,0:T(8,128)(2,1)S(1)} %get-tuple-element.1166), channel_id=1, source_target_pairs={{0,0},{2,1},{1,2},{3,3},{4,4},{6,5},{5,6},{7,7},{8,8},{10,9},{9,10... | collective-permute-start | bytes 1179656 | tf_op jit(solution)/shard_map/ppermute | solution.py:1080
  564.6 13.8 %collective-permute-start.106 = (bf16[2,48,768]{2,1,0:T(8,128)(2,1)S(1)}, bf16[2,48,768]{2,1,0:T(8,128)(2,1)S(1)}, u32[]{:S(2)}, u32[]{:S(2)}) collective-permute-start(bf16[2,48,768]{2,1,0:T(8,128)(2,1)S(1)} %get-tuple-element.1232), channel_id=1, source_target_pairs={{1,0},{0,1},{3,2},{2,3},{5,4},{4,5},{7,6},{6,7},{9,8},{8,9},{11,10... | collective-permute-start | bytes 442376 | tf_op jit(solution)/shard_map/ppermute | solution.py:1080
  (178 other events, 1550.1 us)

commit v4 on v3

--- a/solution.py
+++ b/solution.py
@@ -491,8 +491,10 @@
     )(pos_w, dyl, dy, gp, n1, c1, vec, *inner_bufs, *outer_bufs, *attn_bufs, *after)
 
 
-def attn_back_kernel(*refs):
-    sources, do_ref, pack_ref, sum_ref, wide_ref = refs[:4], refs[4], refs[5], refs[6], refs[7]
+def attn_back_kernel(waits, *refs):
+    sources, do_ref = refs[:4], refs[4]
+    refs = refs[waits:]
+    pack_ref, sum_ref, wide_ref = refs[5], refs[6], refs[7]
     held, sems, pair_sems = refs[8:12], refs[12], refs[13]
     q_ref, kt_ref, v_ref, p_ref = held
     tokens, width = q_ref.shape
@@ -536,15 +538,15 @@
     sum_ref[...] = jnp.broadcast_to(colsum(low.astype(F32)), sum_ref.shape)
 
 
-def attn_backward(q, kt, v, p, do):
+def attn_backward(q, kt, v, p, do, after=()):
     tokens, width = q.shape
     return pl.pallas_call(
-        attn_back_kernel,
+        functools.partial(attn_back_kernel, len(after)),
         out_shape=(
             shape((5, tokens, width), BF16),
             shape((8, width), F32),
         ),
-        in_specs=[HBM] * 4 + [VMEM],
+        in_specs=[HBM] * 4 + [VMEM] + [ANY] * len(after),
         out_specs=[VMEM] * 2,
         scratch_shapes=[pltpu.VMEM((width, tokens), F32)]
         + [pltpu.VMEM(each.shape, each.dtype) for each in (q, kt, v, p)]
@@ -552,7 +554,7 @@
         compiler_params=params(VMEM_MB),
         cost_estimate=cost(),
         name="attn_backward",
-    )(q, kt, v, p, do)
+    )(q, kt, v, p, do, *after)
 
 
 def input_kernel(first, *refs):
@@ -881,7 +883,7 @@
 
 
 def sum_kernel(config, *refs):
-    fresh, first, second, third, fourth, small = config
+    fresh, first, second, third, fourth, small, waits = config
     refs = list(refs)
 
     def take(count):
@@ -896,6 +898,7 @@
     pairs = take(2) if third else None
     lasts = take(2) if fourth else None
     tables = take(2 if small == 1 else 1) if small else None
+    take(waits)
     to_x, to_y = take(2) if fresh or first or fourth else (None, None)
     at = 0
     if fresh:
@@ -940,9 +943,9 @@
         to[to.shape[0] - 1] = value.astype(BF16)
 
 
-def sum_round(fresh, got_x, got_y, first, second, third, fourth, small):
+def sum_round(fresh, got_x, got_y, first, second, third, fourth, small, after):
     stage, table = small
-    config = tuple(value is not None for value in (fresh, first, second, third, fourth)) + (stage,)
+    config = tuple(value is not None for value in (fresh, first, second, third, fourth)) + (stage, len(after))
     sample = fresh or first or second or third or fourth
     rows, width = sample[-1].shape[-2:]
     inputs, outputs = [], []
@@ -971,12 +974,12 @@
         pl.pallas_call(
             functools.partial(sum_kernel, config),
             out_shape=tuple(outputs),
-            in_specs=[VMEM] * len(inputs),
+            in_specs=[VMEM] * len(inputs) + [ANY] * len(after),
             out_specs=[VMEM] * len(outputs),
             compiler_params=params(VMEM_MB),
             cost_estimate=cost(),
             name="sum_round",
-        )(*inputs)
+        )(*inputs, *after)
     )
 
     def take(wanted, count):
@@ -1170,7 +1173,7 @@
     total_chunks = 3 * layers
     groups = []
     if staged:
-        edges = [0, 1, 2] + list(range(3, total_chunks + 1, 3))
+        edges = [0, 1, 2, 3] + list(range(4, total_chunks, 2)) + [total_chunks]
         groups = [range(low, high) for low, high in zip(edges[:-1], edges[1:])]
     where_of = {i: (g, i - group[0]) for g, group in enumerate(groups) for i in group}
     stage_z = [None] * len(groups)
@@ -1251,13 +1254,10 @@
         upstream = move(upstream[0], net["swap"])
     if staged:
         sent, got = {}, {}
-        zplan = {
-            -LAG: [(1, 1), (2, 2)],
-            -LAG + 1: [(1, 2), (2, 3)],
-            -LAG + 2: [(1, 3)],
-            -LAG + 3: [(2, 4)],
-            -LAG + 4: [(1, 4)],
-        }
+        zplan = {r: [(1, r + 2), (2, r + 3)] for r in range(-1, 2)}
+        for r in range(2, 2 * len(groups)):
+            g = (r + 6) // 2 + (r % 2)
+            zplan[r] = [(1 + r % 2, g)]
         spread = [net["z2"], net["z1"]]
         for r in range(-LAG, total_chunks + LAG):
             inputs, plan = [], []
@@ -1341,11 +1341,26 @@
 
     def side_work():
         step = len(rounds)
-        last = total_chunks
-        if step == 0:
+        last = total_chunks + 1
+        if step == 2:
+            loose["after"] = (loose["hidden"], loose["pool"])
+        if step == 3:
             loose["pooled"] = move(loose.pop("pool") / counts[:, None], net["swap"])
+            loose["after"] = (loose["pooled"],)
+        if step == last + 1:
+            loose["grad"] = move(loose.pop("grad"), net["swap"])
+            loose["after"] = (loose["grad"],)
         if step == last + 2:
-            loose["grad"] = move(loose.pop("grad"), net["swap"])
+            done = list(finish(2, pos_g, ended()[0::3][::-1]))
+            loose["outer"] = done
+            loose["after"] = (done[0],)
+
+    def ended():
+        found = []
+        for now in rounds:
+            if "total" in now:
+                found.append((now["total"], now["got_y"], ends[len(found)]))
+        return found
 
     def settle(state):
         return fence(state)
@@ -1355,7 +1370,6 @@
             if fresh is not None:
                 parts.append(fresh)
             return state(()) if callable(state) else state
-        side_work()
         s = len(rounds)
         past = rounds[s - LAG] if s >= LAG else {}
         pick = lambda key: past.get(key)
@@ -1369,6 +1383,7 @@
             pick("third"),
             pick("fourth"),
             loose.pop("small", (0, None)),
+            tuple(loose.pop("after", ())),
         )
         now = {}
         if fresh is not None:
@@ -1393,6 +1408,7 @@
             nonlocal table_stage
             table_stage += 1
             loose["small"] = (table_stage, small)
+        side_work()
         if callable(state):
             state = state(sends)
         rounds.append(now)
@@ -1403,7 +1419,7 @@
         return state
 
     top = layers - 1
-    attn_parts = None
+    ready = []
     dyl, dy, head_sums = head
     for layer in reversed(range(layers)):
         attn_bufs, inner_bufs, outer_bufs = chunks[3 * layer : 3 * layer + 3]
@@ -1413,48 +1429,58 @@
         if layer == top:
             outer_parts = settle(outer_grad(gt, far_gt, dyl, got_dyl))
 
-            def first_chain(sends):
-                pack, da, do, sums = chain_backward(*chain_args, after=sends)
-                got_pack = move(pack, net["core"])
-                inner_parts = inner_grad(pos_g, xoh, far_xoh, pack, got_pack)
-                return pack, da, do, sums, got_pack, inner_parts
-
-            pack, da, do, sums, got_pack, inner_parts = advance(outer_parts, first_chain)
-            back, qsum = attn_backward(q, kt, v, p, do)
+            def first_round(sends):
+                return chain_backward(*chain_args, after=sends)
+
+            pack, da, do, sums = advance(outer_parts, first_round)
+            got_pack = move(pack, net["core"])
+
+            def second_round(sends):
+                back, qsum = attn_backward(q, kt, v, p, do, after=sends)
+                return back, qsum, got_pack, inner_grad(pos_g, xoh, far_xoh, pack, got_pack)
+
+            back, qsum, got_pack, inner_parts = advance(None, second_round)
+            ready.append(inner_parts)
+            got_back = move(back, net["core"])
         else:
             pack, da, do, sums = chain_backward(*chain_args)
             outer_parts = outer_grad(gt, far_gt, dyl, got_dyl)
-            state = advance(attn_parts, (pack, da, do, sums, outer_parts))
+            state = advance(ready.pop(0), (pack, da, do, sums, outer_parts))
             pack, da, do, sums, outer_parts = state
+            ready.append(outer_parts)
             got_pack = move(pack, net["core"])
             back, qsum = attn_backward(q, kt, v, p, do)
             inner_parts = inner_grad(pos_g, xoh, far_xoh, pack, got_pack)
-            state = advance(outer_parts, (back, qsum, got_pack, inner_parts))
+            state = advance(ready.pop(0), (back, qsum, got_pack, inner_parts))
             back, qsum, got_pack, inner_parts = state
-        got_back = move(back, net["core"])
+            ready.append(inner_parts)
+            got_back = move(back, net["core"])
         below = None if layer == 0 else (kept[layer - 1][6], kept[layer - 1][7], table[layer - 1])
         total, vsum, *head = input_backward(pos_w, da, back, got_back, attn_bufs, below)
         attn_parts = attn_grad(pos_g, xoh, far_xoh, back, got_back, total, pack, got_pack)
+        attn_parts, head, vsum = advance(ready.pop(0), (attn_parts, head, vsum))
+        ready.append(attn_parts)
         vectors[layer] = (qsum, vsum, head_sums, sums)
-        attn_parts, head, vectors[layer] = advance(inner_parts, (attn_parts, head, vectors[layer]))
         if layer:
             dyl, dy, head_sums = head
     grad = head[0]
     vectors = collect(vectors, 16)
-    loose["vectors"], loose["grad"] = vectors, grad
-    advance(attn_parts, None)
+    loose["grad"] = grad
+    while ready:
+        if len(ready) == 1:
+            loose["vectors"] = vectors
+        advance(ready.pop(0), None)
     results = []
     if staged:
         for _ in range(4 * LAG):
             advance(None, None)
-        for s, now in enumerate(rounds):
-            if "total" in now:
-                results.append((now["total"], now["got_y"], ends[len(results)]))
+        results = ended()
 
     if staged:
         stacked = []
-        for kind, first in ((0, 2), (1, 1), (2, 0)):
+        for kind, first in ((0, 2), (1, 1)):
             stacked += list(finish(kind, pos_g, results[first::3][::-1]))
+        stacked += loose["outer"]
         hidden_out, pooled, tokens_grad = (loose[key] for key in ("hidden", "pooled", "grad"))
         vectors = loose["small"][1][0]
         got_vectors = rounds[-1]["got_y"][-1].astype(F32)

time: 615 us -> 604 us (0.982)
  waiting for transfers between devices: 257 us -> 231 us
  local copies, waits for them, and re-layouts: 30.1 us -> 42.2 us
    ppermute x111 -> x117, waiting for transfers between devices: 257 us -> 231 us  [move(): return lax.ppermute(value, AXES, perm)]
    unnamed x264 -> x280, local copies, waits for them, and re-layouts: 29.1 us -> 41.2 us
    ppermute x111 -> x117, starting transfers between devices: 113 us -> 115 us  [move(): return lax.ppermute(value, AXES, perm)]
    pallas_call x16 -> x18, Pallas kernels: 29.7 us -> 30.4 us  [copy_blocks(): pl.pallas_call(functools.partial(copy_kernel, plan, len(inputs)), out_sha...]
  transfers between devices with their start and end apart: 111 -> 117, of which waited for: 60 -> 62; matrix products, arithmetic and copies ran while one was open for 1% -> 1% of each run, Pallas kernels for 25% -> 28%
where the time goes in v4:
time: 604 us; the launch traced here: 595 us
  waiting for transfers between devices  231 us (38%)
  Pallas kernels  200 us (33%)
  starting transfers between devices  115 us (19%)
  local copies, waits for them, and re-layouts  42.2 us (7%)
    ppermute x117, waiting for transfers between devices, move(): return lax.ppermute(value, AXES, perm)  231 us
    ppermute x117, starting transfers between devices, move(): return lax.ppermute(value, AXES, perm)  115 us
    unnamed x280, local copies, waits for them, and re-layouts  41.2 us
    pallas_call x3, Pallas kernels, attn_forward(): pl.pallas_call(attn_kernel, out_shape=(shape((tokens, width), F32),) + ke...  39.6 us
    pallas_call x18, Pallas kernels, copy_blocks(): pl.pallas_call(functools.partial(copy_kernel, plan, len(inputs)), out_sha...  30.4 us
    pallas_call x3, Pallas kernels, chain_backward(): pl.pallas_call(functools.partial(chain_kernel, 384, len(after)), out_shap...  24.9 us
    pallas_call x3, Pallas kernels, attn_backward(): pl.pallas_call(functools.partial(attn_back_kernel, len(after)), out_shape...  23.4 us
    pallas_call x3, Pallas kernels, inner_forward(): pl.pallas_call(functools.partial(inner_kernel, 384), out_shape=(shape((to...  19.4 us
  transfers between devices with their start and end apart: 117, of which 62 were waited for; matrix products, arithmetic and copies ran while one was open for 1% of the time, Pallas kernels for 28%

profile of v4, /device:TPU:0, one launch (start us, length us, event | category | flops | bytes accessed | tf_op | source)
XLA Modules:
  0.0 594.8 jit_solution(9707512824681619687)
XLA Ops:
  9.3 4.1 collective-permute-start
  16.1 3.9 collective-permute-done.1
  24.9 2.5 collective-permute-start.5
  28.8 5.1 collective-permute-done.5.refs_1_
  35.8 2.7 collective-permute-start.11
  46.6 11.2 %collective-permute-done.13 = f32[3,12,768]{2,1,0:T(8,128)S(1)} collective-permute-done((f32[3,12,768]{2,1,0:T(8,128)S(1)}, f32[3,12,768]{2,1,0:T(8,128)S(1)}, u32[]{:S(2)}, u32[]{:S(2)}) %collective-permute-start.13) | collective-permute-done | bytes 110624 | tf_op jit(solution)/shard_map/ppermute | solution.py:1083
  65.5 10.9 %collective-permute-done.18 = f32[3,12,768]{2,1,0:T(8,128)S(1)} collective-permute-done((f32[3,12,768]{2,1,0:T(8,128)S(1)}, f32[3,12,768]{2,1,0:T(8,128)S(1)}, u32[]{:S(2)}, u32[]{:S(2)}) %collective-permute-start.18) | collective-permute-done | bytes 110624 | tf_op jit(solution)/shard_map/ppermute | solution.py:1083
  77.1 3.2 collective-permute-done.14.refs_4_
  90.4 12.0 %collective-permute-done.23.refs_1_ = bf16[4,48,768]{2,1,0:T(8,128)(2,1)S(1)} collective-permute-done((bf16[4,48,768]{2,1,0:T(8,128)(2,1)S(1)}, bf16[4,48,768]{2,1,0:T(8,128)(2,1)S(1)}, u32[]{:S(2)}, u32[]{:S(2)}) %collective-permute-start.23) | collective-permute-done | bytes 294944 | tf_op jit(solution)/shard_map/ppermute | solution.py:1083
  109.0 4.2 gather_round.14
  122.5 13.2 %attn_forward.3 = (f32[256,768]{1,0:T(8,128)S(1)}, f32[256,768]{1,0:T(8,128)S(1)}, f32[256,128]{1,0:T(8,128)S(1)}, bf16[256,768]{1,0:T(8,128)(2,1)S(1)}, bf16[76...) custom-call(s32[4]{0:T(128)S(1)} %pad_add_fusion.2.pos_ref.refs_0_.r, ...), custom_call_target="tpu_custom_call" | custom-call | flops 1 | bytes 1 | tf_op jit(solution)/shard_map/attn_forward/pallas_call | solution.py:265
  138.3 3.8 gather_round.15
  146.4 7.7 %inner_forward.3 = (bf16[256,3072]{1,0:T(8,128)(2,1)S(1)}, bf16[256,3072]{1,0:T(8,128)(2,1)S(1)}, bf16[2,2,2,4,48,256]{5,4,3,2,1,0:T(8,128)(2,1)S(1)}, bf16[2,2,2,4,48,256]{5,4,3,2,1,0:T(8,128)(2,1)S(1)}) custom-call(s32[4]{0:T(128)S(1)} %pad_add_fusion.2.pos_ref.refs_0_.refs_1_, s32[4]{0:T(128)S(1)} %pad_add_fusion.2.pos_ref.refs_0_.refs_1_, ...), custom_call_target="tpu_custom_call" | custom-call | flops 1 | bytes 1 | tf_op jit(solution)/shard_map/inner_forward/pallas_call | solution.py:348
  154.2 5.3 collective-permute-done.31.refs_1_
  162.5 3.3 collective-permute-done.28.refs_4_
  172.2 3.3 outer_forward.3
  177.3 9.1 %collective-permute-done.37.refs_1_ = bf16[8,48,768]{2,1,0:T(8,128)(2,1)S(1)} collective-permute-done((bf16[8,48,768]{2,1,0:T(8,128)(2,1)S(1)}, bf16[8,48,768]{2,1,0:T(8,128)(2,1)S(1)}, u32[]{:S(2)}, u32[]{:S(2)}) %collective-permute-start.37) | collective-permute-done | bytes 589856 | tf_op jit(solution)/shard_map/ppermute | solution.py:1083
  186.4 5.0 collective-permute-done.34.refs_4_
  198.6 13.2 %attn_forward.4 = (f32[256,768]{1,0:T(8,128)S(1)}, f32[256,768]{1,0:T(8,128)S(1)}, f32[256,128]{1,0:T(8,128)S(1)}, bf16[256,768]{1,0:T(8,128)(2,1)S(1)}, bf16[76...) custom-call(s32[4]{0:T(128)S(1)} %pad_add_fusion.2.pos_ref.refs_0_.r, ...), custom_call_target="tpu_custom_call" | custom-call | flops 1 | bytes 1 | tf_op jit(solution)/shard_map/attn_forward/pallas_call | solution.py:265
  222.6 5.9 inner_forward.4
  230.0 2.5 collective-permute-done.48.tb_ref.xb_ref
  233.5 10.2 %collective-permute-done.43.refs_4_ = bf16[12,48,768]{2,1,0:T(8,128)(2,1)S(1)} collective-permute-done((bf16[12,48,768]{2,1,0:T(8,128)(2,1)S(1)}, bf16[12,48,768]{2,1,0:T(8,128)(2,1)S(1)}, u32[]{:S(2)}, u32[]{:S(2)}) %collective-permute-start.43) | collective-permute-done | bytes 884768 | tf_op jit(solution)/shard_map/ppermute | solution.py:1083
  248.1 2.9 outer_forward.4
  252.8 15.3 %collective-permute-done.49.refs_2_ = bf16[12,48,768]{2,1,0:T(8,128)(2,1)S(1)} collective-permute-done((bf16[12,48,768]{2,1,0:T(8,128)(2,1)S(1)}, bf16[12,48,768]{2,1,0:T(8,128)(2,1)S(1)}, u32[]{:S(2)}, u32[]{:S(2)}) %collective-permute-start.49) | collective-permute-done | bytes 884768 | tf_op jit(solution)/shard_map/ppermute | solution.py:1083
  272.6 13.2 %attn_forward.5 = (f32[256,768]{1,0:T(8,128)S(1)}, f32[256,768]{1,0:T(8,128)S(1)}, f32[256,128]{1,0:T(8,128)S(1)}, bf16[256,768]{1,0:T(8,128)(2,1)S(1)}, bf16[76...) custom-call(s32[4]{0:T(128)S(1)} %pad_add_fusion.2.pos_ref.refs_0_.r, ...), custom_call_target="tpu_custom_call" | custom-call | flops 1 | bytes 1 | tf_op jit(solution)/shard_map/attn_forward/pallas_call | solution.py:265
  290.6 3.0 collective-permute-start.57
  293.6 5.9 inner_forward.5
  300.4 2.7 collective-permute-done.59.tb_ref.xb_ref
  303.1 3.3 outer_forward.5
  313.5 7.9 %chain_backward.3 = (bf16[256,3840]{1,0:T(8,128)(2,1)S(1)}, f32[256,768]{1,0:T(8,128)S(1)}, bf16[256,768]{1,0:T(8,128)(2,1)S(1)}, f32[16,768]{1,0:T(8,128)S(1)}) custom-call(s32[4]{0:T(128)S(1)} %pad_add_fusion.2.pos_ref.refs_0_.refs_1_, bf16[256,768]{1,0:T(8,128)(2,1)S(1)} %get-tuple-element.953.da_ref.refs_1_, f32[256,768]{1,0:T(8,128)S(1)} %get-tuple-element.960.refs_2_, ...), custom_call_target="tpu_custom_call" | custom-call | flops 1 | bytes 1 | tf_op jit(solution)/shard_map/chain_backward/pallas_call | solution.py:470
  322.3 3.2 collective-permute-done.64.refs_0_
  329.8 7.8 %attn_backward.3 = (bf16[5,256,768]{2,1,0:T(8,128)(2,1)S(1)}, f32[8,768]{1,0:T(8,128)S(1)}) custom-call(bf16[256,768]{1,0:T(8,128)(2,1)S(1)} %copy-done.103, bf16[768,512]{1,0:T(8,128)(2,1)S(1)} %copy-done.65, bf16[512,768]{1,0:T(8,128)(2,1)S(1)} %copy-done.67, bf16[12,512,256]{2,1,0:T(8,128)(2,1)S(1)} %copy-done.34, ...), custom_call_target="tpu_custom_call" | custom-call | flops 1 | bytes 1 | tf_op jit(solution)/shard_map/attn_backward/pallas_call | solution.py:543
  343.8 3.4 collective-permute-start.70
  349.8 4.5 input_backward.3
  356.8 2.8 attn_grad.3
  360.4 3.2 collective-permute-done.70.refs_3_
  369.2 2.6 collective-permute-start.73
  371.8 7.7 %chain_backward.4 = (bf16[256,3840]{1,0:T(8,128)(2,1)S(1)}, f32[256,768]{1,0:T(8,128)S(1)}, bf16[256,768]{1,0:T(8,128)(2,1)S(1)}, f32[16,768]{1,0:T(8,128)S(1)}) custom-call(s32[4]{0:T(128)S(1)} %pad_add_fusion.2.pos_ref.refs_0_.refs_1_, bf16[256,768]{1,0:T(8,128)(2,1)S(1)} %get-tuple-element.1032.refs_1_.da_ref, f32[256,768]{1,0:T(8,128)S(1)} %copy-done.63, ...), custom_call_target="tpu_custom_call" | custom-call | flops 1 | bytes 1 | tf_op jit(solution)/shard_map/chain_backward/pallas_call | solution.py:470
  381.1 6.3 %collective-permute-done.74.refs_2_ = bf16[12,48,768]{2,1,0:T(8,128)(2,1)S(1)} collective-permute-done((bf16[12,48,768]{2,1,0:T(8,128)(2,1)S(1)}, bf16[12,48,768]{2,1,0:T(8,128)(2,1)S(1)}, u32[]{:S(2)}, u32[]{:S(2)}) %collective-permute-start.74) | collective-permute-done | bytes 884768 | tf_op jit(solution)/shard_map/ppermute | solution.py:1083
  390.8 6.1 %collective-permute-start.78 = (bf16[14,48,768]{2,1,0:T(8,128)(2,1)S(1)}, bf16[14,48,768]{2,1,0:T(8,128)(2,1)S(1)}, u32[]{:S(2)}, u32[]{:S(2)}) collective-permute-start(bf16[14,48,768]{2,1,0:T(8,128)(2,1)S(1)} %get-tuple-element.1055), channel_id=1, source_target_pairs={{1,0},{0,1},{3,2},{2,3},{5,4},{4,5},{7,6},{6,7},{9,8},{8,9},{11,10... | collective-permute-start | bytes 3096584 | tf_op jit(solution)/shard_map/ppermute | solution.py:1083
  398.1 7.8 %attn_backward.4 = (bf16[5,256,768]{2,1,0:T(8,128)(2,1)S(1)}, f32[8,768]{1,0:T(8,128)S(1)}) custom-call(bf16[256,768]{1,0:T(8,128)(2,1)S(1)} %copy-done.107, bf16[768,512]{1,0:T(8,128)(2,1)S(1)} %copy-done.81, bf16[512,768]{1,0:T(8,128)(2,1)S(1)} %copy-done.83, bf16[12,512,256]{2,1,0:T(8,128)(2,1)S(1)} %copy-done.38, ...), custom_call_target="tpu_custom_call" | custom-call | flops 1 | bytes 1 | tf_op jit(solution)/shard_map/attn_backward/pallas_call | solution.py:543
  408.4 8.9 %collective-permute-done.77.refs_2_ = bf16[12,48,768]{2,1,0:T(8,128)(2,1)S(1)} collective-permute-done((bf16[12,48,768]{2,1,0:T(8,128)(2,1)S(1)}, bf16[12,48,768]{2,1,0:T(8,128)(2,1)S(1)}, u32[]{:S(2)}, u32[]{:S(2)}) %collective-permute-start.77) | collective-permute-done | bytes 884768 | tf_op jit(solution)/shard_map/ppermute | solution.py:1083
  417.3 3.1 collective-permute-done.78.refs_3_.refs_5_
  424.6 4.1 input_backward.4
  428.8 2.8 attn_grad.4
  433.8 9.3 %collective-permute-done.82.refs_2_ = bf16[12,48,768]{2,1,0:T(8,128)(2,1)S(1)} collective-permute-done((bf16[12,48,768]{2,1,0:T(8,128)(2,1)S(1)}, bf16[12,48,768]{2,1,0:T(8,128)(2,1)S(1)}, u32[]{:S(2)}, u32[]{:S(2)}) %collective-permute-start.82) | collective-permute-done | bytes 884768 | tf_op jit(solution)/shard_map/ppermute | solution.py:1083
  448.8 9.3 %chain_backward.5 = (bf16[256,3840]{1,0:T(8,128)(2,1)S(1)}, f32[256,768]{1,0:T(8,128)S(1)}, bf16[256,768]{1,0:T(8,128)(2,1)S(1)}, f32[16,768]{1,0:T(8,128)S(1)}) custom-call(s32[4]{0:T(128)S(1)} %pad_add_fusion.2.pos_ref.refs_0_.refs_1_, bf16[256,768]{1,0:T(8,128)(2,1)S(1)} %get-tuple-element.1126.refs_1_.da_ref, ...), custom_call_target="tpu_custom_call" | custom-call | flops 1 | bytes 1 | tf_op jit(solution)/shard_map/chain_backward/pallas_call | solution.py:470
  459.7 5.4 collective-permute-done.87.refs_2_
  465.1 3.1 collective-permute-done.88.refs_3_.refs_5_
  473.6 7.8 %attn_backward.5 = (bf16[5,256,768]{2,1,0:T(8,128)(2,1)S(1)}, f32[8,768]{1,0:T(8,128)S(1)}) custom-call(bf16[256,768]{1,0:T(8,128)(2,1)S(1)} %copy-done.105, bf16[768,512]{1,0:T(8,128)(2,1)S(1)} %copy-done.77, bf16[512,768]{1,0:T(8,128)(2,1)S(1)} %copy-done.79, bf16[12,512,256]{2,1,0:T(8,128)(2,1)S(1)} %copy-done.36, ...), custom_call_target="tpu_custom_call" | custom-call | flops 1 | bytes 1 | tf_op jit(solution)/shard_map/attn_backward/pallas_call | solution.py:543
  481.4 2.5 inner_grad.5
  483.9 7.1 %collective-permute-done.92.refs_2_ = bf16[12,48,768]{2,1,0:T(8,128)(2,1)S(1)} collective-permute-done((bf16[12,48,768]{2,1,0:T(8,128)(2,1)S(1)}, bf16[12,48,768]{2,1,0:T(8,128)(2,1)S(1)}, u32[]{:S(2)}, u32[]{:S(2)}) %collective-permute-start.92) | collective-permute-done | bytes 884768 | tf_op jit(solution)/shard_map/ppermute | solution.py:1083
  491.1 3.1 collective-permute-done.93.refs_3_.refs_5_
  499.5 4.0 input_backward.5
  503.5 2.8 attn_grad.5
  508.7 8.3 %collective-permute-done.97.refs_2_ = bf16[12,48,768]{2,1,0:T(8,128)(2,1)S(1)} collective-permute-done((bf16[12,48,768]{2,1,0:T(8,128)(2,1)S(1)}, bf16[12,48,768]{2,1,0:T(8,128)(2,1)S(1)}, u32[]{:S(2)}, u32[]{:S(2)}) %collective-permute-start.97) | collective-permute-done | bytes 884768 | tf_op jit(solution)/shard_map/ppermute | solution.py:1083
  517.0 3.1 collective-permute-done.98.refs_3_.refs_4_
  525.6 6.5 %collective-permute-done.102.refs_9_ = bf16[2,48,768]{2,1,0:T(8,128)(2,1)S(1)} collective-permute-done((bf16[2,48,768]{2,1,0:T(8,128)(2,1)S(1)}, bf16[2,48,768]{2,1,0:T(8,128)(2,1)S(1)}, u32[]{:S(2)}, u32[]{:S(2)}) %collective-permute-start.102) | collective-permute-done | bytes 147488 | tf_op jit(solution)/shard_map/ppermute | solution.py:1083
  533.8 8.3 %collective-permute-done.103.refs_0_ = bf16[12,48,768]{2,1,0:T(8,128)(2,1)S(1)} collective-permute-done((bf16[12,48,768]{2,1,0:T(8,128)(2,1)S(1)}, bf16[12,48,768]{2,1,0:T(8,128)(2,1)S(1)}, u32[]{:S(2)}, u32[]{:S(2)}) %collective-permute-start.103) | collective-permute-done | bytes 884768 | tf_op jit(solution)/shard_map/ppermute | solution.py:1083
  542.1 3.1 collective-permute-done.104.refs_1_.refs_4_
  551.2 5.1 collective-permute-done.107.refs_7_
  558.8 2.6 collective-permute-start.113
  563.4 6.3 %collective-permute-done.111.refs_3_ = bf16[2,48,768]{2,1,0:T(8,128)(2,1)S(1)} collective-permute-done((bf16[2,48,768]{2,1,0:T(8,128)(2,1)S(1)}, bf16[2,48,768]{2,1,0:T(8,128)(2,1)S(1)}, u32[]{:S(2)}, u32[]{:S(2)}) %collective-permute-start.111) | collective-permute-done | bytes 147488 | tf_op jit(solution)/shard_map/ppermute | solution.py:1083
  579.0 2.7 collective-permute-done.114.refs_1_
  (548 shorter events, 221.1 us)
Async XLA Ops:
  0.8 19.3 %collective-permute-start.3 = (bf16[256,768]{1,0:T(8,128)(2,1)}, bf16[256,768]{1,0:T(8,128)(2,1)S(1)}, u32[]{:S(2)}, u32[]{:S(2)}) collective-permute-start(bf16[256,768]{1,0:T(8,128)(2,1)} %bitcast.50), channel_id=1, source_target_pairs={{0,0},{2,1},{1,2},{3,3},{4,4},{6,5},{5,6},{7,7},{8,8},{10,9},{9,10... | collective-permute-start | bytes 1179656 | tf_op jit(solution)/shard_map/ppermute | solution.py:1083
  20.1 14.7 %collective-permute-start.8 = (bf16[256,768]{1,0:T(8,128)(2,1)S(1)}, bf16[256,768]{1,0:T(8,128)(2,1)S(1)}, u32[]{:S(2)}, u32[]{:S(2)}) collective-permute-start(bf16[256,768]{1,0:T(8,128)(2,1)S(1)} %collective-permute-done.3), channel_id=1, source_target_pairs={{2,0},{3,1},{0,2},{1,3},{6,4},{7,5},{4,6},{5,7},{10,8},{11,9},{8,1... | collective-permute-start | bytes 1179656 | tf_op jit(solution)/shard_map/ppermute | solution.py:1083
  35.8 22.1 %collective-permute-start.11 = (bf16[4,48,768]{2,1,0:T(8,128)(2,1)S(1)}, bf16[4,48,768]{2,1,0:T(8,128)(2,1)S(1)}, u32[]{:S(2)}, u32[]{:S(2)}) collective-permute-start(bf16[4,48,768]{2,1,0:T(8,128)(2,1)S(1)} %gather_z.8.refs_0_), channel_id=1, source_target_pairs={{8,0},{9,1},{10,2},{11,3},{12,4},{13,5},{14,6},{15,7},{0,8},{1,9},... | collective-permute-start | bytes 884744 | tf_op jit(solution)/shard_map/ppermute | solution.py:1083
  39.9 18.0 %collective-permute-start.9 = (bf16[4,48,768]{2,1,0:T(8,128)(2,1)S(1)}, bf16[4,48,768]{2,1,0:T(8,128)(2,1)S(1)}, u32[]{:S(2)}, u32[]{:S(2)}) collective-permute-start(bf16[4,48,768]{2,1,0:T(8,128)(2,1)S(1)} %get-tuple-element.677.refs_2_), channel_id=1, source_target_pairs={{4,0},{5,1},{6,2},{7,3},{0,4},{1,5},{2,6},{3,7},{12,8},{13,9},{14,... | collective-permute-start | bytes 884744 | tf_op jit(solution)/shard_map/ppermute | solution.py:1083
  41.4 16.5 %collective-permute-start.10 = (bf16[4,48,768]{2,1,0:T(8,128)(2,1)S(1)}, bf16[4,48,768]{2,1,0:T(8,128)(2,1)S(1)}, u32[]{:S(2)}, u32[]{:S(2)}) collective-permute-start(bf16[4,48,768]{2,1,0:T(8,128)(2,1)S(1)} %get-tuple-element.678.refs_3_), channel_id=1, source_target_pairs={{1,0},{0,1},{3,2},{2,3},{5,4},{4,5},{7,6},{6,7},{9,8},{8,9},{11,10... | collective-permute-start | bytes 884744 | tf_op jit(solution)/shard_map/ppermute | solution.py:1083
  42.7 15.2 %collective-permute-start.12 = (bf16[2,48,768]{2,1,0:T(8,128)(2,1)S(1)}, bf16[2,48,768]{2,1,0:T(8,128)(2,1)S(1)}, u32[]{:S(2)}, u32[]{:S(2)}) collective-permute-start(bf16[2,48,768]{2,1,0:T(8,128)(2,1)S(1)} %pack.9.refs_0_), channel_id=1, source_target_pairs={{16,0},{17,1},{18,2},{19,3},{20,4},{21,5},{22,6},{23,7},{24,8},{25... | collective-permute-start | bytes 442376 | tf_op jit(solution)/shard_map/ppermute | solution.py:1083
  59.6 20.7 %collective-permute-start.14 = (bf16[12,48,768]{2,1,0:T(8,128)(2,1)S(1)}, bf16[12,48,768]{2,1,0:T(8,128)(2,1)S(1)}, u32[]{:S(2)}, u32[]{:S(2)}) collective-permute-start(bf16[12,48,768]{2,1,0:T(8,128)(2,1)S(1)} %get-tuple-element.695.refs_2_), channel_id=1, source_target_pairs={{4,0},{5,1},{6,2},{7,3},{0,4},{1,5},{2,6},{3,7},{12,8},{13,9},{14,... | collective-permute-start | bytes 2654216 | tf_op jit(solution)/shard_map/ppermute | solution.py:1083
  60.3 20.1 %collective-permute-start.15 = (bf16[12,48,768]{2,1,0:T(8,128)(2,1)S(1)}, bf16[12,48,768]{2,1,0:T(8,128)(2,1)S(1)}, u32[]{:S(2)}, u32[]{:S(2)}) collective-permute-start(bf16[12,48,768]{2,1,0:T(8,128)(2,1)S(1)} %get-tuple-element.696.refs_3_), channel_id=1, source_target_pairs={{1,0},{0,1},{3,2},{2,3},{5,4},{4,5},{7,6},{6,7},{9,8},{8,9},{11,10... | collective-permute-start | bytes 2654216 | tf_op jit(solution)/shard_map/ppermute | solution.py:1083
  62.7 14.4 %collective-permute-start.16 = (bf16[4,48,768]{2,1,0:T(8,128)(2,1)S(1)}, bf16[4,48,768]{2,1,0:T(8,128)(2,1)S(1)}, u32[]{:S(2)}, u32[]{:S(2)}) collective-permute-start(bf16[4,48,768]{2,1,0:T(8,128)(2,1)S(1)} %gather_z.9.refs_0_), channel_id=1, source_target_pairs={{8,0},{9,1},{10,2},{11,3},{12,4},{13,5},{14,6},{15,7},{0,8},{1,9},... | collective-permute-start | bytes 884744 | tf_op jit(solution)/shard_map/ppermute | solution.py:1083
  82.6 24.9 %collective-permute-start.21 = (bf16[32,48,768]{2,1,0:T(8,128)(2,1)S(1)}, bf16[32,48,768]{2,1,0:T(8,128)(2,1)S(1)}, u32[]{:S(2)}, u32[]{:S(2)}) collective-permute-start(bf16[32,48,768]{2,1,0:T(8,128)(2,1)S(1)} %get-tuple-element.742.refs_7_.refs_11_.refs_4_), channel_id=1, source_target_pairs={{2,0},{3,1},{0,2},{1,3},{6,4},{7,5},{4,6},{5,7},{10,8},{11,9},{8,1... | collective-permute-start | bytes 7077896 | tf_op jit(solution)/shard_map/ppermute | solution.py:1083
  84.1 22.0 %collective-permute-start.19 = (bf16[12,48,768]{2,1,0:T(8,128)(2,1)S(1)}, bf16[12,48,768]{2,1,0:T(8,128)(2,1)S(1)}, u32[]{:S(2)}, u32[]{:S(2)}) collective-permute-start(bf16[12,48,768]{2,1,0:T(8,128)(2,1)S(1)} %get-tuple-element.713.refs_2_), channel_id=1, source_target_pairs={{4,0},{5,1},{6,2},{7,3},{0,4},{1,5},{2,6},{3,7},{12,8},{13,9},{14,... | collective-permute-start | bytes 2654216 | tf_op jit(solution)/shard_map/ppermute | solution.py:1083
  85.8 21.8 %collective-permute-start.20 = (bf16[12,48,768]{2,1,0:T(8,128)(2,1)S(1)}, bf16[12,48,768]{2,1,0:T(8,128)(2,1)S(1)}, u32[]{:S(2)}, u32[]{:S(2)}) collective-permute-start(bf16[12,48,768]{2,1,0:T(8,128)(2,1)S(1)} %get-tuple-element.714.refs_3_), channel_id=1, source_target_pairs={{1,0},{0,1},{3,2},{2,3},{5,4},{4,5},{7,6},{6,7},{9,8},{8,9},{11,10... | collective-permute-start | bytes 2654216 | tf_op jit(solution)/shard_map/ppermute | solution.py:1083
  88.2 14.2 %collective-permute-start.23 = (bf16[4,48,768]{2,1,0:T(8,128)(2,1)S(1)}, bf16[4,48,768]{2,1,0:T(8,128)(2,1)S(1)}, u32[]{:S(2)}, u32[]{:S(2)}) collective-permute-start(bf16[4,48,768]{2,1,0:T(8,128)(2,1)S(1)} %pack.11.refs_0_), channel_id=1, source_target_pairs={{16,0},{17,1},{18,2},{19,3},{20,4},{21,5},{22,6},{23,7},{24,8},{25... | collective-permute-start | bytes 884744 | tf_op jit(solution)/shard_map/ppermute | solution.py:1083
  89.2 15.2 %collective-permute-start.22 = (bf16[4,48,768]{2,1,0:T(8,128)(2,1)S(1)}, bf16[4,48,768]{2,1,0:T(8,128)(2,1)S(1)}, u32[]{:S(2)}, u32[]{:S(2)}) collective-permute-start(bf16[4,48,768]{2,1,0:T(8,128)(2,1)S(1)} %gather_z.10.refs_0_), channel_id=1, source_target_pairs={{8,0},{9,1},{10,2},{11,3},{12,4},{13,5},{14,6},{15,7},{0,8},{1,9},... | collective-permute-start | bytes 884744 | tf_op jit(solution)/shard_map/ppermute | solution.py:1083
  113.2 25.1 %collective-permute-start.26 = (bf16[32,48,768]{2,1,0:T(8,128)(2,1)}, bf16[32,48,768]{2,1,0:T(8,128)(2,1)}, u32[]{:S(2)}, u32[]{:S(2)}) collective-permute-start(bf16[32,48,768]{2,1,0:T(8,128)(2,1)} %get-tuple-element.784.refs_4_.refs_7_), channel_id=1, source_target_pairs={{2,0},{3,1},{0,2},{1,3},{6,4},{7,5},{4,6},{5,7},{10,8},{11,9},{8,1... | collective-permute-start | bytes 7077896 | tf_op jit(solution)/shard_map/ppermute | solution.py:1083
  113.2 25.0 %collective-permute-start.24 = (bf16[12,48,768]{2,1,0:T(8,128)(2,1)}, bf16[12,48,768]{2,1,0:T(8,128)(2,1)}, u32[]{:S(2)}, u32[]{:S(2)}) collective-permute-start(bf16[12,48,768]{2,1,0:T(8,128)(2,1)} %get-tuple-element.732.refs_2_), channel_id=1, source_target_pairs={{4,0},{5,1},{6,2},{7,3},{0,4},{1,5},{2,6},{3,7},{12,8},{13,9},{14,... | collective-permute-start | bytes 2654216 | tf_op jit(solution)/shard_map/ppermute | solution.py:1083
  113.7 24.6 %collective-permute-start.25 = (bf16[12,48,768]{2,1,0:T(8,128)(2,1)}, bf16[12,48,768]{2,1,0:T(8,128)(2,1)}, u32[]{:S(2)}, u32[]{:S(2)}) collective-permute-start(bf16[12,48,768]{2,1,0:T(8,128)(2,1)} %get-tuple-element.733.refs_3_), channel_id=1, source_target_pairs={{1,0},{0,1},{3,2},{2,3},{5,4},{4,5},{7,6},{6,7},{9,8},{8,9},{11,10... | collective-permute-start | bytes 2654216 | tf_op jit(solution)/shard_map/ppermute | solution.py:1083
  116.0 22.3 %collective-permute-start.27 = (bf16[8,48,768]{2,1,0:T(8,128)(2,1)S(1)}, bf16[8,48,768]{2,1,0:T(8,128)(2,1)}, u32[]{:S(2)}, u32[]{:S(2)}) collective-permute-start(bf16[8,48,768]{2,1,0:T(8,128)(2,1)S(1)} %gather_z.11.refs_0_), channel_id=1, source_target_pairs={{8,0},{9,1},{10,2},{11,3},{12,4},{13,5},{14,6},{15,7},{0,8},{1,9},... | collective-permute-start | bytes 1769480 | tf_op jit(solution)/shard_map/ppermute | solution.py:1083
  142.2 25.0 %collective-permute-start.30 = (bf16[32,48,768]{2,1,0:T(8,128)(2,1)S(1)}, bf16[32,48,768]{2,1,0:T(8,128)(2,1)S(1)}, u32[]{:S(2)}, u32[]{:S(2)}) collective-permute-start(bf16[32,48,768]{2,1,0:T(8,128)(2,1)S(1)} %get-tuple-element.802.refs_4_.refs_9_), channel_id=1, source_target_pairs={{2,0},{3,1},{0,2},{1,3},{6,4},{7,5},{4,6},{5,7},{10,8},{11,9},{8,1... | collective-permute-start | bytes 7077896 | tf_op jit(solution)/shard_map/ppermute | solution.py:1083
  142.9 16.7 %collective-permute-start.31 = (bf16[4,48,768]{2,1,0:T(8,128)(2,1)S(1)}, bf16[4,48,768]{2,1,0:T(8,128)(2,1)S(1)}, u32[]{:S(2)}, u32[]{:S(2)}) collective-permute-start(bf16[4,48,768]{2,1,0:T(8,128)(2,1)S(1)} %pack.12.refs_0_), channel_id=1, source_target_pairs={{16,0},{17,1},{18,2},{19,3},{20,4},{21,5},{22,6},{23,7},{24,8},{25... | collective-permute-start | bytes 884744 | tf_op jit(solution)/shard_map/ppermute | solution.py:1083
  144.1 21.8 %collective-permute-start.28 = (bf16[12,48,768]{2,1,0:T(8,128)(2,1)S(1)}, bf16[12,48,768]{2,1,0:T(8,128)(2,1)S(1)}, u32[]{:S(2)}, u32[]{:S(2)}) collective-permute-start(bf16[12,48,768]{2,1,0:T(8,128)(2,1)S(1)} %get-tuple-element.764.refs_2_), channel_id=1, source_target_pairs={{4,0},{5,1},{6,2},{7,3},{0,4},{1,5},{2,6},{3,7},{12,8},{13,9},{14,... | collective-permute-start | bytes 2654216 | tf_op jit(solution)/shard_map/ppermute | solution.py:1083
  145.7 21.5 %collective-permute-start.29 = (bf16[12,48,768]{2,1,0:T(8,128)(2,1)S(1)}, bf16[12,48,768]{2,1,0:T(8,128)(2,1)S(1)}, u32[]{:S(2)}, u32[]{:S(2)}) collective-permute-start(bf16[12,48,768]{2,1,0:T(8,128)(2,1)S(1)} %get-tuple-element.765.refs_3_), channel_id=1, source_target_pairs={{1,0},{0,1},{3,2},{2,3},{5,4},{4,5},{7,6},{6,7},{9,8},{8,9},{11,10... | collective-permute-start | bytes 2654216 | tf_op jit(solution)/shard_map/ppermute | solution.py:1083
  169.3 22.2 %collective-permute-start.36 = (bf16[32,48,768]{2,1,0:T(8,128)(2,1)S(1)}, bf16[32,48,768]{2,1,0:T(8,128)(2,1)S(1)}, u32[]{:S(2)}, u32[]{:S(2)}) collective-permute-start(bf16[32,48,768]{2,1,0:T(8,128)(2,1)S(1)} %get-tuple-element.840.refs_7_.refs_11_.refs_4_), channel_id=1, source_target_pairs={{2,0},{3,1},{0,2},{1,3},{6,4},{7,5},{4,6},{5,7},{10,8},{11,9},{8,1... | collective-permute-start | bytes 7077896 | tf_op jit(solution)/shard_map/ppermute | solution.py:1083
  169.4 22.1 %collective-permute-start.34 = (bf16[12,48,768]{2,1,0:T(8,128)(2,1)S(1)}, bf16[12,48,768]{2,1,0:T(8,128)(2,1)S(1)}, u32[]{:S(2)}, u32[]{:S(2)}) collective-permute-start(bf16[12,48,768]{2,1,0:T(8,128)(2,1)S(1)} %get-tuple-element.794.refs_2_), channel_id=1, source_target_pairs={{4,0},{5,1},{6,2},{7,3},{0,4},{1,5},{2,6},{3,7},{12,8},{13,9},{14,... | collective-permute-start | bytes 2654216 | tf_op jit(solution)/shard_map/ppermute | solution.py:1083
  169.8 21.7 %collective-permute-start.35 = (bf16[12,48,768]{2,1,0:T(8,128)(2,1)S(1)}, bf16[12,48,768]{2,1,0:T(8,128)(2,1)S(1)}, u32[]{:S(2)}, u32[]{:S(2)}) collective-permute-start(bf16[12,48,768]{2,1,0:T(8,128)(2,1)S(1)} %get-tuple-element.795.refs_3_), channel_id=1, source_target_pairs={{1,0},{0,1},{3,2},{2,3},{5,4},{4,5},{7,6},{6,7},{9,8},{8,9},{11,10... | collective-permute-start | bytes 2654216 | tf_op jit(solution)/shard_map/ppermute | solution.py:1083
  171.2 15.2 %collective-permute-start.37 = (bf16[8,48,768]{2,1,0:T(8,128)(2,1)S(1)}, bf16[8,48,768]{2,1,0:T(8,128)(2,1)S(1)}, u32[]{:S(2)}, u32[]{:S(2)}) collective-permute-start(bf16[8,48,768]{2,1,0:T(8,128)(2,1)S(1)} %gather_z.12.refs_0_), channel_id=1, source_target_pairs={{8,0},{9,1},{10,2},{11,3},{12,4},{13,5},{14,6},{15,7},{0,8},{1,9},... | collective-permute-start | bytes 1769480 | tf_op jit(solution)/shard_map/ppermute | solution.py:1083
  193.7 23.5 %collective-permute-start.41 = (bf16[32,48,768]{2,1,0:T(8,128)(2,1)S(1)}, bf16[32,48,768]{2,1,0:T(8,128)(2,1)S(1)}, u32[]{:S(2)}, u32[]{:S(2)}) collective-permute-start(bf16[32,48,768]{2,1,0:T(8,128)(2,1)S(1)} %get-tuple-element.872.refs_4_.refs_7_), channel_id=1, source_target_pairs={{2,0},{3,1},{0,2},{1,3},{6,4},{7,5},{4,6},{5,7},{10,8},{11,9},{8,1... | collective-permute-start | bytes 7077896 | tf_op jit(solution)/shard_map/ppermute | solution.py:1083
  193.8 22.1 %collective-permute-start.39 = (bf16[12,48,768]{2,1,0:T(8,128)(2,1)S(1)}, bf16[12,48,768]{2,1,0:T(8,128)(2,1)S(1)}, u32[]{:S(2)}, u32[]{:S(2)}) collective-permute-start(bf16[12,48,768]{2,1,0:T(8,128)(2,1)S(1)} %get-tuple-element.828.refs_2_), channel_id=1, source_target_pairs={{4,0},{5,1},{6,2},{7,3},{0,4},{1,5},{2,6},{3,7},{12,8},{13,9},{14,... | collective-permute-start | bytes 2654216 | tf_op jit(solution)/shard_map/ppermute | solution.py:1083
  195.6 21.7 %collective-permute-start.40 = (bf16[12,48,768]{2,1,0:T(8,128)(2,1)S(1)}, bf16[12,48,768]{2,1,0:T(8,128)(2,1)S(1)}, u32[]{:S(2)}, u32[]{:S(2)}) collective-permute-start(bf16[12,48,768]{2,1,0:T(8,128)(2,1)S(1)} %get-tuple-element.829.refs_3_), channel_id=1, source_target_pairs={{1,0},{0,1},{3,2},{2,3},{5,4},{4,5},{7,6},{6,7},{9,8},{8,9},{11,10... | collective-permute-start | bytes 2654216 | tf_op jit(solution)/shard_map/ppermute | solution.py:1083
  197.0 17.9 %collective-permute-start.42 = (bf16[2,48,768]{2,1,0:T(8,128)(2,1)S(1)}, bf16[2,48,768]{2,1,0:T(8,128)(2,1)S(1)}, u32[]{:S(2)}, u32[]{:S(2)}) collective-permute-start(bf16[2,48,768]{2,1,0:T(8,128)(2,1)S(1)} %pack.13.refs_0_), channel_id=1, source_target_pairs={{16,0},{17,1},{18,2},{19,3},{20,4},{21,5},{22,6},{23,7},{24,8},{25... | collective-permute-start | bytes 442376 | tf_op jit(solution)/shard_map/ppermute | solution.py:1083
  219.5 24.2 %collective-permute-start.45 = (bf16[32,48,768]{2,1,0:T(8,128)(2,1)S(1)}, bf16[32,48,768]{2,1,0:T(8,128)(2,1)S(1)}, u32[]{:S(2)}, u32[]{:S(2)}) collective-permute-start(bf16[32,48,768]{2,1,0:T(8,128)(2,1)S(1)} %get-tuple-element.888.refs_4_.refs_9_), channel_id=1, source_target_pairs={{2,0},{3,1},{0,2},{1,3},{6,4},{7,5},{4,6},{5,7},{10,8},{11,9},{8,1... | collective-permute-start | bytes 7077896 | tf_op jit(solution)/shard_map/ppermute | solution.py:1083
  221.9 21.8 %collective-permute-start.43 = (bf16[12,48,768]{2,1,0:T(8,128)(2,1)S(1)}, bf16[12,48,768]{2,1,0:T(8,128)(2,1)S(1)}, u32[]{:S(2)}, u32[]{:S(2)}) collective-permute-start(bf16[12,48,768]{2,1,0:T(8,128)(2,1)S(1)} %get-tuple-element.856.refs_2_), channel_id=1, source_target_pairs={{4,0},{5,1},{6,2},{7,3},{0,4},{1,5},{2,6},{3,7},{12,8},{13,9},{14,... | collective-permute-start | bytes 2654216 | tf_op jit(solution)/shard_map/ppermute | solution.py:1083
  222.2 21.5 %collective-permute-start.44 = (bf16[12,48,768]{2,1,0:T(8,128)(2,1)S(1)}, bf16[12,48,768]{2,1,0:T(8,128)(2,1)S(1)}, u32[]{:S(2)}, u32[]{:S(2)}) collective-permute-start(bf16[12,48,768]{2,1,0:T(8,128)(2,1)S(1)} %get-tuple-element.857.refs_3_), channel_id=1, source_target_pairs={{1,0},{0,1},{3,2},{2,3},{5,4},{4,5},{7,6},{6,7},{9,8},{8,9},{11,10... | collective-permute-start | bytes 2654216 | tf_op jit(solution)/shard_map/ppermute | solution.py:1083
  246.0 23.5 %collective-permute-start.51 = (bf16[32,48,768]{2,1,0:T(8,128)(2,1)S(1)}, bf16[32,48,768]{2,1,0:T(8,128)(2,1)S(1)}, u32[]{:S(2)}, u32[]{:S(2)}) collective-permute-start(bf16[32,48,768]{2,1,0:T(8,128)(2,1)S(1)} %get-tuple-element.912.refs_7_.refs_11_.refs_4_), channel_id=1, source_target_pairs={{2,0},{3,1},{0,2},{1,3},{6,4},{7,5},{4,6},{5,7},{10,8},{11,9},{8,1... | collective-permute-start | bytes 7077896 | tf_op jit(solution)/shard_map/ppermute | solution.py:1083
  246.0 22.1 %collective-permute-start.49 = (bf16[12,48,768]{2,1,0:T(8,128)(2,1)S(1)}, bf16[12,48,768]{2,1,0:T(8,128)(2,1)S(1)}, u32[]{:S(2)}, u32[]{:S(2)}) collective-permute-start(bf16[12,48,768]{2,1,0:T(8,128)(2,1)S(1)} %get-tuple-element.882.refs_0_), channel_id=1, source_target_pairs={{4,0},{5,1},{6,2},{7,3},{0,4},{1,5},{2,6},{3,7},{12,8},{13,9},{14,... | collective-permute-start | bytes 2654216 | tf_op jit(solution)/shard_map/ppermute | solution.py:1083
  247.8 21.7 %collective-permute-start.50 = (bf16[12,48,768]{2,1,0:T(8,128)(2,1)S(1)}, bf16[12,48,768]{2,1,0:T(8,128)(2,1)S(1)}, u32[]{:S(2)}, u32[]{:S(2)}) collective-permute-start(bf16[12,48,768]{2,1,0:T(8,128)(2,1)S(1)} %get-tuple-element.883.refs_1_), channel_id=1, source_target_pairs={{1,0},{0,1},{3,2},{2,3},{5,4},{4,5},{7,6},{6,7},{9,8},{8,9},{11,10... | collective-permute-start | bytes 2654216 | tf_op jit(solution)/shard_map/ppermute | solution.py:1083
  270.8 18.4 %collective-permute-start.55 = (bf16[32,48,768]{2,1,0:T(8,128)(2,1)S(1)}, bf16[32,48,768]{2,1,0:T(8,128)(2,1)S(1)}, u32[]{:S(2)}, u32[]{:S(2)}) collective-permute-start(bf16[32,48,768]{2,1,0:T(8,128)(2,1)S(1)} %get-tuple-element.937.refs_4_.refs_7_), channel_id=1, source_target_pairs={{2,0},{3,1},{0,2},{1,3},{6,4},{7,5},{4,6},{5,7},{10,8},{11,9},{8,1... | collective-permute-start | bytes 7077896 | tf_op jit(solution)/shard_map/ppermute | solution.py:1083
  270.9 18.3 %collective-permute-start.53 = (bf16[8,48,768]{2,1,0:T(8,128)(2,1)S(1)}, bf16[8,48,768]{2,1,0:T(8,128)(2,1)S(1)}, u32[]{:S(2)}, u32[]{:S(2)}) collective-permute-start(bf16[8,48,768]{2,1,0:T(8,128)(2,1)S(1)} %get-tuple-element.906.refs_0_), channel_id=1, source_target_pairs={{4,0},{5,1},{6,2},{7,3},{0,4},{1,5},{2,6},{3,7},{12,8},{13,9},{14,... | collective-permute-start | bytes 1769480 | tf_op jit(solution)/shard_map/ppermute | solution.py:1083
  271.4 17.9 %collective-permute-start.54 = (bf16[8,48,768]{2,1,0:T(8,128)(2,1)S(1)}, bf16[8,48,768]{2,1,0:T(8,128)(2,1)S(1)}, u32[]{:S(2)}, u32[]{:S(2)}) collective-permute-start(bf16[8,48,768]{2,1,0:T(8,128)(2,1)S(1)} %get-tuple-element.907.refs_1_), channel_id=1, source_target_pairs={{1,0},{0,1},{3,2},{2,3},{5,4},{4,5},{7,6},{6,7},{9,8},{8,9},{11,10... | collective-permute-start | bytes 1769480 | tf_op jit(solution)/shard_map/ppermute | solution.py:1083
  271.7 17.5 %collective-permute-start.56 = (bf16[256,768]{1,0:T(8,128)(2,1)S(1)}, bf16[256,768]{1,0:T(8,128)(2,1)S(1)}, u32[]{:S(2)}, u32[]{:S(2)}) collective-permute-start(bf16[256,768]{1,0:T(8,128)(2,1)S(1)} %bitcast.51), channel_id=1, source_target_pairs={{0,0},{2,1},{1,2},{3,3},{4,4},{6,5},{5,6},{7,7},{8,8},{10,9},{9,10... | collective-permute-start | bytes 1179656 | tf_op jit(solution)/shard_map/ppermute | solution.py:1083
  309.8 15.7 %collective-permute-start.64 = (bf16[8,48,768]{2,1,0:T(8,128)(2,1)S(1)}, bf16[8,48,768]{2,1,0:T(8,128)(2,1)S(1)}, u32[]{:S(2)}, u32[]{:S(2)}) collective-permute-start(bf16[8,48,768]{2,1,0:T(8,128)(2,1)S(1)} %get-tuple-element.958.refs_13_), channel_id=1, source_target_pairs={{4,0},{5,1},{6,2},{7,3},{0,4},{1,5},{2,6},{3,7},{12,8},{13,9},{14,... | collective-permute-start | bytes 1769480 | tf_op jit(solution)/shard_map/ppermute | solution.py:1083
  311.6 15.3 %collective-permute-start.65 = (bf16[8,48,768]{2,1,0:T(8,128)(2,1)S(1)}, bf16[8,48,768]{2,1,0:T(8,128)(2,1)S(1)}, u32[]{:S(2)}, u32[]{:S(2)}) collective-permute-start(bf16[8,48,768]{2,1,0:T(8,128)(2,1)S(1)} %get-tuple-element.959.refs_14_), channel_id=1, source_target_pairs={{1,0},{0,1},{3,2},{2,3},{5,4},{4,5},{7,6},{6,7},{9,8},{8,9},{11,10... | collective-permute-start | bytes 1769480 | tf_op jit(solution)/shard_map/ppermute | solution.py:1083
  327.2 13.8 %collective-permute-start.66 = (bf16[4,48,768]{2,1,0:T(8,128)(2,1)S(1)}, bf16[4,48,768]{2,1,0:T(8,128)(2,1)S(1)}, u32[]{:S(2)}, u32[]{:S(2)}) collective-permute-start(bf16[4,48,768]{2,1,0:T(8,128)(2,1)S(1)} %get-tuple-element.972.refs_5_), channel_id=1, source_target_pairs={{4,0},{5,1},{6,2},{7,3},{0,4},{1,5},{2,6},{3,7},{12,8},{13,9},{14,... | collective-permute-start | bytes 884744 | tf_op jit(solution)/shard_map/ppermute | solution.py:1083
  341.1 23.3 %collective-permute-start.60 = (bf16[256,768]{1,0:T(8,128)(2,1)S(1)}, bf16[256,768]{1,0:T(8,128)(2,1)S(1)}, u32[]{:S(2)}, u32[]{:S(2)}) collective-permute-start(bf16[256,768]{1,0:T(8,128)(2,1)S(1)} %copy-done.134), channel_id=1, source_target_pairs={{0,0},{2,1},{1,2},{3,3},{4,4},{6,5},{5,6},{7,7},{8,8},{10,9},{9,10... | collective-permute-start | bytes 1179656 | tf_op jit(solution)/shard_map/ppermute | solution.py:1083
  342.1 17.5 %collective-permute-start.69 = (bf16[8,48,768]{2,1,0:T(8,128)(2,1)S(1)}, bf16[8,48,768]{2,1,0:T(8,128)(2,1)S(1)}, u32[]{:S(2)}, u32[]{:S(2)}) collective-permute-start(bf16[8,48,768]{2,1,0:T(8,128)(2,1)S(1)} %get-tuple-element.998), channel_id=1, source_target_pairs={{4,0},{5,1},{6,2},{7,3},{0,4},{1,5},{2,6},{3,7},{12,8},{13,9},{14,... | collective-permute-start | bytes 1769480 | tf_op jit(solution)/shard_map/ppermute | solution.py:1083
  343.8 19.7 %collective-permute-start.70 = (bf16[8,48,768]{2,1,0:T(8,128)(2,1)S(1)}, bf16[8,48,768]{2,1,0:T(8,128)(2,1)S(1)}, u32[]{:S(2)}, u32[]{:S(2)}) collective-permute-start(bf16[8,48,768]{2,1,0:T(8,128)(2,1)S(1)} %get-tuple-element.999), channel_id=1, source_target_pairs={{1,0},{0,1},{3,2},{2,3},{5,4},{4,5},{7,6},{6,7},{9,8},{8,9},{11,10... | collective-permute-start | bytes 1769480 | tf_op jit(solution)/shard_map/ppermute | solution.py:1083
  367.1 20.3 %collective-permute-start.74 = (bf16[12,48,768]{2,1,0:T(8,128)(2,1)S(1)}, bf16[12,48,768]{2,1,0:T(8,128)(2,1)S(1)}, u32[]{:S(2)}, u32[]{:S(2)}) collective-permute-start(bf16[12,48,768]{2,1,0:T(8,128)(2,1)S(1)} %get-tuple-element.1028), channel_id=1, source_target_pairs={{4,0},{5,1},{6,2},{7,3},{0,4},{1,5},{2,6},{3,7},{12,8},{13,9},{14,... | collective-permute-start | bytes 2654216 | tf_op jit(solution)/shard_map/ppermute | solution.py:1083
  368.9 20.4 %collective-permute-start.75 = (bf16[12,48,768]{2,1,0:T(8,128)(2,1)S(1)}, bf16[12,48,768]{2,1,0:T(8,128)(2,1)S(1)}, u32[]{:S(2)}, u32[]{:S(2)}) collective-permute-start(bf16[12,48,768]{2,1,0:T(8,128)(2,1)S(1)} %get-tuple-element.1029), channel_id=1, source_target_pairs={{1,0},{0,1},{3,2},{2,3},{5,4},{4,5},{7,6},{6,7},{9,8},{8,9},{11,10... | collective-permute-start | bytes 2654216 | tf_op jit(solution)/shard_map/ppermute | solution.py:1083
  389.3 16.6 %collective-permute-start.80 = (bf16[256,3840]{1,0:T(8,128)(2,1)S(1)}, bf16[256,3840]{1,0:T(8,128)(2,1)S(1)}, u32[]{:S(2)}, u32[]{:S(2)}) collective-permute-start(bf16[256,3840]{1,0:T(8,128)(2,1)S(1)} %get-tuple-element.1064.da_ref), channel_id=1, source_target_pairs={{2,0},{3,1},{0,2},{1,3},{6,4},{7,5},{4,6},{5,7},{10,8},{11,9},{8,1... | collective-permute-start | bytes 5898248 | tf_op jit(solution)/shard_map/ppermute | solution.py:1083
  390.8 29.6 %collective-permute-start.78 = (bf16[14,48,768]{2,1,0:T(8,128)(2,1)S(1)}, bf16[14,48,768]{2,1,0:T(8,128)(2,1)S(1)}, u32[]{:S(2)}, u32[]{:S(2)}) collective-permute-start(bf16[14,48,768]{2,1,0:T(8,128)(2,1)S(1)} %get-tuple-element.1055), channel_id=1, source_target_pairs={{1,0},{0,1},{3,2},{2,3},{5,4},{4,5},{7,6},{6,7},{9,8},{8,9},{11,10... | collective-permute-start | bytes 3096584 | tf_op jit(solution)/shard_map/ppermute | solution.py:1083
  396.9 20.4 %collective-permute-start.77 = (bf16[12,48,768]{2,1,0:T(8,128)(2,1)S(1)}, bf16[12,48,768]{2,1,0:T(8,128)(2,1)S(1)}, u32[]{:S(2)}, u32[]{:S(2)}) collective-permute-start(bf16[12,48,768]{2,1,0:T(8,128)(2,1)S(1)} %get-tuple-element.1054), channel_id=1, source_target_pairs={{4,0},{5,1},{6,2},{7,3},{0,4},{1,5},{2,6},{3,7},{12,8},{13,9},{14,... | collective-permute-start | bytes 2654216 | tf_op jit(solution)/shard_map/ppermute | solution.py:1083
  421.0 22.1 %collective-permute-start.82 = (bf16[12,48,768]{2,1,0:T(8,128)(2,1)S(1)}, bf16[12,48,768]{2,1,0:T(8,128)(2,1)S(1)}, u32[]{:S(2)}, u32[]{:S(2)}) collective-permute-start(bf16[12,48,768]{2,1,0:T(8,128)(2,1)S(1)} %get-tuple-element.1083), channel_id=1, source_target_pairs={{4,0},{5,1},{6,2},{7,3},{0,4},{1,5},{2,6},{3,7},{12,8},{13,9},{14,... | collective-permute-start | bytes 2654216 | tf_op jit(solution)/shard_map/ppermute | solution.py:1083
  421.4 21.8 %collective-permute-start.83 = (bf16[12,48,768]{2,1,0:T(8,128)(2,1)S(1)}, bf16[12,48,768]{2,1,0:T(8,128)(2,1)S(1)}, u32[]{:S(2)}, u32[]{:S(2)}) collective-permute-start(bf16[12,48,768]{2,1,0:T(8,128)(2,1)S(1)} %get-tuple-element.1084), channel_id=1, source_target_pairs={{1,0},{0,1},{3,2},{2,3},{5,4},{4,5},{7,6},{6,7},{9,8},{8,9},{11,10... | collective-permute-start | bytes 2654216 | tf_op jit(solution)/shard_map/ppermute | solution.py:1083
  443.8 24.4 %collective-permute-start.88 = (bf16[14,48,768]{2,1,0:T(8,128)(2,1)S(1)}, bf16[14,48,768]{2,1,0:T(8,128)(2,1)S(1)}, u32[]{:S(2)}, u32[]{:S(2)}) collective-permute-start(bf16[14,48,768]{2,1,0:T(8,128)(2,1)S(1)} %get-tuple-element.1120), channel_id=1, source_target_pairs={{1,0},{0,1},{3,2},{2,3},{5,4},{4,5},{7,6},{6,7},{9,8},{8,9},{11,10... | collective-permute-start | bytes 3096584 | tf_op jit(solution)/shard_map/ppermute | solution.py:1083
  444.1 21.0 %collective-permute-start.87 = (bf16[12,48,768]{2,1,0:T(8,128)(2,1)S(1)}, bf16[12,48,768]{2,1,0:T(8,128)(2,1)S(1)}, u32[]{:S(2)}, u32[]{:S(2)}) collective-permute-start(bf16[12,48,768]{2,1,0:T(8,128)(2,1)S(1)} %get-tuple-element.1119), channel_id=1, source_target_pairs={{4,0},{5,1},{6,2},{7,3},{0,4},{1,5},{2,6},{3,7},{12,8},{13,9},{14,... | collective-permute-start | bytes 2654216 | tf_op jit(solution)/shard_map/ppermute | solution.py:1083
  445.8 13.9 %collective-permute-start.89 = (bf16[4,48,768]{2,1,0:T(8,128)(2,1)S(1)}, bf16[4,48,768]{2,1,0:T(8,128)(2,1)S(1)}, u32[]{:S(2)}, u32[]{:S(2)}) collective-permute-start(bf16[4,48,768]{2,1,0:T(8,128)(2,1)S(1)} %get-tuple-element.1124), channel_id=1, source_target_pairs={{8,0},{9,1},{10,2},{11,3},{12,4},{13,5},{14,6},{15,7},{0,8},{1,9},... | collective-permute-start | bytes 884744 | tf_op jit(solution)/shard_map/ppermute | solution.py:1083
  468.9 25.3 %collective-permute-start.93 = (bf16[14,48,768]{2,1,0:T(8,128)(2,1)S(1)}, bf16[14,48,768]{2,1,0:T(8,128)(2,1)S(1)}, u32[]{:S(2)}, u32[]{:S(2)}) collective-permute-start(bf16[14,48,768]{2,1,0:T(8,128)(2,1)S(1)} %get-tuple-element.1153), channel_id=1, source_target_pairs={{1,0},{0,1},{3,2},{2,3},{5,4},{4,5},{7,6},{6,7},{9,8},{8,9},{11,10... | collective-permute-start | bytes 3096584 | tf_op jit(solution)/shard_map/ppermute | solution.py:1083
  469.2 21.8 %collective-permute-start.92 = (bf16[12,48,768]{2,1,0:T(8,128)(2,1)S(1)}, bf16[12,48,768]{2,1,0:T(8,128)(2,1)S(1)}, u32[]{:S(2)}, u32[]{:S(2)}) collective-permute-start(bf16[12,48,768]{2,1,0:T(8,128)(2,1)S(1)} %get-tuple-element.1152), channel_id=1, source_target_pairs={{4,0},{5,1},{6,2},{7,3},{0,4},{1,5},{2,6},{3,7},{12,8},{13,9},{14,... | collective-permute-start | bytes 2654216 | tf_op jit(solution)/shard_map/ppermute | solution.py:1083
  494.8 25.3 %collective-permute-start.98 = (bf16[14,48,768]{2,1,0:T(8,128)(2,1)S(1)}, bf16[14,48,768]{2,1,0:T(8,128)(2,1)S(1)}, u32[]{:S(2)}, u32[]{:S(2)}) collective-permute-start(bf16[14,48,768]{2,1,0:T(8,128)(2,1)S(1)} %get-tuple-element.1184), channel_id=1, source_target_pairs={{1,0},{0,1},{3,2},{2,3},{5,4},{4,5},{7,6},{6,7},{9,8},{8,9},{11,10... | collective-permute-start | bytes 3096584 | tf_op jit(solution)/shard_map/ppermute | solution.py:1083
  495.1 21.9 %collective-permute-start.97 = (bf16[12,48,768]{2,1,0:T(8,128)(2,1)S(1)}, bf16[12,48,768]{2,1,0:T(8,128)(2,1)S(1)}, u32[]{:S(2)}, u32[]{:S(2)}) collective-permute-start(bf16[12,48,768]{2,1,0:T(8,128)(2,1)S(1)} %get-tuple-element.1183), channel_id=1, source_target_pairs={{4,0},{5,1},{6,2},{7,3},{0,4},{1,5},{2,6},{3,7},{12,8},{13,9},{14,... | collective-permute-start | bytes 2654216 | tf_op jit(solution)/shard_map/ppermute | solution.py:1083
  520.7 24.5 %collective-permute-start.104 = (bf16[14,48,768]{2,1,0:T(8,128)(2,1)S(1)}, bf16[14,48,768]{2,1,0:T(8,128)(2,1)S(1)}, u32[]{:S(2)}, u32[]{:S(2)}) collective-permute-start(bf16[14,48,768]{2,1,0:T(8,128)(2,1)S(1)} %get-tuple-element.1218), channel_id=1, source_target_pairs={{1,0},{0,1},{3,2},{2,3},{5,4},{4,5},{7,6},{6,7},{9,8},{8,9},{11,10... | collective-permute-start | bytes 3096584 | tf_op jit(solution)/shard_map/ppermute | solution.py:1083
  521.1 21.1 %collective-permute-start.103 = (bf16[12,48,768]{2,1,0:T(8,128)(2,1)S(1)}, bf16[12,48,768]{2,1,0:T(8,128)(2,1)S(1)}, u32[]{:S(2)}, u32[]{:S(2)}) collective-permute-start(bf16[12,48,768]{2,1,0:T(8,128)(2,1)S(1)} %get-tuple-element.1217), channel_id=1, source_target_pairs={{4,0},{5,1},{6,2},{7,3},{0,4},{1,5},{2,6},{3,7},{12,8},{13,9},{14,... | collective-permute-start | bytes 2654216 | tf_op jit(solution)/shard_map/ppermute | solution.py:1083
  525.5 19.7 %collective-permute-start.106 = (f32[48,768]{1,0:T(8,128)S(1)}, f32[48,768]{1,0:T(8,128)S(1)}, u32[]{:S(2)}, u32[]{:S(2)}) collective-permute-start(f32[48,768]{1,0:T(8,128)S(1)} %bitcast.43), channel_id=1, source_target_pairs={{2,0},{3,1},{0,2},{1,3},{6,4},{7,5},{4,6},{5,7},{10,8},{11,9},{8,1... | collective-permute-start | bytes 442376 | tf_op jit(solution)/shard_map/ppermute | solution.py:1083
  550.5 20.5 %collective-permute-start.101 = (bf16[256,768]{1,0:T(8,128)(2,1)S(1)}, bf16[256,768]{1,0:T(8,128)(2,1)S(1)}, u32[]{:S(2)}, u32[]{:S(2)}) collective-permute-start(bf16[256,768]{1,0:T(8,128)(2,1)S(1)} %get-tuple-element.1200), channel_id=1, source_target_pairs={{0,0},{2,1},{1,2},{3,3},{4,4},{6,5},{5,6},{7,7},{8,8},{10,9},{9,10... | collective-permute-start | bytes 1179656 | tf_op jit(solution)/shard_map/ppermute | solution.py:1083
  (192 other events, 1500.3 us)

commit v5 on v4

--- a/solution.py
+++ b/solution.py
@@ -833,18 +833,21 @@
     for layer in range(layers):
         copies.append(
             pltpu.make_async_copy(
-                gots[layer].at[pl.ds(offsets[layer], 2)], buf.at[layer], sems.at[layer]
+                gots[layer].at[pl.ds(offsets[layer], 3)], buf.at[layer], sems.at[layer]
             )
         )
         copies[-1].start()
+    for each in copies:
+        each.wait()
     for side in range(2):
         yy = y if side == 0 else 1 - y
-        if side:
-            for each in copies:
-                each.wait()
         for layer in range(layers):
             for part in range(2):
-                value = (buf[layer, part] if side else owns[layer][part].astype(BF16)).astype(F32)
+                if part == 0:
+                    value = owns[layer][side].astype(BF16).astype(F32)
+                    value = value + buf[layer, 1 - side].astype(F32)
+                else:
+                    value = (buf[layer, 2] if side else owns[layer][2].astype(BF16)).astype(F32)
                 if kind == 0:
                     lanes = pl.ds(pl.multiple_of(yy * half, 128), half)
                     for member in range(2):
@@ -873,7 +876,7 @@
         in_specs=[SMEM] + [VMEM] * layers + [ANY] * layers,
         out_specs=[VMEM] * len(outs),
         scratch_shapes=[
-            pltpu.VMEM((layers, 2, rows, width), BF16),
+            pltpu.VMEM((layers, 3, rows, width), BF16),
             pltpu.SemaphoreType.DMA((layers,)),
         ],
         compiler_params=params(VMEM_MB),
@@ -892,48 +895,50 @@
         return out
 
     sends = take(2) if fresh else None
-    got_x, got_y = take(2) if first or second else (None, None)
+    got_x = take(1)[0] if first or second else None
+    got_y = take(1)[0] if first else None
     keeps = take(2) if first else None
     rests = take(2) if second else None
     pairs = take(2) if third else None
     lasts = take(2) if fourth else None
     tables = take(2 if small == 1 else 1) if small else None
     take(waits)
-    to_x, to_y = take(2) if fresh or first or fourth else (None, None)
+    to_x = take(1)[0] if fresh or first else None
+    to_y = take(1)[0] if fresh or fourth else None
     at = 0
     if fresh:
         for out, send in ((to_x, sends[0]), (to_y, sends[1])):
             for half in range(2):
                 out[half * ZS : (half + 1) * ZS] = send[half]
         at = 2 * ZS
-    got = 0
     if first:
-        outs = take(2)
-        for keep, come, rest, send in (
-            (keeps[0], got_x, outs[0], to_y),
-            (keeps[1], got_y, outs[1], to_x),
-        ):
-            rest[...] = (keep[0].astype(F32) + come[:ZS].astype(F32)).astype(BF16)
-            send[at : at + ZS] = (keep[1].astype(F32) + come[ZS : 2 * ZS].astype(F32)).astype(BF16)
-        got = 2 * ZS
-        at += ZS
+        a_rest, b_rest = take(2)
+        for half in range(2):
+            come = got_x[half * ZS : (half + 1) * ZS].astype(F32)
+            a_rest[half] = (keeps[0][half].astype(F32) + come).astype(BF16)
+        b_rest[...] = (keeps[1][0].astype(F32) + got_y[:ZS].astype(F32)).astype(BF16)
+        value = keeps[1][1].astype(F32) + got_y[ZS : 2 * ZS].astype(F32)
+        to_x[at : at + ZS] = value.astype(BF16)
     if second:
         hold, to_z1 = take(2)
-        for part, (rest, come) in enumerate(((rests[0], got_y), (rests[1], got_x))):
-            for k in range(ZS):
-                value = rest[k].astype(F32) + come[got + k].astype(F32)
-                (to_z1 if k % 2 else hold)[k // 2 * 2 + part] = value.astype(BF16)
+        begin = 2 * ZS if first else 0
+        for k in range(ZS):
+            out = to_z1 if k % 2 else hold
+            for half in range(2):
+                out[k // 2 * 3 + half] = rests[0][half, k]
+            value = rests[1][k].astype(F32) + got_x[begin + k].astype(F32)
+            out[k // 2 * 3 + 2] = value.astype(BF16)
     if third:
         hold, to_z2 = take(2)
-        for part in range(2):
-            hold[part] = pairs[0][part].astype(F32) + pairs[1][part].astype(F32)
-            value = pairs[0][2 + part].astype(F32) + pairs[1][2 + part].astype(F32)
-            to_z2[part] = value.astype(BF16)
+        for index in range(3):
+            hold[index] = pairs[0][index].astype(F32) + pairs[1][index].astype(F32)
+            value = pairs[0][3 + index].astype(F32) + pairs[1][3 + index].astype(F32)
+            to_z2[index] = value.astype(BF16)
     if fourth:
         (total,) = take(1)
-        value = lasts[0][...] + lasts[1][:2].astype(F32)
+        value = lasts[0][...] + lasts[1][:3].astype(F32)
         total[...] = value
-        to_y[at : at + 2] = value.astype(BF16)
+        to_y[at : at + 3] = value.astype(BF16)
     if small:
         come = (None, None, got_x, pairs and pairs[1], lasts and lasts[1])[small]
         come = tables[1][...] if small == 1 else come[come.shape[0] - 1]
@@ -952,22 +957,25 @@
     if fresh is not None:
         inputs += [fresh[1], fresh[3]]
     if first is not None or second is not None:
-        inputs += [got_x, got_y]
+        inputs += [got_x]
+    if first is not None:
+        inputs += [got_y]
     for value in (first, second, third, fourth, table):
         if value is not None:
             inputs += list(value)
-    going = 2 * ZS * config[0] + ZS * config[1]
-    if config[0] or config[1] or config[4]:
-        size_x, size_y = max(going, 1) + (stage == 1), going + 2 * config[4] + (stage == 4)
-        outputs += [shape((size_x, rows, width), BF16), shape((size_y, rows, width), BF16)]
+    begin = 2 * ZS * config[0]
+    if config[0] or config[1]:
+        outputs += [shape((begin + ZS * config[1] + (stage == 1), rows, width), BF16)]
+    if config[0] or config[4]:
+        outputs += [shape((begin + 3 * config[4] + (stage == 4), rows, width), BF16)]
     if config[1]:
-        outputs += [shape((ZS, rows, width), BF16)] * 2
+        outputs += [shape((2, ZS, rows, width), BF16), shape((ZS, rows, width), BF16)]
     if config[2]:
-        outputs += [shape((4, rows, width), BF16), shape((4 + (stage == 2), rows, width), BF16)]
+        outputs += [shape((6, rows, width), BF16), shape((6 + (stage == 2), rows, width), BF16)]
     if config[3]:
-        outputs += [shape((2, rows, width), F32), shape((2 + (stage == 3), rows, width), BF16)]
+        outputs += [shape((3, rows, width), F32), shape((3 + (stage == 3), rows, width), BF16)]
     if config[4]:
-        outputs += [shape((2, rows, width), F32)]
+        outputs += [shape((3, rows, width), F32)]
     if config[5]:
         outputs += [shape(table[0].shape, F32)]
     outs = list(
@@ -989,10 +997,12 @@
         del outs[:count]
         return out
 
-    sends = take(config[0] or config[1] or config[4], 2)
+    to_x = take(config[0] or config[1], 1)
+    to_y = take(config[0] or config[4], 1)
     return (
-        sends,
-        going,
+        to_x,
+        to_y,
+        begin,
         take(config[1], 2),
         take(config[2], 2),
         take(config[3], 2),
@@ -1307,7 +1317,7 @@
             for stage, g in zplan.get(r, ()):
                 if g < len(groups):
                     (start_z2 if stage == 2 else start_z1)(g)
-            if spread:
+            if spread and r >= 0:
                 table = table + move(table, spread.pop(0))
             if r == total_chunks - 1:
                 upstream = move(upstream[0], net["swap"])
@@ -1374,10 +1384,10 @@
         past = rounds[s - LAG] if s >= LAG else {}
         pick = lambda key: past.get(key)
         has_home = pick("first") is not None or pick("second") is not None
-        sends, going, first, second, third, fourth, small = sum_round(
+        to_x, to_y, going, first, second, third, fourth, small = sum_round(
             fresh,
             pick("got_x") if has_home else None,
-            pick("got_y") if has_home else None,
+            pick("got_y") if pick("first") is not None else None,
             pick("first"),
             pick("second"),
             pick("third"),
@@ -1385,15 +1395,16 @@
             loose.pop("small", (0, None)),
             tuple(loose.pop("after", ())),
         )
+        sends = (to_x or ()) + (to_y or ())
         now = {}
         if fresh is not None:
             now["first"] = (fresh[0], fresh[2])
         if first is not None:
             now["second"] = first
-        if sends is not None:
-            if going:
-                now["got_x"] = move(sends[0], net["x"])
-            now["got_y"] = move(sends[1], net["y"])
+        if to_x is not None:
+            now["got_x"] = move(to_x[0], net["x"])
+        if to_y is not None:
+            now["got_y"] = move(to_y[0], net["y"])
         if second is not None:
             now["third"] = (second[0], move(second[1], net["z1"]))
         if third is not None:

time: 604 us -> 585 us (0.969)
  waiting for transfers between devices: 231 us -> 192 us
  starting transfers between devices: 115 us -> 143 us
  local copies, waits for them, and re-layouts: 42.2 us -> 34.7 us
    ppermute x117 -> x116, waiting for transfers between devices: 231 us -> 192 us  [move(): return lax.ppermute(value, AXES, perm)]
    ppermute x117 -> x116, starting transfers between devices: 115 us -> 143 us  [move(): return lax.ppermute(value, AXES, perm)]
    unnamed x280 -> x296, local copies, waits for them, and re-layouts: 41.2 us -> 33.7 us
  transfers between devices with their start and end apart: 117 -> 116, of which waited for: 62 -> 62; matrix products, arithmetic and copies ran while one was open for 1% -> 1% of each run, Pallas kernels for 28% -> 29%
where the time goes in v5:
time: 585 us; the launch traced here: 576 us
  Pallas kernels  200 us (34%)
  waiting for transfers between devices  192 us (33%)
  starting transfers between devices  143 us (24%)
  local copies, waits for them, and re-layouts  34.7 us (6%)
    ppermute x116, waiting for transfers between devices, move(): return lax.ppermute(value, AXES, perm)  192 us
    ppermute x116, starting transfers between devices, move(): return lax.ppermute(value, AXES, perm)  143 us
    pallas_call x3, Pallas kernels, attn_forward(): pl.pallas_call(attn_kernel, out_shape=(shape((tokens, width), F32),) + ke...  39.6 us
    unnamed x296, local copies, waits for them, and re-layouts  33.7 us
    pallas_call x18, Pallas kernels, copy_blocks(): pl.pallas_call(functools.partial(copy_kernel, plan, len(inputs)), out_sha...  30.3 us
    pallas_call x3, Pallas kernels, chain_backward(): pl.pallas_call(functools.partial(chain_kernel, 384, len(after)), out_shap...  24.8 us
    pallas_call x3, Pallas kernels, attn_backward(): pl.pallas_call(functools.partial(attn_back_kernel, len(after)), out_shape...  23.3 us
    pallas_call x3, Pallas kernels, inner_forward(): pl.pallas_call(functools.partial(inner_kernel, 384), out_shape=(shape((to...  19.4 us
  transfers between devices with their start and end apart: 116, of which 62 were waited for; matrix products, arithmetic and copies ran while one was open for 1% of the time, Pallas kernels for 29%

profile of v5, /device:TPU:0, one launch (start us, length us, event | category | flops | bytes accessed | tf_op | source)
XLA Modules:
  0.0 576.0 jit_solution(2049834175081554047)
XLA Ops:
  9.3 4.1 collective-permute-start
  16.1 3.9 collective-permute-done.1
  28.8 5.1 collective-permute-done.5.refs_1_
  35.8 2.7 collective-permute-start.11
  45.4 6.1 %collective-permute-done.12.refs_1_ = bf16[2,48,768]{2,1,0:T(8,128)(2,1)S(1)} collective-permute-done((bf16[2,48,768]{2,1,0:T(8,128)(2,1)S(1)}, bf16[2,48,768]{2,1,0:T(8,128)(2,1)S(1)}, u32[]{:S(2)}, u32[]{:S(2)}) %collective-permute-start.12) | collective-permute-done | bytes 147488 | tf_op jit(solution)/shard_map/ppermute | solution.py:1093
  60.0 11.7 %collective-permute-done.17 = f32[3,12,768]{2,1,0:T(8,128)S(1)} collective-permute-done((f32[3,12,768]{2,1,0:T(8,128)S(1)}, f32[3,12,768]{2,1,0:T(8,128)S(1)}, u32[]{:S(2)}, u32[]{:S(2)}) %collective-permute-start.17) | collective-permute-done | bytes 110624 | tf_op jit(solution)/shard_map/ppermute | solution.py:1093
  81.5 5.0 collective-permute-done.23
  87.3 9.5 %collective-permute-done.22.refs_1_ = bf16[4,48,768]{2,1,0:T(8,128)(2,1)S(1)} collective-permute-done((bf16[4,48,768]{2,1,0:T(8,128)(2,1)S(1)}, bf16[4,48,768]{2,1,0:T(8,128)(2,1)S(1)}, u32[]{:S(2)}, u32[]{:S(2)}) %collective-permute-start.22) | collective-permute-done | bytes 294944 | tf_op jit(solution)/shard_map/ppermute | solution.py:1093
  96.7 2.9 collective-permute-done.21.refs_1_
  101.2 4.2 gather_round.14
  114.8 13.2 %attn_forward.3 = (f32[256,768]{1,0:T(8,128)S(1)}, f32[256,768]{1,0:T(8,128)S(1)}, f32[256,128]{1,0:T(8,128)S(1)}, bf16[256,768]{1,0:T(8,128)(2,1)S(1)}, bf16[76...) custom-call(s32[4]{0:T(128)S(1)} %pad_add_fusion.2.pos_ref.refs_0_.r, ...), custom_call_target="tpu_custom_call" | custom-call | flops 1 | bytes 1 | tf_op jit(solution)/shard_map/attn_forward/pallas_call | solution.py:265
  130.5 3.8 gather_round.15
  137.7 7.7 %inner_forward.3 = (bf16[256,3072]{1,0:T(8,128)(2,1)S(1)}, bf16[256,3072]{1,0:T(8,128)(2,1)S(1)}, bf16[2,2,2,4,48,256]{5,4,3,2,1,0:T(8,128)(2,1)S(1)}, bf16[2,2,2,4,48,256]{5,4,3,2,1,0:T(8,128)(2,1)S(1)}) custom-call(s32[4]{0:T(128)S(1)} %pad_add_fusion.2.pos_ref.refs_0_.refs_1_, s32[4]{0:T(128)S(1)} %pad_add_fusion.2.pos_ref.refs_0_.refs_1_, ...), custom_call_target="tpu_custom_call" | custom-call | flops 1 | bytes 1 | tf_op jit(solution)/shard_map/inner_forward/pallas_call | solution.py:348
  145.5 6.4 %collective-permute-done.31.refs_1_ = bf16[4,48,768]{2,1,0:T(8,128)(2,1)S(1)} collective-permute-done((bf16[4,48,768]{2,1,0:T(8,128)(2,1)S(1)}, bf16[4,48,768]{2,1,0:T(8,128)(2,1)S(1)}, u32[]{:S(2)}, u32[]{:S(2)}) %collective-permute-start.31) | collective-permute-done | bytes 294944 | tf_op jit(solution)/shard_map/ppermute | solution.py:1093
  164.8 3.3 outer_forward.3
  169.9 8.3 %collective-permute-done.37.refs_1_ = bf16[8,48,768]{2,1,0:T(8,128)(2,1)S(1)} collective-permute-done((bf16[8,48,768]{2,1,0:T(8,128)(2,1)S(1)}, bf16[8,48,768]{2,1,0:T(8,128)(2,1)S(1)}, u32[]{:S(2)}, u32[]{:S(2)}) %collective-permute-start.37) | collective-permute-done | bytes 589856 | tf_op jit(solution)/shard_map/ppermute | solution.py:1093
  178.1 4.8 collective-permute-done.34.refs_4_
  188.2 2.6 collective-permute-start.42
  190.8 13.2 %attn_forward.4 = (f32[256,768]{1,0:T(8,128)S(1)}, f32[256,768]{1,0:T(8,128)S(1)}, f32[256,128]{1,0:T(8,128)S(1)}, bf16[256,768]{1,0:T(8,128)(2,1)S(1)}, bf16[76...) custom-call(s32[4]{0:T(128)S(1)} %pad_add_fusion.2.pos_ref.refs_0_.r, ...), custom_call_target="tpu_custom_call" | custom-call | flops 1 | bytes 1 | tf_op jit(solution)/shard_map/attn_forward/pallas_call | solution.py:265
  215.2 5.9 %inner_forward.4 = (bf16[256,3072]{1,0:T(8,128)(2,1)S(1)}, bf16[256,3072]{1,0:T(8,128)(2,1)S(1)}, bf16[2,2,2,4,48,256]{5,4,3,2,1,0:T(8,128)(2,1)S(1)}, bf16[2,2,2,4,48,256]{5,4,3,2,1,0:T(8,128)(2,1)S(1)}) custom-call(s32[4]{0:T(128)S(1)} %pad_add_fusion.2.pos_ref.refs_0_.refs_1_, s32[4]{0:T(128)S(1)} %pad_add_fusion.2.pos_ref.refs_0_.refs_1_, ...), custom_call_target="tpu_custom_call" | custom-call | flops 1 | bytes 1 | tf_op jit(solution)/shard_map/inner_forward/pallas_call | solution.py:348
  222.5 2.6 collective-permute-done.48.tb_ref.xb_ref
  226.0 9.8 %collective-permute-done.43.refs_4_ = bf16[12,48,768]{2,1,0:T(8,128)(2,1)S(1)} collective-permute-done((bf16[12,48,768]{2,1,0:T(8,128)(2,1)S(1)}, bf16[12,48,768]{2,1,0:T(8,128)(2,1)S(1)}, u32[]{:S(2)}, u32[]{:S(2)}) %collective-permute-start.43) | collective-permute-done | bytes 884768 | tf_op jit(solution)/shard_map/ppermute | solution.py:1093
  240.4 2.8 outer_forward.4
  245.0 15.3 %collective-permute-done.49.refs_2_ = bf16[12,48,768]{2,1,0:T(8,128)(2,1)S(1)} collective-permute-done((bf16[12,48,768]{2,1,0:T(8,128)(2,1)S(1)}, bf16[12,48,768]{2,1,0:T(8,128)(2,1)S(1)}, u32[]{:S(2)}, u32[]{:S(2)}) %collective-permute-start.49) | collective-permute-done | bytes 884768 | tf_op jit(solution)/shard_map/ppermute | solution.py:1093
  265.2 13.2 %attn_forward.5 = (f32[256,768]{1,0:T(8,128)S(1)}, f32[256,768]{1,0:T(8,128)S(1)}, f32[256,128]{1,0:T(8,128)S(1)}, bf16[256,768]{1,0:T(8,128)(2,1)S(1)}, bf16[76...) custom-call(s32[4]{0:T(128)S(1)} %pad_add_fusion.2.pos_ref.refs_0_.r, ...), custom_call_target="tpu_custom_call" | custom-call | flops 1 | bytes 1 | tf_op jit(solution)/shard_map/attn_forward/pallas_call | solution.py:265
  283.2 2.6 collective-permute-start.57
  285.8 5.9 %inner_forward.5 = (bf16[256,3072]{1,0:T(8,128)(2,1)S(1)}, bf16[256,3072]{1,0:T(8,128)(2,1)S(1)}, bf16[2,2,2,4,48,256]{5,4,3,2,1,0:T(8,128)(2,1)S(1)}, bf16[2,2,2,4,48,256]{5,4,3,2,1,0:T(8,128)(2,1)S(1)}) custom-call(s32[4]{0:T(128)S(1)} %pad_add_fusion.2.pos_ref.refs_0_.refs_1_, s32[4]{0:T(128)S(1)} %pad_add_fusion.2.pos_ref.refs_0_.refs_1_, ...), custom_call_target="tpu_custom_call" | custom-call | flops 1 | bytes 1 | tf_op jit(solution)/shard_map/inner_forward/pallas_call | solution.py:348
  292.7 2.7 collective-permute-done.59.tb_ref.xb_ref
  295.4 3.8 outer_forward.5
  306.3 7.9 %chain_backward.3 = (bf16[256,3840]{1,0:T(8,128)(2,1)S(1)}, f32[256,768]{1,0:T(8,128)S(1)}, bf16[256,768]{1,0:T(8,128)(2,1)S(1)}, f32[16,768]{1,0:T(8,128)S(1)}) custom-call(s32[4]{0:T(128)S(1)} %pad_add_fusion.2.pos_ref.refs_0_.refs_1_, bf16[256,768]{1,0:T(8,128)(2,1)S(1)} %get-tuple-element.951.da_ref.refs_1_, f32[256,768]{1,0:T(8,128)S(1)} %get-tuple-element.958.refs_2_, ...), custom_call_target="tpu_custom_call" | custom-call | flops 1 | bytes 1 | tf_op jit(solution)/shard_map/chain_backward/pallas_call | solution.py:470
  314.3 4.1 collective-permute-done.64.refs_0_
  322.3 7.8 %attn_backward.3 = (bf16[5,256,768]{2,1,0:T(8,128)(2,1)S(1)}, f32[8,768]{1,0:T(8,128)S(1)}) custom-call(bf16[256,768]{1,0:T(8,128)(2,1)S(1)} %copy-done.101, bf16[768,512]{1,0:T(8,128)(2,1)S(1)} %copy-done.81, bf16[512,768]{1,0:T(8,128)(2,1)S(1)} %copy-done.83, bf16[12,512,256]{2,1,0:T(8,128)(2,1)S(1)} %copy-done.32, ...), custom_call_target="tpu_custom_call" | custom-call | flops 1 | bytes 1 | tf_op jit(solution)/shard_map/attn_backward/pallas_call | solution.py:543
  339.0 4.4 input_backward.3
  344.4 2.8 attn_grad.3
  352.0 4.5 collective-permute-start.74
  359.1 7.7 %chain_backward.4 = (bf16[256,3840]{1,0:T(8,128)(2,1)S(1)}, f32[256,768]{1,0:T(8,128)S(1)}, bf16[256,768]{1,0:T(8,128)(2,1)S(1)}, f32[16,768]{1,0:T(8,128)S(1)}) custom-call(s32[4]{0:T(128)S(1)} %pad_add_fusion.2.pos_ref.refs_0_.refs_1_, bf16[256,768]{1,0:T(8,128)(2,1)S(1)} %get-tuple-element.1028.refs_1_.da_ref, f32[256,768]{1,0:T(8,128)S(1)} %copy-done.61, ...), custom_call_target="tpu_custom_call" | custom-call | flops 1 | bytes 1 | tf_op jit(solution)/shard_map/chain_backward/pallas_call | solution.py:470
  371.1 2.9 collective-permute-start.79
  376.0 4.2 collective-permute-start.77
  381.9 7.8 %attn_backward.4 = (bf16[5,256,768]{2,1,0:T(8,128)(2,1)S(1)}, f32[8,768]{1,0:T(8,128)S(1)}) custom-call(bf16[256,768]{1,0:T(8,128)(2,1)S(1)} %copy-done.105, bf16[768,512]{1,0:T(8,128)(2,1)S(1)} %copy-done.77, bf16[512,768]{1,0:T(8,128)(2,1)S(1)} %copy-done.79, bf16[12,512,256]{2,1,0:T(8,128)(2,1)S(1)} %copy-done.36, ...), custom_call_target="tpu_custom_call" | custom-call | flops 1 | bytes 1 | tf_op jit(solution)/shard_map/attn_backward/pallas_call | solution.py:543
  392.5 5.6 collective-permute-done.77.refs_3_.refs_5_
  404.6 2.6 collective-permute-start.80
  407.2 4.0 input_backward.4
  411.2 2.8 attn_grad.4
  414.0 4.8 collective-permute-done.80.refs_11_
  429.9 9.3 %chain_backward.5 = (bf16[256,3840]{1,0:T(8,128)(2,1)S(1)}, f32[256,768]{1,0:T(8,128)S(1)}, bf16[256,768]{1,0:T(8,128)(2,1)S(1)}, f32[16,768]{1,0:T(8,128)S(1)}) custom-call(s32[4]{0:T(128)S(1)} %pad_add_fusion.2.pos_ref.refs_0_.refs_1_, bf16[256,768]{1,0:T(8,128)(2,1)S(1)} %get-tuple-element.1122.refs_1_.da_ref, ...), custom_call_target="tpu_custom_call" | custom-call | flops 1 | bytes 1 | tf_op jit(solution)/shard_map/chain_backward/pallas_call | solution.py:470
  445.0 2.6 collective-permute-start.92
  451.9 7.8 %attn_backward.5 = (bf16[5,256,768]{2,1,0:T(8,128)(2,1)S(1)}, f32[8,768]{1,0:T(8,128)S(1)}) custom-call(bf16[256,768]{1,0:T(8,128)(2,1)S(1)} %copy-done.103, bf16[768,512]{1,0:T(8,128)(2,1)S(1)} %copy-done.73, bf16[512,768]{1,0:T(8,128)(2,1)S(1)} %copy-done.75, bf16[12,512,256]{2,1,0:T(8,128)(2,1)S(1)} %copy-done.34, ...), custom_call_target="tpu_custom_call" | custom-call | flops 1 | bytes 1 | tf_op jit(solution)/shard_map/attn_backward/pallas_call | solution.py:543
  467.7 2.6 collective-permute-start.97
  474.6 4.0 input_backward.5
  478.6 2.8 attn_grad.5
  481.4 5.0 collective-permute-done.95.refs_11_
  490.5 2.6 collective-permute-start.103
  497.6 10.8 %collective-permute-done.101.refs_9_ = bf16[3,48,768]{2,1,0:T(8,128)(2,1)S(1)} collective-permute-done((bf16[3,48,768]{2,1,0:T(8,128)(2,1)S(1)}, bf16[3,48,768]{2,1,0:T(8,128)(2,1)S(1)}, u32[]{:S(2)}, u32[]{:S(2)}) %collective-permute-start.101) | collective-permute-done | bytes 221216 | tf_op jit(solution)/shard_map/ppermute | solution.py:1093
  516.6 2.6 collective-permute-start.108
  519.3 7.0 %collective-permute-done.106.refs_6_ = bf16[3,48,768]{2,1,0:T(8,128)(2,1)S(1)} collective-permute-done((bf16[3,48,768]{2,1,0:T(8,128)(2,1)S(1)}, bf16[3,48,768]{2,1,0:T(8,128)(2,1)S(1)}, u32[]{:S(2)}, u32[]{:S(2)}) %collective-permute-start.106) | collective-permute-done | bytes 221216 | tf_op jit(solution)/shard_map/ppermute | solution.py:1093
  527.4 2.7 collective-permute-start.112
  532.4 3.2 collective-permute-start.111
  535.6 8.3 %collective-permute-done.110.refs_3_ = bf16[3,48,768]{2,1,0:T(8,128)(2,1)S(1)} collective-permute-done((bf16[3,48,768]{2,1,0:T(8,128)(2,1)S(1)}, bf16[3,48,768]{2,1,0:T(8,128)(2,1)S(1)}, u32[]{:S(2)}, u32[]{:S(2)}) %collective-permute-start.110) | collective-permute-done | bytes 221216 | tf_op jit(solution)/shard_map/ppermute | solution.py:1093
  544.8 2.7 collective-permute-start.113
  549.4 2.8 finish.3.refs_3_
  553.4 6.0 %collective-permute-done.113.refs_1_ = bf16[4,48,768]{2,1,0:T(8,128)(2,1)S(1)} collective-permute-done((bf16[4,48,768]{2,1,0:T(8,128)(2,1)S(1)}, bf16[4,48,768]{2,1,0:T(8,128)(2,1)S(1)}, u32[]{:S(2)}, u32[]{:S(2)}) %collective-permute-start.113) | collective-permute-done | bytes 294944 | tf_op jit(solution)/shard_map/ppermute | solution.py:1093
  564.3 2.8 finish.5
  567.1 3.4 collective-permute-done.115.refs_3_
  571.4 2.7 finish.4
  (562 shorter events, 224.3 us)
Async XLA Ops:
  0.8 19.3 %collective-permute-start.3 = (bf16[256,768]{1,0:T(8,128)(2,1)}, bf16[256,768]{1,0:T(8,128)(2,1)S(1)}, u32[]{:S(2)}, u32[]{:S(2)}) collective-permute-start(bf16[256,768]{1,0:T(8,128)(2,1)} %bitcast.50), channel_id=1, source_target_pairs={{0,0},{2,1},{1,2},{3,3},{4,4},{6,5},{5,6},{7,7},{8,8},{10,9},{9,10... | collective-permute-start | bytes 1179656 | tf_op jit(solution)/shard_map/ppermute | solution.py:1093
  20.1 14.7 %collective-permute-start.8 = (bf16[256,768]{1,0:T(8,128)(2,1)S(1)}, bf16[256,768]{1,0:T(8,128)(2,1)S(1)}, u32[]{:S(2)}, u32[]{:S(2)}) collective-permute-start(bf16[256,768]{1,0:T(8,128)(2,1)S(1)} %collective-permute-done.3), channel_id=1, source_target_pairs={{2,0},{3,1},{0,2},{1,3},{6,4},{7,5},{4,6},{5,7},{10,8},{11,9},{8,1... | collective-permute-start | bytes 1179656 | tf_op jit(solution)/shard_map/ppermute | solution.py:1093
  35.8 15.8 %collective-permute-start.11 = (bf16[4,48,768]{2,1,0:T(8,128)(2,1)S(1)}, bf16[4,48,768]{2,1,0:T(8,128)(2,1)S(1)}, u32[]{:S(2)}, u32[]{:S(2)}) collective-permute-start(bf16[4,48,768]{2,1,0:T(8,128)(2,1)S(1)} %gather_z.8.refs_0_), channel_id=1, source_target_pairs={{8,0},{9,1},{10,2},{11,3},{12,4},{13,5},{14,6},{15,7},{0,8},{1,9},... | collective-permute-start | bytes 884744 | tf_op jit(solution)/shard_map/ppermute | solution.py:1093
  53.2 20.7 %collective-permute-start.13 = (bf16[12,48,768]{2,1,0:T(8,128)(2,1)S(1)}, bf16[12,48,768]{2,1,0:T(8,128)(2,1)S(1)}, u32[]{:S(2)}, u32[]{:S(2)}) collective-permute-start(bf16[12,48,768]{2,1,0:T(8,128)(2,1)S(1)} %get-tuple-element.693.refs_2_), channel_id=1, source_target_pairs={{4,0},{5,1},{6,2},{7,3},{0,4},{1,5},{2,6},{3,7},{12,8},{13,9},{14,... | collective-permute-start | bytes 2654216 | tf_op jit(solution)/shard_map/ppermute | solution.py:1093
  54.0 20.1 %collective-permute-start.14 = (bf16[12,48,768]{2,1,0:T(8,128)(2,1)S(1)}, bf16[12,48,768]{2,1,0:T(8,128)(2,1)S(1)}, u32[]{:S(2)}, u32[]{:S(2)}) collective-permute-start(bf16[12,48,768]{2,1,0:T(8,128)(2,1)S(1)} %get-tuple-element.694.refs_3_), channel_id=1, source_target_pairs={{1,0},{0,1},{3,2},{2,3},{5,4},{4,5},{7,6},{6,7},{9,8},{8,9},{11,10... | collective-permute-start | bytes 2654216 | tf_op jit(solution)/shard_map/ppermute | solution.py:1093
  56.4 15.4 %collective-permute-start.15 = (bf16[4,48,768]{2,1,0:T(8,128)(2,1)S(1)}, bf16[4,48,768]{2,1,0:T(8,128)(2,1)S(1)}, u32[]{:S(2)}, u32[]{:S(2)}) collective-permute-start(bf16[4,48,768]{2,1,0:T(8,128)(2,1)S(1)} %gather_z.9.refs_0_), channel_id=1, source_target_pairs={{8,0},{9,1},{10,2},{11,3},{12,4},{13,5},{14,6},{15,7},{0,8},{1,9},... | collective-permute-start | bytes 884744 | tf_op jit(solution)/shard_map/ppermute | solution.py:1093
  57.0 14.7 %collective-permute-start.16 = (bf16[2,48,768]{2,1,0:T(8,128)(2,1)S(1)}, bf16[2,48,768]{2,1,0:T(8,128)(2,1)S(1)}, u32[]{:S(2)}, u32[]{:S(2)}) collective-permute-start(bf16[2,48,768]{2,1,0:T(8,128)(2,1)S(1)} %pack.10.refs_0_), channel_id=1, source_target_pairs={{16,0},{17,1},{18,2},{19,3},{20,4},{21,5},{22,6},{23,7},{24,8},{25... | collective-permute-start | bytes 442376 | tf_op jit(solution)/shard_map/ppermute | solution.py:1093
  76.3 23.5 %collective-permute-start.20 = (bf16[32,48,768]{2,1,0:T(8,128)(2,1)S(1)}, bf16[32,48,768]{2,1,0:T(8,128)(2,1)S(1)}, u32[]{:S(2)}, u32[]{:S(2)}) collective-permute-start(bf16[32,48,768]{2,1,0:T(8,128)(2,1)S(1)} %get-tuple-element.740.refs_7_.refs_11_.refs_4_), channel_id=1, source_target_pairs={{2,0},{3,1},{0,2},{1,3},{6,4},{7,5},{4,6},{5,7},{10,8},{11,9},{8,1... | collective-permute-start | bytes 7077896 | tf_op jit(solution)/shard_map/ppermute | solution.py:1093
  76.3 23.3 %collective-permute-start.18 = (bf16[12,48,768]{2,1,0:T(8,128)(2,1)S(1)}, bf16[12,48,768]{2,1,0:T(8,128)(2,1)S(1)}, u32[]{:S(2)}, u32[]{:S(2)}) collective-permute-start(bf16[12,48,768]{2,1,0:T(8,128)(2,1)S(1)} %get-tuple-element.711.refs_2_), channel_id=1, source_target_pairs={{4,0},{5,1},{6,2},{7,3},{0,4},{1,5},{2,6},{3,7},{12,8},{13,9},{14,... | collective-permute-start | bytes 2654216 | tf_op jit(solution)/shard_map/ppermute | solution.py:1093
  78.1 21.7 %collective-permute-start.19 = (bf16[12,48,768]{2,1,0:T(8,128)(2,1)S(1)}, bf16[12,48,768]{2,1,0:T(8,128)(2,1)S(1)}, u32[]{:S(2)}, u32[]{:S(2)}) collective-permute-start(bf16[12,48,768]{2,1,0:T(8,128)(2,1)S(1)} %get-tuple-element.712.refs_3_), channel_id=1, source_target_pairs={{1,0},{0,1},{3,2},{2,3},{5,4},{4,5},{7,6},{6,7},{9,8},{8,9},{11,10... | collective-permute-start | bytes 2654216 | tf_op jit(solution)/shard_map/ppermute | solution.py:1093
  80.5 16.2 %collective-permute-start.22 = (bf16[4,48,768]{2,1,0:T(8,128)(2,1)S(1)}, bf16[4,48,768]{2,1,0:T(8,128)(2,1)S(1)}, u32[]{:S(2)}, u32[]{:S(2)}) collective-permute-start(bf16[4,48,768]{2,1,0:T(8,128)(2,1)S(1)} %pack.11.refs_0_), channel_id=1, source_target_pairs={{16,0},{17,1},{18,2},{19,3},{20,4},{21,5},{22,6},{23,7},{24,8},{25... | collective-permute-start | bytes 884744 | tf_op jit(solution)/shard_map/ppermute | solution.py:1093
  105.4 25.1 %collective-permute-start.26 = (bf16[32,48,768]{2,1,0:T(8,128)(2,1)}, bf16[32,48,768]{2,1,0:T(8,128)(2,1)}, u32[]{:S(2)}, u32[]{:S(2)}) collective-permute-start(bf16[32,48,768]{2,1,0:T(8,128)(2,1)} %get-tuple-element.782.refs_4_.refs_7_), channel_id=1, source_target_pairs={{2,0},{3,1},{0,2},{1,3},{6,4},{7,5},{4,6},{5,7},{10,8},{11,9},{8,1... | collective-permute-start | bytes 7077896 | tf_op jit(solution)/shard_map/ppermute | solution.py:1093
  105.5 25.0 %collective-permute-start.24 = (bf16[12,48,768]{2,1,0:T(8,128)(2,1)}, bf16[12,48,768]{2,1,0:T(8,128)(2,1)}, u32[]{:S(2)}, u32[]{:S(2)}) collective-permute-start(bf16[12,48,768]{2,1,0:T(8,128)(2,1)} %get-tuple-element.730.refs_2_), channel_id=1, source_target_pairs={{4,0},{5,1},{6,2},{7,3},{0,4},{1,5},{2,6},{3,7},{12,8},{13,9},{14,... | collective-permute-start | bytes 2654216 | tf_op jit(solution)/shard_map/ppermute | solution.py:1093
  105.9 24.6 %collective-permute-start.25 = (bf16[12,48,768]{2,1,0:T(8,128)(2,1)}, bf16[12,48,768]{2,1,0:T(8,128)(2,1)}, u32[]{:S(2)}, u32[]{:S(2)}) collective-permute-start(bf16[12,48,768]{2,1,0:T(8,128)(2,1)} %get-tuple-element.731.refs_3_), channel_id=1, source_target_pairs={{1,0},{0,1},{3,2},{2,3},{5,4},{4,5},{7,6},{6,7},{9,8},{8,9},{11,10... | collective-permute-start | bytes 2654216 | tf_op jit(solution)/shard_map/ppermute | solution.py:1093
  108.2 22.3 %collective-permute-start.27 = (bf16[8,48,768]{2,1,0:T(8,128)(2,1)S(1)}, bf16[8,48,768]{2,1,0:T(8,128)(2,1)}, u32[]{:S(2)}, u32[]{:S(2)}) collective-permute-start(bf16[8,48,768]{2,1,0:T(8,128)(2,1)S(1)} %gather_z.11.refs_0_), channel_id=1, source_target_pairs={{8,0},{9,1},{10,2},{11,3},{12,4},{13,5},{14,6},{15,7},{0,8},{1,9},... | collective-permute-start | bytes 1769480 | tf_op jit(solution)/shard_map/ppermute | solution.py:1093
  134.4 24.3 %collective-permute-start.30 = (bf16[32,48,768]{2,1,0:T(8,128)(2,1)S(1)}, bf16[32,48,768]{2,1,0:T(8,128)(2,1)S(1)}, u32[]{:S(2)}, u32[]{:S(2)}) collective-permute-start(bf16[32,48,768]{2,1,0:T(8,128)(2,1)S(1)} %get-tuple-element.800.refs_4_.refs_9_), channel_id=1, source_target_pairs={{2,0},{3,1},{0,2},{1,3},{6,4},{7,5},{4,6},{5,7},{10,8},{11,9},{8,1... | collective-permute-start | bytes 7077896 | tf_op jit(solution)/shard_map/ppermute | solution.py:1093
  135.1 16.7 %collective-permute-start.31 = (bf16[4,48,768]{2,1,0:T(8,128)(2,1)S(1)}, bf16[4,48,768]{2,1,0:T(8,128)(2,1)S(1)}, u32[]{:S(2)}, u32[]{:S(2)}) collective-permute-start(bf16[4,48,768]{2,1,0:T(8,128)(2,1)S(1)} %pack.12.refs_0_), channel_id=1, source_target_pairs={{16,0},{17,1},{18,2},{19,3},{20,4},{21,5},{22,6},{23,7},{24,8},{25... | collective-permute-start | bytes 884744 | tf_op jit(solution)/shard_map/ppermute | solution.py:1093
  135.2 22.1 %collective-permute-start.28 = (bf16[12,48,768]{2,1,0:T(8,128)(2,1)S(1)}, bf16[12,48,768]{2,1,0:T(8,128)(2,1)S(1)}, u32[]{:S(2)}, u32[]{:S(2)}) collective-permute-start(bf16[12,48,768]{2,1,0:T(8,128)(2,1)S(1)} %get-tuple-element.762.refs_2_), channel_id=1, source_target_pairs={{4,0},{5,1},{6,2},{7,3},{0,4},{1,5},{2,6},{3,7},{12,8},{13,9},{14,... | collective-permute-start | bytes 2654216 | tf_op jit(solution)/shard_map/ppermute | solution.py:1093
  137.0 21.8 %collective-permute-start.29 = (bf16[12,48,768]{2,1,0:T(8,128)(2,1)S(1)}, bf16[12,48,768]{2,1,0:T(8,128)(2,1)S(1)}, u32[]{:S(2)}, u32[]{:S(2)}) collective-permute-start(bf16[12,48,768]{2,1,0:T(8,128)(2,1)S(1)} %get-tuple-element.763.refs_3_), channel_id=1, source_target_pairs={{1,0},{0,1},{3,2},{2,3},{5,4},{4,5},{7,6},{6,7},{9,8},{8,9},{11,10... | collective-permute-start | bytes 2654216 | tf_op jit(solution)/shard_map/ppermute | solution.py:1093
  160.8 22.2 %collective-permute-start.36 = (bf16[32,48,768]{2,1,0:T(8,128)(2,1)S(1)}, bf16[32,48,768]{2,1,0:T(8,128)(2,1)S(1)}, u32[]{:S(2)}, u32[]{:S(2)}) collective-permute-start(bf16[32,48,768]{2,1,0:T(8,128)(2,1)S(1)} %get-tuple-element.838.refs_7_.refs_11_.refs_4_), channel_id=1, source_target_pairs={{2,0},{3,1},{0,2},{1,3},{6,4},{7,5},{4,6},{5,7},{10,8},{11,9},{8,1... | collective-permute-start | bytes 7077896 | tf_op jit(solution)/shard_map/ppermute | solution.py:1093
  160.8 22.1 %collective-permute-start.34 = (bf16[12,48,768]{2,1,0:T(8,128)(2,1)S(1)}, bf16[12,48,768]{2,1,0:T(8,128)(2,1)S(1)}, u32[]{:S(2)}, u32[]{:S(2)}) collective-permute-start(bf16[12,48,768]{2,1,0:T(8,128)(2,1)S(1)} %get-tuple-element.792.refs_2_), channel_id=1, source_target_pairs={{4,0},{5,1},{6,2},{7,3},{0,4},{1,5},{2,6},{3,7},{12,8},{13,9},{14,... | collective-permute-start | bytes 2654216 | tf_op jit(solution)/shard_map/ppermute | solution.py:1093
  161.3 21.7 %collective-permute-start.35 = (bf16[12,48,768]{2,1,0:T(8,128)(2,1)S(1)}, bf16[12,48,768]{2,1,0:T(8,128)(2,1)S(1)}, u32[]{:S(2)}, u32[]{:S(2)}) collective-permute-start(bf16[12,48,768]{2,1,0:T(8,128)(2,1)S(1)} %get-tuple-element.793.refs_3_), channel_id=1, source_target_pairs={{1,0},{0,1},{3,2},{2,3},{5,4},{4,5},{7,6},{6,7},{9,8},{8,9},{11,10... | collective-permute-start | bytes 2654216 | tf_op jit(solution)/shard_map/ppermute | solution.py:1093
  162.7 15.4 %collective-permute-start.37 = (bf16[8,48,768]{2,1,0:T(8,128)(2,1)S(1)}, bf16[8,48,768]{2,1,0:T(8,128)(2,1)S(1)}, u32[]{:S(2)}, u32[]{:S(2)}) collective-permute-start(bf16[8,48,768]{2,1,0:T(8,128)(2,1)S(1)} %gather_z.12.refs_0_), channel_id=1, source_target_pairs={{8,0},{9,1},{10,2},{11,3},{12,4},{13,5},{14,6},{15,7},{0,8},{1,9},... | collective-permute-start | bytes 1769480 | tf_op jit(solution)/shard_map/ppermute | solution.py:1093
  185.2 23.5 %collective-permute-start.41 = (bf16[32,48,768]{2,1,0:T(8,128)(2,1)S(1)}, bf16[32,48,768]{2,1,0:T(8,128)(2,1)S(1)}, u32[]{:S(2)}, u32[]{:S(2)}) collective-permute-start(bf16[32,48,768]{2,1,0:T(8,128)(2,1)S(1)} %get-tuple-element.870.refs_4_.refs_7_), channel_id=1, source_target_pairs={{2,0},{3,1},{0,2},{1,3},{6,4},{7,5},{4,6},{5,7},{10,8},{11,9},{8,1... | collective-permute-start | bytes 7077896 | tf_op jit(solution)/shard_map/ppermute | solution.py:1093
  185.3 22.1 %collective-permute-start.39 = (bf16[12,48,768]{2,1,0:T(8,128)(2,1)S(1)}, bf16[12,48,768]{2,1,0:T(8,128)(2,1)S(1)}, u32[]{:S(2)}, u32[]{:S(2)}) collective-permute-start(bf16[12,48,768]{2,1,0:T(8,128)(2,1)S(1)} %get-tuple-element.826.refs_2_), channel_id=1, source_target_pairs={{4,0},{5,1},{6,2},{7,3},{0,4},{1,5},{2,6},{3,7},{12,8},{13,9},{14,... | collective-permute-start | bytes 2654216 | tf_op jit(solution)/shard_map/ppermute | solution.py:1093
  187.0 21.7 %collective-permute-start.40 = (bf16[12,48,768]{2,1,0:T(8,128)(2,1)S(1)}, bf16[12,48,768]{2,1,0:T(8,128)(2,1)S(1)}, u32[]{:S(2)}, u32[]{:S(2)}) collective-permute-start(bf16[12,48,768]{2,1,0:T(8,128)(2,1)S(1)} %get-tuple-element.827.refs_3_), channel_id=1, source_target_pairs={{1,0},{0,1},{3,2},{2,3},{5,4},{4,5},{7,6},{6,7},{9,8},{8,9},{11,10... | collective-permute-start | bytes 2654216 | tf_op jit(solution)/shard_map/ppermute | solution.py:1093
  188.2 19.0 %collective-permute-start.42 = (bf16[2,48,768]{2,1,0:T(8,128)(2,1)S(1)}, bf16[2,48,768]{2,1,0:T(8,128)(2,1)S(1)}, u32[]{:S(2)}, u32[]{:S(2)}) collective-permute-start(bf16[2,48,768]{2,1,0:T(8,128)(2,1)S(1)} %pack.13.refs_0_), channel_id=1, source_target_pairs={{16,0},{17,1},{18,2},{19,3},{20,4},{21,5},{22,6},{23,7},{24,8},{25... | collective-permute-start | bytes 442376 | tf_op jit(solution)/shard_map/ppermute | solution.py:1093
  211.0 24.9 %collective-permute-start.45 = (bf16[32,48,768]{2,1,0:T(8,128)(2,1)S(1)}, bf16[32,48,768]{2,1,0:T(8,128)(2,1)S(1)}, u32[]{:S(2)}, u32[]{:S(2)}) collective-permute-start(bf16[32,48,768]{2,1,0:T(8,128)(2,1)S(1)} %get-tuple-element.886.refs_4_.refs_9_), channel_id=1, source_target_pairs={{2,0},{3,1},{0,2},{1,3},{6,4},{7,5},{4,6},{5,7},{10,8},{11,9},{8,1... | collective-permute-start | bytes 7077896 | tf_op jit(solution)/shard_map/ppermute | solution.py:1093
  214.1 21.8 %collective-permute-start.43 = (bf16[12,48,768]{2,1,0:T(8,128)(2,1)S(1)}, bf16[12,48,768]{2,1,0:T(8,128)(2,1)S(1)}, u32[]{:S(2)}, u32[]{:S(2)}) collective-permute-start(bf16[12,48,768]{2,1,0:T(8,128)(2,1)S(1)} %get-tuple-element.854.refs_2_), channel_id=1, source_target_pairs={{4,0},{5,1},{6,2},{7,3},{0,4},{1,5},{2,6},{3,7},{12,8},{13,9},{14,... | collective-permute-start | bytes 2654216 | tf_op jit(solution)/shard_map/ppermute | solution.py:1093
  214.5 21.5 %collective-permute-start.44 = (bf16[12,48,768]{2,1,0:T(8,128)(2,1)S(1)}, bf16[12,48,768]{2,1,0:T(8,128)(2,1)S(1)}, u32[]{:S(2)}, u32[]{:S(2)}) collective-permute-start(bf16[12,48,768]{2,1,0:T(8,128)(2,1)S(1)} %get-tuple-element.855.refs_3_), channel_id=1, source_target_pairs={{1,0},{0,1},{3,2},{2,3},{5,4},{4,5},{7,6},{6,7},{9,8},{8,9},{11,10... | collective-permute-start | bytes 2654216 | tf_op jit(solution)/shard_map/ppermute | solution.py:1093
  238.2 23.5 %collective-permute-start.51 = (bf16[32,48,768]{2,1,0:T(8,128)(2,1)S(1)}, bf16[32,48,768]{2,1,0:T(8,128)(2,1)S(1)}, u32[]{:S(2)}, u32[]{:S(2)}) collective-permute-start(bf16[32,48,768]{2,1,0:T(8,128)(2,1)S(1)} %get-tuple-element.910.refs_7_.refs_11_.refs_4_), channel_id=1, source_target_pairs={{2,0},{3,1},{0,2},{1,3},{6,4},{7,5},{4,6},{5,7},{10,8},{11,9},{8,1... | collective-permute-start | bytes 7077896 | tf_op jit(solution)/shard_map/ppermute | solution.py:1093
  238.3 22.1 %collective-permute-start.49 = (bf16[12,48,768]{2,1,0:T(8,128)(2,1)S(1)}, bf16[12,48,768]{2,1,0:T(8,128)(2,1)S(1)}, u32[]{:S(2)}, u32[]{:S(2)}) collective-permute-start(bf16[12,48,768]{2,1,0:T(8,128)(2,1)S(1)} %get-tuple-element.880.refs_0_), channel_id=1, source_target_pairs={{4,0},{5,1},{6,2},{7,3},{0,4},{1,5},{2,6},{3,7},{12,8},{13,9},{14,... | collective-permute-start | bytes 2654216 | tf_op jit(solution)/shard_map/ppermute | solution.py:1093
  240.0 21.7 %collective-permute-start.50 = (bf16[12,48,768]{2,1,0:T(8,128)(2,1)S(1)}, bf16[12,48,768]{2,1,0:T(8,128)(2,1)S(1)}, u32[]{:S(2)}, u32[]{:S(2)}) collective-permute-start(bf16[12,48,768]{2,1,0:T(8,128)(2,1)S(1)} %get-tuple-element.881.refs_1_), channel_id=1, source_target_pairs={{1,0},{0,1},{3,2},{2,3},{5,4},{4,5},{7,6},{6,7},{9,8},{8,9},{11,10... | collective-permute-start | bytes 2654216 | tf_op jit(solution)/shard_map/ppermute | solution.py:1093
  263.1 18.8 %collective-permute-start.55 = (bf16[32,48,768]{2,1,0:T(8,128)(2,1)S(1)}, bf16[32,48,768]{2,1,0:T(8,128)(2,1)S(1)}, u32[]{:S(2)}, u32[]{:S(2)}) collective-permute-start(bf16[32,48,768]{2,1,0:T(8,128)(2,1)S(1)} %get-tuple-element.935.refs_4_.refs_7_), channel_id=1, source_target_pairs={{2,0},{3,1},{0,2},{1,3},{6,4},{7,5},{4,6},{5,7},{10,8},{11,9},{8,1... | collective-permute-start | bytes 7077896 | tf_op jit(solution)/shard_map/ppermute | solution.py:1093
  263.2 18.7 %collective-permute-start.53 = (bf16[8,48,768]{2,1,0:T(8,128)(2,1)S(1)}, bf16[8,48,768]{2,1,0:T(8,128)(2,1)S(1)}, u32[]{:S(2)}, u32[]{:S(2)}) collective-permute-start(bf16[8,48,768]{2,1,0:T(8,128)(2,1)S(1)} %get-tuple-element.904.refs_0_), channel_id=1, source_target_pairs={{4,0},{5,1},{6,2},{7,3},{0,4},{1,5},{2,6},{3,7},{12,8},{13,9},{14,... | collective-permute-start | bytes 1769480 | tf_op jit(solution)/shard_map/ppermute | solution.py:1093
  263.6 18.3 %collective-permute-start.54 = (bf16[8,48,768]{2,1,0:T(8,128)(2,1)S(1)}, bf16[8,48,768]{2,1,0:T(8,128)(2,1)S(1)}, u32[]{:S(2)}, u32[]{:S(2)}) collective-permute-start(bf16[8,48,768]{2,1,0:T(8,128)(2,1)S(1)} %get-tuple-element.905.refs_1_), channel_id=1, source_target_pairs={{1,0},{0,1},{3,2},{2,3},{5,4},{4,5},{7,6},{6,7},{9,8},{8,9},{11,10... | collective-permute-start | bytes 1769480 | tf_op jit(solution)/shard_map/ppermute | solution.py:1093
  264.3 17.5 %collective-permute-start.56 = (bf16[256,768]{1,0:T(8,128)(2,1)S(1)}, bf16[256,768]{1,0:T(8,128)(2,1)S(1)}, u32[]{:S(2)}, u32[]{:S(2)}) collective-permute-start(bf16[256,768]{1,0:T(8,128)(2,1)S(1)} %bitcast.51), channel_id=1, source_target_pairs={{0,0},{2,1},{1,2},{3,3},{4,4},{6,5},{5,6},{7,7},{8,8},{10,9},{9,10... | collective-permute-start | bytes 1179656 | tf_op jit(solution)/shard_map/ppermute | solution.py:1093
  302.7 15.7 %collective-permute-start.64 = (bf16[8,48,768]{2,1,0:T(8,128)(2,1)S(1)}, bf16[8,48,768]{2,1,0:T(8,128)(2,1)S(1)}, u32[]{:S(2)}, u32[]{:S(2)}) collective-permute-start(bf16[8,48,768]{2,1,0:T(8,128)(2,1)S(1)} %get-tuple-element.956.refs_13_), channel_id=1, source_target_pairs={{4,0},{5,1},{6,2},{7,3},{0,4},{1,5},{2,6},{3,7},{12,8},{13,9},{14,... | collective-permute-start | bytes 1769480 | tf_op jit(solution)/shard_map/ppermute | solution.py:1093
  304.4 15.3 %collective-permute-start.65 = (bf16[8,48,768]{2,1,0:T(8,128)(2,1)S(1)}, bf16[8,48,768]{2,1,0:T(8,128)(2,1)S(1)}, u32[]{:S(2)}, u32[]{:S(2)}) collective-permute-start(bf16[8,48,768]{2,1,0:T(8,128)(2,1)S(1)} %get-tuple-element.957.refs_14_), channel_id=1, source_target_pairs={{1,0},{0,1},{3,2},{2,3},{5,4},{4,5},{7,6},{6,7},{9,8},{8,9},{11,10... | collective-permute-start | bytes 1769480 | tf_op jit(solution)/shard_map/ppermute | solution.py:1093
  333.6 15.2 %collective-permute-start.68 = (bf16[8,48,768]{2,1,0:T(8,128)(2,1)S(1)}, bf16[8,48,768]{2,1,0:T(8,128)(2,1)S(1)}, u32[]{:S(2)}, u32[]{:S(2)}) collective-permute-start(bf16[8,48,768]{2,1,0:T(8,128)(2,1)S(1)} %get-tuple-element.994), channel_id=1, source_target_pairs={{4,0},{5,1},{6,2},{7,3},{0,4},{1,5},{2,6},{3,7},{12,8},{13,9},{14,... | collective-permute-start | bytes 1769480 | tf_op jit(solution)/shard_map/ppermute | solution.py:1093
  335.2 15.0 %collective-permute-start.69 = (bf16[8,48,768]{2,1,0:T(8,128)(2,1)S(1)}, bf16[8,48,768]{2,1,0:T(8,128)(2,1)S(1)}, u32[]{:S(2)}, u32[]{:S(2)}) collective-permute-start(bf16[8,48,768]{2,1,0:T(8,128)(2,1)S(1)} %get-tuple-element.995), channel_id=1, source_target_pairs={{1,0},{0,1},{3,2},{2,3},{5,4},{4,5},{7,6},{6,7},{9,8},{8,9},{11,10... | collective-permute-start | bytes 1769480 | tf_op jit(solution)/shard_map/ppermute | solution.py:1093
  351.7 19.4 %collective-permute-start.73 = (bf16[12,48,768]{2,1,0:T(8,128)(2,1)S(1)}, bf16[12,48,768]{2,1,0:T(8,128)(2,1)S(1)}, u32[]{:S(2)}, u32[]{:S(2)}) collective-permute-start(bf16[12,48,768]{2,1,0:T(8,128)(2,1)S(1)} %get-tuple-element.1024), channel_id=1, source_target_pairs={{4,0},{5,1},{6,2},{7,3},{0,4},{1,5},{2,6},{3,7},{12,8},{13,9},{14,... | collective-permute-start | bytes 2654216 | tf_op jit(solution)/shard_map/ppermute | solution.py:1093
  352.0 18.4 %collective-permute-start.74 = (bf16[8,48,768]{2,1,0:T(8,128)(2,1)S(1)}, bf16[8,48,768]{2,1,0:T(8,128)(2,1)S(1)}, u32[]{:S(2)}, u32[]{:S(2)}) collective-permute-start(bf16[8,48,768]{2,1,0:T(8,128)(2,1)S(1)} %get-tuple-element.1025), channel_id=1, source_target_pairs={{1,0},{0,1},{3,2},{2,3},{5,4},{4,5},{7,6},{6,7},{9,8},{8,9},{11,10... | collective-permute-start | bytes 1769480 | tf_op jit(solution)/shard_map/ppermute | solution.py:1093
  371.1 18.6 %collective-permute-start.79 = (bf16[256,3840]{1,0:T(8,128)(2,1)S(1)}, bf16[256,3840]{1,0:T(8,128)(2,1)S(1)}, u32[]{:S(2)}, u32[]{:S(2)}) collective-permute-start(bf16[256,3840]{1,0:T(8,128)(2,1)S(1)} %get-tuple-element.1060.da_ref), channel_id=1, source_target_pairs={{2,0},{3,1},{0,2},{1,3},{6,4},{7,5},{4,6},{5,7},{10,8},{11,9},{8,1... | collective-permute-start | bytes 5898248 | tf_op jit(solution)/shard_map/ppermute | solution.py:1093
  375.6 22.5 %collective-permute-start.76 = (bf16[12,48,768]{2,1,0:T(8,128)(2,1)S(1)}, bf16[12,48,768]{2,1,0:T(8,128)(2,1)S(1)}, u32[]{:S(2)}, u32[]{:S(2)}) collective-permute-start(bf16[12,48,768]{2,1,0:T(8,128)(2,1)S(1)} %get-tuple-element.1050), channel_id=1, source_target_pairs={{4,0},{5,1},{6,2},{7,3},{0,4},{1,5},{2,6},{3,7},{12,8},{13,9},{14,... | collective-permute-start | bytes 2654216 | tf_op jit(solution)/shard_map/ppermute | solution.py:1093
  376.0 22.1 %collective-permute-start.77 = (bf16[11,48,768]{2,1,0:T(8,128)(2,1)S(1)}, bf16[11,48,768]{2,1,0:T(8,128)(2,1)S(1)}, u32[]{:S(2)}, u32[]{:S(2)}) collective-permute-start(bf16[11,48,768]{2,1,0:T(8,128)(2,1)S(1)} %get-tuple-element.1051), channel_id=1, source_target_pairs={{1,0},{0,1},{3,2},{2,3},{5,4},{4,5},{7,6},{6,7},{9,8},{8,9},{11,10... | collective-permute-start | bytes 2433032 | tf_op jit(solution)/shard_map/ppermute | solution.py:1093
  399.6 21.6 %collective-permute-start.81 = (bf16[12,48,768]{2,1,0:T(8,128)(2,1)S(1)}, bf16[12,48,768]{2,1,0:T(8,128)(2,1)S(1)}, u32[]{:S(2)}, u32[]{:S(2)}) collective-permute-start(bf16[12,48,768]{2,1,0:T(8,128)(2,1)S(1)} %get-tuple-element.1079), channel_id=1, source_target_pairs={{4,0},{5,1},{6,2},{7,3},{0,4},{1,5},{2,6},{3,7},{12,8},{13,9},{14,... | collective-permute-start | bytes 2654216 | tf_op jit(solution)/shard_map/ppermute | solution.py:1093
  401.3 18.4 %collective-permute-start.82 = (bf16[8,48,768]{2,1,0:T(8,128)(2,1)S(1)}, bf16[8,48,768]{2,1,0:T(8,128)(2,1)S(1)}, u32[]{:S(2)}, u32[]{:S(2)}) collective-permute-start(bf16[8,48,768]{2,1,0:T(8,128)(2,1)S(1)} %get-tuple-element.1080), channel_id=1, source_target_pairs={{1,0},{0,1},{3,2},{2,3},{5,4},{4,5},{7,6},{6,7},{9,8},{8,9},{11,10... | collective-permute-start | bytes 1769480 | tf_op jit(solution)/shard_map/ppermute | solution.py:1093
  402.9 16.7 %collective-permute-start.83 = (bf16[6,48,768]{2,1,0:T(8,128)(2,1)S(1)}, bf16[6,48,768]{2,1,0:T(8,128)(2,1)S(1)}, u32[]{:S(2)}, u32[]{:S(2)}) collective-permute-start(bf16[6,48,768]{2,1,0:T(8,128)(2,1)S(1)} %get-tuple-element.1084), channel_id=1, source_target_pairs={{8,0},{9,1},{10,2},{11,3},{12,4},{13,5},{14,6},{15,7},{0,8},{1,9},... | collective-permute-start | bytes 1327112 | tf_op jit(solution)/shard_map/ppermute | solution.py:1093
  421.8 21.5 %collective-permute-start.86 = (bf16[12,48,768]{2,1,0:T(8,128)(2,1)S(1)}, bf16[12,48,768]{2,1,0:T(8,128)(2,1)S(1)}, u32[]{:S(2)}, u32[]{:S(2)}) collective-permute-start(bf16[12,48,768]{2,1,0:T(8,128)(2,1)S(1)} %get-tuple-element.1115), channel_id=1, source_target_pairs={{4,0},{5,1},{6,2},{7,3},{0,4},{1,5},{2,6},{3,7},{12,8},{13,9},{14,... | collective-permute-start | bytes 2654216 | tf_op jit(solution)/shard_map/ppermute | solution.py:1093
  423.5 19.8 %collective-permute-start.87 = (bf16[11,48,768]{2,1,0:T(8,128)(2,1)S(1)}, bf16[11,48,768]{2,1,0:T(8,128)(2,1)S(1)}, u32[]{:S(2)}, u32[]{:S(2)}) collective-permute-start(bf16[11,48,768]{2,1,0:T(8,128)(2,1)S(1)} %get-tuple-element.1116), channel_id=1, source_target_pairs={{1,0},{0,1},{3,2},{2,3},{5,4},{4,5},{7,6},{6,7},{9,8},{8,9},{11,10... | collective-permute-start | bytes 2433032 | tf_op jit(solution)/shard_map/ppermute | solution.py:1093
  425.6 16.0 %collective-permute-start.88 = (bf16[6,48,768]{2,1,0:T(8,128)(2,1)S(1)}, bf16[6,48,768]{2,1,0:T(8,128)(2,1)S(1)}, u32[]{:S(2)}, u32[]{:S(2)}) collective-permute-start(bf16[6,48,768]{2,1,0:T(8,128)(2,1)S(1)} %get-tuple-element.1120), channel_id=1, source_target_pairs={{8,0},{9,1},{10,2},{11,3},{12,4},{13,5},{14,6},{15,7},{0,8},{1,9},... | collective-permute-start | bytes 1327112 | tf_op jit(solution)/shard_map/ppermute | solution.py:1093
  443.3 16.4 %collective-permute-start.94 = (bf16[256,3840]{1,0:T(8,128)(2,1)S(1)}, bf16[256,3840]{1,0:T(8,128)(2,1)S(1)}, u32[]{:S(2)}, u32[]{:S(2)}) collective-permute-start(bf16[256,3840]{1,0:T(8,128)(2,1)S(1)} %get-tuple-element.1158.da_ref), channel_id=1, source_target_pairs={{2,0},{3,1},{0,2},{1,3},{6,4},{7,5},{4,6},{5,7},{10,8},{11,9},{8,1... | collective-permute-start | bytes 5898248 | tf_op jit(solution)/shard_map/ppermute | solution.py:1093
  444.0 22.1 %collective-permute-start.91 = (bf16[12,48,768]{2,1,0:T(8,128)(2,1)S(1)}, bf16[12,48,768]{2,1,0:T(8,128)(2,1)S(1)}, u32[]{:S(2)}, u32[]{:S(2)}) collective-permute-start(bf16[12,48,768]{2,1,0:T(8,128)(2,1)S(1)} %get-tuple-element.1148), channel_id=1, source_target_pairs={{4,0},{5,1},{6,2},{7,3},{0,4},{1,5},{2,6},{3,7},{12,8},{13,9},{14,... | collective-permute-start | bytes 2654216 | tf_op jit(solution)/shard_map/ppermute | solution.py:1093
  445.0 21.1 %collective-permute-start.92 = (bf16[11,48,768]{2,1,0:T(8,128)(2,1)S(1)}, bf16[11,48,768]{2,1,0:T(8,128)(2,1)S(1)}, u32[]{:S(2)}, u32[]{:S(2)}) collective-permute-start(bf16[11,48,768]{2,1,0:T(8,128)(2,1)S(1)} %get-tuple-element.1149), channel_id=1, source_target_pairs={{1,0},{0,1},{3,2},{2,3},{5,4},{4,5},{7,6},{6,7},{9,8},{8,9},{11,10... | collective-permute-start | bytes 2433032 | tf_op jit(solution)/shard_map/ppermute | solution.py:1093
  447.7 16.7 %collective-permute-start.93 = (bf16[6,48,768]{2,1,0:T(8,128)(2,1)S(1)}, bf16[6,48,768]{2,1,0:T(8,128)(2,1)S(1)}, u32[]{:S(2)}, u32[]{:S(2)}) collective-permute-start(bf16[6,48,768]{2,1,0:T(8,128)(2,1)S(1)} %get-tuple-element.1153), channel_id=1, source_target_pairs={{8,0},{9,1},{10,2},{11,3},{12,4},{13,5},{14,6},{15,7},{0,8},{1,9},... | collective-permute-start | bytes 1327112 | tf_op jit(solution)/shard_map/ppermute | solution.py:1093
  466.7 22.1 %collective-permute-start.96 = (bf16[12,48,768]{2,1,0:T(8,128)(2,1)S(1)}, bf16[12,48,768]{2,1,0:T(8,128)(2,1)S(1)}, u32[]{:S(2)}, u32[]{:S(2)}) collective-permute-start(bf16[12,48,768]{2,1,0:T(8,128)(2,1)S(1)} %get-tuple-element.1179), channel_id=1, source_target_pairs={{4,0},{5,1},{6,2},{7,3},{0,4},{1,5},{2,6},{3,7},{12,8},{13,9},{14,... | collective-permute-start | bytes 2654216 | tf_op jit(solution)/shard_map/ppermute | solution.py:1093
  467.7 21.1 %collective-permute-start.97 = (bf16[11,48,768]{2,1,0:T(8,128)(2,1)S(1)}, bf16[11,48,768]{2,1,0:T(8,128)(2,1)S(1)}, u32[]{:S(2)}, u32[]{:S(2)}) collective-permute-start(bf16[11,48,768]{2,1,0:T(8,128)(2,1)S(1)} %get-tuple-element.1180), channel_id=1, source_target_pairs={{1,0},{0,1},{3,2},{2,3},{5,4},{4,5},{7,6},{6,7},{9,8},{8,9},{11,10... | collective-permute-start | bytes 2433032 | tf_op jit(solution)/shard_map/ppermute | solution.py:1093
  470.4 16.8 %collective-permute-start.98 = (bf16[6,48,768]{2,1,0:T(8,128)(2,1)S(1)}, bf16[6,48,768]{2,1,0:T(8,128)(2,1)S(1)}, u32[]{:S(2)}, u32[]{:S(2)}) collective-permute-start(bf16[6,48,768]{2,1,0:T(8,128)(2,1)S(1)} %get-tuple-element.1184), channel_id=1, source_target_pairs={{8,0},{9,1},{10,2},{11,3},{12,4},{13,5},{14,6},{15,7},{0,8},{1,9},... | collective-permute-start | bytes 1327112 | tf_op jit(solution)/shard_map/ppermute | solution.py:1093
  489.5 21.3 %collective-permute-start.102 = (bf16[12,48,768]{2,1,0:T(8,128)(2,1)S(1)}, bf16[12,48,768]{2,1,0:T(8,128)(2,1)S(1)}, u32[]{:S(2)}, u32[]{:S(2)}) collective-permute-start(bf16[12,48,768]{2,1,0:T(8,128)(2,1)S(1)} %get-tuple-element.1213), channel_id=1, source_target_pairs={{4,0},{5,1},{6,2},{7,3},{0,4},{1,5},{2,6},{3,7},{12,8},{13,9},{14,... | collective-permute-start | bytes 2654216 | tf_op jit(solution)/shard_map/ppermute | solution.py:1093
  490.5 20.3 %collective-permute-start.103 = (bf16[11,48,768]{2,1,0:T(8,128)(2,1)S(1)}, bf16[11,48,768]{2,1,0:T(8,128)(2,1)S(1)}, u32[]{:S(2)}, u32[]{:S(2)}) collective-permute-start(bf16[11,48,768]{2,1,0:T(8,128)(2,1)S(1)} %get-tuple-element.1214), channel_id=1, source_target_pairs={{1,0},{0,1},{3,2},{2,3},{5,4},{4,5},{7,6},{6,7},{9,8},{8,9},{11,10... | collective-permute-start | bytes 2433032 | tf_op jit(solution)/shard_map/ppermute | solution.py:1093
  493.1 16.0 %collective-permute-start.104 = (bf16[6,48,768]{2,1,0:T(8,128)(2,1)S(1)}, bf16[6,48,768]{2,1,0:T(8,128)(2,1)S(1)}, u32[]{:S(2)}, u32[]{:S(2)}) collective-permute-start(bf16[6,48,768]{2,1,0:T(8,128)(2,1)S(1)} %get-tuple-element.1218), channel_id=1, source_target_pairs={{8,0},{9,1},{10,2},{11,3},{12,4},{13,5},{14,6},{15,7},{0,8},{1,9},... | collective-permute-start | bytes 1327112 | tf_op jit(solution)/shard_map/ppermute | solution.py:1093
  511.4 15.7 %collective-permute-start.109 = (bf16[6,48,768]{2,1,0:T(8,128)(2,1)S(1)}, bf16[6,48,768]{2,1,0:T(8,128)(2,1)S(1)}, u32[]{:S(2)}, u32[]{:S(2)}) collective-permute-start(bf16[6,48,768]{2,1,0:T(8,128)(2,1)S(1)} %get-tuple-element.1249), channel_id=1, source_target_pairs={{8,0},{9,1},{10,2},{11,3},{12,4},{13,5},{14,6},{15,7},{0,8},{1,9},... | collective-permute-start | bytes 1327112 | tf_op jit(solution)/shard_map/ppermute | solution.py:1093
  527.4 17.2 %collective-permute-start.112 = (bf16[7,48,768]{2,1,0:T(8,128)(2,1)S(1)}, bf16[7,48,768]{2,1,0:T(8,128)(2,1)S(1)}, u32[]{:S(2)}, u32[]{:S(2)}) collective-permute-start(bf16[7,48,768]{2,1,0:T(8,128)(2,1)S(1)} %get-tuple-element.1263), channel_id=1, source_target_pairs={{8,0},{9,1},{10,2},{11,3},{12,4},{13,5},{14,6},{15,7},{0,8},{1,9},... | collective-permute-start | bytes 1548296 | tf_op jit(solution)/shard_map/ppermute | solution.py:1093
  (199 other events, 1674.3 us)

commit v6 on v5

--- a/solution.py
+++ b/solution.py
@@ -824,19 +824,22 @@
 
 def finish_kernel(kind, offsets, pos_ref, *refs):
     layers = len(offsets)
-    owns, gots = refs[:layers], refs[layers : 2 * layers]
-    outs, buf, sems = refs[2 * layers : -2], refs[-2], refs[-1]
+    owns, gots = refs[: 2 * layers], refs[2 * layers : 4 * layers]
+    outs, buf, sems = refs[4 * layers : -2], refs[-2], refs[-1]
     rows, width = buf.shape[2:]
     half = width // 2
     y = pos_ref[3]
     copies = []
     for layer in range(layers):
-        copies.append(
-            pltpu.make_async_copy(
-                gots[layer].at[pl.ds(offsets[layer], 3)], buf.at[layer], sems.at[layer]
+        for part, at in enumerate(offsets[layer]):
+            copies.append(
+                pltpu.make_async_copy(
+                    gots[2 * layer + part].at[pl.ds(at, 2 - part)],
+                    buf.at[layer, pl.ds(2 * part, 2 - part)],
+                    sems.at[2 * layer + part],
+                )
             )
-        )
-        copies[-1].start()
+            copies[-1].start()
     for each in copies:
         each.wait()
     for side in range(2):
@@ -844,10 +847,10 @@
         for layer in range(layers):
             for part in range(2):
                 if part == 0:
-                    value = owns[layer][side].astype(BF16).astype(F32)
+                    value = owns[2 * layer][side].astype(BF16).astype(F32)
                     value = value + buf[layer, 1 - side].astype(F32)
                 else:
-                    value = (buf[layer, 2] if side else owns[layer][2].astype(BF16)).astype(F32)
+                    value = (buf[layer, 2] if side else owns[2 * layer + 1][0].astype(BF16)).astype(F32)
                 if kind == 0:
                     lanes = pl.ds(pl.multiple_of(yy * half, 128), half)
                     for member in range(2):
@@ -864,29 +867,29 @@
 
 def finish(kind, pos, results):
     layers = len(results)
-    _, rows, width = results[0][0].shape
+    _, rows, width = results[0][0][0].shape
     outs = {
         0: (shape((layers, rows, width), F32),) * 4,
         1: (shape((layers, rows, 4 * width), F32),),
         2: (shape((layers, 4 * rows, width), F32),),
     }[kind]
     return pl.pallas_call(
-        functools.partial(finish_kernel, kind, tuple(value[2] for value in results)),
+        functools.partial(finish_kernel, kind, tuple((a[2], b[2]) for a, b in results)),
         out_shape=outs,
-        in_specs=[SMEM] + [VMEM] * layers + [ANY] * layers,
+        in_specs=[SMEM] + [VMEM] * (2 * layers) + [ANY] * (2 * layers),
         out_specs=[VMEM] * len(outs),
         scratch_shapes=[
             pltpu.VMEM((layers, 3, rows, width), BF16),
-            pltpu.SemaphoreType.DMA((layers,)),
+            pltpu.SemaphoreType.DMA((2 * layers,)),
         ],
         compiler_params=params(VMEM_MB),
         cost_estimate=cost(),
         name="finish",
-    )(pos, *[value[0] for value in results], *[value[1] for value in results])
+    )(pos, *[part[0] for value in results for part in value], *[part[1] for value in results for part in value])
 
 
 def sum_kernel(config, *refs):
-    fresh, first, second, third, fourth, small, waits = config
+    fresh, first, second, third_a, third_b, fourth_a, fourth_b, small, waits = config
     refs = list(refs)
 
     def take(count):
@@ -898,13 +901,19 @@
     got_x = take(1)[0] if first or second else None
     got_y = take(1)[0] if first else None
     keeps = take(2) if first else None
-    rests = take(2) if second else None
-    pairs = take(2) if third else None
-    lasts = take(2) if fourth else None
+    rest = take(1)[0] if second else None
+    got_z1 = take(1)[0] if third_a or third_b else None
+    pair_a = take(1)[0] if third_a else None
+    pair_b = take(1)[0] if third_b else None
+    got_z2 = take(1)[0] if fourth_a or fourth_b else None
+    last_a = take(1)[0] if fourth_a else None
+    last_b = take(1)[0] if fourth_b else None
     tables = take(2 if small == 1 else 1) if small else None
     take(waits)
     to_x = take(1)[0] if fresh or first else None
-    to_y = take(1)[0] if fresh or fourth else None
+    to_y = take(1)[0] if fresh or fourth_a or fourth_b else None
+    to_z1 = take(1)[0] if first or second else None
+    to_z2 = take(1)[0] if third_a or third_b else None
     at = 0
     if fresh:
         for out, send in ((to_x, sends[0]), (to_y, sends[1])):
@@ -912,71 +921,96 @@
                 out[half * ZS : (half + 1) * ZS] = send[half]
         at = 2 * ZS
     if first:
-        a_rest, b_rest = take(2)
-        for half in range(2):
-            come = got_x[half * ZS : (half + 1) * ZS].astype(F32)
-            a_rest[half] = (keeps[0][half].astype(F32) + come).astype(BF16)
+        b_rest, hold = take(2)
+        for k in range(ZS):
+            for half in range(2):
+                value = keeps[0][half, k].astype(F32) + got_x[half * ZS + k].astype(F32)
+                (to_z1 if k % 2 else hold)[k // 2 * 2 + half] = value.astype(BF16)
         b_rest[...] = (keeps[1][0].astype(F32) + got_y[:ZS].astype(F32)).astype(BF16)
         value = keeps[1][1].astype(F32) + got_y[ZS : 2 * ZS].astype(F32)
         to_x[at : at + ZS] = value.astype(BF16)
     if second:
-        hold, to_z1 = take(2)
+        (hold,) = take(1)
         begin = 2 * ZS if first else 0
         for k in range(ZS):
-            out = to_z1 if k % 2 else hold
-            for half in range(2):
-                out[k // 2 * 3 + half] = rests[0][half, k]
-            value = rests[1][k].astype(F32) + got_x[begin + k].astype(F32)
-            out[k // 2 * 3 + 2] = value.astype(BF16)
-    if third:
-        hold, to_z2 = take(2)
-        for index in range(3):
-            hold[index] = pairs[0][index].astype(F32) + pairs[1][index].astype(F32)
-            value = pairs[0][3 + index].astype(F32) + pairs[1][3 + index].astype(F32)
-            to_z2[index] = value.astype(BF16)
-    if fourth:
-        (total,) = take(1)
-        value = lasts[0][...] + lasts[1][:3].astype(F32)
-        total[...] = value
-        to_y[at : at + 3] = value.astype(BF16)
+            value = (rest[k].astype(F32) + got_x[begin + k].astype(F32)).astype(BF16)
+            if k % 2:
+                to_z1[4 * first + k // 2] = value
+            else:
+                hold[k // 2] = value
+    for here, pair, begin, size, to in (
+        (third_a, pair_a, 0, 2, 0),
+        (third_b, pair_b, 4 * third_a, 1, 2 * third_a),
+    ):
+        if here:
+            (hold,) = take(1)
+            for index in range(size):
+                hold[index] = pair[index].astype(F32) + got_z1[begin + index].astype(F32)
+                value = pair[size + index].astype(F32) + got_z1[begin + size + index].astype(F32)
+                to_z2[to + index] = value.astype(BF16)
+    for here, last, begin, size in ((fourth_a, last_a, 0, 2), (fourth_b, last_b, 2 * fourth_a, 1)):
+        if here:
+            (total,) = take(1)
+            for index in range(size):
+                value = last[index] + got_z2[begin + index].astype(F32)
+                total[index] = value
+                to_y[at + begin + index] = value.astype(BF16)
     if small:
-        come = (None, None, got_x, pairs and pairs[1], lasts and lasts[1])[small]
+        come = (None, None, got_x, got_z1, got_z2)[small]
         come = tables[1][...] if small == 1 else come[come.shape[0] - 1]
         value = tables[0][...] + come.astype(F32)
         refs[0][...] = value
-        to = (None, to_x, to_z1 if second else None, to_z2 if third else None, to_y)[small]
+        to = (None, to_x, to_z1, to_z2, to_y)[small]
         to[to.shape[0] - 1] = value.astype(BF16)
 
 
-def sum_round(fresh, got_x, got_y, first, second, third, fourth, small, after):
+def sum_round(fresh, past, small, after):
+    names = ("first", "second", "third_a", "third_b", "fourth_a", "fourth_b")
     stage, table = small
-    config = tuple(value is not None for value in (fresh, first, second, third, fourth)) + (stage, len(after))
-    sample = fresh or first or second or third or fourth
-    rows, width = sample[-1].shape[-2:]
-    inputs, outputs = [], []
-    if fresh is not None:
+    config = (fresh is not None,) + tuple(name in past for name in names) + (stage, len(after))
+    is_fresh, first, second, third_a, third_b, fourth_a, fourth_b = (int(value) for value in config[:7])
+    sample = fresh[1] if fresh is not None else past[[name for name in names if name in past][0]][0]
+    rows, width = sample.shape[-2:]
+    inputs = []
+    if is_fresh:
         inputs += [fresh[1], fresh[3]]
-    if first is not None or second is not None:
-        inputs += [got_x]
-    if first is not None:
-        inputs += [got_y]
-    for value in (first, second, third, fourth, table):
-        if value is not None:
-            inputs += list(value)
-    begin = 2 * ZS * config[0]
-    if config[0] or config[1]:
-        outputs += [shape((begin + ZS * config[1] + (stage == 1), rows, width), BF16)]
-    if config[0] or config[4]:
-        outputs += [shape((begin + 3 * config[4] + (stage == 4), rows, width), BF16)]
-    if config[1]:
-        outputs += [shape((2, ZS, rows, width), BF16), shape((ZS, rows, width), BF16)]
-    if config[2]:
-        outputs += [shape((6, rows, width), BF16), shape((6 + (stage == 2), rows, width), BF16)]
-    if config[3]:
-        outputs += [shape((3, rows, width), F32), shape((3 + (stage == 3), rows, width), BF16)]
-    if config[4]:
-        outputs += [shape((3, rows, width), F32)]
-    if config[5]:
+    if first or second:
+        inputs += [past["got_x"]]
+    if first:
+        inputs += [past["got_y"]] + list(past["first"])
+    if second:
+        inputs += list(past["second"])
+    if third_a or third_b:
+        inputs += [past["got_z1"]]
+    for name in ("third_a", "third_b"):
+        inputs += list(past.get(name, ()))
+    if fourth_a or fourth_b:
+        inputs += [past["got_z2"]]
+    for name in ("fourth_a", "fourth_b"):
+        inputs += list(past.get(name, ()))
+    if table is not None:
+        inputs += list(table)
+    begin = 2 * ZS * is_fresh
+    sizes = (
+        (is_fresh or first, begin + ZS * first + (stage == 1)),
+        (is_fresh or fourth_a or fourth_b, begin + 2 * fourth_a + fourth_b + (stage == 4)),
+        (first or second, 4 * first + 2 * second + (stage == 2)),
+        (third_a or third_b, 2 * third_a + third_b + (stage == 3)),
+    )
+    outputs = [shape((size, rows, width), BF16) for there, size in sizes if there]
+    if first:
+        outputs += [shape((ZS, rows, width), BF16), shape((4, rows, width), BF16)]
+    if second:
+        outputs += [shape((2, rows, width), BF16)]
+    if third_a:
+        outputs += [shape((2, rows, width), F32)]
+    if third_b:
+        outputs += [shape((1, rows, width), F32)]
+    if fourth_a:
+        outputs += [shape((2, rows, width), F32)]
+    if fourth_b:
+        outputs += [shape((1, rows, width), F32)]
+    if stage:
         outputs += [shape(table[0].shape, F32)]
     outs = list(
         pl.pallas_call(
@@ -997,18 +1031,12 @@
         del outs[:count]
         return out
 
-    to_x = take(config[0] or config[1], 1)
-    to_y = take(config[0] or config[4], 1)
-    return (
-        to_x,
-        to_y,
-        begin,
-        take(config[1], 2),
-        take(config[2], 2),
-        take(config[3], 2),
-        take(config[4], 1),
-        take(stage > 0, 1),
-    )
+    sends = tuple(take(there, 1) for there, _ in sizes)
+    b_rest = take(first, 1)
+    holds = (take(first, 1), take(second, 1))
+    lasts = (take(third_a, 1), take(third_b, 1))
+    totals = (take(fourth_a, 1), take(fourth_b, 1))
+    return sends, begin, b_rest, holds, lasts, totals, take(stage > 0, 1)
 
 
 def collect_kernel(*refs):
@@ -1346,7 +1374,7 @@
     parts = []
     vectors = [None] * layers
     rounds = []
-    ends = []
+    ends = [], []
     table_stage = 1
 
     def side_work():
@@ -1366,11 +1394,11 @@
             loose["after"] = (done[0],)
 
     def ended():
-        found = []
-        for now in rounds:
-            if "total" in now:
-                found.append((now["total"], now["got_y"], ends[len(found)]))
-        return found
+        out = []
+        for each in zip(*ends):
+            if each[1][0] < len(rounds):
+                out.append(tuple((own, rounds[s]["got_y"], at) for s, own, at in each))
+        return out
 
     def settle(state):
         return fence(state)
@@ -1381,37 +1409,30 @@
                 parts.append(fresh)
             return state(()) if callable(state) else state
         s = len(rounds)
-        past = rounds[s - LAG] if s >= LAG else {}
-        pick = lambda key: past.get(key)
-        has_home = pick("first") is not None or pick("second") is not None
-        to_x, to_y, going, first, second, third, fourth, small = sum_round(
-            fresh,
-            pick("got_x") if has_home else None,
-            pick("got_y") if pick("first") is not None else None,
-            pick("first"),
-            pick("second"),
-            pick("third"),
-            pick("fourth"),
-            loose.pop("small", (0, None)),
-            tuple(loose.pop("after", ())),
+        past = rounds[s - 1] if s else {}
+        sends, begin, b_rest, holds, lasts, totals, small = sum_round(
+            fresh, past, loose.pop("small", (0, None)), tuple(loose.pop("after", ()))
         )
-        sends = (to_x or ()) + (to_y or ())
         now = {}
-        if fresh is not None:
-            now["first"] = (fresh[0], fresh[2])
-        if first is not None:
-            now["second"] = first
-        if to_x is not None:
-            now["got_x"] = move(to_x[0], net["x"])
-        if to_y is not None:
-            now["got_y"] = move(to_y[0], net["y"])
-        if second is not None:
-            now["third"] = (second[0], move(second[1], net["z1"]))
-        if third is not None:
-            now["fourth"] = (third[0], move(third[1], net["z2"]))
-        if fourth is not None:
-            now["total"] = fourth[0]
-            ends.append(going)
+        for name, way, value in zip(
+            ("got_x", "got_y", "got_z1", "got_z2"), ("x", "y", "z1", "z2"), sends
+        ):
+            if value is not None:
+                now[name] = move(value[0], net[way])
+        for name, value in (
+            ("first", fresh and (fresh[0], fresh[2])),
+            ("second", b_rest),
+            ("third_a", holds[0]),
+            ("third_b", holds[1]),
+            ("fourth_a", lasts[0]),
+            ("fourth_b", lasts[1]),
+        ):
+            if value is not None:
+                now[name] = value
+        for part, value in enumerate(totals):
+            if value is not None:
+                ends[part].append((s, value[0], begin + (2 if part and totals[0] is not None else 0)))
+        sends = tuple(value[0] for value in sends if value is not None)
         if "vectors" in loose:
             small = loose.pop("vectors").reshape(-1, width)
             loose["small"] = (1, (small, move(small, net["core"])))

time: 585 us -> 579 us (0.990)
  starting transfers between devices: 143 us -> 110 us
  waiting for transfers between devices: 192 us -> 208 us
  local copies, waits for them, and re-layouts: 34.7 us -> 44 us
    ppermute x116 -> x120, starting transfers between devices: 143 us -> 110 us  [move(): return lax.ppermute(value, AXES, perm)]
    ppermute x116 -> x120, waiting for transfers between devices: 192 us -> 208 us  [move(): return lax.ppermute(value, AXES, perm)]
    unnamed x296 -> x300, local copies, waits for them, and re-layouts: 33.7 us -> 43 us
  transfers between devices with their start and end apart: 116 -> 120, of which waited for: 62 -> 67; matrix products, arithmetic and copies ran while one was open for 1% -> 1% of each run, Pallas kernels for 29% -> 29%
where the time goes in v6:
time: 579 us; the launch traced here: 570 us
  waiting for transfers between devices  208 us (36%)
  Pallas kernels  199 us (34%)
  starting transfers between devices  110 us (19%)
  local copies, waits for them, and re-layouts  44 us (8%)
    ppermute x120, waiting for transfers between devices, move(): return lax.ppermute(value, AXES, perm)  208 us
    ppermute x120, starting transfers between devices, move(): return lax.ppermute(value, AXES, perm)  110 us
    unnamed x300, local copies, waits for them, and re-layouts  43 us
    pallas_call x3, Pallas kernels, attn_forward(): pl.pallas_call(attn_kernel, out_shape=(shape((tokens, width), F32),) + ke...  39.5 us
    pallas_call x18, Pallas kernels, copy_blocks(): pl.pallas_call(functools.partial(copy_kernel, plan, len(inputs)), out_sha...  30.3 us
    pallas_call x3, Pallas kernels, chain_backward(): pl.pallas_call(functools.partial(chain_kernel, 384, len(after)), out_shap...  24.9 us
    pallas_call x3, Pallas kernels, attn_backward(): pl.pallas_call(functools.partial(attn_back_kernel, len(after)), out_shape...  23.3 us
    pallas_call x3, Pallas kernels, inner_forward(): pl.pallas_call(functools.partial(inner_kernel, 384), out_shape=(shape((to...  19.4 us
  transfers between devices with their start and end apart: 120, of which 67 were waited for; matrix products, arithmetic and copies ran while one was open for 1% of the time, Pallas kernels for 29%

profile of v6, /device:TPU:0, one launch (start us, length us, event | category | flops | bytes accessed | tf_op | source)
XLA Modules:
  0.0 569.6 jit_solution(6344172007711299811)
XLA Ops:
  0.8 4.6 collective-permute-start.3
  12.2 4.1 collective-permute-start
  18.9 3.0 collective-permute-done.1
  25.3 3.1 collective-permute-start.5
  29.7 5.0 collective-permute-done.5.refs_1_
  47.7 5.1 collective-permute-done.12.refs_1_
  61.2 12.0 %collective-permute-done.17 = f32[3,12,768]{2,1,0:T(8,128)S(1)} collective-permute-done((f32[3,12,768]{2,1,0:T(8,128)S(1)}, f32[3,12,768]{2,1,0:T(8,128)S(1)}, u32[]{:S(2)}, u32[]{:S(2)}) %collective-permute-start.17) | collective-permute-done | bytes 110624 | tf_op jit(solution)/shard_map/ppermute | solution.py:1121
  83.0 5.0 collective-permute-done.23
  88.7 9.5 %collective-permute-done.22.refs_1_ = bf16[4,48,768]{2,1,0:T(8,128)(2,1)S(1)} collective-permute-done((bf16[4,48,768]{2,1,0:T(8,128)(2,1)S(1)}, bf16[4,48,768]{2,1,0:T(8,128)(2,1)S(1)}, u32[]{:S(2)}, u32[]{:S(2)}) %collective-permute-start.22) | collective-permute-done | bytes 294944 | tf_op jit(solution)/shard_map/ppermute | solution.py:1121
  98.2 2.9 collective-permute-done.21.refs_1_
  102.6 4.2 gather_round.14
  116.2 13.2 %attn_forward.3 = (f32[256,768]{1,0:T(8,128)S(1)}, f32[256,768]{1,0:T(8,128)S(1)}, f32[256,128]{1,0:T(8,128)S(1)}, bf16[256,768]{1,0:T(8,128)(2,1)S(1)}, bf16[76...) custom-call(s32[4]{0:T(128)S(1)} %pad_add_fusion.2.pos_ref.refs_0_.r, ...), custom_call_target="tpu_custom_call" | custom-call | flops 1 | bytes 1 | tf_op jit(solution)/shard_map/attn_forward/pallas_call | solution.py:265
  132.0 3.8 gather_round.15
  138.8 7.7 %inner_forward.3 = (bf16[256,3072]{1,0:T(8,128)(2,1)S(1)}, bf16[256,3072]{1,0:T(8,128)(2,1)S(1)}, bf16[2,2,2,4,48,256]{5,4,3,2,1,0:T(8,128)(2,1)S(1)}, bf16[2,2,2,4,48,256]{5,4,3,2,1,0:T(8,128)(2,1)S(1)}) custom-call(s32[4]{0:T(128)S(1)} %pad_add_fusion.2.pos_ref.refs_0_.refs_1_, s32[4]{0:T(128)S(1)} %pad_add_fusion.2.pos_ref.refs_0_.refs_1_, ...), custom_call_target="tpu_custom_call" | custom-call | flops 1 | bytes 1 | tf_op jit(solution)/shard_map/inner_forward/pallas_call | solution.py:348
  146.6 6.7 %collective-permute-done.31.refs_1_ = bf16[4,48,768]{2,1,0:T(8,128)(2,1)S(1)} collective-permute-done((bf16[4,48,768]{2,1,0:T(8,128)(2,1)S(1)}, bf16[4,48,768]{2,1,0:T(8,128)(2,1)S(1)}, u32[]{:S(2)}, u32[]{:S(2)}) %collective-permute-start.31) | collective-permute-done | bytes 294944 | tf_op jit(solution)/shard_map/ppermute | solution.py:1121
  156.3 2.5 collective-permute-done.28.refs_4_
  166.1 3.3 outer_forward.3
  171.2 8.3 %collective-permute-done.37.refs_1_ = bf16[8,48,768]{2,1,0:T(8,128)(2,1)S(1)} collective-permute-done((bf16[8,48,768]{2,1,0:T(8,128)(2,1)S(1)}, bf16[8,48,768]{2,1,0:T(8,128)(2,1)S(1)}, u32[]{:S(2)}, u32[]{:S(2)}) %collective-permute-start.37) | collective-permute-done | bytes 589856 | tf_op jit(solution)/shard_map/ppermute | solution.py:1121
  179.5 4.9 collective-permute-done.34.refs_4_
  189.6 2.6 collective-permute-start.42
  192.2 13.2 %attn_forward.4 = (f32[256,768]{1,0:T(8,128)S(1)}, f32[256,768]{1,0:T(8,128)S(1)}, f32[256,128]{1,0:T(8,128)S(1)}, bf16[256,768]{1,0:T(8,128)(2,1)S(1)}, bf16[76...) custom-call(s32[4]{0:T(128)S(1)} %pad_add_fusion.2.pos_ref.refs_0_.r, ...), custom_call_target="tpu_custom_call" | custom-call | flops 1 | bytes 1 | tf_op jit(solution)/shard_map/attn_forward/pallas_call | solution.py:265
  216.5 5.9 %inner_forward.4 = (bf16[256,3072]{1,0:T(8,128)(2,1)S(1)}, bf16[256,3072]{1,0:T(8,128)(2,1)S(1)}, bf16[2,2,2,4,48,256]{5,4,3,2,1,0:T(8,128)(2,1)S(1)}, bf16[2,2,2,4,48,256]{5,4,3,2,1,0:T(8,128)(2,1)S(1)}) custom-call(s32[4]{0:T(128)S(1)} %pad_add_fusion.2.pos_ref.refs_0_.refs_1_, s32[4]{0:T(128)S(1)} %pad_add_fusion.2.pos_ref.refs_0_.refs_1_, ...), custom_call_target="tpu_custom_call" | custom-call | flops 1 | bytes 1 | tf_op jit(solution)/shard_map/inner_forward/pallas_call | solution.py:348
  223.8 2.6 collective-permute-done.48.tb_ref.xb_ref
  227.4 10.0 %collective-permute-done.43.refs_4_ = bf16[12,48,768]{2,1,0:T(8,128)(2,1)S(1)} collective-permute-done((bf16[12,48,768]{2,1,0:T(8,128)(2,1)S(1)}, bf16[12,48,768]{2,1,0:T(8,128)(2,1)S(1)}, u32[]{:S(2)}, u32[]{:S(2)}) %collective-permute-start.43) | collective-permute-done | bytes 884768 | tf_op jit(solution)/shard_map/ppermute | solution.py:1121
  241.7 2.8 outer_forward.4
  246.4 15.4 %collective-permute-done.49.refs_2_ = bf16[12,48,768]{2,1,0:T(8,128)(2,1)S(1)} collective-permute-done((bf16[12,48,768]{2,1,0:T(8,128)(2,1)S(1)}, bf16[12,48,768]{2,1,0:T(8,128)(2,1)S(1)}, u32[]{:S(2)}, u32[]{:S(2)}) %collective-permute-start.49) | collective-permute-done | bytes 884768 | tf_op jit(solution)/shard_map/ppermute | solution.py:1121
  266.5 13.2 %attn_forward.5 = (f32[256,768]{1,0:T(8,128)S(1)}, f32[256,768]{1,0:T(8,128)S(1)}, f32[256,128]{1,0:T(8,128)S(1)}, bf16[256,768]{1,0:T(8,128)(2,1)S(1)}, bf16[76...) custom-call(s32[4]{0:T(128)S(1)} %pad_add_fusion.2.pos_ref.refs_0_.r, ...), custom_call_target="tpu_custom_call" | custom-call | flops 1 | bytes 1 | tf_op jit(solution)/shard_map/attn_forward/pallas_call | solution.py:265
  284.4 2.8 collective-permute-start.57
  287.2 5.9 %inner_forward.5 = (bf16[256,3072]{1,0:T(8,128)(2,1)S(1)}, bf16[256,3072]{1,0:T(8,128)(2,1)S(1)}, bf16[2,2,2,4,48,256]{5,4,3,2,1,0:T(8,128)(2,1)S(1)}, bf16[2,2,2,4,48,256]{5,4,3,2,1,0:T(8,128)(2,1)S(1)}) custom-call(s32[4]{0:T(128)S(1)} %pad_add_fusion.2.pos_ref.refs_0_.refs_1_, s32[4]{0:T(128)S(1)} %pad_add_fusion.2.pos_ref.refs_0_.refs_1_, ...), custom_call_target="tpu_custom_call" | custom-call | flops 1 | bytes 1 | tf_op jit(solution)/shard_map/inner_forward/pallas_call | solution.py:348
  294.0 2.7 collective-permute-done.59.tb_ref.xb_ref
  296.7 3.2 outer_forward.5
  307.1 7.9 %chain_backward.3 = (bf16[256,3840]{1,0:T(8,128)(2,1)S(1)}, f32[256,768]{1,0:T(8,128)S(1)}, bf16[256,768]{1,0:T(8,128)(2,1)S(1)}, f32[16,768]{1,0:T(8,128)S(1)}) custom-call(s32[4]{0:T(128)S(1)} %pad_add_fusion.2.pos_ref.refs_0_.refs_1_, bf16[256,768]{1,0:T(8,128)(2,1)S(1)} %get-tuple-element.976.da_ref.refs_1_, f32[256,768]{1,0:T(8,128)S(1)} %get-tuple-element.983.refs_2_, ...), custom_call_target="tpu_custom_call" | custom-call | flops 1 | bytes 1 | tf_op jit(solution)/shard_map/chain_backward/pallas_call | solution.py:470
  315.9 3.2 collective-permute-done.64.refs_0_
  323.4 7.8 %attn_backward.3 = (bf16[5,256,768]{2,1,0:T(8,128)(2,1)S(1)}, f32[8,768]{1,0:T(8,128)S(1)}) custom-call(bf16[256,768]{1,0:T(8,128)(2,1)S(1)} %copy-done.105, bf16[768,512]{1,0:T(8,128)(2,1)S(1)} %copy-done.65, bf16[512,768]{1,0:T(8,128)(2,1)S(1)} %copy-done.67, bf16[12,512,256]{2,1,0:T(8,128)(2,1)S(1)} %copy-done.34, ...), custom_call_target="tpu_custom_call" | custom-call | flops 1 | bytes 1 | tf_op jit(solution)/shard_map/attn_backward/pallas_call | solution.py:543
  331.3 2.5 inner_grad.3
  338.0 3.1 collective-permute-start.61
  343.6 2.6 collective-permute-start.72
  346.3 4.5 input_backward.3
  353.3 2.8 attn_grad.3
  365.9 7.7 %chain_backward.4 = (bf16[256,3840]{1,0:T(8,128)(2,1)S(1)}, f32[256,768]{1,0:T(8,128)S(1)}, bf16[256,768]{1,0:T(8,128)(2,1)S(1)}, f32[16,768]{1,0:T(8,128)S(1)}) custom-call(s32[4]{0:T(128)S(1)} %pad_add_fusion.2.pos_ref.refs_0_.refs_1_, bf16[256,768]{1,0:T(8,128)(2,1)S(1)} %get-tuple-element.1060.refs_1_.da_ref, f32[256,768]{1,0:T(8,128)S(1)} %copy-done.63, ...), custom_call_target="tpu_custom_call" | custom-call | flops 1 | bytes 1 | tf_op jit(solution)/shard_map/chain_backward/pallas_call | solution.py:470
  375.3 6.7 %collective-permute-done.75.refs_3_.refs_10_ = bf16[10,48,768]{2,1,0:T(8,128)(2,1)S(1)} collective-permute-done((bf16[10,48,768]{2,1,0:T(8,128)(2,1)S(1)}, bf16[10,48,768]{2,1,0:T(8,128)(2,1)S(1)}, u32[]{:S(2)}, u32[]{:S(2)}) %collective-permute-start.75) | collective-permute-done | bytes 737312 | tf_op jit(solution)/shard_map/ppermute | solution.py:1121
  382.0 3.1 collective-permute-done.74.refs_2_
  387.0 4.8 collective-permute-start.80
  393.4 7.8 %attn_backward.4 = (bf16[5,256,768]{2,1,0:T(8,128)(2,1)S(1)}, f32[8,768]{1,0:T(8,128)S(1)}) custom-call(bf16[256,768]{1,0:T(8,128)(2,1)S(1)} %copy-done.109, bf16[768,512]{1,0:T(8,128)(2,1)S(1)} %copy-done.81, bf16[512,768]{1,0:T(8,128)(2,1)S(1)} %copy-done.83, bf16[12,512,256]{2,1,0:T(8,128)(2,1)S(1)} %copy-done.38, ...), custom_call_target="tpu_custom_call" | custom-call | flops 1 | bytes 1 | tf_op jit(solution)/shard_map/attn_backward/pallas_call | solution.py:543
  401.2 2.5 inner_grad.4
  413.0 4.0 input_backward.4
  417.0 2.8 attn_grad.4
  419.8 6.3 %collective-permute-done.87.refs_10_ = bf16[3,48,768]{2,1,0:T(8,128)(2,1)S(1)} collective-permute-done((bf16[3,48,768]{2,1,0:T(8,128)(2,1)S(1)}, bf16[3,48,768]{2,1,0:T(8,128)(2,1)S(1)}, u32[]{:S(2)}, u32[]{:S(2)}) %collective-permute-start.87) | collective-permute-done | bytes 221216 | tf_op jit(solution)/shard_map/ppermute | solution.py:1121
  428.3 2.9 collective-permute-done.84.refs_2_
  435.7 9.3 %chain_backward.5 = (bf16[256,3840]{1,0:T(8,128)(2,1)S(1)}, f32[256,768]{1,0:T(8,128)S(1)}, bf16[256,768]{1,0:T(8,128)(2,1)S(1)}, f32[16,768]{1,0:T(8,128)S(1)}) custom-call(s32[4]{0:T(128)S(1)} %pad_add_fusion.2.pos_ref.refs_0_.refs_1_, bf16[256,768]{1,0:T(8,128)(2,1)S(1)} %get-tuple-element.1160.refs_1_.da_ref, ...), custom_call_target="tpu_custom_call" | custom-call | flops 1 | bytes 1 | tf_op jit(solution)/shard_map/chain_backward/pallas_call | solution.py:470
  457.7 7.8 %attn_backward.5 = (bf16[5,256,768]{2,1,0:T(8,128)(2,1)S(1)}, f32[8,768]{1,0:T(8,128)S(1)}) custom-call(bf16[256,768]{1,0:T(8,128)(2,1)S(1)} %copy-done.107, bf16[768,512]{1,0:T(8,128)(2,1)S(1)} %copy-done.77, bf16[512,768]{1,0:T(8,128)(2,1)S(1)} %copy-done.79, bf16[12,512,256]{2,1,0:T(8,128)(2,1)S(1)} %copy-done.36, ...), custom_call_target="tpu_custom_call" | custom-call | flops 1 | bytes 1 | tf_op jit(solution)/shard_map/attn_backward/pallas_call | solution.py:543
  465.5 2.5 inner_grad.5
  468.0 2.8 collective-permute-done.97.refs_10_
  480.4 4.0 input_backward.5
  484.4 2.8 attn_grad.5
  487.2 6.4 %collective-permute-done.102.refs_10_ = bf16[3,48,768]{2,1,0:T(8,128)(2,1)S(1)} collective-permute-done((bf16[3,48,768]{2,1,0:T(8,128)(2,1)S(1)}, bf16[3,48,768]{2,1,0:T(8,128)(2,1)S(1)}, u32[]{:S(2)}, u32[]{:S(2)}) %collective-permute-start.102) | collective-permute-done | bytes 221216 | tf_op jit(solution)/shard_map/ppermute | solution.py:1121
  503.3 12.2 %collective-permute-done.108.refs_8_ = bf16[3,48,768]{2,1,0:T(8,128)(2,1)S(1)} collective-permute-done((bf16[3,48,768]{2,1,0:T(8,128)(2,1)S(1)}, bf16[3,48,768]{2,1,0:T(8,128)(2,1)S(1)}, u32[]{:S(2)}, u32[]{:S(2)}) %collective-permute-start.108) | collective-permute-done | bytes 221216 | tf_op jit(solution)/shard_map/ppermute | solution.py:1121
  527.8 6.5 %collective-permute-done.113.refs_5_ = bf16[3,48,768]{2,1,0:T(8,128)(2,1)S(1)} collective-permute-done((bf16[3,48,768]{2,1,0:T(8,128)(2,1)S(1)}, bf16[3,48,768]{2,1,0:T(8,128)(2,1)S(1)}, u32[]{:S(2)}, u32[]{:S(2)}) %collective-permute-start.113) | collective-permute-done | bytes 221216 | tf_op jit(solution)/shard_map/ppermute | solution.py:1121
  539.3 3.3 collective-permute-done.114.refs_7_.refs_6_
  542.6 4.7 collective-permute-done.115.refs_0_
  550.1 2.8 finish.3.refs_3_
  553.0 4.5 collective-permute-done.118.refs_0_
  560.9 2.8 finish.5
  565.0 2.8 finish.4
  (574 shorter events, 219.7 us)
Async XLA Ops:
  0.8 21.8 %collective-permute-start.3 = (bf16[256,768]{1,0:T(8,128)(2,1)}, bf16[256,768]{1,0:T(8,128)(2,1)}, u32[]{:S(2)}, u32[]{:S(2)}) collective-permute-start(bf16[256,768]{1,0:T(8,128)(2,1)} %bitcast.52), channel_id=1, source_target_pairs={{0,0},{2,1},{1,2},{3,3},{4,4},{6,5},{5,6},{7,7},{8,8},{10,9},{9,10... | collective-permute-start | bytes 1179656 | tf_op jit(solution)/shard_map/ppermute | solution.py:1121
  37.1 15.8 %collective-permute-start.11 = (bf16[4,48,768]{2,1,0:T(8,128)(2,1)S(1)}, bf16[4,48,768]{2,1,0:T(8,128)(2,1)S(1)}, u32[]{:S(2)}, u32[]{:S(2)}) collective-permute-start(bf16[4,48,768]{2,1,0:T(8,128)(2,1)S(1)} %gather_z.8.refs_0_), channel_id=1, source_target_pairs={{8,0},{9,1},{10,2},{11,3},{12,4},{13,5},{14,6},{15,7},{0,8},{1,9},... | collective-permute-start | bytes 884744 | tf_op jit(solution)/shard_map/ppermute | solution.py:1121
  54.6 20.6 %collective-permute-start.13 = (bf16[12,48,768]{2,1,0:T(8,128)(2,1)S(1)}, bf16[12,48,768]{2,1,0:T(8,128)(2,1)S(1)}, u32[]{:S(2)}, u32[]{:S(2)}) collective-permute-start(bf16[12,48,768]{2,1,0:T(8,128)(2,1)S(1)} %get-tuple-element.718.refs_2_), channel_id=1, source_target_pairs={{4,0},{5,1},{6,2},{7,3},{0,4},{1,5},{2,6},{3,7},{12,8},{13,9},{14,... | collective-permute-start | bytes 2654216 | tf_op jit(solution)/shard_map/ppermute | solution.py:1121
  55.2 20.2 %collective-permute-start.14 = (bf16[12,48,768]{2,1,0:T(8,128)(2,1)S(1)}, bf16[12,48,768]{2,1,0:T(8,128)(2,1)S(1)}, u32[]{:S(2)}, u32[]{:S(2)}) collective-permute-start(bf16[12,48,768]{2,1,0:T(8,128)(2,1)S(1)} %get-tuple-element.719.refs_3_), channel_id=1, source_target_pairs={{1,0},{0,1},{3,2},{2,3},{5,4},{4,5},{7,6},{6,7},{9,8},{8,9},{11,10... | collective-permute-start | bytes 2654216 | tf_op jit(solution)/shard_map/ppermute | solution.py:1121
  57.5 15.7 %collective-permute-start.15 = (bf16[4,48,768]{2,1,0:T(8,128)(2,1)S(1)}, bf16[4,48,768]{2,1,0:T(8,128)(2,1)S(1)}, u32[]{:S(2)}, u32[]{:S(2)}) collective-permute-start(bf16[4,48,768]{2,1,0:T(8,128)(2,1)S(1)} %gather_z.9.refs_0_), channel_id=1, source_target_pairs={{8,0},{9,1},{10,2},{11,3},{12,4},{13,5},{14,6},{15,7},{0,8},{1,9},... | collective-permute-start | bytes 884744 | tf_op jit(solution)/shard_map/ppermute | solution.py:1121
  77.6 23.5 %collective-permute-start.20 = (bf16[32,48,768]{2,1,0:T(8,128)(2,1)S(1)}, bf16[32,48,768]{2,1,0:T(8,128)(2,1)S(1)}, u32[]{:S(2)}, u32[]{:S(2)}) collective-permute-start(bf16[32,48,768]{2,1,0:T(8,128)(2,1)S(1)} %get-tuple-element.765.refs_7_.refs_11_.refs_4_), channel_id=1, source_target_pairs={{2,0},{3,1},{0,2},{1,3},{6,4},{7,5},{4,6},{5,7},{10,8},{11,9},{8,1... | collective-permute-start | bytes 7077896 | tf_op jit(solution)/shard_map/ppermute | solution.py:1121
  77.7 23.4 %collective-permute-start.18 = (bf16[12,48,768]{2,1,0:T(8,128)(2,1)S(1)}, bf16[12,48,768]{2,1,0:T(8,128)(2,1)S(1)}, u32[]{:S(2)}, u32[]{:S(2)}) collective-permute-start(bf16[12,48,768]{2,1,0:T(8,128)(2,1)S(1)} %get-tuple-element.736.refs_2_), channel_id=1, source_target_pairs={{4,0},{5,1},{6,2},{7,3},{0,4},{1,5},{2,6},{3,7},{12,8},{13,9},{14,... | collective-permute-start | bytes 2654216 | tf_op jit(solution)/shard_map/ppermute | solution.py:1121
  79.4 21.7 %collective-permute-start.19 = (bf16[12,48,768]{2,1,0:T(8,128)(2,1)S(1)}, bf16[12,48,768]{2,1,0:T(8,128)(2,1)S(1)}, u32[]{:S(2)}, u32[]{:S(2)}) collective-permute-start(bf16[12,48,768]{2,1,0:T(8,128)(2,1)S(1)} %get-tuple-element.737.refs_3_), channel_id=1, source_target_pairs={{1,0},{0,1},{3,2},{2,3},{5,4},{4,5},{7,6},{6,7},{9,8},{8,9},{11,10... | collective-permute-start | bytes 2654216 | tf_op jit(solution)/shard_map/ppermute | solution.py:1121
  82.0 16.2 %collective-permute-start.22 = (bf16[4,48,768]{2,1,0:T(8,128)(2,1)S(1)}, bf16[4,48,768]{2,1,0:T(8,128)(2,1)S(1)}, u32[]{:S(2)}, u32[]{:S(2)}) collective-permute-start(bf16[4,48,768]{2,1,0:T(8,128)(2,1)S(1)} %pack.11.refs_0_), channel_id=1, source_target_pairs={{16,0},{17,1},{18,2},{19,3},{20,4},{21,5},{22,6},{23,7},{24,8},{25... | collective-permute-start | bytes 884744 | tf_op jit(solution)/shard_map/ppermute | solution.py:1121
  106.8 25.2 %collective-permute-start.26 = (bf16[32,48,768]{2,1,0:T(8,128)(2,1)}, bf16[32,48,768]{2,1,0:T(8,128)(2,1)}, u32[]{:S(2)}, u32[]{:S(2)}) collective-permute-start(bf16[32,48,768]{2,1,0:T(8,128)(2,1)} %get-tuple-element.807.refs_4_.refs_7_), channel_id=1, source_target_pairs={{2,0},{3,1},{0,2},{1,3},{6,4},{7,5},{4,6},{5,7},{10,8},{11,9},{8,1... | collective-permute-start | bytes 7077896 | tf_op jit(solution)/shard_map/ppermute | solution.py:1121
  106.8 25.1 %collective-permute-start.24 = (bf16[12,48,768]{2,1,0:T(8,128)(2,1)}, bf16[12,48,768]{2,1,0:T(8,128)(2,1)}, u32[]{:S(2)}, u32[]{:S(2)}) collective-permute-start(bf16[12,48,768]{2,1,0:T(8,128)(2,1)} %get-tuple-element.755.refs_2_), channel_id=1, source_target_pairs={{4,0},{5,1},{6,2},{7,3},{0,4},{1,5},{2,6},{3,7},{12,8},{13,9},{14,... | collective-permute-start | bytes 2654216 | tf_op jit(solution)/shard_map/ppermute | solution.py:1121
  107.3 24.7 %collective-permute-start.25 = (bf16[12,48,768]{2,1,0:T(8,128)(2,1)}, bf16[12,48,768]{2,1,0:T(8,128)(2,1)}, u32[]{:S(2)}, u32[]{:S(2)}) collective-permute-start(bf16[12,48,768]{2,1,0:T(8,128)(2,1)} %get-tuple-element.756.refs_3_), channel_id=1, source_target_pairs={{1,0},{0,1},{3,2},{2,3},{5,4},{4,5},{7,6},{6,7},{9,8},{8,9},{11,10... | collective-permute-start | bytes 2654216 | tf_op jit(solution)/shard_map/ppermute | solution.py:1121
  109.7 22.3 %collective-permute-start.27 = (bf16[8,48,768]{2,1,0:T(8,128)(2,1)S(1)}, bf16[8,48,768]{2,1,0:T(8,128)(2,1)}, u32[]{:S(2)}, u32[]{:S(2)}) collective-permute-start(bf16[8,48,768]{2,1,0:T(8,128)(2,1)S(1)} %gather_z.11.refs_0_), channel_id=1, source_target_pairs={{8,0},{9,1},{10,2},{11,3},{12,4},{13,5},{14,6},{15,7},{0,8},{1,9},... | collective-permute-start | bytes 1769480 | tf_op jit(solution)/shard_map/ppermute | solution.py:1121
  135.9 24.3 %collective-permute-start.30 = (bf16[32,48,768]{2,1,0:T(8,128)(2,1)S(1)}, bf16[32,48,768]{2,1,0:T(8,128)(2,1)S(1)}, u32[]{:S(2)}, u32[]{:S(2)}) collective-permute-start(bf16[32,48,768]{2,1,0:T(8,128)(2,1)S(1)} %get-tuple-element.825.refs_4_.refs_9_), channel_id=1, source_target_pairs={{2,0},{3,1},{0,2},{1,3},{6,4},{7,5},{4,6},{5,7},{10,8},{11,9},{8,1... | collective-permute-start | bytes 7077896 | tf_op jit(solution)/shard_map/ppermute | solution.py:1121
  136.6 16.7 %collective-permute-start.31 = (bf16[4,48,768]{2,1,0:T(8,128)(2,1)S(1)}, bf16[4,48,768]{2,1,0:T(8,128)(2,1)S(1)}, u32[]{:S(2)}, u32[]{:S(2)}) collective-permute-start(bf16[4,48,768]{2,1,0:T(8,128)(2,1)S(1)} %pack.12.refs_0_), channel_id=1, source_target_pairs={{16,0},{17,1},{18,2},{19,3},{20,4},{21,5},{22,6},{23,7},{24,8},{25... | collective-permute-start | bytes 884744 | tf_op jit(solution)/shard_map/ppermute | solution.py:1121
  136.7 22.1 %collective-permute-start.28 = (bf16[12,48,768]{2,1,0:T(8,128)(2,1)S(1)}, bf16[12,48,768]{2,1,0:T(8,128)(2,1)S(1)}, u32[]{:S(2)}, u32[]{:S(2)}) collective-permute-start(bf16[12,48,768]{2,1,0:T(8,128)(2,1)S(1)} %get-tuple-element.787.refs_2_), channel_id=1, source_target_pairs={{4,0},{5,1},{6,2},{7,3},{0,4},{1,5},{2,6},{3,7},{12,8},{13,9},{14,... | collective-permute-start | bytes 2654216 | tf_op jit(solution)/shard_map/ppermute | solution.py:1121
  138.4 21.8 %collective-permute-start.29 = (bf16[12,48,768]{2,1,0:T(8,128)(2,1)S(1)}, bf16[12,48,768]{2,1,0:T(8,128)(2,1)S(1)}, u32[]{:S(2)}, u32[]{:S(2)}) collective-permute-start(bf16[12,48,768]{2,1,0:T(8,128)(2,1)S(1)} %get-tuple-element.788.refs_3_), channel_id=1, source_target_pairs={{1,0},{0,1},{3,2},{2,3},{5,4},{4,5},{7,6},{6,7},{9,8},{8,9},{11,10... | collective-permute-start | bytes 2654216 | tf_op jit(solution)/shard_map/ppermute | solution.py:1121
  162.2 22.2 %collective-permute-start.36 = (bf16[32,48,768]{2,1,0:T(8,128)(2,1)S(1)}, bf16[32,48,768]{2,1,0:T(8,128)(2,1)S(1)}, u32[]{:S(2)}, u32[]{:S(2)}) collective-permute-start(bf16[32,48,768]{2,1,0:T(8,128)(2,1)S(1)} %get-tuple-element.863.refs_7_.refs_11_.refs_4_), channel_id=1, source_target_pairs={{2,0},{3,1},{0,2},{1,3},{6,4},{7,5},{4,6},{5,7},{10,8},{11,9},{8,1... | collective-permute-start | bytes 7077896 | tf_op jit(solution)/shard_map/ppermute | solution.py:1121
  162.3 22.1 %collective-permute-start.34 = (bf16[12,48,768]{2,1,0:T(8,128)(2,1)S(1)}, bf16[12,48,768]{2,1,0:T(8,128)(2,1)S(1)}, u32[]{:S(2)}, u32[]{:S(2)}) collective-permute-start(bf16[12,48,768]{2,1,0:T(8,128)(2,1)S(1)} %get-tuple-element.817.refs_2_), channel_id=1, source_target_pairs={{4,0},{5,1},{6,2},{7,3},{0,4},{1,5},{2,6},{3,7},{12,8},{13,9},{14,... | collective-permute-start | bytes 2654216 | tf_op jit(solution)/shard_map/ppermute | solution.py:1121
  162.7 21.7 %collective-permute-start.35 = (bf16[12,48,768]{2,1,0:T(8,128)(2,1)S(1)}, bf16[12,48,768]{2,1,0:T(8,128)(2,1)S(1)}, u32[]{:S(2)}, u32[]{:S(2)}) collective-permute-start(bf16[12,48,768]{2,1,0:T(8,128)(2,1)S(1)} %get-tuple-element.818.refs_3_), channel_id=1, source_target_pairs={{1,0},{0,1},{3,2},{2,3},{5,4},{4,5},{7,6},{6,7},{9,8},{8,9},{11,10... | collective-permute-start | bytes 2654216 | tf_op jit(solution)/shard_map/ppermute | solution.py:1121
  164.0 15.4 %collective-permute-start.37 = (bf16[8,48,768]{2,1,0:T(8,128)(2,1)S(1)}, bf16[8,48,768]{2,1,0:T(8,128)(2,1)S(1)}, u32[]{:S(2)}, u32[]{:S(2)}) collective-permute-start(bf16[8,48,768]{2,1,0:T(8,128)(2,1)S(1)} %gather_z.12.refs_0_), channel_id=1, source_target_pairs={{8,0},{9,1},{10,2},{11,3},{12,4},{13,5},{14,6},{15,7},{0,8},{1,9},... | collective-permute-start | bytes 1769480 | tf_op jit(solution)/shard_map/ppermute | solution.py:1121
  186.7 23.5 %collective-permute-start.41 = (bf16[32,48,768]{2,1,0:T(8,128)(2,1)S(1)}, bf16[32,48,768]{2,1,0:T(8,128)(2,1)S(1)}, u32[]{:S(2)}, u32[]{:S(2)}) collective-permute-start(bf16[32,48,768]{2,1,0:T(8,128)(2,1)S(1)} %get-tuple-element.895.refs_4_.refs_7_), channel_id=1, source_target_pairs={{2,0},{3,1},{0,2},{1,3},{6,4},{7,5},{4,6},{5,7},{10,8},{11,9},{8,1... | collective-permute-start | bytes 7077896 | tf_op jit(solution)/shard_map/ppermute | solution.py:1121
  186.8 22.1 %collective-permute-start.39 = (bf16[12,48,768]{2,1,0:T(8,128)(2,1)S(1)}, bf16[12,48,768]{2,1,0:T(8,128)(2,1)S(1)}, u32[]{:S(2)}, u32[]{:S(2)}) collective-permute-start(bf16[12,48,768]{2,1,0:T(8,128)(2,1)S(1)} %get-tuple-element.851.refs_2_), channel_id=1, source_target_pairs={{4,0},{5,1},{6,2},{7,3},{0,4},{1,5},{2,6},{3,7},{12,8},{13,9},{14,... | collective-permute-start | bytes 2654216 | tf_op jit(solution)/shard_map/ppermute | solution.py:1121
  188.5 21.7 %collective-permute-start.40 = (bf16[12,48,768]{2,1,0:T(8,128)(2,1)S(1)}, bf16[12,48,768]{2,1,0:T(8,128)(2,1)S(1)}, u32[]{:S(2)}, u32[]{:S(2)}) collective-permute-start(bf16[12,48,768]{2,1,0:T(8,128)(2,1)S(1)} %get-tuple-element.852.refs_3_), channel_id=1, source_target_pairs={{1,0},{0,1},{3,2},{2,3},{5,4},{4,5},{7,6},{6,7},{9,8},{8,9},{11,10... | collective-permute-start | bytes 2654216 | tf_op jit(solution)/shard_map/ppermute | solution.py:1121
  189.6 19.0 %collective-permute-start.42 = (bf16[2,48,768]{2,1,0:T(8,128)(2,1)S(1)}, bf16[2,48,768]{2,1,0:T(8,128)(2,1)S(1)}, u32[]{:S(2)}, u32[]{:S(2)}) collective-permute-start(bf16[2,48,768]{2,1,0:T(8,128)(2,1)S(1)} %pack.13.refs_0_), channel_id=1, source_target_pairs={{16,0},{17,1},{18,2},{19,3},{20,4},{21,5},{22,6},{23,7},{24,8},{25... | collective-permute-start | bytes 442376 | tf_op jit(solution)/shard_map/ppermute | solution.py:1121
  212.5 24.9 %collective-permute-start.45 = (bf16[32,48,768]{2,1,0:T(8,128)(2,1)S(1)}, bf16[32,48,768]{2,1,0:T(8,128)(2,1)S(1)}, u32[]{:S(2)}, u32[]{:S(2)}) collective-permute-start(bf16[32,48,768]{2,1,0:T(8,128)(2,1)S(1)} %get-tuple-element.911.refs_4_.refs_9_), channel_id=1, source_target_pairs={{2,0},{3,1},{0,2},{1,3},{6,4},{7,5},{4,6},{5,7},{10,8},{11,9},{8,1... | collective-permute-start | bytes 7077896 | tf_op jit(solution)/shard_map/ppermute | solution.py:1121
  215.6 21.8 %collective-permute-start.43 = (bf16[12,48,768]{2,1,0:T(8,128)(2,1)S(1)}, bf16[12,48,768]{2,1,0:T(8,128)(2,1)S(1)}, u32[]{:S(2)}, u32[]{:S(2)}) collective-permute-start(bf16[12,48,768]{2,1,0:T(8,128)(2,1)S(1)} %get-tuple-element.879.refs_2_), channel_id=1, source_target_pairs={{4,0},{5,1},{6,2},{7,3},{0,4},{1,5},{2,6},{3,7},{12,8},{13,9},{14,... | collective-permute-start | bytes 2654216 | tf_op jit(solution)/shard_map/ppermute | solution.py:1121
  215.9 21.5 %collective-permute-start.44 = (bf16[12,48,768]{2,1,0:T(8,128)(2,1)S(1)}, bf16[12,48,768]{2,1,0:T(8,128)(2,1)S(1)}, u32[]{:S(2)}, u32[]{:S(2)}) collective-permute-start(bf16[12,48,768]{2,1,0:T(8,128)(2,1)S(1)} %get-tuple-element.880.refs_3_), channel_id=1, source_target_pairs={{1,0},{0,1},{3,2},{2,3},{5,4},{4,5},{7,6},{6,7},{9,8},{8,9},{11,10... | collective-permute-start | bytes 2654216 | tf_op jit(solution)/shard_map/ppermute | solution.py:1121
  239.6 23.5 %collective-permute-start.51 = (bf16[32,48,768]{2,1,0:T(8,128)(2,1)S(1)}, bf16[32,48,768]{2,1,0:T(8,128)(2,1)S(1)}, u32[]{:S(2)}, u32[]{:S(2)}) collective-permute-start(bf16[32,48,768]{2,1,0:T(8,128)(2,1)S(1)} %get-tuple-element.935.refs_7_.refs_11_.refs_4_), channel_id=1, source_target_pairs={{2,0},{3,1},{0,2},{1,3},{6,4},{7,5},{4,6},{5,7},{10,8},{11,9},{8,1... | collective-permute-start | bytes 7077896 | tf_op jit(solution)/shard_map/ppermute | solution.py:1121
  239.7 22.1 %collective-permute-start.49 = (bf16[12,48,768]{2,1,0:T(8,128)(2,1)S(1)}, bf16[12,48,768]{2,1,0:T(8,128)(2,1)S(1)}, u32[]{:S(2)}, u32[]{:S(2)}) collective-permute-start(bf16[12,48,768]{2,1,0:T(8,128)(2,1)S(1)} %get-tuple-element.905.refs_0_), channel_id=1, source_target_pairs={{4,0},{5,1},{6,2},{7,3},{0,4},{1,5},{2,6},{3,7},{12,8},{13,9},{14,... | collective-permute-start | bytes 2654216 | tf_op jit(solution)/shard_map/ppermute | solution.py:1121
  241.5 21.7 %collective-permute-start.50 = (bf16[12,48,768]{2,1,0:T(8,128)(2,1)S(1)}, bf16[12,48,768]{2,1,0:T(8,128)(2,1)S(1)}, u32[]{:S(2)}, u32[]{:S(2)}) collective-permute-start(bf16[12,48,768]{2,1,0:T(8,128)(2,1)S(1)} %get-tuple-element.906.refs_1_), channel_id=1, source_target_pairs={{1,0},{0,1},{3,2},{2,3},{5,4},{4,5},{7,6},{6,7},{9,8},{8,9},{11,10... | collective-permute-start | bytes 2654216 | tf_op jit(solution)/shard_map/ppermute | solution.py:1121
  264.5 18.6 %collective-permute-start.55 = (bf16[32,48,768]{2,1,0:T(8,128)(2,1)S(1)}, bf16[32,48,768]{2,1,0:T(8,128)(2,1)S(1)}, u32[]{:S(2)}, u32[]{:S(2)}) collective-permute-start(bf16[32,48,768]{2,1,0:T(8,128)(2,1)S(1)} %get-tuple-element.960.refs_4_.refs_7_), channel_id=1, source_target_pairs={{2,0},{3,1},{0,2},{1,3},{6,4},{7,5},{4,6},{5,7},{10,8},{11,9},{8,1... | collective-permute-start | bytes 7077896 | tf_op jit(solution)/shard_map/ppermute | solution.py:1121
  264.6 18.5 %collective-permute-start.53 = (bf16[8,48,768]{2,1,0:T(8,128)(2,1)S(1)}, bf16[8,48,768]{2,1,0:T(8,128)(2,1)S(1)}, u32[]{:S(2)}, u32[]{:S(2)}) collective-permute-start(bf16[8,48,768]{2,1,0:T(8,128)(2,1)S(1)} %get-tuple-element.929.refs_0_), channel_id=1, source_target_pairs={{4,0},{5,1},{6,2},{7,3},{0,4},{1,5},{2,6},{3,7},{12,8},{13,9},{14,... | collective-permute-start | bytes 1769480 | tf_op jit(solution)/shard_map/ppermute | solution.py:1121
  265.0 18.1 %collective-permute-start.54 = (bf16[8,48,768]{2,1,0:T(8,128)(2,1)S(1)}, bf16[8,48,768]{2,1,0:T(8,128)(2,1)S(1)}, u32[]{:S(2)}, u32[]{:S(2)}) collective-permute-start(bf16[8,48,768]{2,1,0:T(8,128)(2,1)S(1)} %get-tuple-element.930.refs_1_), channel_id=1, source_target_pairs={{1,0},{0,1},{3,2},{2,3},{5,4},{4,5},{7,6},{6,7},{9,8},{8,9},{11,10... | collective-permute-start | bytes 1769480 | tf_op jit(solution)/shard_map/ppermute | solution.py:1121
  265.7 17.4 %collective-permute-start.56 = (bf16[256,768]{1,0:T(8,128)(2,1)S(1)}, bf16[256,768]{1,0:T(8,128)(2,1)S(1)}, u32[]{:S(2)}, u32[]{:S(2)}) collective-permute-start(bf16[256,768]{1,0:T(8,128)(2,1)S(1)} %bitcast.53), channel_id=1, source_target_pairs={{0,0},{2,1},{1,2},{3,3},{4,4},{6,5},{5,6},{7,7},{8,8},{10,9},{9,10... | collective-permute-start | bytes 1179656 | tf_op jit(solution)/shard_map/ppermute | solution.py:1121
  303.4 15.7 %collective-permute-start.64 = (bf16[8,48,768]{2,1,0:T(8,128)(2,1)S(1)}, bf16[8,48,768]{2,1,0:T(8,128)(2,1)S(1)}, u32[]{:S(2)}, u32[]{:S(2)}) collective-permute-start(bf16[8,48,768]{2,1,0:T(8,128)(2,1)S(1)} %get-tuple-element.981.refs_13_), channel_id=1, source_target_pairs={{4,0},{5,1},{6,2},{7,3},{0,4},{1,5},{2,6},{3,7},{12,8},{13,9},{14,... | collective-permute-start | bytes 1769480 | tf_op jit(solution)/shard_map/ppermute | solution.py:1121
  305.2 15.3 %collective-permute-start.65 = (bf16[8,48,768]{2,1,0:T(8,128)(2,1)S(1)}, bf16[8,48,768]{2,1,0:T(8,128)(2,1)S(1)}, u32[]{:S(2)}, u32[]{:S(2)}) collective-permute-start(bf16[8,48,768]{2,1,0:T(8,128)(2,1)S(1)} %get-tuple-element.982.refs_14_), channel_id=1, source_target_pairs={{1,0},{0,1},{3,2},{2,3},{5,4},{4,5},{7,6},{6,7},{9,8},{8,9},{11,10... | collective-permute-start | bytes 1769480 | tf_op jit(solution)/shard_map/ppermute | solution.py:1121
  334.9 22.5 %collective-permute-start.69 = (bf16[8,48,768]{2,1,0:T(8,128)(2,1)S(1)}, bf16[8,48,768]{2,1,0:T(8,128)(2,1)S(1)}, u32[]{:S(2)}, u32[]{:S(2)}) collective-permute-start(bf16[8,48,768]{2,1,0:T(8,128)(2,1)S(1)} %get-tuple-element.1022), channel_id=1, source_target_pairs={{4,0},{5,1},{6,2},{7,3},{0,4},{1,5},{2,6},{3,7},{12,8},{13,9},{14,... | collective-permute-start | bytes 1769480 | tf_op jit(solution)/shard_map/ppermute | solution.py:1121
  336.6 21.6 %collective-permute-start.70 = (bf16[8,48,768]{2,1,0:T(8,128)(2,1)S(1)}, bf16[8,48,768]{2,1,0:T(8,128)(2,1)S(1)}, u32[]{:S(2)}, u32[]{:S(2)}) collective-permute-start(bf16[8,48,768]{2,1,0:T(8,128)(2,1)S(1)} %get-tuple-element.1023), channel_id=1, source_target_pairs={{1,0},{0,1},{3,2},{2,3},{5,4},{4,5},{7,6},{6,7},{9,8},{8,9},{11,10... | collective-permute-start | bytes 1769480 | tf_op jit(solution)/shard_map/ppermute | solution.py:1121
  336.9 22.1 %collective-permute-start.60 = (bf16[256,768]{1,0:T(8,128)(2,1)S(1)}, bf16[256,768]{1,0:T(8,128)(2,1)S(1)}, u32[]{:S(2)}, u32[]{:S(2)}) collective-permute-start(bf16[256,768]{1,0:T(8,128)(2,1)S(1)} %copy-done.144), channel_id=1, source_target_pairs={{0,0},{2,1},{1,2},{3,3},{4,4},{6,5},{5,6},{7,7},{8,8},{10,9},{9,10... | collective-permute-start | bytes 1179656 | tf_op jit(solution)/shard_map/ppermute | solution.py:1121
  363.6 21.4 %collective-permute-start.74 = (bf16[12,48,768]{2,1,0:T(8,128)(2,1)S(1)}, bf16[12,48,768]{2,1,0:T(8,128)(2,1)S(1)}, u32[]{:S(2)}, u32[]{:S(2)}) collective-permute-start(bf16[12,48,768]{2,1,0:T(8,128)(2,1)S(1)} %get-tuple-element.1054), channel_id=1, source_target_pairs={{4,0},{5,1},{6,2},{7,3},{0,4},{1,5},{2,6},{3,7},{12,8},{13,9},{14,... | collective-permute-start | bytes 2654216 | tf_op jit(solution)/shard_map/ppermute | solution.py:1121
  364.1 17.9 %collective-permute-start.75 = (bf16[10,48,768]{2,1,0:T(8,128)(2,1)S(1)}, bf16[10,48,768]{2,1,0:T(8,128)(2,1)S(1)}, u32[]{:S(2)}, u32[]{:S(2)}) collective-permute-start(bf16[10,48,768]{2,1,0:T(8,128)(2,1)S(1)} %get-tuple-element.1055), channel_id=1, source_target_pairs={{1,0},{0,1},{3,2},{2,3},{5,4},{4,5},{7,6},{6,7},{9,8},{8,9},{11,10... | collective-permute-start | bytes 2211848 | tf_op jit(solution)/shard_map/ppermute | solution.py:1121
  385.0 16.1 %collective-permute-start.83 = (bf16[256,3840]{1,0:T(8,128)(2,1)S(1)}, bf16[256,3840]{1,0:T(8,128)(2,1)S(1)}, u32[]{:S(2)}, u32[]{:S(2)}) collective-permute-start(bf16[256,3840]{1,0:T(8,128)(2,1)S(1)} %get-tuple-element.1094.da_ref), channel_id=1, source_target_pairs={{2,0},{3,1},{0,2},{1,3},{6,4},{7,5},{4,6},{5,7},{10,8},{11,9},{8,1... | collective-permute-start | bytes 5898248 | tf_op jit(solution)/shard_map/ppermute | solution.py:1121
  386.6 20.7 %collective-permute-start.79 = (bf16[12,48,768]{2,1,0:T(8,128)(2,1)S(1)}, bf16[12,48,768]{2,1,0:T(8,128)(2,1)S(1)}, u32[]{:S(2)}, u32[]{:S(2)}) collective-permute-start(bf16[12,48,768]{2,1,0:T(8,128)(2,1)S(1)} %get-tuple-element.1084), channel_id=1, source_target_pairs={{4,0},{5,1},{6,2},{7,3},{0,4},{1,5},{2,6},{3,7},{12,8},{13,9},{14,... | collective-permute-start | bytes 2654216 | tf_op jit(solution)/shard_map/ppermute | solution.py:1121
  387.0 20.2 %collective-permute-start.80 = (bf16[9,48,768]{2,1,0:T(8,128)(2,1)S(1)}, bf16[9,48,768]{2,1,0:T(8,128)(2,1)S(1)}, u32[]{:S(2)}, u32[]{:S(2)}) collective-permute-start(bf16[9,48,768]{2,1,0:T(8,128)(2,1)S(1)} %get-tuple-element.1085), channel_id=1, source_target_pairs={{1,0},{0,1},{3,2},{2,3},{5,4},{4,5},{7,6},{6,7},{9,8},{8,9},{11,10... | collective-permute-start | bytes 1990664 | tf_op jit(solution)/shard_map/ppermute | solution.py:1121
  391.8 15.4 %collective-permute-start.81 = (bf16[6,48,768]{2,1,0:T(8,128)(2,1)S(1)}, bf16[6,48,768]{2,1,0:T(8,128)(2,1)S(1)}, u32[]{:S(2)}, u32[]{:S(2)}) collective-permute-start(bf16[6,48,768]{2,1,0:T(8,128)(2,1)S(1)} %get-tuple-element.1086), channel_id=1, source_target_pairs={{8,0},{9,1},{10,2},{11,3},{12,4},{13,5},{14,6},{15,7},{0,8},{1,9},... | collective-permute-start | bytes 1327112 | tf_op jit(solution)/shard_map/ppermute | solution.py:1121
  409.6 21.6 %collective-permute-start.84 = (bf16[12,48,768]{2,1,0:T(8,128)(2,1)S(1)}, bf16[12,48,768]{2,1,0:T(8,128)(2,1)S(1)}, u32[]{:S(2)}, u32[]{:S(2)}) collective-permute-start(bf16[12,48,768]{2,1,0:T(8,128)(2,1)S(1)} %get-tuple-element.1115), channel_id=1, source_target_pairs={{4,0},{5,1},{6,2},{7,3},{0,4},{1,5},{2,6},{3,7},{12,8},{13,9},{14,... | collective-permute-start | bytes 2654216 | tf_op jit(solution)/shard_map/ppermute | solution.py:1121
  410.0 18.3 %collective-permute-start.85 = (bf16[10,48,768]{2,1,0:T(8,128)(2,1)S(1)}, bf16[10,48,768]{2,1,0:T(8,128)(2,1)S(1)}, u32[]{:S(2)}, u32[]{:S(2)}) collective-permute-start(bf16[10,48,768]{2,1,0:T(8,128)(2,1)S(1)} %get-tuple-element.1116), channel_id=1, source_target_pairs={{1,0},{0,1},{3,2},{2,3},{5,4},{4,5},{7,6},{6,7},{9,8},{8,9},{11,10... | collective-permute-start | bytes 2211848 | tf_op jit(solution)/shard_map/ppermute | solution.py:1121
  411.5 16.7 %collective-permute-start.86 = (bf16[6,48,768]{2,1,0:T(8,128)(2,1)S(1)}, bf16[6,48,768]{2,1,0:T(8,128)(2,1)S(1)}, u32[]{:S(2)}, u32[]{:S(2)}) collective-permute-start(bf16[6,48,768]{2,1,0:T(8,128)(2,1)S(1)} %get-tuple-element.1117), channel_id=1, source_target_pairs={{8,0},{9,1},{10,2},{11,3},{12,4},{13,5},{14,6},{15,7},{0,8},{1,9},... | collective-permute-start | bytes 1327112 | tf_op jit(solution)/shard_map/ppermute | solution.py:1121
  431.8 20.8 %collective-permute-start.89 = (bf16[12,48,768]{2,1,0:T(8,128)(2,1)S(1)}, bf16[12,48,768]{2,1,0:T(8,128)(2,1)S(1)}, u32[]{:S(2)}, u32[]{:S(2)}) collective-permute-start(bf16[12,48,768]{2,1,0:T(8,128)(2,1)S(1)} %get-tuple-element.1153), channel_id=1, source_target_pairs={{4,0},{5,1},{6,2},{7,3},{0,4},{1,5},{2,6},{3,7},{12,8},{13,9},{14,... | collective-permute-start | bytes 2654216 | tf_op jit(solution)/shard_map/ppermute | solution.py:1121
  432.3 19.5 %collective-permute-start.90 = (bf16[11,48,768]{2,1,0:T(8,128)(2,1)S(1)}, bf16[11,48,768]{2,1,0:T(8,128)(2,1)S(1)}, u32[]{:S(2)}, u32[]{:S(2)}) collective-permute-start(bf16[11,48,768]{2,1,0:T(8,128)(2,1)S(1)} %get-tuple-element.1154), channel_id=1, source_target_pairs={{1,0},{0,1},{3,2},{2,3},{5,4},{4,5},{7,6},{6,7},{9,8},{8,9},{11,10... | collective-permute-start | bytes 2433032 | tf_op jit(solution)/shard_map/ppermute | solution.py:1121
  434.2 16.0 %collective-permute-start.91 = (bf16[6,48,768]{2,1,0:T(8,128)(2,1)S(1)}, bf16[6,48,768]{2,1,0:T(8,128)(2,1)S(1)}, u32[]{:S(2)}, u32[]{:S(2)}) collective-permute-start(bf16[6,48,768]{2,1,0:T(8,128)(2,1)S(1)} %get-tuple-element.1155), channel_id=1, source_target_pairs={{8,0},{9,1},{10,2},{11,3},{12,4},{13,5},{14,6},{15,7},{0,8},{1,9},... | collective-permute-start | bytes 1327112 | tf_op jit(solution)/shard_map/ppermute | solution.py:1121
  453.3 22.1 %collective-permute-start.94 = (bf16[12,48,768]{2,1,0:T(8,128)(2,1)S(1)}, bf16[12,48,768]{2,1,0:T(8,128)(2,1)S(1)}, u32[]{:S(2)}, u32[]{:S(2)}) collective-permute-start(bf16[12,48,768]{2,1,0:T(8,128)(2,1)S(1)} %get-tuple-element.1187), channel_id=1, source_target_pairs={{4,0},{5,1},{6,2},{7,3},{0,4},{1,5},{2,6},{3,7},{12,8},{13,9},{14,... | collective-permute-start | bytes 2654216 | tf_op jit(solution)/shard_map/ppermute | solution.py:1121
  453.9 20.7 %collective-permute-start.95 = (bf16[11,48,768]{2,1,0:T(8,128)(2,1)S(1)}, bf16[11,48,768]{2,1,0:T(8,128)(2,1)S(1)}, u32[]{:S(2)}, u32[]{:S(2)}) collective-permute-start(bf16[11,48,768]{2,1,0:T(8,128)(2,1)S(1)} %get-tuple-element.1188), channel_id=1, source_target_pairs={{1,0},{0,1},{3,2},{2,3},{5,4},{4,5},{7,6},{6,7},{9,8},{8,9},{11,10... | collective-permute-start | bytes 2433032 | tf_op jit(solution)/shard_map/ppermute | solution.py:1121
  456.2 16.7 %collective-permute-start.96 = (bf16[6,48,768]{2,1,0:T(8,128)(2,1)S(1)}, bf16[6,48,768]{2,1,0:T(8,128)(2,1)S(1)}, u32[]{:S(2)}, u32[]{:S(2)}) collective-permute-start(bf16[6,48,768]{2,1,0:T(8,128)(2,1)S(1)} %get-tuple-element.1189), channel_id=1, source_target_pairs={{8,0},{9,1},{10,2},{11,3},{12,4},{13,5},{14,6},{15,7},{0,8},{1,9},... | collective-permute-start | bytes 1327112 | tf_op jit(solution)/shard_map/ppermute | solution.py:1121
  476.0 22.1 %collective-permute-start.99 = (bf16[12,48,768]{2,1,0:T(8,128)(2,1)S(1)}, bf16[12,48,768]{2,1,0:T(8,128)(2,1)S(1)}, u32[]{:S(2)}, u32[]{:S(2)}) collective-permute-start(bf16[12,48,768]{2,1,0:T(8,128)(2,1)S(1)} %get-tuple-element.1219), channel_id=1, source_target_pairs={{4,0},{5,1},{6,2},{7,3},{0,4},{1,5},{2,6},{3,7},{12,8},{13,9},{14,... | collective-permute-start | bytes 2654216 | tf_op jit(solution)/shard_map/ppermute | solution.py:1121
  476.6 20.8 %collective-permute-start.100 = (bf16[11,48,768]{2,1,0:T(8,128)(2,1)S(1)}, bf16[11,48,768]{2,1,0:T(8,128)(2,1)S(1)}, u32[]{:S(2)}, u32[]{:S(2)}) collective-permute-start(bf16[11,48,768]{2,1,0:T(8,128)(2,1)S(1)} %get-tuple-element.1220), channel_id=1, source_target_pairs={{1,0},{0,1},{3,2},{2,3},{5,4},{4,5},{7,6},{6,7},{9,8},{8,9},{11,10... | collective-permute-start | bytes 2433032 | tf_op jit(solution)/shard_map/ppermute | solution.py:1121
  478.9 16.8 %collective-permute-start.101 = (bf16[6,48,768]{2,1,0:T(8,128)(2,1)S(1)}, bf16[6,48,768]{2,1,0:T(8,128)(2,1)S(1)}, u32[]{:S(2)}, u32[]{:S(2)}) collective-permute-start(bf16[6,48,768]{2,1,0:T(8,128)(2,1)S(1)} %get-tuple-element.1221), channel_id=1, source_target_pairs={{8,0},{9,1},{10,2},{11,3},{12,4},{13,5},{14,6},{15,7},{0,8},{1,9},... | collective-permute-start | bytes 1327112 | tf_op jit(solution)/shard_map/ppermute | solution.py:1121
  498.8 21.3 %collective-permute-start.105 = (bf16[12,48,768]{2,1,0:T(8,128)(2,1)S(1)}, bf16[12,48,768]{2,1,0:T(8,128)(2,1)S(1)}, u32[]{:S(2)}, u32[]{:S(2)}) collective-permute-start(bf16[12,48,768]{2,1,0:T(8,128)(2,1)S(1)} %get-tuple-element.1254), channel_id=1, source_target_pairs={{4,0},{5,1},{6,2},{7,3},{0,4},{1,5},{2,6},{3,7},{12,8},{13,9},{14,... | collective-permute-start | bytes 2654216 | tf_op jit(solution)/shard_map/ppermute | solution.py:1121
  499.3 20.0 %collective-permute-start.106 = (bf16[11,48,768]{2,1,0:T(8,128)(2,1)S(1)}, bf16[11,48,768]{2,1,0:T(8,128)(2,1)S(1)}, u32[]{:S(2)}, u32[]{:S(2)}) collective-permute-start(bf16[11,48,768]{2,1,0:T(8,128)(2,1)S(1)} %get-tuple-element.1255), channel_id=1, source_target_pairs={{1,0},{0,1},{3,2},{2,3},{5,4},{4,5},{7,6},{6,7},{9,8},{8,9},{11,10... | collective-permute-start | bytes 2433032 | tf_op jit(solution)/shard_map/ppermute | solution.py:1121
  501.6 16.0 %collective-permute-start.107 = (bf16[6,48,768]{2,1,0:T(8,128)(2,1)S(1)}, bf16[6,48,768]{2,1,0:T(8,128)(2,1)S(1)}, u32[]{:S(2)}, u32[]{:S(2)}) collective-permute-start(bf16[6,48,768]{2,1,0:T(8,128)(2,1)S(1)} %get-tuple-element.1256), channel_id=1, source_target_pairs={{8,0},{9,1},{10,2},{11,3},{12,4},{13,5},{14,6},{15,7},{0,8},{1,9},... | collective-permute-start | bytes 1327112 | tf_op jit(solution)/shard_map/ppermute | solution.py:1121
  503.2 16.9 %collective-permute-start.109 = (f32[48,768]{1,0:T(8,128)S(1)}, f32[48,768]{1,0:T(8,128)S(1)}, u32[]{:S(2)}, u32[]{:S(2)}) collective-permute-start(f32[48,768]{1,0:T(8,128)S(1)} %bitcast.45), channel_id=1, source_target_pairs={{2,0},{3,1},{0,2},{1,3},{6,4},{7,5},{4,6},{5,7},{10,8},{11,9},{8,1... | collective-permute-start | bytes 442376 | tf_op jit(solution)/shard_map/ppermute | solution.py:1121
  520.6 15.7 %collective-permute-start.112 = (bf16[6,48,768]{2,1,0:T(8,128)(2,1)S(1)}, bf16[6,48,768]{2,1,0:T(8,128)(2,1)S(1)}, u32[]{:S(2)}, u32[]{:S(2)}) collective-permute-start(bf16[6,48,768]{2,1,0:T(8,128)(2,1)S(1)} %get-tuple-element.1288), channel_id=1, source_target_pairs={{8,0},{9,1},{10,2},{11,3},{12,4},{13,5},{14,6},{15,7},{0,8},{1,9},... | collective-permute-start | bytes 1327112 | tf_op jit(solution)/shard_map/ppermute | solution.py:1121
  525.0 23.6 %collective-permute-start.104 = (bf16[256,768]{1,0:T(8,128)(2,1)S(1)}, bf16[256,768]{1,0:T(8,128)(2,1)S(1)}, u32[]{:S(2)}, u32[]{:S(2)}) collective-permute-start(bf16[256,768]{1,0:T(8,128)(2,1)S(1)} %get-tuple-element.1236), channel_id=1, source_target_pairs={{0,0},{2,1},{1,2},{3,3},{4,4},{6,5},{5,6},{7,7},{8,8},{10,9},{9,10... | collective-permute-start | bytes 1179656 | tf_op jit(solution)/shard_map/ppermute | solution.py:1121
  (205 other events, 1634.3 us)

commit v7 on v6

--- a/solution.py
+++ b/solution.py
@@ -12,7 +12,7 @@
 BLOCKS = 16
 ZS = 4
 LAG = 1
-VMEM_MB = 24
+VMEM_MB = 20
 EPS = 1e-06
 MASKED = -1e30
 AXES = ("dp", "seq")

time: 579 us -> 574 us (level)
  starting transfers between devices: 110 us -> 129 us
  waiting for transfers between devices: 208 us -> 191 us
  local copies, waits for them, and re-layouts: 44 us -> 38.1 us
    ppermute x120, starting transfers between devices: 110 us -> 129 us  [move(): return lax.ppermute(value, AXES, perm)]
    ppermute x120, waiting for transfers between devices: 208 us -> 191 us  [move(): return lax.ppermute(value, AXES, perm)]
    unnamed x300 -> x256, local copies, waits for them, and re-layouts: 43 us -> 37.1 us
  transfers between devices with their start and end apart: 120 -> 120, of which waited for: 67 -> 64; matrix products, arithmetic and copies ran while one was open for 1% -> 1% of each run, Pallas kernels for 29% -> 29%
where the time goes in v7:
time: 574 us; the launch traced here: 565 us
  Pallas kernels  199 us (35%)
  waiting for transfers between devices  191 us (33%)
  starting transfers between devices  129 us (22%)
  local copies, waits for them, and re-layouts  38.1 us (7%)
    ppermute x120, waiting for transfers between devices, move(): return lax.ppermute(value, AXES, perm)  191 us
    ppermute x120, starting transfers between devices, move(): return lax.ppermute(value, AXES, perm)  129 us
    pallas_call x3, Pallas kernels, attn_forward(): pl.pallas_call(attn_kernel, out_shape=(shape((tokens, width), F32),) + ke...  39.5 us
    unnamed x256, local copies, waits for them, and re-layouts  37.1 us
    pallas_call x18, Pallas kernels, copy_blocks(): pl.pallas_call(functools.partial(copy_kernel, plan, len(inputs)), out_sha...  30.4 us
    pallas_call x3, Pallas kernels, chain_backward(): pl.pallas_call(functools.partial(chain_kernel, 384, len(after)), out_shap...  24.9 us
    pallas_call x3, Pallas kernels, attn_backward(): pl.pallas_call(functools.partial(attn_back_kernel, len(after)), out_shape...  23.3 us
    pallas_call x3, Pallas kernels, inner_forward(): pl.pallas_call(functools.partial(inner_kernel, 384), out_shape=(shape((to...  19.4 us
  transfers between devices with their start and end apart: 120, of which 64 were waited for; matrix products, arithmetic and copies ran while one was open for 1% of the time, Pallas kernels for 29%

profile of v7, /device:TPU:0, one launch (start us, length us, event | category | flops | bytes accessed | tf_op | source)
XLA Modules:
  0.0 564.5 jit_solution(318119338143368824)
XLA Ops:
  0.8 4.6 collective-permute-start.3
  12.2 4.1 collective-permute-start
  18.9 3.0 collective-permute-done.1
  25.3 3.1 collective-permute-start.5
  29.7 5.0 collective-permute-done.5.refs_1_
  47.7 5.1 collective-permute-done.12.refs_1_
  61.2 12.0 %collective-permute-done.17 = f32[3,12,768]{2,1,0:T(8,128)S(1)} collective-permute-done((f32[3,12,768]{2,1,0:T(8,128)S(1)}, f32[3,12,768]{2,1,0:T(8,128)S(1)}, u32[]{:S(2)}, u32[]{:S(2)}) %collective-permute-start.17) | collective-permute-done | bytes 110624 | tf_op jit(solution)/shard_map/ppermute | solution.py:1121
  83.0 5.0 collective-permute-done.23
  88.7 9.5 %collective-permute-done.22.refs_1_ = bf16[4,48,768]{2,1,0:T(8,128)(2,1)S(1)} collective-permute-done((bf16[4,48,768]{2,1,0:T(8,128)(2,1)S(1)}, bf16[4,48,768]{2,1,0:T(8,128)(2,1)S(1)}, u32[]{:S(2)}, u32[]{:S(2)}) %collective-permute-start.22) | collective-permute-done | bytes 294944 | tf_op jit(solution)/shard_map/ppermute | solution.py:1121
  98.2 2.9 collective-permute-done.21.refs_1_
  102.6 4.2 gather_round.14
  116.4 13.2 %attn_forward.3 = (f32[256,768]{1,0:T(8,128)S(1)}, f32[256,768]{1,0:T(8,128)S(1)}, f32[256,128]{1,0:T(8,128)S(1)}, bf16[256,768]{1,0:T(8,128)(2,1)S(1)}, bf16[76...) custom-call(s32[4]{0:T(128)S(1)} %pad_add_fusion.2.pos_ref.refs_0_.r, ...), custom_call_target="tpu_custom_call" | custom-call | flops 1 | bytes 1 | tf_op jit(solution)/shard_map/attn_forward/pallas_call | solution.py:265
  132.1 3.8 gather_round.15
  138.9 7.7 %inner_forward.3 = (bf16[256,3072]{1,0:T(8,128)(2,1)S(1)}, bf16[256,3072]{1,0:T(8,128)(2,1)S(1)}, bf16[2,2,2,4,48,256]{5,4,3,2,1,0:T(8,128)(2,1)S(1)}, bf16[2,2,2,4,48,256]{5,4,3,2,1,0:T(8,128)(2,1)S(1)}) custom-call(s32[4]{0:T(128)S(1)} %pad_add_fusion.2.pos_ref.refs_0_.refs_1_, s32[4]{0:T(128)S(1)} %pad_add_fusion.2.pos_ref.refs_0_.refs_1_, ...), custom_call_target="tpu_custom_call" | custom-call | flops 1 | bytes 1 | tf_op jit(solution)/shard_map/inner_forward/pallas_call | solution.py:348
  147.6 5.9 %collective-permute-done.31.refs_1_ = bf16[4,48,768]{2,1,0:T(8,128)(2,1)S(1)} collective-permute-done((bf16[4,48,768]{2,1,0:T(8,128)(2,1)S(1)}, bf16[4,48,768]{2,1,0:T(8,128)(2,1)S(1)}, u32[]{:S(2)}, u32[]{:S(2)}) %collective-permute-start.31) | collective-permute-done | bytes 294944 | tf_op jit(solution)/shard_map/ppermute | solution.py:1121
  155.5 3.5 collective-permute-done.28.refs_4_
  166.2 3.3 outer_forward.3
  171.3 8.2 %collective-permute-done.37.refs_1_ = bf16[8,48,768]{2,1,0:T(8,128)(2,1)S(1)} collective-permute-done((bf16[8,48,768]{2,1,0:T(8,128)(2,1)S(1)}, bf16[8,48,768]{2,1,0:T(8,128)(2,1)S(1)}, u32[]{:S(2)}, u32[]{:S(2)}) %collective-permute-start.37) | collective-permute-done | bytes 589856 | tf_op jit(solution)/shard_map/ppermute | solution.py:1121
  179.6 4.9 collective-permute-done.34.refs_4_
  189.7 2.6 collective-permute-start.42
  192.3 13.2 %attn_forward.4 = (f32[256,768]{1,0:T(8,128)S(1)}, f32[256,768]{1,0:T(8,128)S(1)}, f32[256,128]{1,0:T(8,128)S(1)}, bf16[256,768]{1,0:T(8,128)(2,1)S(1)}, bf16[76...) custom-call(s32[4]{0:T(128)S(1)} %pad_add_fusion.2.pos_ref.refs_0_.r, ...), custom_call_target="tpu_custom_call" | custom-call | flops 1 | bytes 1 | tf_op jit(solution)/shard_map/attn_forward/pallas_call | solution.py:265
  216.7 5.9 %inner_forward.4 = (bf16[256,3072]{1,0:T(8,128)(2,1)S(1)}, bf16[256,3072]{1,0:T(8,128)(2,1)S(1)}, bf16[2,2,2,4,48,256]{5,4,3,2,1,0:T(8,128)(2,1)S(1)}, bf16[2,2,2,4,48,256]{5,4,3,2,1,0:T(8,128)(2,1)S(1)}) custom-call(s32[4]{0:T(128)S(1)} %pad_add_fusion.2.pos_ref.refs_0_.refs_1_, s32[4]{0:T(128)S(1)} %pad_add_fusion.2.pos_ref.refs_0_.refs_1_, ...), custom_call_target="tpu_custom_call" | custom-call | flops 1 | bytes 1 | tf_op jit(solution)/shard_map/inner_forward/pallas_call | solution.py:348
  225.1 2.6 collective-permute-done.48.tb_ref.xb_ref
  229.4 8.0 %collective-permute-done.43.refs_4_ = bf16[12,48,768]{2,1,0:T(8,128)(2,1)S(1)} collective-permute-done((bf16[12,48,768]{2,1,0:T(8,128)(2,1)S(1)}, bf16[12,48,768]{2,1,0:T(8,128)(2,1)S(1)}, u32[]{:S(2)}, u32[]{:S(2)}) %collective-permute-start.43) | collective-permute-done | bytes 884768 | tf_op jit(solution)/shard_map/ppermute | solution.py:1121
  242.1 2.8 outer_forward.4
  246.7 15.2 %collective-permute-done.49.refs_2_ = bf16[12,48,768]{2,1,0:T(8,128)(2,1)S(1)} collective-permute-done((bf16[12,48,768]{2,1,0:T(8,128)(2,1)S(1)}, bf16[12,48,768]{2,1,0:T(8,128)(2,1)S(1)}, u32[]{:S(2)}, u32[]{:S(2)}) %collective-permute-start.49) | collective-permute-done | bytes 884768 | tf_op jit(solution)/shard_map/ppermute | solution.py:1121
  266.7 13.2 %attn_forward.5 = (f32[256,768]{1,0:T(8,128)S(1)}, f32[256,768]{1,0:T(8,128)S(1)}, f32[256,128]{1,0:T(8,128)S(1)}, bf16[256,768]{1,0:T(8,128)(2,1)S(1)}, bf16[76...) custom-call(s32[4]{0:T(128)S(1)} %pad_add_fusion.2.pos_ref.refs_0_.r, ...), custom_call_target="tpu_custom_call" | custom-call | flops 1 | bytes 1 | tf_op jit(solution)/shard_map/attn_forward/pallas_call | solution.py:265
  283.8 2.8 collective-permute-start.57
  286.6 5.9 %inner_forward.5 = (bf16[256,3072]{1,0:T(8,128)(2,1)S(1)}, bf16[256,3072]{1,0:T(8,128)(2,1)S(1)}, bf16[2,2,2,4,48,256]{5,4,3,2,1,0:T(8,128)(2,1)S(1)}, bf16[2,2,2,4,48,256]{5,4,3,2,1,0:T(8,128)(2,1)S(1)}) custom-call(s32[4]{0:T(128)S(1)} %pad_add_fusion.2.pos_ref.refs_0_.refs_1_, s32[4]{0:T(128)S(1)} %pad_add_fusion.2.pos_ref.refs_0_.refs_1_, ...), custom_call_target="tpu_custom_call" | custom-call | flops 1 | bytes 1 | tf_op jit(solution)/shard_map/inner_forward/pallas_call | solution.py:348
  294.4 2.8 collective-permute-done.59.tb_ref.xb_ref
  297.2 3.2 outer_forward.5
  309.8 7.9 %chain_backward.3 = (bf16[256,3840]{1,0:T(8,128)(2,1)S(1)}, f32[256,768]{1,0:T(8,128)S(1)}, bf16[256,768]{1,0:T(8,128)(2,1)S(1)}, f32[16,768]{1,0:T(8,128)S(1)}) custom-call(s32[4]{0:T(128)S(1)} %pad_add_fusion.2.pos_ref.refs_0_.refs_1_, bf16[256,768]{1,0:T(8,128)(2,1)S(1)} %get-tuple-element.976.da_ref.refs_1_, f32[256,768]{1,0:T(8,128)S(1)} %get-tuple-element.983.refs_2_, ...), custom_call_target="tpu_custom_call" | custom-call | flops 1 | bytes 1 | tf_op jit(solution)/shard_map/chain_backward/pallas_call | solution.py:470
  317.7 4.1 collective-permute-done.64.refs_0_
  326.2 7.8 %attn_backward.3 = (bf16[5,256,768]{2,1,0:T(8,128)(2,1)S(1)}, f32[8,768]{1,0:T(8,128)S(1)}) custom-call(bf16[256,768]{1,0:T(8,128)(2,1)S(1)} %get-tuple-element.999.refs_0_, bf16[768,512]{1,0:T(8,128)(2,1)S(1)} %copy-done.63, bf16[512,768]{1,0:T(8,128)(2,1)S(1)} %copy-done.65, bf16[12,512,256]{2,1,0:T(8,128)(2,1)S(1)} %copy-done.30, ...), custom_call_target="tpu_custom_call" | custom-call | flops 1 | bytes 1 | tf_op jit(solution)/shard_map/attn_backward/pallas_call | solution.py:543
  339.9 3.1 collective-permute-start.61
  345.5 2.6 collective-permute-start.72
  348.2 4.5 input_backward.3
  352.7 2.8 attn_grad.3
  356.7 2.9 collective-permute-start.75
  361.3 2.6 collective-permute-start.77
  363.9 7.7 %chain_backward.4 = (bf16[256,3840]{1,0:T(8,128)(2,1)S(1)}, f32[256,768]{1,0:T(8,128)S(1)}, bf16[256,768]{1,0:T(8,128)(2,1)S(1)}, f32[16,768]{1,0:T(8,128)S(1)}) custom-call(s32[4]{0:T(128)S(1)} %pad_add_fusion.2.pos_ref.refs_0_.refs_1_, bf16[256,768]{1,0:T(8,128)(2,1)S(1)} %get-tuple-element.1060.refs_1_.da_ref, ...), custom_call_target="tpu_custom_call" | custom-call | flops 1 | bytes 1 | tf_op jit(solution)/shard_map/chain_backward/pallas_call | solution.py:470
  373.2 3.4 collective-permute-done.75.refs_3_.refs_10_
  380.6 4.5 collective-permute-start.80
  386.8 2.6 collective-permute-start.82
  389.3 7.8 %attn_backward.4 = (bf16[5,256,768]{2,1,0:T(8,128)(2,1)S(1)}, f32[8,768]{1,0:T(8,128)S(1)}) custom-call(bf16[256,768]{1,0:T(8,128)(2,1)S(1)} %copy-done.93, bf16[768,512]{1,0:T(8,128)(2,1)S(1)} %copy-done.81, bf16[512,768]{1,0:T(8,128)(2,1)S(1)} %copy-done.83, bf16[12,512,256]{2,1,0:T(8,128)(2,1)S(1)} %copy-done.34, ...), custom_call_target="tpu_custom_call" | custom-call | flops 1 | bytes 1 | tf_op jit(solution)/shard_map/attn_backward/pallas_call | solution.py:543
  405.1 2.6 collective-permute-start.87
  407.7 4.0 input_backward.4
  411.7 2.8 attn_grad.4
  414.5 4.9 collective-permute-done.87.refs_10_
  421.6 3.1 collective-permute-done.84.refs_2_
  427.8 2.6 collective-permute-start.92
  430.4 9.3 %chain_backward.5 = (bf16[256,3840]{1,0:T(8,128)(2,1)S(1)}, f32[256,768]{1,0:T(8,128)S(1)}, bf16[256,768]{1,0:T(8,128)(2,1)S(1)}, f32[16,768]{1,0:T(8,128)S(1)}) custom-call(s32[4]{0:T(128)S(1)} %pad_add_fusion.2.pos_ref.refs_0_.refs_1_, bf16[256,768]{1,0:T(8,128)(2,1)S(1)} %get-tuple-element.1160.refs_1_.da_ref, ...), custom_call_target="tpu_custom_call" | custom-call | flops 1 | bytes 1 | tf_op jit(solution)/shard_map/chain_backward/pallas_call | solution.py:470
  452.4 7.8 %attn_backward.5 = (bf16[5,256,768]{2,1,0:T(8,128)(2,1)S(1)}, f32[8,768]{1,0:T(8,128)S(1)}) custom-call(bf16[256,768]{1,0:T(8,128)(2,1)S(1)} %copy-done.91, bf16[768,512]{1,0:T(8,128)(2,1)S(1)} %copy-done.77, bf16[512,768]{1,0:T(8,128)(2,1)S(1)} %copy-done.79, bf16[12,512,256]{2,1,0:T(8,128)(2,1)S(1)} %copy-done.32, ...), custom_call_target="tpu_custom_call" | custom-call | flops 1 | bytes 1 | tf_op jit(solution)/shard_map/attn_backward/pallas_call | solution.py:543
  475.1 4.0 input_backward.5
  479.1 2.8 attn_grad.5
  481.8 5.0 collective-permute-done.102.refs_10_
  498.0 10.8 %collective-permute-done.108.refs_8_ = bf16[3,48,768]{2,1,0:T(8,128)(2,1)S(1)} collective-permute-done((bf16[3,48,768]{2,1,0:T(8,128)(2,1)S(1)}, bf16[3,48,768]{2,1,0:T(8,128)(2,1)S(1)}, u32[]{:S(2)}, u32[]{:S(2)}) %collective-permute-start.108) | collective-permute-done | bytes 221216 | tf_op jit(solution)/shard_map/ppermute | solution.py:1121
  521.5 6.5 %collective-permute-done.113.refs_5_ = bf16[3,48,768]{2,1,0:T(8,128)(2,1)S(1)} collective-permute-done((bf16[3,48,768]{2,1,0:T(8,128)(2,1)S(1)}, bf16[3,48,768]{2,1,0:T(8,128)(2,1)S(1)}, u32[]{:S(2)}, u32[]{:S(2)}) %collective-permute-start.113) | collective-permute-done | bytes 221216 | tf_op jit(solution)/shard_map/ppermute | solution.py:1121
  536.0 2.8 collective-permute-done.115.refs_0_
  538.8 6.5 %collective-permute-done.116.refs_2_ = bf16[3,48,768]{2,1,0:T(8,128)(2,1)S(1)} collective-permute-done((bf16[3,48,768]{2,1,0:T(8,128)(2,1)S(1)}, bf16[3,48,768]{2,1,0:T(8,128)(2,1)S(1)}, u32[]{:S(2)}, u32[]{:S(2)}) %collective-permute-start.116) | collective-permute-done | bytes 221216 | tf_op jit(solution)/shard_map/ppermute | solution.py:1121
  545.6 2.8 finish.3.refs_3_
  548.4 3.2 collective-permute-done.118.refs_0_
  556.1 2.8 finish.5
  559.9 2.8 finish.4
  (530 shorter events, 223.4 us)
Async XLA Ops:
  0.8 21.8 %collective-permute-start.3 = (bf16[256,768]{1,0:T(8,128)(2,1)}, bf16[256,768]{1,0:T(8,128)(2,1)}, u32[]{:S(2)}, u32[]{:S(2)}) collective-permute-start(bf16[256,768]{1,0:T(8,128)(2,1)} %bitcast.52), channel_id=1, source_target_pairs={{0,0},{2,1},{1,2},{3,3},{4,4},{6,5},{5,6},{7,7},{8,8},{10,9},{9,10... | collective-permute-start | bytes 1179656 | tf_op jit(solution)/shard_map/ppermute | solution.py:1121
  37.1 15.8 %collective-permute-start.11 = (bf16[4,48,768]{2,1,0:T(8,128)(2,1)S(1)}, bf16[4,48,768]{2,1,0:T(8,128)(2,1)S(1)}, u32[]{:S(2)}, u32[]{:S(2)}) collective-permute-start(bf16[4,48,768]{2,1,0:T(8,128)(2,1)S(1)} %gather_z.8.refs_0_), channel_id=1, source_target_pairs={{8,0},{9,1},{10,2},{11,3},{12,4},{13,5},{14,6},{15,7},{0,8},{1,9},... | collective-permute-start | bytes 884744 | tf_op jit(solution)/shard_map/ppermute | solution.py:1121
  54.6 20.6 %collective-permute-start.13 = (bf16[12,48,768]{2,1,0:T(8,128)(2,1)S(1)}, bf16[12,48,768]{2,1,0:T(8,128)(2,1)S(1)}, u32[]{:S(2)}, u32[]{:S(2)}) collective-permute-start(bf16[12,48,768]{2,1,0:T(8,128)(2,1)S(1)} %get-tuple-element.718.refs_2_), channel_id=1, source_target_pairs={{4,0},{5,1},{6,2},{7,3},{0,4},{1,5},{2,6},{3,7},{12,8},{13,9},{14,... | collective-permute-start | bytes 2654216 | tf_op jit(solution)/shard_map/ppermute | solution.py:1121
  55.2 20.2 %collective-permute-start.14 = (bf16[12,48,768]{2,1,0:T(8,128)(2,1)S(1)}, bf16[12,48,768]{2,1,0:T(8,128)(2,1)S(1)}, u32[]{:S(2)}, u32[]{:S(2)}) collective-permute-start(bf16[12,48,768]{2,1,0:T(8,128)(2,1)S(1)} %get-tuple-element.719.refs_3_), channel_id=1, source_target_pairs={{1,0},{0,1},{3,2},{2,3},{5,4},{4,5},{7,6},{6,7},{9,8},{8,9},{11,10... | collective-permute-start | bytes 2654216 | tf_op jit(solution)/shard_map/ppermute | solution.py:1121
  57.5 15.7 %collective-permute-start.15 = (bf16[4,48,768]{2,1,0:T(8,128)(2,1)S(1)}, bf16[4,48,768]{2,1,0:T(8,128)(2,1)S(1)}, u32[]{:S(2)}, u32[]{:S(2)}) collective-permute-start(bf16[4,48,768]{2,1,0:T(8,128)(2,1)S(1)} %gather_z.9.refs_0_), channel_id=1, source_target_pairs={{8,0},{9,1},{10,2},{11,3},{12,4},{13,5},{14,6},{15,7},{0,8},{1,9},... | collective-permute-start | bytes 884744 | tf_op jit(solution)/shard_map/ppermute | solution.py:1121
  77.6 23.5 %collective-permute-start.20 = (bf16[32,48,768]{2,1,0:T(8,128)(2,1)S(1)}, bf16[32,48,768]{2,1,0:T(8,128)(2,1)S(1)}, u32[]{:S(2)}, u32[]{:S(2)}) collective-permute-start(bf16[32,48,768]{2,1,0:T(8,128)(2,1)S(1)} %get-tuple-element.765.refs_7_.refs_11_.refs_4_), channel_id=1, source_target_pairs={{2,0},{3,1},{0,2},{1,3},{6,4},{7,5},{4,6},{5,7},{10,8},{11,9},{8,1... | collective-permute-start | bytes 7077896 | tf_op jit(solution)/shard_map/ppermute | solution.py:1121
  77.7 23.4 %collective-permute-start.18 = (bf16[12,48,768]{2,1,0:T(8,128)(2,1)S(1)}, bf16[12,48,768]{2,1,0:T(8,128)(2,1)S(1)}, u32[]{:S(2)}, u32[]{:S(2)}) collective-permute-start(bf16[12,48,768]{2,1,0:T(8,128)(2,1)S(1)} %get-tuple-element.736.refs_2_), channel_id=1, source_target_pairs={{4,0},{5,1},{6,2},{7,3},{0,4},{1,5},{2,6},{3,7},{12,8},{13,9},{14,... | collective-permute-start | bytes 2654216 | tf_op jit(solution)/shard_map/ppermute | solution.py:1121
  79.4 21.7 %collective-permute-start.19 = (bf16[12,48,768]{2,1,0:T(8,128)(2,1)S(1)}, bf16[12,48,768]{2,1,0:T(8,128)(2,1)S(1)}, u32[]{:S(2)}, u32[]{:S(2)}) collective-permute-start(bf16[12,48,768]{2,1,0:T(8,128)(2,1)S(1)} %get-tuple-element.737.refs_3_), channel_id=1, source_target_pairs={{1,0},{0,1},{3,2},{2,3},{5,4},{4,5},{7,6},{6,7},{9,8},{8,9},{11,10... | collective-permute-start | bytes 2654216 | tf_op jit(solution)/shard_map/ppermute | solution.py:1121
  82.0 16.2 %collective-permute-start.22 = (bf16[4,48,768]{2,1,0:T(8,128)(2,1)S(1)}, bf16[4,48,768]{2,1,0:T(8,128)(2,1)S(1)}, u32[]{:S(2)}, u32[]{:S(2)}) collective-permute-start(bf16[4,48,768]{2,1,0:T(8,128)(2,1)S(1)} %pack.11.refs_0_), channel_id=1, source_target_pairs={{16,0},{17,1},{18,2},{19,3},{20,4},{21,5},{22,6},{23,7},{24,8},{25... | collective-permute-start | bytes 884744 | tf_op jit(solution)/shard_map/ppermute | solution.py:1121
  106.8 25.3 %collective-permute-start.26 = (bf16[32,48,768]{2,1,0:T(8,128)(2,1)}, bf16[32,48,768]{2,1,0:T(8,128)(2,1)}, u32[]{:S(2)}, u32[]{:S(2)}) collective-permute-start(bf16[32,48,768]{2,1,0:T(8,128)(2,1)} %get-tuple-element.807.refs_4_.refs_7_), channel_id=1, source_target_pairs={{2,0},{3,1},{0,2},{1,3},{6,4},{7,5},{4,6},{5,7},{10,8},{11,9},{8,1... | collective-permute-start | bytes 7077896 | tf_op jit(solution)/shard_map/ppermute | solution.py:1121
  106.9 25.2 %collective-permute-start.24 = (bf16[12,48,768]{2,1,0:T(8,128)(2,1)}, bf16[12,48,768]{2,1,0:T(8,128)(2,1)}, u32[]{:S(2)}, u32[]{:S(2)}) collective-permute-start(bf16[12,48,768]{2,1,0:T(8,128)(2,1)} %get-tuple-element.755.refs_2_), channel_id=1, source_target_pairs={{4,0},{5,1},{6,2},{7,3},{0,4},{1,5},{2,6},{3,7},{12,8},{13,9},{14,... | collective-permute-start | bytes 2654216 | tf_op jit(solution)/shard_map/ppermute | solution.py:1121
  107.3 24.8 %collective-permute-start.25 = (bf16[12,48,768]{2,1,0:T(8,128)(2,1)}, bf16[12,48,768]{2,1,0:T(8,128)(2,1)}, u32[]{:S(2)}, u32[]{:S(2)}) collective-permute-start(bf16[12,48,768]{2,1,0:T(8,128)(2,1)} %get-tuple-element.756.refs_3_), channel_id=1, source_target_pairs={{1,0},{0,1},{3,2},{2,3},{5,4},{4,5},{7,6},{6,7},{9,8},{8,9},{11,10... | collective-permute-start | bytes 2654216 | tf_op jit(solution)/shard_map/ppermute | solution.py:1121
  109.8 22.4 %collective-permute-start.27 = (bf16[8,48,768]{2,1,0:T(8,128)(2,1)S(1)}, bf16[8,48,768]{2,1,0:T(8,128)(2,1)}, u32[]{:S(2)}, u32[]{:S(2)}) collective-permute-start(bf16[8,48,768]{2,1,0:T(8,128)(2,1)S(1)} %gather_z.11.refs_0_), channel_id=1, source_target_pairs={{8,0},{9,1},{10,2},{11,3},{12,4},{13,5},{14,6},{15,7},{0,8},{1,9},... | collective-permute-start | bytes 1769480 | tf_op jit(solution)/shard_map/ppermute | solution.py:1121
  136.0 24.3 %collective-permute-start.30 = (bf16[32,48,768]{2,1,0:T(8,128)(2,1)S(1)}, bf16[32,48,768]{2,1,0:T(8,128)(2,1)S(1)}, u32[]{:S(2)}, u32[]{:S(2)}) collective-permute-start(bf16[32,48,768]{2,1,0:T(8,128)(2,1)S(1)} %get-tuple-element.825.refs_4_.refs_9_), channel_id=1, source_target_pairs={{2,0},{3,1},{0,2},{1,3},{6,4},{7,5},{4,6},{5,7},{10,8},{11,9},{8,1... | collective-permute-start | bytes 7077896 | tf_op jit(solution)/shard_map/ppermute | solution.py:1121
  136.7 16.7 %collective-permute-start.31 = (bf16[4,48,768]{2,1,0:T(8,128)(2,1)S(1)}, bf16[4,48,768]{2,1,0:T(8,128)(2,1)S(1)}, u32[]{:S(2)}, u32[]{:S(2)}) collective-permute-start(bf16[4,48,768]{2,1,0:T(8,128)(2,1)S(1)} %pack.12.refs_0_), channel_id=1, source_target_pairs={{16,0},{17,1},{18,2},{19,3},{20,4},{21,5},{22,6},{23,7},{24,8},{25... | collective-permute-start | bytes 884744 | tf_op jit(solution)/shard_map/ppermute | solution.py:1121
  136.8 22.1 %collective-permute-start.28 = (bf16[12,48,768]{2,1,0:T(8,128)(2,1)S(1)}, bf16[12,48,768]{2,1,0:T(8,128)(2,1)S(1)}, u32[]{:S(2)}, u32[]{:S(2)}) collective-permute-start(bf16[12,48,768]{2,1,0:T(8,128)(2,1)S(1)} %get-tuple-element.787.refs_2_), channel_id=1, source_target_pairs={{4,0},{5,1},{6,2},{7,3},{0,4},{1,5},{2,6},{3,7},{12,8},{13,9},{14,... | collective-permute-start | bytes 2654216 | tf_op jit(solution)/shard_map/ppermute | solution.py:1121
  138.6 21.8 %collective-permute-start.29 = (bf16[12,48,768]{2,1,0:T(8,128)(2,1)S(1)}, bf16[12,48,768]{2,1,0:T(8,128)(2,1)S(1)}, u32[]{:S(2)}, u32[]{:S(2)}) collective-permute-start(bf16[12,48,768]{2,1,0:T(8,128)(2,1)S(1)} %get-tuple-element.788.refs_3_), channel_id=1, source_target_pairs={{1,0},{0,1},{3,2},{2,3},{5,4},{4,5},{7,6},{6,7},{9,8},{8,9},{11,10... | collective-permute-start | bytes 2654216 | tf_op jit(solution)/shard_map/ppermute | solution.py:1121
  162.4 22.2 %collective-permute-start.36 = (bf16[32,48,768]{2,1,0:T(8,128)(2,1)S(1)}, bf16[32,48,768]{2,1,0:T(8,128)(2,1)S(1)}, u32[]{:S(2)}, u32[]{:S(2)}) collective-permute-start(bf16[32,48,768]{2,1,0:T(8,128)(2,1)S(1)} %get-tuple-element.863.refs_7_.refs_11_.refs_4_), channel_id=1, source_target_pairs={{2,0},{3,1},{0,2},{1,3},{6,4},{7,5},{4,6},{5,7},{10,8},{11,9},{8,1... | collective-permute-start | bytes 7077896 | tf_op jit(solution)/shard_map/ppermute | solution.py:1121
  162.5 22.1 %collective-permute-start.34 = (bf16[12,48,768]{2,1,0:T(8,128)(2,1)S(1)}, bf16[12,48,768]{2,1,0:T(8,128)(2,1)S(1)}, u32[]{:S(2)}, u32[]{:S(2)}) collective-permute-start(bf16[12,48,768]{2,1,0:T(8,128)(2,1)S(1)} %get-tuple-element.817.refs_2_), channel_id=1, source_target_pairs={{4,0},{5,1},{6,2},{7,3},{0,4},{1,5},{2,6},{3,7},{12,8},{13,9},{14,... | collective-permute-start | bytes 2654216 | tf_op jit(solution)/shard_map/ppermute | solution.py:1121
  162.9 21.7 %collective-permute-start.35 = (bf16[12,48,768]{2,1,0:T(8,128)(2,1)S(1)}, bf16[12,48,768]{2,1,0:T(8,128)(2,1)S(1)}, u32[]{:S(2)}, u32[]{:S(2)}) collective-permute-start(bf16[12,48,768]{2,1,0:T(8,128)(2,1)S(1)} %get-tuple-element.818.refs_3_), channel_id=1, source_target_pairs={{1,0},{0,1},{3,2},{2,3},{5,4},{4,5},{7,6},{6,7},{9,8},{8,9},{11,10... | collective-permute-start | bytes 2654216 | tf_op jit(solution)/shard_map/ppermute | solution.py:1121
  164.2 15.4 %collective-permute-start.37 = (bf16[8,48,768]{2,1,0:T(8,128)(2,1)S(1)}, bf16[8,48,768]{2,1,0:T(8,128)(2,1)S(1)}, u32[]{:S(2)}, u32[]{:S(2)}) collective-permute-start(bf16[8,48,768]{2,1,0:T(8,128)(2,1)S(1)} %gather_z.12.refs_0_), channel_id=1, source_target_pairs={{8,0},{9,1},{10,2},{11,3},{12,4},{13,5},{14,6},{15,7},{0,8},{1,9},... | collective-permute-start | bytes 1769480 | tf_op jit(solution)/shard_map/ppermute | solution.py:1121
  186.8 23.5 %collective-permute-start.41 = (bf16[32,48,768]{2,1,0:T(8,128)(2,1)S(1)}, bf16[32,48,768]{2,1,0:T(8,128)(2,1)S(1)}, u32[]{:S(2)}, u32[]{:S(2)}) collective-permute-start(bf16[32,48,768]{2,1,0:T(8,128)(2,1)S(1)} %get-tuple-element.895.refs_4_.refs_7_), channel_id=1, source_target_pairs={{2,0},{3,1},{0,2},{1,3},{6,4},{7,5},{4,6},{5,7},{10,8},{11,9},{8,1... | collective-permute-start | bytes 7077896 | tf_op jit(solution)/shard_map/ppermute | solution.py:1121
  186.9 22.2 %collective-permute-start.39 = (bf16[12,48,768]{2,1,0:T(8,128)(2,1)S(1)}, bf16[12,48,768]{2,1,0:T(8,128)(2,1)S(1)}, u32[]{:S(2)}, u32[]{:S(2)}) collective-permute-start(bf16[12,48,768]{2,1,0:T(8,128)(2,1)S(1)} %get-tuple-element.851.refs_2_), channel_id=1, source_target_pairs={{4,0},{5,1},{6,2},{7,3},{0,4},{1,5},{2,6},{3,7},{12,8},{13,9},{14,... | collective-permute-start | bytes 2654216 | tf_op jit(solution)/shard_map/ppermute | solution.py:1121
  188.7 21.7 %collective-permute-start.40 = (bf16[12,48,768]{2,1,0:T(8,128)(2,1)S(1)}, bf16[12,48,768]{2,1,0:T(8,128)(2,1)S(1)}, u32[]{:S(2)}, u32[]{:S(2)}) collective-permute-start(bf16[12,48,768]{2,1,0:T(8,128)(2,1)S(1)} %get-tuple-element.852.refs_3_), channel_id=1, source_target_pairs={{1,0},{0,1},{3,2},{2,3},{5,4},{4,5},{7,6},{6,7},{9,8},{8,9},{11,10... | collective-permute-start | bytes 2654216 | tf_op jit(solution)/shard_map/ppermute | solution.py:1121
  189.7 19.4 %collective-permute-start.42 = (bf16[2,48,768]{2,1,0:T(8,128)(2,1)S(1)}, bf16[2,48,768]{2,1,0:T(8,128)(2,1)S(1)}, u32[]{:S(2)}, u32[]{:S(2)}) collective-permute-start(bf16[2,48,768]{2,1,0:T(8,128)(2,1)S(1)} %pack.13.refs_0_), channel_id=1, source_target_pairs={{16,0},{17,1},{18,2},{19,3},{20,4},{21,5},{22,6},{23,7},{24,8},{25... | collective-permute-start | bytes 442376 | tf_op jit(solution)/shard_map/ppermute | solution.py:1121
  212.6 24.9 %collective-permute-start.45 = (bf16[32,48,768]{2,1,0:T(8,128)(2,1)S(1)}, bf16[32,48,768]{2,1,0:T(8,128)(2,1)S(1)}, u32[]{:S(2)}, u32[]{:S(2)}) collective-permute-start(bf16[32,48,768]{2,1,0:T(8,128)(2,1)S(1)} %get-tuple-element.911.refs_4_.refs_9_), channel_id=1, source_target_pairs={{2,0},{3,1},{0,2},{1,3},{6,4},{7,5},{4,6},{5,7},{10,8},{11,9},{8,1... | collective-permute-start | bytes 7077896 | tf_op jit(solution)/shard_map/ppermute | solution.py:1121
  215.7 21.8 %collective-permute-start.43 = (bf16[12,48,768]{2,1,0:T(8,128)(2,1)S(1)}, bf16[12,48,768]{2,1,0:T(8,128)(2,1)S(1)}, u32[]{:S(2)}, u32[]{:S(2)}) collective-permute-start(bf16[12,48,768]{2,1,0:T(8,128)(2,1)S(1)} %get-tuple-element.879.refs_2_), channel_id=1, source_target_pairs={{4,0},{5,1},{6,2},{7,3},{0,4},{1,5},{2,6},{3,7},{12,8},{13,9},{14,... | collective-permute-start | bytes 2654216 | tf_op jit(solution)/shard_map/ppermute | solution.py:1121
  216.1 21.5 %collective-permute-start.44 = (bf16[12,48,768]{2,1,0:T(8,128)(2,1)S(1)}, bf16[12,48,768]{2,1,0:T(8,128)(2,1)S(1)}, u32[]{:S(2)}, u32[]{:S(2)}) collective-permute-start(bf16[12,48,768]{2,1,0:T(8,128)(2,1)S(1)} %get-tuple-element.880.refs_3_), channel_id=1, source_target_pairs={{1,0},{0,1},{3,2},{2,3},{5,4},{4,5},{7,6},{6,7},{9,8},{8,9},{11,10... | collective-permute-start | bytes 2654216 | tf_op jit(solution)/shard_map/ppermute | solution.py:1121
  239.8 23.5 %collective-permute-start.51 = (bf16[32,48,768]{2,1,0:T(8,128)(2,1)S(1)}, bf16[32,48,768]{2,1,0:T(8,128)(2,1)S(1)}, u32[]{:S(2)}, u32[]{:S(2)}) collective-permute-start(bf16[32,48,768]{2,1,0:T(8,128)(2,1)S(1)} %get-tuple-element.935.refs_7_.refs_11_.refs_4_), channel_id=1, source_target_pairs={{2,0},{3,1},{0,2},{1,3},{6,4},{7,5},{4,6},{5,7},{10,8},{11,9},{8,1... | collective-permute-start | bytes 7077896 | tf_op jit(solution)/shard_map/ppermute | solution.py:1121
  239.8 22.1 %collective-permute-start.49 = (bf16[12,48,768]{2,1,0:T(8,128)(2,1)S(1)}, bf16[12,48,768]{2,1,0:T(8,128)(2,1)S(1)}, u32[]{:S(2)}, u32[]{:S(2)}) collective-permute-start(bf16[12,48,768]{2,1,0:T(8,128)(2,1)S(1)} %get-tuple-element.905.refs_0_), channel_id=1, source_target_pairs={{4,0},{5,1},{6,2},{7,3},{0,4},{1,5},{2,6},{3,7},{12,8},{13,9},{14,... | collective-permute-start | bytes 2654216 | tf_op jit(solution)/shard_map/ppermute | solution.py:1121
  241.6 21.7 %collective-permute-start.50 = (bf16[12,48,768]{2,1,0:T(8,128)(2,1)S(1)}, bf16[12,48,768]{2,1,0:T(8,128)(2,1)S(1)}, u32[]{:S(2)}, u32[]{:S(2)}) collective-permute-start(bf16[12,48,768]{2,1,0:T(8,128)(2,1)S(1)} %get-tuple-element.906.refs_1_), channel_id=1, source_target_pairs={{1,0},{0,1},{3,2},{2,3},{5,4},{4,5},{7,6},{6,7},{9,8},{8,9},{11,10... | collective-permute-start | bytes 2654216 | tf_op jit(solution)/shard_map/ppermute | solution.py:1121
  264.7 17.8 %collective-permute-start.55 = (bf16[32,48,768]{2,1,0:T(8,128)(2,1)S(1)}, bf16[32,48,768]{2,1,0:T(8,128)(2,1)S(1)}, u32[]{:S(2)}, u32[]{:S(2)}) collective-permute-start(bf16[32,48,768]{2,1,0:T(8,128)(2,1)S(1)} %get-tuple-element.960.refs_4_.refs_7_), channel_id=1, source_target_pairs={{2,0},{3,1},{0,2},{1,3},{6,4},{7,5},{4,6},{5,7},{10,8},{11,9},{8,1... | collective-permute-start | bytes 7077896 | tf_op jit(solution)/shard_map/ppermute | solution.py:1121
  264.7 17.7 %collective-permute-start.53 = (bf16[8,48,768]{2,1,0:T(8,128)(2,1)S(1)}, bf16[8,48,768]{2,1,0:T(8,128)(2,1)S(1)}, u32[]{:S(2)}, u32[]{:S(2)}) collective-permute-start(bf16[8,48,768]{2,1,0:T(8,128)(2,1)S(1)} %get-tuple-element.929.refs_0_), channel_id=1, source_target_pairs={{4,0},{5,1},{6,2},{7,3},{0,4},{1,5},{2,6},{3,7},{12,8},{13,9},{14,... | collective-permute-start | bytes 1769480 | tf_op jit(solution)/shard_map/ppermute | solution.py:1121
  265.2 17.3 %collective-permute-start.54 = (bf16[8,48,768]{2,1,0:T(8,128)(2,1)S(1)}, bf16[8,48,768]{2,1,0:T(8,128)(2,1)S(1)}, u32[]{:S(2)}, u32[]{:S(2)}) collective-permute-start(bf16[8,48,768]{2,1,0:T(8,128)(2,1)S(1)} %get-tuple-element.930.refs_1_), channel_id=1, source_target_pairs={{1,0},{0,1},{3,2},{2,3},{5,4},{4,5},{7,6},{6,7},{9,8},{8,9},{11,10... | collective-permute-start | bytes 1769480 | tf_op jit(solution)/shard_map/ppermute | solution.py:1121
  265.8 16.7 %collective-permute-start.56 = (bf16[256,768]{1,0:T(8,128)(2,1)S(1)}, bf16[256,768]{1,0:T(8,128)(2,1)S(1)}, u32[]{:S(2)}, u32[]{:S(2)}) collective-permute-start(bf16[256,768]{1,0:T(8,128)(2,1)S(1)} %bitcast.53), channel_id=1, source_target_pairs={{0,0},{2,1},{1,2},{3,3},{4,4},{6,5},{5,6},{7,7},{8,8},{10,9},{9,10... | collective-permute-start | bytes 1179656 | tf_op jit(solution)/shard_map/ppermute | solution.py:1121
  306.1 15.7 %collective-permute-start.64 = (bf16[8,48,768]{2,1,0:T(8,128)(2,1)S(1)}, bf16[8,48,768]{2,1,0:T(8,128)(2,1)S(1)}, u32[]{:S(2)}, u32[]{:S(2)}) collective-permute-start(bf16[8,48,768]{2,1,0:T(8,128)(2,1)S(1)} %get-tuple-element.981.refs_13_), channel_id=1, source_target_pairs={{4,0},{5,1},{6,2},{7,3},{0,4},{1,5},{2,6},{3,7},{12,8},{13,9},{14,... | collective-permute-start | bytes 1769480 | tf_op jit(solution)/shard_map/ppermute | solution.py:1121
  307.9 15.3 %collective-permute-start.65 = (bf16[8,48,768]{2,1,0:T(8,128)(2,1)S(1)}, bf16[8,48,768]{2,1,0:T(8,128)(2,1)S(1)}, u32[]{:S(2)}, u32[]{:S(2)}) collective-permute-start(bf16[8,48,768]{2,1,0:T(8,128)(2,1)S(1)} %get-tuple-element.982.refs_14_), channel_id=1, source_target_pairs={{1,0},{0,1},{3,2},{2,3},{5,4},{4,5},{7,6},{6,7},{9,8},{8,9},{11,10... | collective-permute-start | bytes 1769480 | tf_op jit(solution)/shard_map/ppermute | solution.py:1121
  336.8 18.7 %collective-permute-start.69 = (bf16[8,48,768]{2,1,0:T(8,128)(2,1)S(1)}, bf16[8,48,768]{2,1,0:T(8,128)(2,1)S(1)}, u32[]{:S(2)}, u32[]{:S(2)}) collective-permute-start(bf16[8,48,768]{2,1,0:T(8,128)(2,1)S(1)} %get-tuple-element.1022), channel_id=1, source_target_pairs={{4,0},{5,1},{6,2},{7,3},{0,4},{1,5},{2,6},{3,7},{12,8},{13,9},{14,... | collective-permute-start | bytes 1769480 | tf_op jit(solution)/shard_map/ppermute | solution.py:1121
  338.6 17.0 %collective-permute-start.70 = (bf16[8,48,768]{2,1,0:T(8,128)(2,1)S(1)}, bf16[8,48,768]{2,1,0:T(8,128)(2,1)S(1)}, u32[]{:S(2)}, u32[]{:S(2)}) collective-permute-start(bf16[8,48,768]{2,1,0:T(8,128)(2,1)S(1)} %get-tuple-element.1023), channel_id=1, source_target_pairs={{1,0},{0,1},{3,2},{2,3},{5,4},{4,5},{7,6},{6,7},{9,8},{8,9},{11,10... | collective-permute-start | bytes 1769480 | tf_op jit(solution)/shard_map/ppermute | solution.py:1121
  338.8 16.7 %collective-permute-start.60 = (bf16[256,768]{1,0:T(8,128)(2,1)S(1)}, bf16[256,768]{1,0:T(8,128)(2,1)S(1)}, u32[]{:S(2)}, u32[]{:S(2)}) collective-permute-start(bf16[256,768]{1,0:T(8,128)(2,1)S(1)} %copy-done.122), channel_id=1, source_target_pairs={{0,0},{2,1},{1,2},{3,3},{4,4},{6,5},{5,6},{7,7},{8,8},{10,9},{9,10... | collective-permute-start | bytes 1179656 | tf_op jit(solution)/shard_map/ppermute | solution.py:1121
  356.3 20.9 %collective-permute-start.74 = (bf16[12,48,768]{2,1,0:T(8,128)(2,1)S(1)}, bf16[12,48,768]{2,1,0:T(8,128)(2,1)S(1)}, u32[]{:S(2)}, u32[]{:S(2)}) collective-permute-start(bf16[12,48,768]{2,1,0:T(8,128)(2,1)S(1)} %get-tuple-element.1054), channel_id=1, source_target_pairs={{4,0},{5,1},{6,2},{7,3},{0,4},{1,5},{2,6},{3,7},{12,8},{13,9},{14,... | collective-permute-start | bytes 2654216 | tf_op jit(solution)/shard_map/ppermute | solution.py:1121
  356.7 20.0 %collective-permute-start.75 = (bf16[10,48,768]{2,1,0:T(8,128)(2,1)S(1)}, bf16[10,48,768]{2,1,0:T(8,128)(2,1)S(1)}, u32[]{:S(2)}, u32[]{:S(2)}) collective-permute-start(bf16[10,48,768]{2,1,0:T(8,128)(2,1)S(1)} %get-tuple-element.1055), channel_id=1, source_target_pairs={{1,0},{0,1},{3,2},{2,3},{5,4},{4,5},{7,6},{6,7},{9,8},{8,9},{11,10... | collective-permute-start | bytes 2211848 | tf_op jit(solution)/shard_map/ppermute | solution.py:1121
  377.2 19.9 %collective-permute-start.83 = (bf16[256,3840]{1,0:T(8,128)(2,1)S(1)}, bf16[256,3840]{1,0:T(8,128)(2,1)S(1)}, u32[]{:S(2)}, u32[]{:S(2)}) collective-permute-start(bf16[256,3840]{1,0:T(8,128)(2,1)S(1)} %get-tuple-element.1094.da_ref), channel_id=1, source_target_pairs={{2,0},{3,1},{0,2},{1,3},{6,4},{7,5},{4,6},{5,7},{10,8},{11,9},{8,1... | collective-permute-start | bytes 5898248 | tf_op jit(solution)/shard_map/ppermute | solution.py:1121
  380.1 20.1 %collective-permute-start.79 = (bf16[12,48,768]{2,1,0:T(8,128)(2,1)S(1)}, bf16[12,48,768]{2,1,0:T(8,128)(2,1)S(1)}, u32[]{:S(2)}, u32[]{:S(2)}) collective-permute-start(bf16[12,48,768]{2,1,0:T(8,128)(2,1)S(1)} %get-tuple-element.1084), channel_id=1, source_target_pairs={{4,0},{5,1},{6,2},{7,3},{0,4},{1,5},{2,6},{3,7},{12,8},{13,9},{14,... | collective-permute-start | bytes 2654216 | tf_op jit(solution)/shard_map/ppermute | solution.py:1121
  380.6 19.6 %collective-permute-start.80 = (bf16[9,48,768]{2,1,0:T(8,128)(2,1)S(1)}, bf16[9,48,768]{2,1,0:T(8,128)(2,1)S(1)}, u32[]{:S(2)}, u32[]{:S(2)}) collective-permute-start(bf16[9,48,768]{2,1,0:T(8,128)(2,1)S(1)} %get-tuple-element.1085), channel_id=1, source_target_pairs={{1,0},{0,1},{3,2},{2,3},{5,4},{4,5},{7,6},{6,7},{9,8},{8,9},{11,10... | collective-permute-start | bytes 1990664 | tf_op jit(solution)/shard_map/ppermute | solution.py:1121
  385.1 15.1 %collective-permute-start.81 = (bf16[6,48,768]{2,1,0:T(8,128)(2,1)S(1)}, bf16[6,48,768]{2,1,0:T(8,128)(2,1)S(1)}, u32[]{:S(2)}, u32[]{:S(2)}) collective-permute-start(bf16[6,48,768]{2,1,0:T(8,128)(2,1)S(1)} %get-tuple-element.1086), channel_id=1, source_target_pairs={{8,0},{9,1},{10,2},{11,3},{12,4},{13,5},{14,6},{15,7},{0,8},{1,9},... | collective-permute-start | bytes 1327112 | tf_op jit(solution)/shard_map/ppermute | solution.py:1121
  403.1 21.6 %collective-permute-start.84 = (bf16[12,48,768]{2,1,0:T(8,128)(2,1)S(1)}, bf16[12,48,768]{2,1,0:T(8,128)(2,1)S(1)}, u32[]{:S(2)}, u32[]{:S(2)}) collective-permute-start(bf16[12,48,768]{2,1,0:T(8,128)(2,1)S(1)} %get-tuple-element.1115), channel_id=1, source_target_pairs={{4,0},{5,1},{6,2},{7,3},{0,4},{1,5},{2,6},{3,7},{12,8},{13,9},{14,... | collective-permute-start | bytes 2654216 | tf_op jit(solution)/shard_map/ppermute | solution.py:1121
  403.5 18.1 %collective-permute-start.85 = (bf16[10,48,768]{2,1,0:T(8,128)(2,1)S(1)}, bf16[10,48,768]{2,1,0:T(8,128)(2,1)S(1)}, u32[]{:S(2)}, u32[]{:S(2)}) collective-permute-start(bf16[10,48,768]{2,1,0:T(8,128)(2,1)S(1)} %get-tuple-element.1116), channel_id=1, source_target_pairs={{1,0},{0,1},{3,2},{2,3},{5,4},{4,5},{7,6},{6,7},{9,8},{8,9},{11,10... | collective-permute-start | bytes 2211848 | tf_op jit(solution)/shard_map/ppermute | solution.py:1121
  404.3 16.7 %collective-permute-start.86 = (bf16[6,48,768]{2,1,0:T(8,128)(2,1)S(1)}, bf16[6,48,768]{2,1,0:T(8,128)(2,1)S(1)}, u32[]{:S(2)}, u32[]{:S(2)}) collective-permute-start(bf16[6,48,768]{2,1,0:T(8,128)(2,1)S(1)} %get-tuple-element.1117), channel_id=1, source_target_pairs={{8,0},{9,1},{10,2},{11,3},{12,4},{13,5},{14,6},{15,7},{0,8},{1,9},... | collective-permute-start | bytes 1327112 | tf_op jit(solution)/shard_map/ppermute | solution.py:1121
  425.3 20.8 %collective-permute-start.89 = (bf16[12,48,768]{2,1,0:T(8,128)(2,1)S(1)}, bf16[12,48,768]{2,1,0:T(8,128)(2,1)S(1)}, u32[]{:S(2)}, u32[]{:S(2)}) collective-permute-start(bf16[12,48,768]{2,1,0:T(8,128)(2,1)S(1)} %get-tuple-element.1153), channel_id=1, source_target_pairs={{4,0},{5,1},{6,2},{7,3},{0,4},{1,5},{2,6},{3,7},{12,8},{13,9},{14,... | collective-permute-start | bytes 2654216 | tf_op jit(solution)/shard_map/ppermute | solution.py:1121
  425.7 18.9 %collective-permute-start.90 = (bf16[11,48,768]{2,1,0:T(8,128)(2,1)S(1)}, bf16[11,48,768]{2,1,0:T(8,128)(2,1)S(1)}, u32[]{:S(2)}, u32[]{:S(2)}) collective-permute-start(bf16[11,48,768]{2,1,0:T(8,128)(2,1)S(1)} %get-tuple-element.1154), channel_id=1, source_target_pairs={{1,0},{0,1},{3,2},{2,3},{5,4},{4,5},{7,6},{6,7},{9,8},{8,9},{11,10... | collective-permute-start | bytes 2433032 | tf_op jit(solution)/shard_map/ppermute | solution.py:1121
  427.0 16.0 %collective-permute-start.91 = (bf16[6,48,768]{2,1,0:T(8,128)(2,1)S(1)}, bf16[6,48,768]{2,1,0:T(8,128)(2,1)S(1)}, u32[]{:S(2)}, u32[]{:S(2)}) collective-permute-start(bf16[6,48,768]{2,1,0:T(8,128)(2,1)S(1)} %get-tuple-element.1155), channel_id=1, source_target_pairs={{8,0},{9,1},{10,2},{11,3},{12,4},{13,5},{14,6},{15,7},{0,8},{1,9},... | collective-permute-start | bytes 1327112 | tf_op jit(solution)/shard_map/ppermute | solution.py:1121
  446.7 22.1 %collective-permute-start.94 = (bf16[12,48,768]{2,1,0:T(8,128)(2,1)S(1)}, bf16[12,48,768]{2,1,0:T(8,128)(2,1)S(1)}, u32[]{:S(2)}, u32[]{:S(2)}) collective-permute-start(bf16[12,48,768]{2,1,0:T(8,128)(2,1)S(1)} %get-tuple-element.1187), channel_id=1, source_target_pairs={{4,0},{5,1},{6,2},{7,3},{0,4},{1,5},{2,6},{3,7},{12,8},{13,9},{14,... | collective-permute-start | bytes 2654216 | tf_op jit(solution)/shard_map/ppermute | solution.py:1121
  447.2 20.3 %collective-permute-start.95 = (bf16[11,48,768]{2,1,0:T(8,128)(2,1)S(1)}, bf16[11,48,768]{2,1,0:T(8,128)(2,1)S(1)}, u32[]{:S(2)}, u32[]{:S(2)}) collective-permute-start(bf16[11,48,768]{2,1,0:T(8,128)(2,1)S(1)} %get-tuple-element.1188), channel_id=1, source_target_pairs={{1,0},{0,1},{3,2},{2,3},{5,4},{4,5},{7,6},{6,7},{9,8},{8,9},{11,10... | collective-permute-start | bytes 2433032 | tf_op jit(solution)/shard_map/ppermute | solution.py:1121
  449.0 16.7 %collective-permute-start.96 = (bf16[6,48,768]{2,1,0:T(8,128)(2,1)S(1)}, bf16[6,48,768]{2,1,0:T(8,128)(2,1)S(1)}, u32[]{:S(2)}, u32[]{:S(2)}) collective-permute-start(bf16[6,48,768]{2,1,0:T(8,128)(2,1)S(1)} %get-tuple-element.1189), channel_id=1, source_target_pairs={{8,0},{9,1},{10,2},{11,3},{12,4},{13,5},{14,6},{15,7},{0,8},{1,9},... | collective-permute-start | bytes 1327112 | tf_op jit(solution)/shard_map/ppermute | solution.py:1121
  469.4 22.1 %collective-permute-start.99 = (bf16[12,48,768]{2,1,0:T(8,128)(2,1)S(1)}, bf16[12,48,768]{2,1,0:T(8,128)(2,1)S(1)}, u32[]{:S(2)}, u32[]{:S(2)}) collective-permute-start(bf16[12,48,768]{2,1,0:T(8,128)(2,1)S(1)} %get-tuple-element.1219), channel_id=1, source_target_pairs={{4,0},{5,1},{6,2},{7,3},{0,4},{1,5},{2,6},{3,7},{12,8},{13,9},{14,... | collective-permute-start | bytes 2654216 | tf_op jit(solution)/shard_map/ppermute | solution.py:1121
  469.9 20.3 %collective-permute-start.100 = (bf16[11,48,768]{2,1,0:T(8,128)(2,1)S(1)}, bf16[11,48,768]{2,1,0:T(8,128)(2,1)S(1)}, u32[]{:S(2)}, u32[]{:S(2)}) collective-permute-start(bf16[11,48,768]{2,1,0:T(8,128)(2,1)S(1)} %get-tuple-element.1220), channel_id=1, source_target_pairs={{1,0},{0,1},{3,2},{2,3},{5,4},{4,5},{7,6},{6,7},{9,8},{8,9},{11,10... | collective-permute-start | bytes 2433032 | tf_op jit(solution)/shard_map/ppermute | solution.py:1121
  471.7 16.8 %collective-permute-start.101 = (bf16[6,48,768]{2,1,0:T(8,128)(2,1)S(1)}, bf16[6,48,768]{2,1,0:T(8,128)(2,1)S(1)}, u32[]{:S(2)}, u32[]{:S(2)}) collective-permute-start(bf16[6,48,768]{2,1,0:T(8,128)(2,1)S(1)} %get-tuple-element.1221), channel_id=1, source_target_pairs={{8,0},{9,1},{10,2},{11,3},{12,4},{13,5},{14,6},{15,7},{0,8},{1,9},... | collective-permute-start | bytes 1327112 | tf_op jit(solution)/shard_map/ppermute | solution.py:1121
  492.2 21.3 %collective-permute-start.105 = (bf16[12,48,768]{2,1,0:T(8,128)(2,1)S(1)}, bf16[12,48,768]{2,1,0:T(8,128)(2,1)S(1)}, u32[]{:S(2)}, u32[]{:S(2)}) collective-permute-start(bf16[12,48,768]{2,1,0:T(8,128)(2,1)S(1)} %get-tuple-element.1254), channel_id=1, source_target_pairs={{4,0},{5,1},{6,2},{7,3},{0,4},{1,5},{2,6},{3,7},{12,8},{13,9},{14,... | collective-permute-start | bytes 2654216 | tf_op jit(solution)/shard_map/ppermute | solution.py:1121
  492.6 19.5 %collective-permute-start.106 = (bf16[11,48,768]{2,1,0:T(8,128)(2,1)S(1)}, bf16[11,48,768]{2,1,0:T(8,128)(2,1)S(1)}, u32[]{:S(2)}, u32[]{:S(2)}) collective-permute-start(bf16[11,48,768]{2,1,0:T(8,128)(2,1)S(1)} %get-tuple-element.1255), channel_id=1, source_target_pairs={{1,0},{0,1},{3,2},{2,3},{5,4},{4,5},{7,6},{6,7},{9,8},{8,9},{11,10... | collective-permute-start | bytes 2433032 | tf_op jit(solution)/shard_map/ppermute | solution.py:1121
  494.4 16.0 %collective-permute-start.107 = (bf16[6,48,768]{2,1,0:T(8,128)(2,1)S(1)}, bf16[6,48,768]{2,1,0:T(8,128)(2,1)S(1)}, u32[]{:S(2)}, u32[]{:S(2)}) collective-permute-start(bf16[6,48,768]{2,1,0:T(8,128)(2,1)S(1)} %get-tuple-element.1256), channel_id=1, source_target_pairs={{8,0},{9,1},{10,2},{11,3},{12,4},{13,5},{14,6},{15,7},{0,8},{1,9},... | collective-permute-start | bytes 1327112 | tf_op jit(solution)/shard_map/ppermute | solution.py:1121
  497.9 15.6 %collective-permute-start.109 = (f32[48,768]{1,0:T(8,128)S(1)}, f32[48,768]{1,0:T(8,128)S(1)}, u32[]{:S(2)}, u32[]{:S(2)}) collective-permute-start(f32[48,768]{1,0:T(8,128)S(1)} %bitcast.45), channel_id=1, source_target_pairs={{2,0},{3,1},{0,2},{1,3},{6,4},{7,5},{4,6},{5,7},{10,8},{11,9},{8,1... | collective-permute-start | bytes 442376 | tf_op jit(solution)/shard_map/ppermute | solution.py:1121
  514.0 15.7 %collective-permute-start.112 = (bf16[6,48,768]{2,1,0:T(8,128)(2,1)S(1)}, bf16[6,48,768]{2,1,0:T(8,128)(2,1)S(1)}, u32[]{:S(2)}, u32[]{:S(2)}) collective-permute-start(bf16[6,48,768]{2,1,0:T(8,128)(2,1)S(1)} %get-tuple-element.1288), channel_id=1, source_target_pairs={{8,0},{9,1},{10,2},{11,3},{12,4},{13,5},{14,6},{15,7},{0,8},{1,9},... | collective-permute-start | bytes 1327112 | tf_op jit(solution)/shard_map/ppermute | solution.py:1121
  519.7 25.7 %collective-permute-start.104 = (bf16[256,768]{1,0:T(8,128)(2,1)S(1)}, bf16[256,768]{1,0:T(8,128)(2,1)S(1)}, u32[]{:S(2)}, u32[]{:S(2)}) collective-permute-start(bf16[256,768]{1,0:T(8,128)(2,1)S(1)} %get-tuple-element.1236), channel_id=1, source_target_pairs={{0,0},{2,1},{1,2},{3,3},{4,4},{6,5},{5,6},{7,7},{8,8},{10,9},{9,10... | collective-permute-start | bytes 1179656 | tf_op jit(solution)/shard_map/ppermute | solution.py:1121
  (183 other events, 1577.1 us)
